TPU v7x, 512 devices: a whole 4x4x16 slice. The times are simulated.
512 devices in a mesh: dp: 16 (over x, y), expert: 32 (over z, core).
Axes of the slice: x: 4, y: 4, z: 16, core: 2. Of those that a mesh axis runs over, the one named last changes fastest.
Arguments:
- out_grad: bfloat16 [65536, 5120], P(('dp', 'expert')), may hold values from -6 to 6
- route_ids: int32 [65536, 6], P(('dp', 'expert')), may hold values from 0 to 159, as said below
- route_slots: int32 [65536, 6], P(('dp', 'expert')), may hold values from 0 to 4, as said below
- route_probs: float32 [65536, 6], P(('dp', 'expert')), may hold values from 0.03 to 0.5
- saved_pre: bfloat16 [32, 2560, 1536], P('expert', 'dp'), may hold values from -8 to 8
- w_gate: bfloat16 [32, 5120, 768], P('expert', 'dp'), may hold values from -0.078125 to 0.078125
- w_up: bfloat16 [32, 5120, 768], P('expert', 'dp'), may hold values from -0.078125 to 0.078125
- w_down: bfloat16 [32, 768, 5120], P('expert', None, 'dp'), may hold values from -0.21875 to 0.21875
Outputs:
- input_grad: bfloat16 [65536, 5120], P(('dp', 'expert'))
- grad_down: bfloat16 [32, 768, 5120], P('expert', None, 'dp')
Inputs may be any that keep to these rules, and one draw needn't show every extreme that they name: `route_ids`: each row names 6 different experts. Among the 128 rows of one device every expert is named between 4 and 5 times, and some expert exactly 5 times. `route_slots`: among the 128 rows of one device, the routes to one expert have distinct slots.
All inputs are finite; a program needn't handle non-finite values.
Results may differ from a plain program's by a relative error of at most 0.022.
Values may be sent and summed in bfloat16 or wider, within the bound.
No kernel may reach another device: no remote copies, remote signals or barrier semaphores. Data moves between devices by JAX's collectives and lax.ppermute only.
A program may use at most 128 MiB of HBM per device.

v0:
```python
import jax
import jax.numpy as jnp
from jax import lax
from jax.sharding import PartitionSpec as P


def local_grads(hidden_grad, pre_rows, hidden):
    pre = pre_rows.astype(jnp.float32)
    gate_pre = pre[:, :hidden]
    up_pre = pre[:, hidden:]
    sig = jax.nn.sigmoid(gate_pre)
    lift = gate_pre * sig
    act_rows = (lift * up_pre).astype(jnp.bfloat16)
    gate_grad = (hidden_grad * up_pre * sig * (1.0 + gate_pre * (1.0 - sig))).astype(jnp.bfloat16)
    up_grad = (hidden_grad * lift).astype(jnp.bfloat16)
    return (act_rows, gate_grad, up_grad)


def by_rows(left, right):
    return lax.dot_general(
        left, right, (((0,), (0,)), ((), ())), preferred_element_type=jnp.float32
    )


def by_cols(left, right):
    return lax.dot_general(
        left, right, (((1,), (1,)), ((), ())), preferred_element_type=jnp.float32
    )


def per_device(out_grad, route_ids, route_slots, route_probs, saved_pre, w_gate, w_up, w_down):
    n_dp = lax.axis_size("dp")
    n_exp = lax.axis_size("expert")
    tok_count = out_grad.shape[0]
    model_width = out_grad.shape[1]
    rows_own = saved_pre.shape[1]
    slot_cap = rows_own // n_exp
    hidden = w_gate.shape[2]
    slice_width = w_gate.shape[1]
    slots_all = rows_own * n_dp
    slot_index = route_ids * slot_cap + route_slots
    slot_iota = lax.broadcasted_iota(jnp.int32, (rows_own, tok_count, route_ids.shape[1]), 0)
    matches = slot_iota == slot_index[None, :, :]
    select = jnp.sum(matches.astype(jnp.float32), axis=2).astype(jnp.bfloat16)
    route_weight = jnp.sum(jnp.where(matches, route_probs[None, :, :], 0.0), axis=(1, 2))
    picked = jnp.dot(select, out_grad, preferred_element_type=jnp.float32)
    send_rows = (
        (route_weight[:, None] * picked)
        .astype(jnp.bfloat16)
        .reshape(1, n_exp, slot_cap, model_width)
    )
    arrived = lax.all_to_all(
        lax.all_to_all(send_rows, "dp", split_axis=3, concat_axis=0, tiled=True),
        "expert",
        split_axis=1,
        concat_axis=1,
        tiled=True,
    )
    arrived = arrived.reshape(slots_all, slice_width)
    pre_own = saved_pre[0]
    gate_w = w_gate[0]
    up_w = w_up[0]
    down_w = w_down[0]
    hidden_grad = lax.psum_scatter(
        by_cols(arrived, down_w).astype(jnp.bfloat16), "dp", scatter_dimension=0, tiled=True
    ).astype(jnp.float32)
    act_rows, gate_grad, up_grad = local_grads(hidden_grad, pre_own, hidden)
    piece_act = lax.all_gather(act_rows, "dp", axis=0, tiled=True)
    piece_gate = lax.all_gather(gate_grad, "dp", axis=0, tiled=True)
    piece_up = lax.all_gather(up_grad, "dp", axis=0, tiled=True)
    down_sum = by_rows(piece_act, arrived)
    slot_rows = by_cols(piece_gate, gate_w) + by_cols(piece_up, up_w)
    slot_sum = slot_rows
    down_sum, slot_sum = (down_sum, slot_sum)
    slot_grad = slot_sum.astype(jnp.bfloat16).reshape(n_dp, n_exp, slot_cap, slice_width)
    returned = lax.all_to_all(
        lax.all_to_all(slot_grad, "dp", split_axis=0, concat_axis=3, tiled=True),
        "expert",
        split_axis=1,
        concat_axis=1,
        tiled=True,
    )
    returned = returned.reshape(rows_own, model_width)
    input_grad = by_rows(select, returned).astype(jnp.bfloat16)
    grad_down = down_sum.astype(jnp.bfloat16)[None]
    return (input_grad, grad_down)


def solution(mesh):
    return jax.shard_map(
        per_device,
        mesh=mesh,
        in_specs=(
            P(("dp", "expert"), None),
            P(("dp", "expert"), None),
            P(("dp", "expert"), None),
            P(("dp", "expert"), None),
            P("expert", "dp", None),
            P("expert", "dp", None),
            P("expert", "dp", None),
            P("expert", None, "dp"),
        ),
        out_specs=(P(("dp", "expert"), None), P("expert", None, "dp")),
        check_vma=False,
    )
```

profile of v0, /device:TPU:1, one launch (start us, length us, event | category | flops | bytes accessed | tf_op | source)
XLA Modules:
  0.0 629.4 jit_solution(4874177386350825496)
XLA Ops:
  7.2 0.8 multiply_add_fusion
  8.0 0.8 convert_reduce_fusion
  9.5 2.4 reshape.21
  11.8 11.7 %copy.39 = bf16[1,32,5,5120]{1,2,0,3:T(8,128)(2,1)} copy(bf16[1,32,5,5120]{3,2,1,0:T(8,128)(2,1)} %reshape.21) | data formatting | bytes 3276800 | tf_op jit(solution)/shard_map/reshape | solution.py:50
  23.5 12.6 %reshape.27 = bf16[16,2,25600]{2,1,0:T(2,128)(2,1)S(1)} reshape(bf16[5120,1,5,32]{3,2,1,0:T(8,128)(2,1)} %bitcast.37) | data formatting | bytes 3276800
  36.1 28.1 %all_to_all.46 = bf16[16,2,25600]{2,1,0:T(2,128)(2,1)} all-to-all(bf16[16,2,25600]{2,1,0:T(2,128)(2,1)S(1)} %reshape.27), channel_id=1, replica_groups=mesh['dp'=16,'expert'=32] {'dp'}, dimensions={0} | all-to-all | bytes 3276800 | tf_op jit(solution)/shard_map/all_to_all | solution.py:53
  64.2 13.2 %reshape.28 = bf16[5120,1,5,32]{3,2,1,0:T(8,128)(2,1)} reshape(bf16[16,2,25600]{2,1,0:T(2,128)(2,1)} %all_to_all.46) | data formatting | bytes 3276800
  77.4 8.7 %copy.41 = bf16[16,32,5,320]{3,0,2,1:T(8,128)(2,1)S(1)} copy(bf16[16,32,5,320]{1,2,3,0:T(8,128)(2,1)} %bitcast.38) | data formatting | bytes 3276800 | tf_op jit(solution)/shard_map/all_to_all | solution.py:53
  86.2 114.2 %all_to_all.47 = bf16[16,32,5,320]{3,0,2,1:T(8,128)(2,1)S(1)} all-to-all(bf16[16,32,5,320]{3,0,2,1:T(8,128)(2,1)S(1)} %copy.41), channel_id=1, replica_groups=mesh['dp'=16,'expert'=32] {'expert'}, dimensions={1} | all-to-all | bytes 3276800 | tf_op jit(solution)/shard_map/all_to_all | solution.py:52
  200.3 2.4 copy.42
  202.8 4.1 reshape.22
  206.9 4.1 convolution_convert_fusion.1
  211.0 0.9 copy-done.4
  212.0 77.7 %reduce-scatter.2.cloned.1.call-done = bf16[160,768]{1,0:T(8,128)(2,1)} async-done(((bf16[2560,768]{1,0:T(8,128)(2,1)}), bf16[160,768]{1,0:T(8,128)(2,1)}) %reduce-scatter.2.cloned.1.call-update) | async-done | bytes 245776 | tf_op jit(solution)/shard_map/reduce_scatter | solution.py:64
  289.7 2.0 fusion.6
  292.6 67.6 %all-gather.4.cloned.1.call-done = bf16[2560,768]{1,0:T(8,128)(2,1)} async-done(((bf16[160,768]{1,0:T(8,128)(2,1)}), bf16[2560,768]{1,0:T(8,128)(2,1)}) %all-gather.4.cloned.1.call-update) | async-done | bytes 3932176 | tf_op jit(solution)/shard_map/all_gather | solution.py:69
  360.2 5.4 fusion.8
  365.6 63.7 %all-gather.6.cloned.1.call-done = bf16[2560,768]{1,0:T(8,128)(2,1)} async-done(((bf16[160,768]{1,0:T(8,128)(2,1)}), bf16[2560,768]{1,0:T(8,128)(2,1)}) %all-gather.6.cloned.1.call-update) | async-done | bytes 3932176 | tf_op jit(solution)/shard_map/all_gather | solution.py:70
  429.3 5.8 fusion.1
  435.1 3.6 copy.43
  438.7 2.5 reshape.23
  441.2 3.5 copy.44
  444.7 5.0 all-to-all-start.2
  450.3 25.2 %all-to-all-done.2 = bf16[16,32,5,320]{3,1,2,0:T(8,128)(2,1)S(1)} async-done(((bf16[16,32,5,320]{3,1,2,0:T(8,128)(2,1)}), bf16[16,32,5,320]{3,1,2,0:T(8,128)(2,1)S(1)}, u32[]{:S(2)}, u32[]{:S(2)}) %all-to-all-start.2) | async-done | bytes 1638432 | tf_op jit(solution)/shard_map/all_to_all | solution.py:77
  475.5 2.0 copy.49
  477.6 4.9 reshape.26
  482.5 16.4 %all-to-all-start.3 = ((bf16[1,32,5,5120]{3,2,0,1:T(8,128)(2,1)}), bf16[1,32,5,5120]{3,2,0,1:T(8,128)(2,1)}, u32[]{:S(2)}, u32[]{:S(2)}) async-start(bf16[1,32,5,5120]{3,2,0,1:T(8,128)(2,1)} %reshape.26), calls=%async_computation.4 | async-start | bytes 5242880 | tf_op jit(solution)/shard_map/all_to_all | solution.py:76
  498.9 22.1 %all-gather.8.cloned.1.call-done = bf16[2560,768]{1,0:T(8,128)(2,1)} async-done(((bf16[160,768]{1,0:T(8,128)(2,1)}), bf16[2560,768]{1,0:T(8,128)(2,1)}) %all-gather.8.cloned.1.call-update) | async-done | bytes 3932176 | tf_op jit(solution)/shard_map/all_gather | solution.py:68
  521.0 4.5 fusion.2
  525.5 93.0 %all-to-all-done.3 = bf16[1,32,5,5120]{3,2,0,1:T(8,128)(2,1)} async-done(((bf16[1,32,5,5120]{3,2,0,1:T(8,128)(2,1)}), bf16[1,32,5,5120]{3,2,0,1:T(8,128)(2,1)}, u32[]{:S(2)}, u32[]{:S(2)}) %all-to-all-start.3) | async-done | bytes 1638432 | tf_op jit(solution)/shard_map/all_to_all | solution.py:76
  618.5 2.8 reshape.24
  621.3 1.6 convolution_convert_fusion
  (25 shorter events, 2.1 us)
Async XLA Ops:
  7.2 1.7 copy-start
  7.2 282.6 %reduce-scatter.2.cloned.1.call-start = ((), (), s32[]{:S(2)}) async-start(), calls=%async_computation.5 | async-start | bytes 4177920 | tf_op jit(solution)/shard_map/reduce_scatter | solution.py:64
  202.8 4.1 copy-start.5
  206.8 4.1 copy-start.2
  210.9 1.0 copy-start.4
  210.9 149.3 %copy-start.6 = (bf16[1,320,768]{2,1,0:T(8,128)(2,1)S(1)}, bf16[1,320,768]{2,1,0:T(8,128)(2,1)}, u32[]{:S(2)}) copy-start(bf16[1,320,768]{2,1,0:T(8,128)(2,1)} %param.13) | copy-start | bytes 1474564
  211.0 149.2 %all-gather.4.cloned.1.call-start = ((), (), s32[]{:S(2)}) async-start(), calls=%async_computation.6 | async-start | bytes 4177920 | tf_op jit(solution)/shard_map/all_gather | solution.py:69
  291.8 137.5 %all-gather.6.cloned.1.call-start = ((), (), s32[]{:S(2)}) async-start(), calls=%async_computation.7 | async-start | bytes 4177920 | tf_op jit(solution)/shard_map/all_gather | solution.py:70
  292.5 136.8 %copy-start.7 = (bf16[1,320,768]{2,1,0:T(8,128)(2,1)S(1)}, bf16[1,320,768]{2,1,0:T(8,128)(2,1)}, u32[]{:S(2)}) copy-start(bf16[1,320,768]{2,1,0:T(8,128)(2,1)} %param.14) | copy-start | bytes 1474564
  444.7 30.8 %all-to-all-start.2 = ((bf16[16,32,5,320]{3,1,2,0:T(8,128)(2,1)}), bf16[16,32,5,320]{3,1,2,0:T(8,128)(2,1)S(1)}, u32[]{:S(2)}, u32[]{:S(2)}) async-start(bf16[16,32,5,320]{3,1,2,0:T(8,128)(2,1)} %copy.44), calls=%async_computation.3 | async-start | bytes 3932160 | tf_op jit(solution)/shard_map/all_to_all | solution.py:77
  449.7 71.3 %all-gather.8.cloned.1.call-start = ((), (), s32[]{:S(2)}) async-start(), calls=%async_computation.8 | async-start | bytes 4177920 | tf_op jit(solution)/shard_map/all_gather | solution.py:68
  482.5 38.6 %copy-start.3 = (bf16[2560,320]{1,0:T(8,128)(2,1)S(1)}, bf16[2560,320]{1,0:T(8,128)(2,1)}, u32[]{:S(2)}) copy-start(bf16[2560,320]{1,0:T(8,128)(2,1)} %copy-done.2) | copy-start | bytes 4915204
  482.5 136.1 %all-to-all-start.3 = ((bf16[1,32,5,5120]{3,2,0,1:T(8,128)(2,1)}), bf16[1,32,5,5120]{3,2,0,1:T(8,128)(2,1)}, u32[]{:S(2)}, u32[]{:S(2)}) async-start(bf16[1,32,5,5120]{3,2,0,1:T(8,128)(2,1)} %reshape.26), calls=%async_computation.4 | async-start | bytes 5242880 | tf_op jit(solution)/shard_map/all_to_all | solution.py:76
  521.0 101.9 %copy-start.1 = (bf16[128,5120]{1,0:T(8,128)(2,1)S(1)}, bf16[128,5120]{1,0:T(8,128)(2,1)}, u32[]{:S(2)}) copy-start(bf16[128,5120]{1,0:T(8,128)(2,1)} %param.8) | copy-start | bytes 3932164
Sparse Core Ops, SparseCore 0:
  211.1 78.6 reduce-scatter.1
  293.4 66.7 all-gather.3
  363.8 65.4 all-gather.5
  453.3 67.6 all-gather.7
where the time goes:
time: 633 us; the launch traced here: 629 us
  waiting for transfers between devices  350 us (55%)
  blocking collectives  142 us (22%)
  local copies, waits for them, and re-layouts  75.4 us (12%)
  matrix products  21.9 us (3%)
  starting transfers between devices  21.7 us (3%)
  between operations  13.9 us (2%)
    all_to_all x1, blocking collectives, per_device(): lax.all_to_all(lax.all_to_all(send_rows, 'dp', split_axis=3, concat_axis=...  114 us
    all_to_all x1, waiting for transfers between devices, per_device(): lax.all_to_all(lax.all_to_all(slot_grad, 'dp', split_axis=0, concat_axis=...  93 us
    reduce_scatter x1, waiting for transfers between devices, per_device(): lax.psum_scatter(by_cols(arrived, down_w).astype(jnp.bfloat16), 'dp', sca...  77.7 us
    all_gather x1, waiting for transfers between devices, per_device(): piece_gate = lax.all_gather(gate_grad, 'dp', axis=0, tiled=True)  67.6 us
    all_gather x1, waiting for transfers between devices, per_device(): piece_up = lax.all_gather(up_grad, 'dp', axis=0, tiled=True)  63.7 us
    all_to_all x1, blocking collectives, per_device(): lax.all_to_all(send_rows, 'dp', split_axis=3, concat_axis=0, tiled=True)  28.1 us
    unnamed x18, local copies, waits for them, and re-layouts  26.9 us
    all_to_all x1, waiting for transfers between devices, per_device(): lax.all_to_all(slot_grad, 'dp', split_axis=0, concat_axis=3, tiled=True)  25.2 us
  transfers between devices with their start and end apart: 6, of which 6 were waited for; matrix products, arithmetic and copies ran while one was open for 3% of the time, Pallas kernels for 0%

commit v1 on v0

v1 whole, which is shorter than its diff:
```python
import jax
import jax.numpy as jnp
from jax import lax
from jax.experimental import pallas as pl
from jax.experimental.pallas import tpu as pltpu
from jax.sharding import Mesh, PartitionSpec as P

BF = jnp.bfloat16
F32 = jnp.float32

N_EXP = 32
CAP = 5
TOK = 128
GX = 4
GY = 4
WIDE = 1280
HALF = 640
PIECE = 256
HID = 768
LEAD = 4
ROWS_A = N_EXP * LEAD
ROWS_B = N_EXP
VMEM_LIMIT = 40 * 1024 * 1024


def iota(shape, dim):
    return lax.broadcasted_iota(jnp.int32, shape, dim)


def nn(left, right):
    return lax.dot_general(left, right, (((1,), (0,)), ((), ())), preferred_element_type=F32)


def nt(left, right):
    return lax.dot_general(left, right, (((1,), (1,)), ((), ())), preferred_element_type=F32)


def tn(left, right):
    return lax.dot_general(left, right, (((0,), (0,)), ((), ())), preferred_element_type=F32)


def one_hot(mask):
    return jnp.where(mask, 1.0, 0.0).astype(BF)


def call(body, out_shape, flops=0, moved=0, **kwargs):
    return pl.pallas_call(
        body,
        out_shape=out_shape,
        compiler_params=pltpu.CompilerParams(vmem_limit_bytes=VMEM_LIMIT),
        cost_estimate=pl.CostEstimate(flops=flops, bytes_accessed=moved, transcendentals=0),
        **kwargs,
    )


def arr(*dims, dtype=BF):
    return jax.ShapeDtypeStruct(dims, dtype)


def match_rows(code, probs, row_code):
    hits = jnp.zeros((256, TOK), F32)
    weight = jnp.zeros((256, TOK), F32)
    for k in range(code.shape[0]):
        same = row_code == code[k : k + 1, :]
        hits = hits + jnp.where(same, 1.0, 0.0)
        if probs is not None:
            weight = weight + jnp.where(same, probs[k : k + 1, :], 0.0)
    return hits, jnp.sum(weight, axis=1, keepdims=True)


def select_a(ids_ref, slots_ref, probs):
    code = ids_ref[...] * CAP + slots_ref[...]
    row = iota((256, TOK), 0)
    hits, weight = match_rows(code, probs, (row // 8) * CAP + row % 4)
    lower = (row % 8) < 4
    return (
        jnp.concatenate([jnp.where(lower, hits, 0.0), jnp.where(lower, 0.0, hits)], axis=1).astype(BF),
        weight,
    )


def select_b(ids_ref, slots_ref, probs):
    code = ids_ref[...] * CAP + slots_ref[...]
    row = iota((256, TOK), 0)
    hits, weight = match_rows(code, probs, (row // 8) * CAP + LEAD)
    return (
        jnp.concatenate([jnp.where(row % 8 == j, hits, 0.0) for j in range(5)], axis=1).astype(BF),
        weight,
    )


def spread_a():
    row = iota((256, 256), 0)
    col = iota((256, 256), 1)
    return one_hot(col == ((row % 128) // 4) * 8 + (row // 128) * 4 + row % 4)


def collect_a():
    row = iota((256, 256), 0)
    col = iota((256, 256), 1)
    return one_hot(row == ((col % 128) // 4) * 8 + (col // 128) * 4 + col % 4)


def spread_b():
    row = iota((160, 256), 0)
    col = iota((160, 256), 1)
    return one_hot(col == (row % 32) * 8 + row // 32)


def collect_b():
    row = iota((256, 160), 0)
    col = iota((256, 160), 1)
    return one_hot(row == (col % 32) * 8 + col // 32)


def pick_kernel(og_ref, ids_ref, slots_ref, probs_ref, msg_ref):
    pick, weight = select_a(ids_ref, slots_ref, probs_ref[...])
    for g in range(GX):
        at = g * WIDE
        both = jnp.concatenate([og_ref[:, at : at + HALF], og_ref[:, at + HALF : at + WIDE]], axis=0)
        rows = nn(pick, both) * weight
        msg_ref[g * N_EXP : (g + 1) * N_EXP] = rows.reshape(N_EXP, 8, HALF).astype(BF)


def pick_last_kernel(og_ref, ids_ref, slots_ref, probs_ref, after_ref, msg_ref):
    pick, weight = select_b(ids_ref, slots_ref, probs_ref[...])
    for g in range(GX):
        at = g * WIDE
        pieces = jnp.concatenate(
            [og_ref[:, at + j * PIECE : at + (j + 1) * PIECE] for j in range(5)], axis=0
        )
        rows = nn(pick, pieces) * weight
        msg_ref[g * N_EXP : (g + 1) * N_EXP] = rows.reshape(N_EXP, 8, PIECE).astype(BF)


def order_kernel(pre_ref, out_ref):
    row = iota((160, 160), 0)
    col = iota((160, 160), 1)
    lead = (row // 4) * CAP + row % 4
    last = (row - ROWS_A) * CAP + LEAD
    moved = nn(one_hot(col == jnp.where(row < ROWS_A, lead, last)), pre_ref[...]).astype(BF)
    for g in range(GX):
        out_ref[g] = moved


def hidden_a_kernel(recv_ref, down_ref, sent_ref, part_ref):
    spread = spread_a()
    for g in range(GX):
        rows = recv_ref[g * N_EXP : (g + 1) * N_EXP].astype(F32).reshape(256, HALF).astype(BF)
        halves = nn(spread, rows).astype(BF)
        sent_ref[g * ROWS_A : (g + 1) * ROWS_A, :HALF] = halves[:ROWS_A]
        sent_ref[g * ROWS_A : (g + 1) * ROWS_A, HALF:] = halves[ROWS_A:]
    for g in range(GX):
        part_ref[g] = nn(sent_ref[g * ROWS_A : (g + 1) * ROWS_A, :], down_ref[...]).astype(BF)


def hidden_b_kernel(recv_ref, down_ref, sent_ref, part_ref):
    spread = spread_b()
    for g in range(GX):
        rows = recv_ref[g * N_EXP : (g + 1) * N_EXP].astype(F32).reshape(256, PIECE).astype(BF)
        pieces = nn(spread, rows).astype(BF)
        for j in range(5):
            sent_ref[g * ROWS_B : (g + 1) * ROWS_B, j * PIECE : (j + 1) * PIECE] = pieces[
                j * ROWS_B : (j + 1) * ROWS_B
            ]
    part = nn(sent_ref[...], down_ref[...]).astype(BF)
    for g in range(GX):
        part_ref[g] = part[g * ROWS_B : (g + 1) * ROWS_B]


def total_kernel(part_ref, out_ref):
    total = part_ref[0].astype(F32)
    for g in range(1, GX):
        total = total + part_ref[g].astype(F32)
    total = total.astype(BF)
    for g in range(GX):
        out_ref[g] = total


def unit_grads(hidden_grad, pre):
    gate_pre = pre[:, :HID].astype(F32)
    up_pre = pre[:, HID:].astype(F32)
    sig = jax.nn.sigmoid(gate_pre)
    gate_grad = (hidden_grad * up_pre * sig * (1.0 + gate_pre * (1.0 - sig))).astype(BF)
    up_grad = (hidden_grad * (gate_pre * sig)).astype(BF)
    return jnp.concatenate([gate_grad, up_grad], axis=1)


def back_a_kernel(hidden_ref, pre_ref, in_ref, msg_ref):
    collect = collect_a()
    for g in range(GX):
        grads = unit_grads(hidden_ref[g].astype(F32), pre_ref[g, :ROWS_A, :])
        rows = nt(grads, in_ref[...]).astype(BF)
        both = jnp.concatenate([rows[:, :HALF], rows[:, HALF:]], axis=0)
        msg_ref[g * N_EXP : (g + 1) * N_EXP] = nn(collect, both).reshape(N_EXP, 8, HALF).astype(BF)


def back_b_kernel(hidden_ref, pre_ref, in_ref, msg_ref):
    collect = collect_b()
    hidden = jnp.concatenate([hidden_ref[g] for g in range(GX)], axis=0).astype(F32)
    pre = jnp.concatenate([pre_ref[g, ROWS_A:, :] for g in range(GX)], axis=0)
    rows = nt(unit_grads(hidden, pre), in_ref[...]).astype(BF)
    for g in range(GX):
        own = rows[g * ROWS_B : (g + 1) * ROWS_B]
        pieces = jnp.concatenate([own[:, j * PIECE : (j + 1) * PIECE] for j in range(5)], axis=0)
        msg_ref[g * N_EXP : (g + 1) * N_EXP] = nn(collect, pieces).reshape(N_EXP, 8, PIECE).astype(BF)


def down_kernel(sent_a_ref, sent_b_ref, pre_ref, out_ref):
    def act_of(pre):
        gate_pre = pre[:, :HID].astype(F32)
        return (gate_pre * jax.nn.sigmoid(gate_pre) * pre[:, HID:].astype(F32)).astype(BF)

    act = jnp.concatenate(
        [act_of(pre_ref[g, :ROWS_A, :]) for g in range(GX)]
        + [act_of(pre_ref[g, ROWS_A:, :]) for g in range(GX)],
        axis=0,
    )
    for j in range(GY):
        at = j * 320
        sent = jnp.concatenate([sent_a_ref[...], sent_b_ref[...]], axis=0)
        if j == 0:
            full = tn(sent, act)
        out_ref[j] = full[at : at + 320].astype(BF)


def down_total_kernel(part_ref, out_ref):
    total = part_ref[0].astype(F32)
    for g in range(1, GY):
        total = total + part_ref[g].astype(F32)
    out_ref[...] = total.astype(BF)


def gather_kernel(ret_a_ref, ret_b_ref, ids_ref, slots_ref, out_ref):
    pick_a, _ = select_a(ids_ref, slots_ref, None)
    pick_b, _ = select_b(ids_ref, slots_ref, None)
    for g in range(GX):
        rows_a = ret_a_ref[g * N_EXP : (g + 1) * N_EXP].astype(F32).reshape(256, HALF).astype(BF)
        rows_b = ret_b_ref[g * N_EXP : (g + 1) * N_EXP].astype(F32).reshape(256, PIECE).astype(BF)
        halves = tn(pick_a, rows_a)
        pieces = tn(pick_b, rows_b)
        lead = jnp.concatenate([halves[:TOK], halves[TOK:]], axis=1)
        last = jnp.concatenate([pieces[j * TOK : (j + 1) * TOK] for j in range(5)], axis=1)
        out_ref[:, g * WIDE : (g + 1) * WIDE] = (lead + last).astype(BF)


def swap(value, axes):
    return lax.all_to_all(value, axes, 0, 0, tiled=True)


def per_device(out_grad, route_ids, route_slots, route_probs, saved_pre, w_gate, w_up, w_down):
    ids, slots, probs = route_ids.T, route_slots.T, route_probs.T
    peers = ("gx", "expert")
    down_w = lax.all_gather(w_down[0].T, "gy", axis=0, tiled=True)
    in_w = lax.all_gather(jnp.concatenate([w_gate[0], w_up[0]], axis=1), "gy", axis=0, tiled=True)

    msg_a = call(pick_kernel, arr(GX * N_EXP, 8, HALF), 1 << 29, 1 << 22)(out_grad, ids, slots, probs)
    recv_a = swap(msg_a, peers)
    pre = swap(call(order_kernel, arr(GX, 160, 2 * HID), 1 << 27, 1 << 21)(saved_pre[0]), "gx")

    sent_a, part_a = call(
        hidden_a_kernel, (arr(GX * ROWS_A, WIDE), arr(GX, ROWS_A, HID)), 1 << 30, 1 << 22
    )(recv_a, down_w)
    msg_b = call(
        pick_last_kernel,
        arr(GX * N_EXP, 8, PIECE),
        1 << 29,
        1 << 21,
        in_specs=[pl.BlockSpec(memory_space=pltpu.VMEM)] * 4 + [pl.BlockSpec(memory_space=pl.ANY)],
    )(out_grad, ids, slots, probs, recv_a)
    recv_b = swap(msg_b, peers)
    hidden_a = swap(call(total_kernel, arr(GX, ROWS_A, HID), 0, 1 << 21)(swap(part_a, "gx")), "gx")
    back_a = swap(
        call(back_a_kernel, arr(GX * N_EXP, 8, HALF), 1 << 31, 1 << 23)(hidden_a, pre, in_w), peers
    )

    sent_b, part_b = call(
        hidden_b_kernel, (arr(GX * ROWS_B, WIDE), arr(GX, ROWS_B, HID)), 1 << 28, 1 << 22
    )(recv_b, down_w)
    hidden_b = swap(call(total_kernel, arr(GX, ROWS_B, HID), 0, 1 << 19)(swap(part_b, "gx")), "gx")
    back_b = swap(
        call(back_b_kernel, arr(GX * N_EXP, 8, PIECE), 1 << 29, 1 << 23)(hidden_b, pre, in_w), peers
    )

    down_part = call(down_kernel, arr(GY, 320, HID), 1 << 30, 1 << 23)(sent_a, sent_b, pre)
    grad_down = call(down_total_kernel, arr(320, HID), 0, 1 << 21)(swap(down_part, "gy"))
    input_grad = call(gather_kernel, arr(TOK, GX * WIDE), 1 << 30, 1 << 22)(back_a, back_b, ids, slots)
    return (input_grad, grad_down.T[None])


def solution(mesh):
    devices = mesh.devices
    grid = Mesh(devices.reshape((GX, GY) + devices.shape[1:]), ("gx", "gy", "expert"))
    rows = P(("gx", "gy", "expert"), None)
    return jax.shard_map(
        per_device,
        mesh=grid,
        in_specs=(
            rows,
            rows,
            rows,
            rows,
            P("expert", ("gx", "gy"), None),
            P("expert", ("gx", "gy"), None),
            P("expert", ("gx", "gy"), None),
            P("expert", None, ("gx", "gy")),
        ),
        out_specs=(rows, P("expert", None, ("gx", "gy"))),
        check_vma=False,
    )
```

time: 633 us -> 372 us (0.59)
  blocking collectives: 142 us -> 0 us
  waiting for transfers between devices: 350 us -> 226 us
  starting transfers between devices: 21.7 us -> 78.4 us
  local copies, waits for them, and re-layouts: 75.4 us -> 26.4 us
  Pallas kernels: 0 us -> 22.4 us
  matrix products: 21.9 us -> 0 us
    all_gather x3 -> x2, waiting for transfers between devices: 154 us -> 0.04 us  [the longest x1 0.02 us: per_device(): down_w = lax.all_gather(w_down[0].T, 'gy', axis=0, tiled=True)]
    all_to_all x2 -> x0, blocking collectives: 142 us -> none  [the longest x1 114 us: per_device(): lax.all_to_all(lax.all_to_all(send_rows, 'dp', split_axis=3, concat_axis=...]
    all_to_all x2 -> x10, waiting for transfers between devices: 118 us -> 225 us  [swap(): return lax.all_to_all(value, axes, 0, 0, tiled=True)]
    reduce_scatter x1 -> x0, waiting for transfers between devices: 77.7 us -> none  [per_device(): lax.psum_scatter(by_cols(arrived, down_w).astype(jnp.bfloat16), 'dp', sca...]
    all_to_all x2 -> x10, starting transfers between devices: 21.4 us -> 78.4 us  [swap(): return lax.all_to_all(value, axes, 0, 0, tiled=True)]
    reshape x6 -> x0, local copies, waits for them, and re-layouts: 26.9 us -> none  [the longest x2 14 us: per_device(): send_rows = (route_weight[:, None] * picked).astype(jnp.bfloat16).reshape...]
    pallas_call x0 -> x12, Pallas kernels: none -> 22.4 us  [the longest x1 7.57 us: per_device(): call(back_a_kernel, arr(GX * N_EXP, 8, HALF), 1 << 31, 1 << 23)]
    dot_general x6 -> x0, matrix products: 21.9 us -> none  [the longest x3 15.2 us: by_cols(): lax.dot_general(left, right, (((1,), (1,)), ((), ())), preferred_element_...]
  transfers between devices with their start and end apart: 6 -> 12, of which waited for: 6 -> 10; matrix products, arithmetic and copies ran while one was open for 3% -> 1% of each run, Pallas kernels for 0% -> 5%
where the time goes in v1:
time: 372 us; the launch traced here: 370 us
  waiting for transfers between devices  226 us (61%)
  starting transfers between devices  78.4 us (21%)
  local copies, waits for them, and re-layouts  26.4 us (7%)
  Pallas kernels  22.4 us (6%)
  between operations  14.3 us (4%)
    all_to_all x10, waiting for transfers between devices, swap(): return lax.all_to_all(value, axes, 0, 0, tiled=True)  225 us
    all_to_all x10, starting transfers between devices, swap(): return lax.all_to_all(value, axes, 0, 0, tiled=True)  78.4 us
    unnamed x56, local copies, waits for them, and re-layouts  26.4 us
    pallas_call x1, Pallas kernels, per_device(): call(back_a_kernel, arr(GX * N_EXP, 8, HALF), 1 << 31, 1 << 23)  7.57 us
  transfers between devices with their start and end apart: 12, of which 10 were waited for; matrix products, arithmetic and copies ran while one was open for 1% of the time, Pallas kernels for 5%

profile of v1, /device:TPU:1, one launch (start us, length us, event | category | flops | bytes accessed | tf_op | source)
XLA Modules:
  0.0 370.1 jit_solution(6132765786018333866)
XLA Ops:
  12.3 20.4 %all-to-all-start = ((bf16[128,8,640]{2,1,0:T(8,128)(2,1)}), bf16[128,8,640]{2,1,0:T(8,128)(2,1)S(1)}, u32[]{:S(2)}, u32[]{:S(2)}) async-start(bf16[128,8,640]{2,1,0:T(8,128)(2,1)} %copy-done.9), calls=%async_computation | async-start | bytes 2621440 | tf_op jit(solution)/shard_map/all_to_all | solution.py:248
  34.7 1.3 copy-done.2
  36.1 62.1 %all-to-all-done.recv_ref.after_ref = bf16[128,8,640]{2,1,0:T(8,128)(2,1)S(1)} async-done(((bf16[128,8,640]{2,1,0:T(8,128)(2,1)}), bf16[128,8,640]{2,1,0:T(8,128)(2,1)S(1)}, u32[]{:S(2)}, u32[]{:S(2)}) %all-to-all-start) | async-done | bytes 1310752 | tf_op jit(solution)/shard_map/all_to_all | solution.py:248
  99.3 3.8 %all-to-all-start.3 = ((bf16[4,160,1536]{2,1,0:T(8,128)(2,1)}), bf16[4,160,1536]{2,1,0:T(8,128)(2,1)S(1)}, u32[]{:S(2)}, u32[]{:S(2)}) async-start(bf16[4,160,1536]{2,1,0:T(8,128)(2,1)} %copy-done.2), calls=%async_computation.3 | async-start | bytes 3932160 | tf_op jit(solution)/shard_map/all_to_all | solution.py:248
  103.1 2.4 pad_maximum_fusion
  108.3 17.6 %all-to-all-done.3.pre_ref = bf16[4,160,1536]{2,1,0:T(8,128)(2,1)S(1)} async-done(((bf16[4,160,1536]{2,1,0:T(8,128)(2,1)}), bf16[4,160,1536]{2,1,0:T(8,128)(2,1)S(1)}, u32[]{:S(2)}, u32[]{:S(2)}) %all-to-all-start.3) | async-done | bytes 1966112 | tf_op jit(solution)/shard_map/all_to_all | solution.py:248
  126.0 9.8 %all-to-all-start.5 = ((bf16[128,8,256]{2,1,0:T(8,128)(2,1)}), bf16[128,8,256]{2,1,0:T(8,128)(2,1)S(1)}, u32[]{:S(2)}, u32[]{:S(2)}) async-start(bf16[128,8,256]{2,1,0:T(8,128)(2,1)} %copy-done.10), calls=%async_computation.5 | async-start | bytes 1048576 | tf_op jit(solution)/shard_map/all_to_all | solution.py:248
  137.1 1.6 copy-done.11
  138.7 1.6 shard_map.96
  142.2 26.7 %all-to-all-done.5.recv_ref = bf16[128,8,256]{2,1,0:T(8,128)(2,1)S(1)} async-done(((bf16[128,8,256]{2,1,0:T(8,128)(2,1)}), bf16[128,8,256]{2,1,0:T(8,128)(2,1)S(1)}, u32[]{:S(2)}, u32[]{:S(2)}) %all-to-all-start.5) | async-done | bytes 524320 | tf_op jit(solution)/shard_map/all_to_all | solution.py:248
  168.9 3.6 all-to-all-start.1
  172.5 1.5 copy-done.12
  176.2 6.6 %all-to-all-done.1.part_ref = bf16[4,128,768]{2,1,0:T(8,128)(2,1)S(1)} async-done(((bf16[4,128,768]{2,1,0:T(8,128)(2,1)}), bf16[4,128,768]{2,1,0:T(8,128)(2,1)S(1)}, u32[]{:S(2)}, u32[]{:S(2)}) %all-to-all-start.1) | async-done | bytes 786464 | tf_op jit(solution)/shard_map/all_to_all | solution.py:248
  182.8 3.4 all-to-all-start.6
  187.2 4.1 %all-to-all-done.6.part_ref = bf16[4,32,768]{2,1,0:T(8,128)(2,1)S(1)} async-done(((bf16[4,32,768]{2,1,0:T(8,128)(2,1)}), bf16[4,32,768]{2,1,0:T(8,128)(2,1)S(1)}, u32[]{:S(2)}, u32[]{:S(2)}) %all-to-all-start.6) | async-done | bytes 196640 | tf_op jit(solution)/shard_map/all_to_all | solution.py:248
  191.4 3.5 all-to-all-start.2
  195.6 7.6 %all-to-all-done.2.hidden_ref = bf16[4,128,768]{2,1,0:T(8,128)(2,1)S(1)} async-done(((bf16[4,128,768]{2,1,0:T(8,128)(2,1)}), bf16[4,128,768]{2,1,0:T(8,128)(2,1)S(1)}, u32[]{:S(2)}, u32[]{:S(2)}) %all-to-all-start.2) | async-done | bytes 786464 | tf_op jit(solution)/shard_map/all_to_all | solution.py:248
  203.2 3.4 all-to-all-start.7
  207.9 1.8 shard_map.105
  209.7 1.3 copy-done.3
  211.7 4.4 %all-to-all-start.9 = ((bf16[4,320,768]{2,1,0:T(8,128)(2,1)}), bf16[4,320,768]{2,1,0:T(8,128)(2,1)}, u32[]{:S(2)}, u32[]{:S(2)}) async-start(bf16[4,320,768]{2,1,0:T(8,128)(2,1)} %copy-done.3), calls=%async_computation.9 | async-start | bytes 3932160 | tf_op jit(solution)/shard_map/all_to_all | solution.py:248
  216.2 2.1 copy-done
  218.3 2.7 shard_map.103
  221.0 13.4 %all-to-all-done.9.part_ref = bf16[4,320,768]{2,1,0:T(8,128)(2,1)} async-done(((bf16[4,320,768]{2,1,0:T(8,128)(2,1)}), bf16[4,320,768]{2,1,0:T(8,128)(2,1)}, u32[]{:S(2)}, u32[]{:S(2)}) %all-to-all-start.9) | async-done | bytes 1966112 | tf_op jit(solution)/shard_map/all_to_all | solution.py:248
  234.4 19.0 %all-to-all-start.8 = ((bf16[128,8,256]{2,1,0:T(8,128)(2,1)}), bf16[128,8,256]{2,1,0:T(8,128)(2,1)S(1)}, u32[]{:S(2)}, u32[]{:S(2)}) async-start(bf16[128,8,256]{2,1,0:T(8,128)(2,1)} %shard_map.103), calls=%async_computation.8 | async-start | bytes 1048576 | tf_op jit(solution)/shard_map/all_to_all | solution.py:248
  253.5 2.1 copy-done.1
  255.6 7.6 %shard_map.99 = bf16[128,8,640]{2,1,0:T(8,128)(2,1)} custom-call(bf16[4,128,768]{2,1,0:T(8,128)(2,1)S(1)} %all-to-all-done.2.hidden_ref, bf16[4,160,1536]{2,1,0:T(8,128)(2,1)S(1)} %all-to-all-done.3.pre_ref, bf16[1280,1536]{1,0:T(8,128)(2,1)S(1)} %copy-done.1), custom_call_target="tpu_custom_call" | custom-call | flops 2147483648 | bytes 8388608 | tf_op jit(solution)/shard_map/pallas_call | solution.py:274
  263.1 23.5 %all-to-all-done.8.ret_b_ref = bf16[128,8,256]{2,1,0:T(8,128)(2,1)S(1)} async-done(((bf16[128,8,256]{2,1,0:T(8,128)(2,1)}), bf16[128,8,256]{2,1,0:T(8,128)(2,1)S(1)}, u32[]{:S(2)}, u32[]{:S(2)}) %all-to-all-start.8) | async-done | bytes 524320 | tf_op jit(solution)/shard_map/all_to_all | solution.py:248
  287.5 7.2 %all-to-all-start.4 = ((bf16[128,8,640]{2,1,0:T(8,128)(2,1)}), bf16[128,8,640]{2,1,0:T(8,128)(2,1)S(1)}, u32[]{:S(2)}, u32[]{:S(2)}) async-start(bf16[128,8,640]{2,1,0:T(8,128)(2,1)} %shard_map.99), calls=%async_computation.4 | async-start | bytes 2621440 | tf_op jit(solution)/shard_map/all_to_all | solution.py:248
  294.6 2.6 shard_map.106
  297.2 63.0 %all-to-all-done.4.ret_a_ref = bf16[128,8,640]{2,1,0:T(8,128)(2,1)S(1)} async-done(((bf16[128,8,640]{2,1,0:T(8,128)(2,1)}), bf16[128,8,640]{2,1,0:T(8,128)(2,1)S(1)}, u32[]{:S(2)}, u32[]{:S(2)}) %all-to-all-start.4) | async-done | bytes 1310752 | tf_op jit(solution)/shard_map/all_to_all | solution.py:248
  361.2 2.1 shard_map.104
  (63 shorter events, 22.0 us)
Async XLA Ops:
  7.2 1.3 copy-start.4
  11.2 1.1 copy-start.9
  12.3 85.9 %all-to-all-start = ((bf16[128,8,640]{2,1,0:T(8,128)(2,1)}), bf16[128,8,640]{2,1,0:T(8,128)(2,1)S(1)}, u32[]{:S(2)}, u32[]{:S(2)}) async-start(bf16[128,8,640]{2,1,0:T(8,128)(2,1)} %copy-done.9), calls=%async_computation | async-start | bytes 2621440 | tf_op jit(solution)/shard_map/all_to_all | solution.py:248
  32.7 103.1 %all-gather.3.cloned.1.call-start = ((), (), s32[]{:S(2)}) async-start(), calls=%async_computation.10 | async-start | bytes 2457600 | tf_op jit(solution)/shard_map/all_gather | solution.py:254
  33.4 1.0 copy-start.18
  34.7 1.3 copy-start.2
  98.2 1.1 copy-start.6
  99.3 26.7 %all-to-all-start.3 = ((bf16[4,160,1536]{2,1,0:T(8,128)(2,1)}), bf16[4,160,1536]{2,1,0:T(8,128)(2,1)S(1)}, u32[]{:S(2)}, u32[]{:S(2)}) async-start(bf16[4,160,1536]{2,1,0:T(8,128)(2,1)} %copy-done.2), calls=%async_computation.3 | async-start | bytes 3932160 | tf_op jit(solution)/shard_map/all_to_all | solution.py:248
  103.1 2.5 copy-start.5
  103.1 2.5 copy-start.23
  103.1 2.5 copy-start.25
  103.1 2.5 copy-start.27
  103.1 113.0 %all-gather.5.cloned.1.call-start = ((), (), s32[]{:S(2)}) async-start(), calls=%async_computation.11 | async-start | bytes 4915200 | tf_op jit(solution)/shard_map/all_gather | solution.py:255
  105.6 1.3 copy-start.7
  126.0 43.0 %all-to-all-start.5 = ((bf16[128,8,256]{2,1,0:T(8,128)(2,1)}), bf16[128,8,256]{2,1,0:T(8,128)(2,1)S(1)}, u32[]{:S(2)}, u32[]{:S(2)}) async-start(bf16[128,8,256]{2,1,0:T(8,128)(2,1)} %copy-done.10), calls=%async_computation.5 | async-start | bytes 1048576 | tf_op jit(solution)/shard_map/all_to_all | solution.py:248
  135.8 1.3 copy-start.8
  137.1 1.6 copy-start.11
  140.3 1.1 copy-start.13
  168.9 13.9 %all-to-all-start.1 = ((bf16[4,128,768]{2,1,0:T(8,128)(2,1)}), bf16[4,128,768]{2,1,0:T(8,128)(2,1)S(1)}, u32[]{:S(2)}, u32[]{:S(2)}) async-start(bf16[4,128,768]{2,1,0:T(8,128)(2,1)} %copy-done.15), calls=%async_computation.1 | async-start | bytes 1572864 | tf_op jit(solution)/shard_map/all_to_all | solution.py:248
  172.5 1.5 copy-start.12
  182.8 8.5 %all-to-all-start.6 = ((bf16[4,32,768]{2,1,0:T(8,128)(2,1)}), bf16[4,32,768]{2,1,0:T(8,128)(2,1)S(1)}, u32[]{:S(2)}, u32[]{:S(2)}) async-start(bf16[4,32,768]{2,1,0:T(8,128)(2,1)} %copy-done.21), calls=%async_computation.6 | async-start | bytes 393216 | tf_op jit(solution)/shard_map/all_to_all | solution.py:248
  187.2 19.3 %copy-start.20 = (bf16[128,1280]{1,0:T(8,128)(2,1)S(1)}, bf16[128,1280]{1,0:T(8,128)(2,1)}, u32[]{:S(2)}) copy-start(bf16[128,1280]{1,0:T(8,128)(2,1)} %copy-done.19) | copy-start | bytes 983044
  191.4 11.8 %all-to-all-start.2 = ((bf16[4,128,768]{2,1,0:T(8,128)(2,1)}), bf16[4,128,768]{2,1,0:T(8,128)(2,1)S(1)}, u32[]{:S(2)}, u32[]{:S(2)}) async-start(bf16[4,128,768]{2,1,0:T(8,128)(2,1)} %shard_map.97), calls=%async_computation.2 | async-start | bytes 1572864 | tf_op jit(solution)/shard_map/all_to_all | solution.py:248
  203.2 8.5 %all-to-all-start.7 = ((bf16[4,32,768]{2,1,0:T(8,128)(2,1)}), bf16[4,32,768]{2,1,0:T(8,128)(2,1)S(1)}, u32[]{:S(2)}, u32[]{:S(2)}) async-start(bf16[4,32,768]{2,1,0:T(8,128)(2,1)} %shard_map.102), calls=%async_computation.7 | async-start | bytes 393216 | tf_op jit(solution)/shard_map/all_to_all | solution.py:248
  206.5 1.3 copy-start.14
  209.7 1.3 copy-start.3
  211.7 22.7 %all-to-all-start.9 = ((bf16[4,320,768]{2,1,0:T(8,128)(2,1)}), bf16[4,320,768]{2,1,0:T(8,128)(2,1)}, u32[]{:S(2)}, u32[]{:S(2)}) async-start(bf16[4,320,768]{2,1,0:T(8,128)(2,1)} %copy-done.3), calls=%async_computation.9 | async-start | bytes 3932160 | tf_op jit(solution)/shard_map/all_to_all | solution.py:248
  216.1 2.1 copy-start
  234.4 52.3 %all-to-all-start.8 = ((bf16[128,8,256]{2,1,0:T(8,128)(2,1)}), bf16[128,8,256]{2,1,0:T(8,128)(2,1)S(1)}, u32[]{:S(2)}, u32[]{:S(2)}) async-start(bf16[128,8,256]{2,1,0:T(8,128)(2,1)} %shard_map.103), calls=%async_computation.8 | async-start | bytes 1048576 | tf_op jit(solution)/shard_map/all_to_all | solution.py:248
  253.5 2.1 copy-start.1
  287.5 72.7 %all-to-all-start.4 = ((bf16[128,8,640]{2,1,0:T(8,128)(2,1)}), bf16[128,8,640]{2,1,0:T(8,128)(2,1)S(1)}, u32[]{:S(2)}, u32[]{:S(2)}) async-start(bf16[128,8,640]{2,1,0:T(8,128)(2,1)} %shard_map.99), calls=%async_computation.4 | async-start | bytes 2621440 | tf_op jit(solution)/shard_map/all_to_all | solution.py:248
  360.1 1.0 copy-start.17
  (8 other events, 6.0 us)
Sparse Core Ops, SparseCore 0:
  35.6 38.5 all-gather.2
  106.0 48.9 all-gather.4

commit v2 on v0

v2 whole, which is shorter than its diff:
```python
import jax
import jax.numpy as jnp
from jax import lax
from jax.experimental import pallas as pl
from jax.experimental.pallas import tpu as pltpu
from jax.sharding import Mesh, PartitionSpec as P

BF = jnp.bfloat16
F32 = jnp.float32

N_EXP = 32
CAP = 5
TOK = 128
GX = 4
GY = 4
WIDE = 1280
HALF = 640
HID = 768
ROWS = N_EXP * CAP
PAIRS = 2 * N_EXP
VMEM_LIMIT = 40 * 1024 * 1024


def iota(shape, dim):
    return lax.broadcasted_iota(jnp.int32, shape, dim)


def nn(left, right):
    return lax.dot_general(left, right, (((1,), (0,)), ((), ())), preferred_element_type=F32)


def nt(left, right):
    return lax.dot_general(left, right, (((1,), (1,)), ((), ())), preferred_element_type=F32)


def tn(left, right):
    return lax.dot_general(left, right, (((0,), (0,)), ((), ())), preferred_element_type=F32)


def one_hot(mask):
    return jnp.where(mask, 1.0, 0.0).astype(BF)


def call(body, out_shape, flops=0, moved=0, **kwargs):
    return pl.pallas_call(
        body,
        out_shape=out_shape,
        compiler_params=pltpu.CompilerParams(vmem_limit_bytes=VMEM_LIMIT),
        cost_estimate=pl.CostEstimate(flops=flops, bytes_accessed=moved, transcendentals=0),
        **kwargs,
    )


def arr(*dims, dtype=BF):
    return jax.ShapeDtypeStruct(dims, dtype)


def select(ids_ref, slots_ref, probs):
    code = ids_ref[...] * CAP + slots_ref[...]
    shape = (CAP * PAIRS, TOK)
    row = iota(shape, 0)
    row_code = ((row % PAIRS) // 2) * CAP + row // PAIRS
    hits = jnp.zeros(shape, F32)
    weight = jnp.zeros(shape, F32)
    for k in range(code.shape[0]):
        same = row_code == code[k : k + 1, :]
        hits = hits + jnp.where(same, 1.0, 0.0)
        if probs is not None:
            weight = weight + jnp.where(same, probs[k : k + 1, :], 0.0)
    lower = row % 2 == 0
    pick = jnp.concatenate([jnp.where(lower, hits, 0.0), jnp.where(lower, 0.0, hits)], axis=1)
    return pick.astype(BF), jnp.sum(weight, axis=1, keepdims=True)


def split_halves():
    row = iota((PAIRS, PAIRS), 0)
    col = iota((PAIRS, PAIRS), 1)
    return one_hot(col == (row % N_EXP) * 2 + row // N_EXP)


def join_halves():
    row = iota((PAIRS, PAIRS), 0)
    col = iota((PAIRS, PAIRS), 1)
    return one_hot(row == (col % N_EXP) * 2 + col // N_EXP)


def pick_kernel(og_ref, ids_ref, slots_ref, probs_ref, msg_ref, pick_ref, weight_ref):
    @pl.when(pl.program_id(0) == 0)
    def _():
        pick, weight = select(ids_ref, slots_ref, probs_ref[...])
        pick_ref[...] = pick
        weight_ref[...] = jnp.broadcast_to(weight, weight_ref.shape)

    both = jnp.concatenate([og_ref[:, :HALF], og_ref[:, HALF:]], axis=0)
    rows = nn(pick_ref[...], both)
    for s in range(CAP):
        span = slice(s * PAIRS, (s + 1) * PAIRS)
        own = rows[span] * weight_ref[span, :1]
        msg_ref[:, :, s * HALF : (s + 1) * HALF] = own.reshape(N_EXP, 2, HALF).astype(BF)


def hidden_kernel(at_ref, recv_ref, weights_ref, after_ref, sent_ref, *part_refs):
    split = split_halves()
    for r in range(GX):
        g = lax.rem(at_ref[0] + (GX - r), GX)
        for s in range(CAP):
            rows = recv_ref[pl.ds(g * N_EXP, N_EXP), :, s * HALF : (s + 1) * HALF]
            rows = rows.astype(F32).reshape(PAIRS, HALF).astype(BF)
            halves = nn(split, rows).astype(BF)
            at = r * ROWS + s * N_EXP
            sent_ref[at : at + N_EXP, :HALF] = halves[:N_EXP]
            sent_ref[at : at + N_EXP, HALF:] = halves[N_EXP:]
    for r in range(GX):
        part_refs[r][...] = nn(sent_ref[r * ROWS : (r + 1) * ROWS, :], weights_ref[:, :HID]).astype(BF)


def back_kernel(at_ref, hidden_0, hidden_1, hidden_2, hidden_3, gate_ref, up_ref, weights_ref, msg_ref):
    join = join_halves()
    grads = []
    for r, hidden_ref in enumerate((hidden_0, hidden_1, hidden_2, hidden_3)):
        hidden = hidden_ref[...].astype(F32)
        span = slice(r * ROWS, (r + 1) * ROWS)
        gate_grad = (hidden * gate_ref[span, :].astype(F32)).astype(BF)
        up_grad = (hidden * up_ref[span, :].astype(F32)).astype(BF)
        grads.append(jnp.concatenate([gate_grad, up_grad], axis=1))
    rows = nt(jnp.concatenate(grads, axis=0), weights_ref[:, HID:]).astype(BF)
    for r in range(GX):
        g = lax.rem(at_ref[0] + (GX - r), GX)
        for s in range(CAP):
            own = rows[r * ROWS + s * N_EXP : r * ROWS + (s + 1) * N_EXP]
            both = jnp.concatenate([own[:, :HALF], own[:, HALF:]], axis=0)
            msg_ref[pl.ds(g * N_EXP, N_EXP), :, s * HALF : (s + 1) * HALF] = (
                nn(join, both).reshape(N_EXP, 2, HALF).astype(BF)
            )


def gather_kernel(ret_ref, ids_ref, slots_ref, out_ref):
    pick, _ = select(ids_ref, slots_ref, None)
    for g in range(GX):
        rows = jnp.concatenate(
            [
                ret_ref[g * N_EXP : (g + 1) * N_EXP, :, s * HALF : (s + 1) * HALF]
                .astype(F32)
                .reshape(PAIRS, HALF)
                .astype(BF)
                for s in range(CAP)
            ],
            axis=0,
        )
        halves = tn(pick, rows).astype(BF)
        out_ref[:, g * WIDE : g * WIDE + HALF] = halves[:TOK]
        out_ref[:, g * WIDE + HALF : (g + 1) * WIDE] = halves[TOK:]


def pack_kernel(down_ref, gate_ref, up_ref, after_ref, out_ref):
    out_ref[:, :HID] = down_ref[...]
    out_ref[:, HID : 2 * HID] = gate_ref[...]
    out_ref[:, 2 * HID :] = up_ref[...]


def order_kernel(pre_ref, after_ref, out_ref):
    row = iota((ROWS, ROWS), 0)
    col = iota((ROWS, ROWS), 1)
    swap_rows = one_hot(col == (row % N_EXP) * CAP + row // N_EXP)
    out_ref[...] = nn(swap_rows, pre_ref[...]).astype(BF)


def factor_kernel(pre_0, pre_1, pre_2, pre_3, gate_ref, up_ref, act_ref):
    for r, pre_ref in enumerate((pre_0, pre_1, pre_2, pre_3)):
        for s in range(CAP):
            span = slice(s * N_EXP, (s + 1) * N_EXP)
            to = slice(r * ROWS + s * N_EXP, r * ROWS + (s + 1) * N_EXP)
            gate_pre = pre_ref[span, :HID].astype(F32)
            up_pre = pre_ref[span, HID:].astype(F32)
            sig = jax.nn.sigmoid(gate_pre)
            lift = gate_pre * sig
            gate_ref[to, :] = (up_pre * sig * (1.0 + gate_pre * (1.0 - sig))).astype(BF)
            up_ref[to, :] = lift.astype(BF)
            act_ref[to, :] = (lift * up_pre).astype(BF)


def total_kernel(part_0, part_1, part_2, part_3, out_ref):
    total = part_0[...].astype(F32) + part_1[...].astype(F32)
    out_ref[...] = (total + (part_2[...].astype(F32) + part_3[...].astype(F32))).astype(BF)


def down_kernel(sent_ref, act_ref, after_ref, out_ref):
    out_ref[...] = tn(sent_ref[...], act_ref[...]).astype(BF)


def swap(value):
    return lax.all_to_all(value, ("gx", "expert"), 0, 0, tiled=True)


def step(value, r):
    return lax.ppermute(value, "gx", [(i, (i + r) % GX) for i in range(GX)])


def per_device(out_grad, route_ids, route_slots, route_probs, saved_pre, w_gate, w_up, w_down):
    ids, slots, probs = route_ids.T, route_slots.T, route_probs.T
    at = lax.axis_index("gx").reshape(1)
    smem = pl.BlockSpec(memory_space=pltpu.SMEM)
    vmem = pl.BlockSpec(memory_space=pltpu.VMEM)

    anywhere = pl.BlockSpec(memory_space=pl.ANY)

    msg = call(
        pick_kernel,
        arr(GX * N_EXP, 2, CAP * HALF),
        1 << 29,
        1 << 22,
        grid=(GX,),
        in_specs=[pl.BlockSpec((TOK, WIDE), lambda g: (0, g))]
        + [pl.BlockSpec(ids.shape, lambda g: (0, 0))] * 3,
        out_specs=pl.BlockSpec((N_EXP, 2, CAP * HALF), lambda g: (g, 0, 0)),
        scratch_shapes=[pltpu.VMEM((CAP * PAIRS, 2 * TOK), BF), pltpu.VMEM((CAP * PAIRS, 128), F32)],
    )(out_grad, ids, slots, probs)
    recv = swap(msg)
    packed = call(
        pack_kernel, arr(320, 3 * HID), 0, 1 << 22, in_specs=[vmem] * 3 + [anywhere]
    )(w_down[0].T, w_gate[0], w_up[0], msg)
    weights = lax.all_gather(packed, "gy", axis=0, tiled=True)
    pre = call(order_kernel, arr(ROWS, 2 * HID), 1 << 27, 1 << 21, in_specs=[vmem, anywhere])(
        saved_pre[0], msg
    )
    gate_of, up_of, act = call(factor_kernel, (arr(GX * ROWS, HID),) * 3, 1 << 25, 1 << 23)(
        pre, *[step(pre, r) for r in range(1, GX)]
    )

    sent, *parts = call(
        hidden_kernel,
        (arr(GX * ROWS, WIDE),) + (arr(ROWS, HID),) * GX,
        1 << 31,
        1 << 23,
        in_specs=[smem, vmem, vmem, anywhere],
    )(at, recv, weights, act)
    hidden = call(total_kernel, arr(ROWS, HID), 0, 1 << 20)(
        parts[0], *[step(parts[GX - r], r) for r in range(1, GX)]
    )
    back = call(
        back_kernel,
        arr(GX * N_EXP, 2, CAP * HALF),
        1 << 32,
        1 << 23,
        in_specs=[smem] + [vmem] * 7,
    )(at, hidden, *[step(hidden, r) for r in range(1, GX)], gate_of, up_of, weights)
    ret = swap(back)

    down = call(
        down_kernel, arr(WIDE, HID), 1 << 31, 1 << 22, in_specs=[vmem, vmem, anywhere]
    )(sent, act, back)
    grad_down = lax.psum_scatter(down, "gy", scatter_dimension=0, tiled=True)
    input_grad = call(gather_kernel, arr(TOK, GX * WIDE), 1 << 30, 1 << 22)(ret, ids, slots)
    return (input_grad, grad_down.T[None])


def solution(mesh):
    devices = mesh.devices
    grid = Mesh(devices.reshape((GX, GY) + devices.shape[1:]), ("gx", "gy", "expert"))
    rows = P(("gx", "gy", "expert"), None)
    return jax.shard_map(
        per_device,
        mesh=grid,
        in_specs=(
            rows,
            rows,
            rows,
            rows,
            P("expert", ("gx", "gy"), None),
            P("expert", ("gx", "gy"), None),
            P("expert", ("gx", "gy"), None),
            P("expert", None, ("gx", "gy")),
        ),
        out_specs=(rows, P("expert", None, ("gx", "gy"))),
        check_vma=False,
    )
```

time: 633 us -> 265 us (0.42)
  waiting for transfers between devices: 350 us -> 153 us
  blocking collectives: 142 us -> 0 us
  local copies, waits for them, and re-layouts: 75.4 us -> 14.2 us
  starting transfers between devices: 21.7 us -> 60.7 us
  matrix products: 21.9 us -> 0 us
  Pallas kernels: 0 us -> 21.2 us
    all_gather x3 -> x1, waiting for transfers between devices: 154 us -> 0.01 us  [per_device(): weights = lax.all_gather(packed, 'gy', axis=0, tiled=True)]
    all_to_all x2 -> x0, blocking collectives: 142 us -> none  [the longest x1 114 us: per_device(): lax.all_to_all(lax.all_to_all(send_rows, 'dp', split_axis=3, concat_axis=...]
    reduce_scatter x1, waiting for transfers between devices: 77.7 us -> 0.01 us  [per_device(): grad_down = lax.psum_scatter(down, 'gy', scatter_dimension=0, tiled=True)]
    ppermute x0 -> x9, waiting for transfers between devices: none -> 44 us  [step(): return lax.ppermute(value, 'gx', [(i, (i + r) % GX) for i in range(GX)])]
    ppermute x0 -> x9, starting transfers between devices: none -> 31.7 us  [step(): return lax.ppermute(value, 'gx', [(i, (i + r) % GX) for i in range(GX)])]
    reshape x6 -> x0, local copies, waits for them, and re-layouts: 26.9 us -> none  [the longest x2 14 us: per_device(): send_rows = (route_weight[:, None] * picked).astype(jnp.bfloat16).reshape...]
    dot_general x6 -> x0, matrix products: 21.9 us -> none  [the longest x3 15.2 us: by_cols(): lax.dot_general(left, right, (((1,), (1,)), ((), ())), preferred_element_...]
    pallas_call x0 -> x9, Pallas kernels: none -> 21.2 us  [the longest x1 6.19 us: per_device(): call(back_kernel, arr(GX * N_EXP, 2, CAP * HALF), 1 << 32, 1 << 23, in_sp...]
  transfers between devices with their start and end apart: 6 -> 13, of which waited for: 6 -> 9; matrix products, arithmetic and copies ran while one was open for 3% -> 0% of each run, Pallas kernels for 0% -> 3%
where the time goes in v2:
time: 265 us; the launch traced here: 264 us
  waiting for transfers between devices  153 us (58%)
  starting transfers between devices  60.7 us (23%)
  Pallas kernels  21.2 us (8%)
  local copies, waits for them, and re-layouts  14.2 us (5%)
  between operations  14.2 us (5%)
    all_to_all x2, waiting for transfers between devices, swap(): return lax.all_to_all(value, ('gx', 'expert'), 0, 0, tiled=True)  109 us
    ppermute x9, waiting for transfers between devices, step(): return lax.ppermute(value, 'gx', [(i, (i + r) % GX) for i in range(GX)])  44 us
    ppermute x9, starting transfers between devices, step(): return lax.ppermute(value, 'gx', [(i, (i + r) % GX) for i in range(GX)])  31.7 us
    all_to_all x2, starting transfers between devices, swap(): return lax.all_to_all(value, ('gx', 'expert'), 0, 0, tiled=True)  28.8 us
    unnamed x44, local copies, waits for them, and re-layouts  14.2 us
    pallas_call x1, Pallas kernels, per_device(): call(back_kernel, arr(GX * N_EXP, 2, CAP * HALF), 1 << 32, 1 << 23, in_sp...  6.19 us
  transfers between devices with their start and end apart: 13, of which 9 were waited for; matrix products, arithmetic and copies ran while one was open for 0% of the time, Pallas kernels for 3%

profile of v2, /device:TPU:1, one launch (start us, length us, event | category | flops | bytes accessed | tf_op | source)
XLA Modules:
  0.0 263.8 jit_solution(1398876561263980958)
XLA Ops:
  7.2 1.3 copy-done.2
  10.6 3.9 %shard_map.95.after_ref = bf16[128,2,3200]{2,1,0:T(2,128)(2,1)} custom-call(bf16[128,5120]{1,0:T(8,128)(2,1)S(1)} %copy-done.2, s32[6,128]{1,0:T(8,128)S(1)} %bitcast.18, s32[6,128]{1,0:T(8,128)S(1)} %bitcast.20, f32[6,128]{1,0:T(8,128)S(1)} %bitcast.17), custom_call_target="tpu_custom_call" | custom-call | flops 536870912 | bytes 4194304 | tf_op jit(solution)/shard_map/pallas_call | solution.py:207
  14.5 1.3 shard_map.96
  15.8 20.5 %all-to-all-start = ((bf16[128,2,3200]{2,1,0:T(2,128)(2,1)}), bf16[128,2,3200]{2,1,0:T(2,128)(2,1)S(1)}, u32[]{:S(2)}, u32[]{:S(2)}) async-start(bf16[128,2,3200]{2,1,0:T(2,128)(2,1)} %shard_map.95.after_ref), calls=%async_computation | async-start | bytes 3276800 | tf_op jit(solution)/shard_map/all_to_all | solution.py:192
  36.7 5.0 %collective-permute-start.2 = (bf16[160,1536]{1,0:T(8,128)(2,1)S(1)}, bf16[160,1536]{1,0:T(8,128)(2,1)S(1)}, u32[]{:S(2)}, u32[]{:S(2)}) collective-permute-start(bf16[160,1536]{1,0:T(8,128)(2,1)S(1)} %shard_map.97.pre_0), channel_id=1, source_target_pairs={{0,384},{128,0},{256,128},{384,256},{1,385},{129,1},{257,129},{385... | collective-permute-start | bytes 1474568 | tf_op jit(solution)/shard_map/ppermute | solution.py:196
  41.7 2.0 collective-permute-start.1
  43.8 2.7 %collective-permute-start = (bf16[160,1536]{1,0:T(8,128)(2,1)S(1)}, bf16[160,1536]{1,0:T(8,128)(2,1)}, u32[]{:S(2)}, u32[]{:S(2)}) collective-permute-start(bf16[160,1536]{1,0:T(8,128)(2,1)S(1)} %shard_map.97.pre_0), channel_id=1, source_target_pairs={{0,128},{128,256},{256,384},{384,0},{1,129},{129,257},{257,385},{3... | collective-permute-start | bytes 1474568 | tf_op jit(solution)/shard_map/ppermute | solution.py:196
  46.5 22.3 %collective-permute-done.2.pre_3 = bf16[160,1536]{1,0:T(8,128)(2,1)S(1)} collective-permute-done((bf16[160,1536]{1,0:T(8,128)(2,1)S(1)}, bf16[160,1536]{1,0:T(8,128)(2,1)S(1)}, u32[]{:S(2)}, u32[]{:S(2)}) %collective-permute-start.2) | collective-permute-done | bytes 491552 | tf_op jit(solution)/shard_map/ppermute | solution.py:196
  70.3 5.2 %collective-permute-done.pre_1 = bf16[160,1536]{1,0:T(8,128)(2,1)} collective-permute-done((bf16[160,1536]{1,0:T(8,128)(2,1)S(1)}, bf16[160,1536]{1,0:T(8,128)(2,1)}, u32[]{:S(2)}, u32[]{:S(2)}) %collective-permute-start) | collective-permute-done | bytes 491552 | tf_op jit(solution)/shard_map/ppermute | solution.py:196
  75.6 1.0 copy-done.8
  76.6 1.0 copy-done.10
  77.7 1.9 shard_map.98
  81.5 34.4 %all-to-all-done.recv_ref = bf16[128,2,3200]{2,1,0:T(2,128)(2,1)S(1)} async-done(((bf16[128,2,3200]{2,1,0:T(2,128)(2,1)}), bf16[128,2,3200]{2,1,0:T(2,128)(2,1)S(1)}, u32[]{:S(2)}, u32[]{:S(2)}) %all-to-all-start) | async-done | bytes 1638432 | tf_op jit(solution)/shard_map/all_to_all | solution.py:192
  115.9 2.7 %copy-done = bf16[1280,2304]{1,0:T(8,128)(2,1)S(1)} copy-done((bf16[1280,2304]{1,0:T(8,128)(2,1)S(1)}, bf16[1280,2304]{1,0:T(8,128)(2,1)}, u32[]{:S(2)}) %copy-start) | copy-done | bytes 5898264
  118.6 2.2 shard_map.99
  120.8 1.2 copy-done.16
  122.0 3.3 %collective-permute-start.3 = (bf16[160,768]{1,0:T(8,128)(2,1)S(1)}, bf16[160,768]{1,0:T(8,128)(2,1)S(1)}, u32[]{:S(2)}, u32[]{:S(2)}) collective-permute-start(bf16[160,768]{1,0:T(8,128)(2,1)S(1)} %get-tuple-element.12), channel_id=1, source_target_pairs={{0,128},{128,256},{256,384},{384,0},{1,129},{129,257},{257,385},{3... | collective-permute-start | bytes 737288 | tf_op jit(solution)/shard_map/ppermute | solution.py:196
  125.3 3.4 %collective-permute-start.4 = (bf16[160,768]{1,0:T(8,128)(2,1)S(1)}, bf16[160,768]{1,0:T(8,128)(2,1)S(1)}, u32[]{:S(2)}, u32[]{:S(2)}) collective-permute-start(bf16[160,768]{1,0:T(8,128)(2,1)S(1)} %get-tuple-element.13), channel_id=1, source_target_pairs={{0,256},{128,384},{256,0},{384,128},{1,257},{129,385},{257,1},{385... | collective-permute-start | bytes 737288 | tf_op jit(solution)/shard_map/ppermute | solution.py:196
  128.7 4.0 %collective-permute-start.5 = (bf16[160,768]{1,0:T(8,128)(2,1)S(1)}, bf16[160,768]{1,0:T(8,128)(2,1)S(1)}, u32[]{:S(2)}, u32[]{:S(2)}) collective-permute-start(bf16[160,768]{1,0:T(8,128)(2,1)S(1)} %get-tuple-element.14), channel_id=1, source_target_pairs={{0,384},{128,0},{256,128},{384,256},{1,385},{129,1},{257,129},{385... | collective-permute-start | bytes 737288 | tf_op jit(solution)/shard_map/ppermute | solution.py:196
  132.6 4.6 %collective-permute-done.4.part_2 = bf16[160,768]{1,0:T(8,128)(2,1)S(1)} collective-permute-done((bf16[160,768]{1,0:T(8,128)(2,1)S(1)}, bf16[160,768]{1,0:T(8,128)(2,1)S(1)}, u32[]{:S(2)}, u32[]{:S(2)}) %collective-permute-start.4) | collective-permute-done | bytes 245792 | tf_op jit(solution)/shard_map/ppermute | solution.py:196
  137.3 1.9 collective-permute-done.5.part_3
  139.3 5.1 %collective-permute-start.8 = (bf16[160,768]{1,0:T(8,128)(2,1)S(1)}, bf16[160,768]{1,0:T(8,128)(2,1)S(1)}, u32[]{:S(2)}, u32[]{:S(2)}) collective-permute-start(bf16[160,768]{1,0:T(8,128)(2,1)S(1)} %shard_map.100.hidden_0), channel_id=1, source_target_pairs={{0,384},{128,0},{256,128},{384,256},{1,385},{129,1},{257,129},{385... | collective-permute-start | bytes 737288 | tf_op jit(solution)/shard_map/ppermute | solution.py:196
  144.4 4.3 %collective-permute-start.7 = (bf16[160,768]{1,0:T(8,128)(2,1)S(1)}, bf16[160,768]{1,0:T(8,128)(2,1)S(1)}, u32[]{:S(2)}, u32[]{:S(2)}) collective-permute-start(bf16[160,768]{1,0:T(8,128)(2,1)S(1)} %shard_map.100.hidden_0), channel_id=1, source_target_pairs={{0,256},{128,384},{256,0},{384,128},{1,257},{129,385},{257,1},{385... | collective-permute-start | bytes 737288 | tf_op jit(solution)/shard_map/ppermute | solution.py:196
  148.7 1.9 collective-permute-start.6
  150.9 2.7 %collective-permute-done.7.hidden_2 = bf16[160,768]{1,0:T(8,128)(2,1)S(1)} collective-permute-done((bf16[160,768]{1,0:T(8,128)(2,1)S(1)}, bf16[160,768]{1,0:T(8,128)(2,1)S(1)}, u32[]{:S(2)}, u32[]{:S(2)}) %collective-permute-start.7) | collective-permute-done | bytes 245792 | tf_op jit(solution)/shard_map/ppermute | solution.py:196
  153.5 7.1 %collective-permute-done.6.hidden_1 = bf16[160,768]{1,0:T(8,128)(2,1)S(1)} collective-permute-done((bf16[160,768]{1,0:T(8,128)(2,1)S(1)}, bf16[160,768]{1,0:T(8,128)(2,1)S(1)}, u32[]{:S(2)}, u32[]{:S(2)}) %collective-permute-start.6) | collective-permute-done | bytes 245792 | tf_op jit(solution)/shard_map/ppermute | solution.py:196
  160.6 6.2 %shard_map.101.after_ref = bf16[128,2,3200]{2,1,0:T(2,128)(2,1)} custom-call(s32[1]{0:T(128)} %bitcast.at_ref, bf16[160,768]{1,0:T(8,128)(2,1)S(1)} %shard_map.100.hidden_0, bf16[160,768]{1,0:T(8,128)(2,1)S(1)} %collective-permute-done.6.hidden_1, bf16[160,768]{1,0:T(8,128)(2,1)S(1)} %collective-permute-done.7.hidden_2, ...), custom_call_target="tpu_custom_call" | custom-call | flops 4294967296 | bytes 8388608 | tf_op jit(solution)/shard_map/pallas_call | solution.py:240
  166.8 8.3 %all-to-all-start.1 = ((bf16[128,2,3200]{2,1,0:T(2,128)(2,1)}), bf16[128,2,3200]{2,1,0:T(2,128)(2,1)S(1)}, u32[]{:S(2)}, u32[]{:S(2)}) async-start(bf16[128,2,3200]{2,1,0:T(2,128)(2,1)} %shard_map.101.after_ref), calls=%async_computation.1 | async-start | bytes 3276800 | tf_op jit(solution)/shard_map/all_to_all | solution.py:192
  175.2 1.4 copy-done.17
  176.6 3.1 %shard_map.103 = bf16[1280,768]{1,0:T(8,128)(2,1)} custom-call(bf16[640,1280]{1,0:T(8,128)(2,1)S(1)} %copy-done.17, bf16[640,768]{1,0:T(8,128)(2,1)S(1)} %get-tuple-element.10.after_ref.act_ref, bf16[128,2,3200]{2,1,0:T(2,128)(2,1)} %shard_map.101.after_ref), custom_call_target="tpu_custom_call" | custom-call | flops 2147483648 | bytes 4194304 | tf_op jit(solution)/shard_map/pallas_call | solution.py:249
  179.7 75.0 %all-to-all-done.1.ret_ref = bf16[128,2,3200]{2,1,0:T(2,128)(2,1)S(1)} async-done(((bf16[128,2,3200]{2,1,0:T(2,128)(2,1)}), bf16[128,2,3200]{2,1,0:T(2,128)(2,1)S(1)}, u32[]{:S(2)}, u32[]{:S(2)}) %all-to-all-start.1) | async-done | bytes 1638432 | tf_op jit(solution)/shard_map/all_to_all | solution.py:192
  254.7 2.3 shard_map.102
  (49 shorter events, 6.3 us)
Async XLA Ops:
  7.2 108.8 %all-gather.2.cloned.1.call-start = ((), (), s32[]{:S(2)}) async-start(), calls=%async_computation.3 | async-start | bytes 7372800 | tf_op jit(solution)/shard_map/all_gather | solution.py:222
  7.2 1.3 copy-start.2
  10.6 3.9 %copy-start.4 = (bf16[1,768,320]{1,2,0:T(8,128)(2,1)S(1)}, bf16[1,768,320]{1,2,0:T(8,128)(2,1)}, u32[]{:S(2)}) copy-start(bf16[1,768,320]{1,2,0:T(8,128)(2,1)} %param.15) | copy-start | bytes 1474564
  10.6 3.9 %copy-start.5 = (bf16[1,320,768]{2,1,0:T(8,128)(2,1)S(1)}, bf16[1,320,768]{2,1,0:T(8,128)(2,1)}, u32[]{:S(2)}) copy-start(bf16[1,320,768]{2,1,0:T(8,128)(2,1)} %param.13) | copy-start | bytes 1474564
  10.6 3.9 %copy-start.6 = (bf16[1,320,768]{2,1,0:T(8,128)(2,1)S(1)}, bf16[1,320,768]{2,1,0:T(8,128)(2,1)}, u32[]{:S(2)}) copy-start(bf16[1,320,768]{2,1,0:T(8,128)(2,1)} %param.14) | copy-start | bytes 1474564
  15.8 20.6 %copy-start.3 = (bf16[1,160,1536]{2,1,0:T(8,128)(2,1)S(1)}, bf16[1,160,1536]{2,1,0:T(8,128)(2,1)}, u32[]{:S(2)}) copy-start(bf16[1,160,1536]{2,1,0:T(8,128)(2,1)} %param.12) | copy-start | bytes 1474564
  15.8 100.1 %all-to-all-start = ((bf16[128,2,3200]{2,1,0:T(2,128)(2,1)}), bf16[128,2,3200]{2,1,0:T(2,128)(2,1)S(1)}, u32[]{:S(2)}, u32[]{:S(2)}) async-start(bf16[128,2,3200]{2,1,0:T(2,128)(2,1)} %shard_map.95.after_ref), calls=%async_computation | async-start | bytes 3276800 | tf_op jit(solution)/shard_map/all_to_all | solution.py:192
  36.7 32.1 %collective-permute-start.2 = (bf16[160,1536]{1,0:T(8,128)(2,1)S(1)}, bf16[160,1536]{1,0:T(8,128)(2,1)S(1)}, u32[]{:S(2)}, u32[]{:S(2)}) collective-permute-start(bf16[160,1536]{1,0:T(8,128)(2,1)S(1)} %shard_map.97.pre_0), channel_id=1, source_target_pairs={{0,384},{128,0},{256,128},{384,256},{1,385},{129,1},{257,129},{385... | collective-permute-start | bytes 1474568 | tf_op jit(solution)/shard_map/ppermute | solution.py:196
  41.7 27.8 %collective-permute-start.1 = (bf16[160,1536]{1,0:T(8,128)(2,1)S(1)}, bf16[160,1536]{1,0:T(8,128)(2,1)S(1)}, u32[]{:S(2)}, u32[]{:S(2)}) collective-permute-start(bf16[160,1536]{1,0:T(8,128)(2,1)S(1)} %shard_map.97.pre_0), channel_id=1, source_target_pairs={{0,256},{128,384},{256,0},{384,128},{1,257},{129,385},{257,1},{385... | collective-permute-start | bytes 1474568 | tf_op jit(solution)/shard_map/ppermute | solution.py:196
  43.8 31.8 %collective-permute-start = (bf16[160,1536]{1,0:T(8,128)(2,1)S(1)}, bf16[160,1536]{1,0:T(8,128)(2,1)}, u32[]{:S(2)}, u32[]{:S(2)}) collective-permute-start(bf16[160,1536]{1,0:T(8,128)(2,1)S(1)} %shard_map.97.pre_0), channel_id=1, source_target_pairs={{0,128},{128,256},{256,384},{384,0},{1,129},{129,257},{257,385},{3... | collective-permute-start | bytes 1474568 | tf_op jit(solution)/shard_map/ppermute | solution.py:196
  68.8 0.8 copy-start.7
  69.6 0.8 copy-start.9
  75.6 1.0 copy-start.8
  76.6 1.0 copy-start.10
  79.6 0.9 copy-start.18
  80.6 0.9 copy-start.20
  115.9 2.7 %copy-start = (bf16[1280,2304]{1,0:T(8,128)(2,1)S(1)}, bf16[1280,2304]{1,0:T(8,128)(2,1)}, u32[]{:S(2)}) copy-start(bf16[1280,2304]{1,0:T(8,128)(2,1)} %all-gather.2.cloned.1.call-done.weights_ref) | copy-start | bytes 17694724
  118.6 42.0 %copy-start.1 = (bf16[1280,2304]{1,0:T(8,128)(2,1)S(1)}, bf16[1280,2304]{1,0:T(8,128)(2,1)}, u32[]{:S(2)}) copy-start(bf16[1280,2304]{1,0:T(8,128)(2,1)} %all-gather.2.cloned.1.call-done.weights_ref) | copy-start | bytes 17694724
  118.6 42.0 %copy-start.19 = (bf16[640,768]{1,0:T(8,128)(2,1)S(1)}, bf16[640,768]{1,0:T(8,128)(2,1)}, u32[]{:S(2)}) copy-start(bf16[640,768]{1,0:T(8,128)(2,1)} %copy-done.18) | copy-start | bytes 2949124
  118.6 42.0 %copy-start.21 = (bf16[640,768]{1,0:T(8,128)(2,1)S(1)}, bf16[640,768]{1,0:T(8,128)(2,1)}, u32[]{:S(2)}) copy-start(bf16[640,768]{1,0:T(8,128)(2,1)} %copy-done.20) | copy-start | bytes 2949124
  120.8 1.2 copy-start.16
  122.0 10.6 %collective-permute-start.3 = (bf16[160,768]{1,0:T(8,128)(2,1)S(1)}, bf16[160,768]{1,0:T(8,128)(2,1)S(1)}, u32[]{:S(2)}, u32[]{:S(2)}) collective-permute-start(bf16[160,768]{1,0:T(8,128)(2,1)S(1)} %get-tuple-element.12), channel_id=1, source_target_pairs={{0,128},{128,256},{256,384},{384,0},{1,129},{129,257},{257,385},{3... | collective-permute-start | bytes 737288 | tf_op jit(solution)/shard_map/ppermute | solution.py:196
  125.3 12.0 %collective-permute-start.4 = (bf16[160,768]{1,0:T(8,128)(2,1)S(1)}, bf16[160,768]{1,0:T(8,128)(2,1)S(1)}, u32[]{:S(2)}, u32[]{:S(2)}) collective-permute-start(bf16[160,768]{1,0:T(8,128)(2,1)S(1)} %get-tuple-element.13), channel_id=1, source_target_pairs={{0,256},{128,384},{256,0},{384,128},{1,257},{129,385},{257,1},{385... | collective-permute-start | bytes 737288 | tf_op jit(solution)/shard_map/ppermute | solution.py:196
  128.7 10.5 %collective-permute-start.5 = (bf16[160,768]{1,0:T(8,128)(2,1)S(1)}, bf16[160,768]{1,0:T(8,128)(2,1)S(1)}, u32[]{:S(2)}, u32[]{:S(2)}) collective-permute-start(bf16[160,768]{1,0:T(8,128)(2,1)S(1)} %get-tuple-element.14), channel_id=1, source_target_pairs={{0,384},{128,0},{256,128},{384,256},{1,385},{129,1},{257,129},{385... | collective-permute-start | bytes 737288 | tf_op jit(solution)/shard_map/ppermute | solution.py:196
  139.3 11.6 %collective-permute-start.8 = (bf16[160,768]{1,0:T(8,128)(2,1)S(1)}, bf16[160,768]{1,0:T(8,128)(2,1)S(1)}, u32[]{:S(2)}, u32[]{:S(2)}) collective-permute-start(bf16[160,768]{1,0:T(8,128)(2,1)S(1)} %shard_map.100.hidden_0), channel_id=1, source_target_pairs={{0,384},{128,0},{256,128},{384,256},{1,385},{129,1},{257,129},{385... | collective-permute-start | bytes 737288 | tf_op jit(solution)/shard_map/ppermute | solution.py:196
  144.4 9.2 %collective-permute-start.7 = (bf16[160,768]{1,0:T(8,128)(2,1)S(1)}, bf16[160,768]{1,0:T(8,128)(2,1)S(1)}, u32[]{:S(2)}, u32[]{:S(2)}) collective-permute-start(bf16[160,768]{1,0:T(8,128)(2,1)S(1)} %shard_map.100.hidden_0), channel_id=1, source_target_pairs={{0,256},{128,384},{256,0},{384,128},{1,257},{129,385},{257,1},{385... | collective-permute-start | bytes 737288 | tf_op jit(solution)/shard_map/ppermute | solution.py:196
  148.7 11.9 %collective-permute-start.6 = (bf16[160,768]{1,0:T(8,128)(2,1)S(1)}, bf16[160,768]{1,0:T(8,128)(2,1)S(1)}, u32[]{:S(2)}, u32[]{:S(2)}) collective-permute-start(bf16[160,768]{1,0:T(8,128)(2,1)S(1)} %shard_map.100.hidden_0), channel_id=1, source_target_pairs={{0,128},{128,256},{256,384},{384,0},{1,129},{129,257},{257,385},{3... | collective-permute-start | bytes 737288 | tf_op jit(solution)/shard_map/ppermute | solution.py:196
  166.8 87.9 %all-to-all-start.1 = ((bf16[128,2,3200]{2,1,0:T(2,128)(2,1)}), bf16[128,2,3200]{2,1,0:T(2,128)(2,1)S(1)}, u32[]{:S(2)}, u32[]{:S(2)}) async-start(bf16[128,2,3200]{2,1,0:T(2,128)(2,1)} %shard_map.101.after_ref), calls=%async_computation.1 | async-start | bytes 3276800 | tf_op jit(solution)/shard_map/all_to_all | solution.py:192
  175.1 81.8 %reduce-scatter.2.cloned.1.call-start = ((), (), s32[]{:S(2)}) async-start(), calls=%async_computation.4 | async-start | bytes 2457600 | tf_op jit(solution)/shard_map/reduce_scatter | solution.py:252
  175.2 1.4 copy-start.17
  179.7 75.0 %copy-start.13 = (s32[128,6]{0,1:T(8,128)S(1)}, s32[128,6]{0,1:T(8,128)}, u32[]{:S(2)}) copy-start(s32[128,6]{0,1:T(8,128)} %param.9) | copy-start | bytes 9220
  179.7 75.0 %copy-start.15 = (s32[128,6]{0,1:T(8,128)S(1)}, s32[128,6]{0,1:T(8,128)}, u32[]{:S(2)}) copy-start(s32[128,6]{0,1:T(8,128)} %param.10) | copy-start | bytes 9220
  (3 other events, 2.1 us)
Sparse Core Ops, SparseCore 0:
  15.9 75.3 all-gather.1
  179.8 37.4 reduce-scatter.1

commit v3 on v2

--- a/solution.py
+++ b/solution.py
@@ -18,7 +18,8 @@
 HID = 768
 ROWS = N_EXP * CAP
 PAIRS = 2 * N_EXP
-VMEM_LIMIT = 40 * 1024 * 1024
+VMEM_LIMIT = 20 * 1024 * 1024
+VMEM_MOST = 60 * 1024 * 1024
 
 
 def iota(shape, dim):
@@ -41,11 +42,11 @@
     return jnp.where(mask, 1.0, 0.0).astype(BF)
 
 
-def call(body, out_shape, flops=0, moved=0, **kwargs):
+def call(body, out_shape, flops=0, moved=0, limit=VMEM_LIMIT, **kwargs):
     return pl.pallas_call(
         body,
         out_shape=out_shape,
-        compiler_params=pltpu.CompilerParams(vmem_limit_bytes=VMEM_LIMIT),
+        compiler_params=pltpu.CompilerParams(vmem_limit_bytes=limit),
         cost_estimate=pl.CostEstimate(flops=flops, bytes_accessed=moved, transcendentals=0),
         **kwargs,
     )
@@ -84,22 +85,61 @@
     return one_hot(row == (col % N_EXP) * 2 + col // N_EXP)
 
 
-def pick_kernel(og_ref, ids_ref, slots_ref, probs_ref, msg_ref, pick_ref, weight_ref):
-    @pl.when(pl.program_id(0) == 0)
-    def _():
-        pick, weight = select(ids_ref, slots_ref, probs_ref[...])
-        pick_ref[...] = pick
-        weight_ref[...] = jnp.broadcast_to(weight, weight_ref.shape)
-
-    both = jnp.concatenate([og_ref[:, :HALF], og_ref[:, HALF:]], axis=0)
-    rows = nn(pick_ref[...], both)
-    for s in range(CAP):
-        span = slice(s * PAIRS, (s + 1) * PAIRS)
-        own = rows[span] * weight_ref[span, :1]
-        msg_ref[:, :, s * HALF : (s + 1) * HALF] = own.reshape(N_EXP, 2, HALF).astype(BF)
-
-
-def hidden_kernel(at_ref, recv_ref, weights_ref, after_ref, sent_ref, *part_refs):
+def pick_kernel(
+    og_any, ids_any, slots_any, probs_any, down_any, gate_any, up_any,
+    msg_any, packed_any,
+    og_ref, ids_ref, slots_ref, probs_ref, msg_ref, og_sem, in_sem, out_sem, pack_sem,
+):
+    small = [
+        pltpu.make_async_copy(src, dst, in_sem.at[i])
+        for i, (src, dst) in enumerate(((ids_any, ids_ref), (slots_any, slots_ref), (probs_any, probs_ref)))
+    ]
+    wide = [
+        pltpu.make_async_copy(og_any.at[:, pl.ds(g * WIDE, WIDE)], og_ref.at[g], og_sem.at[g])
+        for g in range(GX)
+    ]
+    packs = [
+        pltpu.make_async_copy(src, packed_any.at[:, pl.ds(i * HID, HID)], pack_sem.at[i])
+        for i, src in enumerate((down_any, gate_any, up_any))
+    ]
+    for copy in small + wide + packs:
+        copy.start()
+    for copy in small:
+        copy.wait()
+    pick, weight = select(ids_ref, slots_ref, probs_ref[...])
+    outs = []
+    for g in range(GX):
+        wide[g].wait()
+        both = jnp.concatenate([og_ref[g, :, :HALF], og_ref[g, :, HALF:]], axis=0)
+        rows = nn(pick, both) * weight
+        for s in range(CAP):
+            own = rows[s * PAIRS : (s + 1) * PAIRS].reshape(N_EXP, 2, HALF).astype(BF)
+            msg_ref[g * N_EXP : (g + 1) * N_EXP, :, s * HALF : (s + 1) * HALF] = own
+        span = pl.ds(g * N_EXP, N_EXP)
+        outs.append(pltpu.make_async_copy(msg_ref.at[span], msg_any.at[span], out_sem.at[g]))
+        outs[-1].start()
+    for copy in outs + packs:
+        copy.wait()
+
+
+def arrange_kernel(at_ref, own_ref, less_ref, more_ref, far_low_ref, far_high_ref, down_ref, in_ref):
+    def put(ref, away, start):
+        rows = ref.shape[0]
+        q = lax.rem(at_ref[1] + away, GY)
+        to = pl.ds(pl.multiple_of(q * 320 + start, 32), rows)
+        down_ref[to, :] = ref[:, :HID]
+        in_ref[to, :] = ref[:, HID:]
+
+    put(own_ref, 0, 0)
+    put(less_ref, GY - 1, 0)
+    put(more_ref, 1, 0)
+    put(far_low_ref, 2, 0)
+    put(far_high_ref, 2, 160)
+
+
+def hidden_kernel(at_ref, recv_ref, down_any, after_ref, sent_ref, part_ref, down_ref, sem):
+    fetch = pltpu.make_async_copy(down_any, down_ref, sem)
+    fetch.start()
     split = split_halves()
     for r in range(GX):
         g = lax.rem(at_ref[0] + (GX - r), GX)
@@ -110,20 +150,22 @@
             at = r * ROWS + s * N_EXP
             sent_ref[at : at + N_EXP, :HALF] = halves[:N_EXP]
             sent_ref[at : at + N_EXP, HALF:] = halves[N_EXP:]
+    fetch.wait()
     for r in range(GX):
-        part_refs[r][...] = nn(sent_ref[r * ROWS : (r + 1) * ROWS, :], weights_ref[:, :HID]).astype(BF)
-
-
-def back_kernel(at_ref, hidden_0, hidden_1, hidden_2, hidden_3, gate_ref, up_ref, weights_ref, msg_ref):
+        g = lax.rem(at_ref[0] + (GX - r), GX)
+        part_ref[g] = nn(sent_ref[r * ROWS : (r + 1) * ROWS, :], down_ref[...]).astype(BF)
+
+
+def back_kernel(at_ref, hidden_ref, gate_ref, up_ref, in_ref, msg_ref):
     join = join_halves()
     grads = []
-    for r, hidden_ref in enumerate((hidden_0, hidden_1, hidden_2, hidden_3)):
-        hidden = hidden_ref[...].astype(F32)
+    for r in range(GX):
+        hidden = hidden_ref[lax.rem(at_ref[0] + (GX - r), GX)].astype(F32)
         span = slice(r * ROWS, (r + 1) * ROWS)
         gate_grad = (hidden * gate_ref[span, :].astype(F32)).astype(BF)
         up_grad = (hidden * up_ref[span, :].astype(F32)).astype(BF)
         grads.append(jnp.concatenate([gate_grad, up_grad], axis=1))
-    rows = nt(jnp.concatenate(grads, axis=0), weights_ref[:, HID:]).astype(BF)
+    rows = nt(jnp.concatenate(grads, axis=0), in_ref[...]).astype(BF)
     for r in range(GX):
         g = lax.rem(at_ref[0] + (GX - r), GX)
         for s in range(CAP):
@@ -152,12 +194,6 @@
         out_ref[:, g * WIDE + HALF : (g + 1) * WIDE] = halves[TOK:]
 
 
-def pack_kernel(down_ref, gate_ref, up_ref, after_ref, out_ref):
-    out_ref[:, :HID] = down_ref[...]
-    out_ref[:, HID : 2 * HID] = gate_ref[...]
-    out_ref[:, 2 * HID :] = up_ref[...]
-
-
 def order_kernel(pre_ref, after_ref, out_ref):
     row = iota((ROWS, ROWS), 0)
     col = iota((ROWS, ROWS), 1)
@@ -179,77 +215,114 @@
             act_ref[to, :] = (lift * up_pre).astype(BF)
 
 
-def total_kernel(part_0, part_1, part_2, part_3, out_ref):
+def total_kernel(part_ref, out_ref):
+    total = (part_ref[0].astype(F32) + part_ref[1].astype(F32)) + (
+        part_ref[2].astype(F32) + part_ref[3].astype(F32)
+    )
+    total = total.astype(BF)
+    for g in range(GX):
+        out_ref[g] = total
+
+
+def down_kernel(at_ref, sent_ref, act_ref, after_ref, out_0, out_1, out_2, out_3, full_ref):
+    full_ref[...] = tn(sent_ref[...], act_ref[...]).astype(BF)
+    for r, out_ref in enumerate((out_0, out_1, out_2, out_3)):
+        q = lax.rem(at_ref[1] + r, GY)
+        out_ref[...] = full_ref[pl.ds(pl.multiple_of(q * 320, 64), 320), :]
+
+
+def down_total_kernel(part_0, part_1, part_2, part_3, out_ref):
     total = part_0[...].astype(F32) + part_1[...].astype(F32)
     out_ref[...] = (total + (part_2[...].astype(F32) + part_3[...].astype(F32))).astype(BF)
 
 
-def down_kernel(sent_ref, act_ref, after_ref, out_ref):
-    out_ref[...] = tn(sent_ref[...], act_ref[...]).astype(BF)
-
-
 def swap(value):
     return lax.all_to_all(value, ("gx", "expert"), 0, 0, tiled=True)
 
 
-def step(value, r):
-    return lax.ppermute(value, "gx", [(i, (i + r) % GX) for i in range(GX)])
+def swap_gx(value):
+    return lax.all_to_all(value, "gx", 0, 0, tiled=True)
+
+
+def step(value, axis, r):
+    return lax.ppermute(value, axis, [(i, (i + r) % 4) for i in range(4)])
 
 
 def per_device(out_grad, route_ids, route_slots, route_probs, saved_pre, w_gate, w_up, w_down):
     ids, slots, probs = route_ids.T, route_slots.T, route_probs.T
-    at = lax.axis_index("gx").reshape(1)
+    at = jnp.stack([lax.axis_index("gx"), lax.axis_index("gy")])
     smem = pl.BlockSpec(memory_space=pltpu.SMEM)
     vmem = pl.BlockSpec(memory_space=pltpu.VMEM)
-
     anywhere = pl.BlockSpec(memory_space=pl.ANY)
 
-    msg = call(
+    msg, packed = call(
         pick_kernel,
-        arr(GX * N_EXP, 2, CAP * HALF),
+        (arr(GX * N_EXP, 2, CAP * HALF), arr(320, 3 * HID)),
         1 << 29,
-        1 << 22,
-        grid=(GX,),
-        in_specs=[pl.BlockSpec((TOK, WIDE), lambda g: (0, g))]
-        + [pl.BlockSpec(ids.shape, lambda g: (0, 0))] * 3,
-        out_specs=pl.BlockSpec((N_EXP, 2, CAP * HALF), lambda g: (g, 0, 0)),
-        scratch_shapes=[pltpu.VMEM((CAP * PAIRS, 2 * TOK), BF), pltpu.VMEM((CAP * PAIRS, 128), F32)],
-    )(out_grad, ids, slots, probs)
+        1 << 23,
+        VMEM_MOST,
+        in_specs=[anywhere] * 7,
+        out_specs=(anywhere, anywhere),
+        scratch_shapes=[
+            pltpu.VMEM((GX, TOK, WIDE), BF),
+            pltpu.VMEM(ids.shape, jnp.int32),
+            pltpu.VMEM(ids.shape, jnp.int32),
+            pltpu.VMEM(ids.shape, F32),
+            pltpu.VMEM((GX * N_EXP, 2, CAP * HALF), BF),
+            pltpu.SemaphoreType.DMA((GX,)),
+            pltpu.SemaphoreType.DMA((3,)),
+            pltpu.SemaphoreType.DMA((GX,)),
+            pltpu.SemaphoreType.DMA((3,)),
+        ],
+    )(out_grad, ids, slots, probs, w_down[0].T, w_gate[0], w_up[0])
     recv = swap(msg)
-    packed = call(
-        pack_kernel, arr(320, 3 * HID), 0, 1 << 22, in_specs=[vmem] * 3 + [anywhere]
-    )(w_down[0].T, w_gate[0], w_up[0], msg)
-    weights = lax.all_gather(packed, "gy", axis=0, tiled=True)
+
+    less, more = step(packed, "gy", 1), step(packed, "gy", 3)
+    far = (step(less[:160], "gy", 1), step(more[160:], "gy", 3))
+    down_w, in_w = call(
+        arrange_kernel,
+        (arr(WIDE, HID), arr(WIDE, 2 * HID)),
+        0,
+        1 << 24,
+        in_specs=[smem] + [vmem] * 5,
+    )(at, packed, less, more, *far)
     pre = call(order_kernel, arr(ROWS, 2 * HID), 1 << 27, 1 << 21, in_specs=[vmem, anywhere])(
         saved_pre[0], msg
     )
     gate_of, up_of, act = call(factor_kernel, (arr(GX * ROWS, HID),) * 3, 1 << 25, 1 << 23)(
-        pre, *[step(pre, r) for r in range(1, GX)]
-    )
-
-    sent, *parts = call(
+        pre, *[step(pre, "gx", r) for r in range(1, GX)]
+    )
+
+    sent, part = call(
         hidden_kernel,
-        (arr(GX * ROWS, WIDE),) + (arr(ROWS, HID),) * GX,
+        (arr(GX * ROWS, WIDE), arr(GX, ROWS, HID)),
         1 << 31,
         1 << 23,
-        in_specs=[smem, vmem, vmem, anywhere],
-    )(at, recv, weights, act)
-    hidden = call(total_kernel, arr(ROWS, HID), 0, 1 << 20)(
-        parts[0], *[step(parts[GX - r], r) for r in range(1, GX)]
-    )
+        VMEM_MOST,
+        in_specs=[smem, vmem, anywhere, anywhere],
+        scratch_shapes=[pltpu.VMEM((WIDE, HID), BF), pltpu.SemaphoreType.DMA],
+    )(at, recv, down_w, act)
+    hidden = swap_gx(call(total_kernel, arr(GX, ROWS, HID), 0, 1 << 21)(swap_gx(part)))
     back = call(
         back_kernel,
         arr(GX * N_EXP, 2, CAP * HALF),
         1 << 32,
         1 << 23,
-        in_specs=[smem] + [vmem] * 7,
-    )(at, hidden, *[step(hidden, r) for r in range(1, GX)], gate_of, up_of, weights)
+        in_specs=[smem] + [vmem] * 4,
+    )(at, hidden, gate_of, up_of, in_w)
     ret = swap(back)
 
-    down = call(
-        down_kernel, arr(WIDE, HID), 1 << 31, 1 << 22, in_specs=[vmem, vmem, anywhere]
-    )(sent, act, back)
-    grad_down = lax.psum_scatter(down, "gy", scatter_dimension=0, tiled=True)
+    downs = call(
+        down_kernel,
+        (arr(320, HID),) * GY,
+        1 << 31,
+        1 << 22,
+        in_specs=[smem, vmem, vmem, anywhere],
+        scratch_shapes=[pltpu.VMEM((WIDE, HID), BF)],
+    )(at, sent, act, back)
+    grad_down = call(down_total_kernel, arr(320, HID), 0, 1 << 21)(
+        downs[0], *[step(downs[r], "gy", r) for r in range(1, GY)]
+    )
     input_grad = call(gather_kernel, arr(TOK, GX * WIDE), 1 << 30, 1 << 22)(ret, ids, slots)
     return (input_grad, grad_down.T[None])
 

time: 265 us -> 304 us (1.15)
  Pallas kernels: 21.2 us -> 69 us
  waiting for transfers between devices: 153 us -> 117 us
  blocking collectives: 0 us -> 33.8 us
  between operations: 14.2 us -> 0.94 us
  starting transfers between devices: 60.7 us -> 71 us
    all_to_all x2, waiting for transfers between devices: 109 us -> 46.4 us  [swap(): return lax.all_to_all(value, ('gx', 'expert'), 0, 0, tiled=True)]
    pallas_call x5 -> x6, Pallas kernels: 10.6 us -> 56.7 us  [the longest x1 45.9 us: per_device(): call(pick_kernel, (arr(GX * N_EXP, 2, CAP * HALF), arr(320, 3 * HID)), 1...]
    all_to_all x0 -> x2, blocking collectives: none -> 33.8 us  [swap_gx(): return lax.all_to_all(value, 'gx', 0, 0, tiled=True)]
    ppermute x9 -> x10, waiting for transfers between devices: 44 us -> 70.5 us  [step(): return lax.ppermute(value, axis, [(i, (i + r) % 4) for i in range(4)])]
    all_to_all x2, starting transfers between devices: 28.8 us -> 36.9 us  [swap(): return lax.all_to_all(value, ('gx', 'expert'), 0, 0, tiled=True)]
    unnamed x44 -> x40, local copies, waits for them, and re-layouts: 14.2 us -> 9.98 us
    ppermute x9 -> x10, starting transfers between devices: 31.7 us -> 34 us  [step(): return lax.ppermute(value, axis, [(i, (i + r) % 4) for i in range(4)])]
  transfers between devices with their start and end apart: 13 -> 12, of which waited for: 9 -> 8; matrix products, arithmetic and copies ran while one was open for 0% -> 1% of each run, Pallas kernels for 3% -> 3%
where the time goes in v3:
time: 304 us; the launch traced here: 303 us
  waiting for transfers between devices  117 us (38%)
  starting transfers between devices  71 us (23%)
  Pallas kernels  69 us (23%)
  blocking collectives  33.8 us (11%)
  local copies, waits for them, and re-layouts  11.8 us (4%)
    ppermute x10, waiting for transfers between devices, step(): return lax.ppermute(value, axis, [(i, (i + r) % 4) for i in range(4)])  70.5 us
    all_to_all x2, waiting for transfers between devices, swap(): return lax.all_to_all(value, ('gx', 'expert'), 0, 0, tiled=True)  46.4 us
    pallas_call x1, Pallas kernels, per_device(): call(pick_kernel, (arr(GX * N_EXP, 2, CAP * HALF), arr(320, 3 * HID)), 1...  45.9 us
    all_to_all x2, starting transfers between devices, swap(): return lax.all_to_all(value, ('gx', 'expert'), 0, 0, tiled=True)  36.9 us
    ppermute x10, starting transfers between devices, step(): return lax.ppermute(value, axis, [(i, (i + r) % 4) for i in range(4)])  34 us
    all_to_all x2, blocking collectives, swap_gx(): return lax.all_to_all(value, 'gx', 0, 0, tiled=True)  33.8 us
    unnamed x40, local copies, waits for them, and re-layouts  9.98 us
    pallas_call x1, Pallas kernels, per_device(): call(back_kernel, arr(GX * N_EXP, 2, CAP * HALF), 1 << 32, 1 << 23, in_sp...  6.73 us
  transfers between devices with their start and end apart: 12, of which 8 were waited for; matrix products, arithmetic and copies ran while one was open for 1% of the time, Pallas kernels for 3%

profile of v3, /device:TPU:1, one launch (start us, length us, event | category | flops | bytes accessed | tf_op | source)
XLA Modules:
  0.0 303.5 jit_solution(15441992187536030616)
XLA Ops:
  0.6 45.9 %shard_map.95 = (bf16[128,2,3200]{2,1,0:T(2,128)(2,1)}, bf16[320,2304]{1,0:T(8,128)(2,1)}) custom-call(bf16[128,5120]{1,0:T(8,128)(2,1)} %og_any.1, s32[6,128]{1,0:T(8,128)} %bitcast.15, s32[6,128]{1,0:T(8,128)} %bitcast.17, f32[6,128]{1,0:T(8,128)} %bitcast.23, bf16[320,768]{1,0:T(8,128)(2,1)} %bitcast.20, bf16[320,768]{1,0:T(8,128)(2,1)} %bitcast.21, ...), custom_call_target="tpu_custom_call" | custom-call | flops 536870912 | bytes 8388608 | tf_op jit(solution)/shard_map/pallas_call | solution.py:258
  46.6 20.9 %all-to-all-start = ((bf16[128,2,3200]{2,1,0:T(2,128)(2,1)}), bf16[128,2,3200]{2,1,0:T(2,128)(2,1)}, u32[]{:S(2)}, u32[]{:S(2)}) async-start(bf16[128,2,3200]{2,1,0:T(2,128)(2,1)} %get-tuple-element.15.after_ref), calls=%async_computation | async-start | bytes 3276800 | tf_op jit(solution)/shard_map/all_to_all | solution.py:240
  67.5 3.3 %collective-permute-start = (bf16[320,2304]{1,0:T(8,128)(2,1)S(1)}, bf16[320,2304]{1,0:T(8,128)(2,1)S(1)}, u32[]{:S(2)}, u32[]{:S(2)}) collective-permute-start(bf16[320,2304]{1,0:T(8,128)(2,1)S(1)} %copy-done.3), channel_id=1, source_target_pairs={{0,32},{32,64},{64,96},{96,0},{1,33},{33,65},{65,97},{97,1},{2,34}... | collective-permute-start | bytes 4423688 | tf_op jit(solution)/shard_map/ppermute | solution.py:248
  70.9 3.4 %collective-permute-start.1 = (bf16[320,2304]{1,0:T(8,128)(2,1)S(1)}, bf16[320,2304]{1,0:T(8,128)(2,1)S(1)}, u32[]{:S(2)}, u32[]{:S(2)}) collective-permute-start(bf16[320,2304]{1,0:T(8,128)(2,1)S(1)} %copy-done.3), channel_id=1, source_target_pairs={{0,96},{32,0},{64,32},{96,64},{1,97},{33,1},{65,33},{97,65},{2,98}... | collective-permute-start | bytes 4423688 | tf_op jit(solution)/shard_map/ppermute | solution.py:248
  74.2 29.6 %collective-permute-done.less_ref = bf16[320,2304]{1,0:T(8,128)(2,1)S(1)} collective-permute-done((bf16[320,2304]{1,0:T(8,128)(2,1)S(1)}, bf16[320,2304]{1,0:T(8,128)(2,1)S(1)}, u32[]{:S(2)}, u32[]{:S(2)}) %collective-permute-start) | collective-permute-done | bytes 1474592 | tf_op jit(solution)/shard_map/ppermute | solution.py:248
  104.8 1.9 collective-permute-start.2
  108.7 4.6 %collective-permute-start.3 = (bf16[160,2304]{1,0:T(8,128)(2,1)}, bf16[160,2304]{1,0:T(8,128)(2,1)}, u32[]{:S(2)}, u32[]{:S(2)}) collective-permute-start(bf16[160,2304]{1,0:T(8,128)(2,1)} %slice.9), channel_id=1, source_target_pairs={{0,96},{32,0},{64,32},{96,64},{1,97},{33,1},{65,33},{97,65},{2,98}... | collective-permute-start | bytes 2211848 | tf_op jit(solution)/shard_map/ppermute | solution.py:248
  114.4 4.2 %collective-permute-start.4 = (bf16[160,1536]{1,0:T(8,128)(2,1)}, bf16[160,1536]{1,0:T(8,128)(2,1)S(1)}, u32[]{:S(2)}, u32[]{:S(2)}) collective-permute-start(bf16[160,1536]{1,0:T(8,128)(2,1)} %shard_map.97.pre_0), channel_id=1, source_target_pairs={{0,128},{128,256},{256,384},{384,0},{1,129},{129,257},{257,385},{3... | collective-permute-start | bytes 1474568 | tf_op jit(solution)/shard_map/ppermute | solution.py:248
  118.6 4.7 %collective-permute-start.5 = (bf16[160,1536]{1,0:T(8,128)(2,1)}, bf16[160,1536]{1,0:T(8,128)(2,1)}, u32[]{:S(2)}, u32[]{:S(2)}) collective-permute-start(bf16[160,1536]{1,0:T(8,128)(2,1)} %shard_map.97.pre_0), channel_id=1, source_target_pairs={{0,256},{128,384},{256,0},{384,128},{1,257},{129,385},{257,1},{385... | collective-permute-start | bytes 1474568 | tf_op jit(solution)/shard_map/ppermute | solution.py:248
  123.3 2.9 collective-permute-start.6
  126.3 7.3 %collective-permute-done.4.pre_1 = bf16[160,1536]{1,0:T(8,128)(2,1)S(1)} collective-permute-done((bf16[160,1536]{1,0:T(8,128)(2,1)}, bf16[160,1536]{1,0:T(8,128)(2,1)S(1)}, u32[]{:S(2)}, u32[]{:S(2)}) %collective-permute-start.4) | collective-permute-done | bytes 491552 | tf_op jit(solution)/shard_map/ppermute | solution.py:248
  133.6 13.5 %collective-permute-done.5.pre_2 = bf16[160,1536]{1,0:T(8,128)(2,1)} collective-permute-done((bf16[160,1536]{1,0:T(8,128)(2,1)}, bf16[160,1536]{1,0:T(8,128)(2,1)}, u32[]{:S(2)}, u32[]{:S(2)}) %collective-permute-start.5) | collective-permute-done | bytes 491552 | tf_op jit(solution)/shard_map/ppermute | solution.py:248
  148.1 2.2 shard_map.98
  153.2 1.4 copy-done.4
  154.6 1.7 shard_map.96
  156.4 1.9 copy-done.10
  158.2 1.3 copy-done.12
  159.5 5.4 %shard_map.99 = (bf16[640,1280]{1,0:T(8,128)(2,1)}, bf16[4,160,768]{2,1,0:T(8,128)(2,1)}) custom-call(s32[2]{0:T(128)} %copy-done.8, bf16[128,2,3200]{2,1,0:T(2,128)(2,1)} %all-to-all-done.recv_ref, bf16[1280,768]{1,0:T(8,128)(2,1)} %copy-done.12, bf16[640,768]{1,0:T(8,128)(2,1)} %copy-done.13), custom_call_target="tpu_custom_call" | custom-call | flops 2147483648 | bytes 8388608 | tf_op jit(solution)/shard_map/pallas_call | solution.py:296
  165.0 18.0 %all_to_all.20.part_ref = bf16[4,160,768]{2,1,0:T(8,128)(2,1)S(1)} all-to-all(bf16[4,160,768]{2,1,0:T(8,128)(2,1)} %get-tuple-element.19), channel_id=1, replica_groups=mesh['gx'=4,'gy'=4,'expert'=32] {'gx'}, dimensions={0} | all-to-all | bytes 1966080 | tf_op jit(solution)/shard_map/all_to_all | solution.py:244
  183.1 15.8 %all_to_all.21.hidden_ref = bf16[4,160,768]{2,1,0:T(8,128)(2,1)S(1)} all-to-all(bf16[4,160,768]{2,1,0:T(8,128)(2,1)S(1)} %shard_map.100), channel_id=1, replica_groups=mesh['gx'=4,'gy'=4,'expert'=32] {'gx'}, dimensions={0} | all-to-all | bytes 1966080 | tf_op jit(solution)/shard_map/all_to_all | solution.py:244
  198.9 6.7 %shard_map.101.after_ref = bf16[128,2,3200]{2,1,0:T(2,128)(2,1)} custom-call(s32[2]{0:T(128)S(1)} %copy-done.9, bf16[4,160,768]{2,1,0:T(8,128)(2,1)S(1)} %all_to_all.21.hidden_ref, bf16[640,768]{1,0:T(8,128)(2,1)S(1)} %copy-done.16, bf16[640,768]{1,0:T(8,128)(2,1)S(1)} %copy-done.18, bf16[1280,1536]{1,0:T(8,128)(2,1)S(1)} %copy-done.11), custom_call_target="tpu_custom_call" | custom-call | flops 4294967296 | bytes 8388608 | tf_op jit(solution)/shard_map/pallas_call | solution.py:306
  205.7 16.0 %all-to-all-start.3 = ((bf16[128,2,3200]{2,1,0:T(2,128)(2,1)}), bf16[128,2,3200]{2,1,0:T(2,128)(2,1)S(1)}, u32[]{:S(2)}, u32[]{:S(2)}) async-start(bf16[128,2,3200]{2,1,0:T(2,128)(2,1)} %shard_map.101.after_ref), calls=%async_computation.3 | async-start | bytes 3276800 | tf_op jit(solution)/shard_map/all_to_all | solution.py:240
  221.7 1.4 copy-done.19
  223.1 2.4 shard_map.103
  225.6 1.9 collective-permute-start.7
  227.5 4.2 %collective-permute-start.8 = (bf16[320,768]{1,0:T(8,128)(2,1)S(1)}, bf16[320,768]{1,0:T(8,128)(2,1)S(1)}, u32[]{:S(2)}, u32[]{:S(2)}) collective-permute-start(bf16[320,768]{1,0:T(8,128)(2,1)S(1)} %get-tuple-element.26), channel_id=1, source_target_pairs={{0,64},{32,96},{64,0},{96,32},{1,65},{33,97},{65,1},{97,33},{2,66}... | collective-permute-start | bytes 1474568 | tf_op jit(solution)/shard_map/ppermute | solution.py:248
  231.7 3.0 collective-permute-start.9
  234.7 6.2 %collective-permute-done.7.part_1 = bf16[320,768]{1,0:T(8,128)(2,1)S(1)} collective-permute-done((bf16[320,768]{1,0:T(8,128)(2,1)S(1)}, bf16[320,768]{1,0:T(8,128)(2,1)S(1)}, u32[]{:S(2)}, u32[]{:S(2)}) %collective-permute-start.7) | collective-permute-done | bytes 491552 | tf_op jit(solution)/shard_map/ppermute | solution.py:248
  240.9 9.8 %collective-permute-done.8.part_2 = bf16[320,768]{1,0:T(8,128)(2,1)S(1)} collective-permute-done((bf16[320,768]{1,0:T(8,128)(2,1)S(1)}, bf16[320,768]{1,0:T(8,128)(2,1)S(1)}, u32[]{:S(2)}, u32[]{:S(2)}) %collective-permute-start.8) | collective-permute-done | bytes 491552 | tf_op jit(solution)/shard_map/ppermute | solution.py:248
  250.7 3.1 %collective-permute-done.9.part_3 = bf16[320,768]{1,0:T(8,128)(2,1)S(1)} collective-permute-done((bf16[320,768]{1,0:T(8,128)(2,1)S(1)}, bf16[320,768]{1,0:T(8,128)(2,1)S(1)}, u32[]{:S(2)}, u32[]{:S(2)}) %collective-permute-start.9) | collective-permute-done | bytes 491552 | tf_op jit(solution)/shard_map/ppermute | solution.py:248
  254.9 46.4 %all-to-all-done.3.ret_ref = bf16[128,2,3200]{2,1,0:T(2,128)(2,1)S(1)} async-done(((bf16[128,2,3200]{2,1,0:T(2,128)(2,1)}), bf16[128,2,3200]{2,1,0:T(2,128)(2,1)S(1)}, u32[]{:S(2)}, u32[]{:S(2)}) %all-to-all-start.3) | async-done | bytes 1638432 | tf_op jit(solution)/shard_map/all_to_all | solution.py:240
  301.2 2.3 shard_map.102
  (47 shorter events, 9.1 us)
Async XLA Ops:
  46.5 21.0 %copy-start.3 = (bf16[320,2304]{1,0:T(8,128)(2,1)S(1)}, bf16[320,2304]{1,0:T(8,128)(2,1)}, u32[]{:S(2)}) copy-start(bf16[320,2304]{1,0:T(8,128)(2,1)} %get-tuple-element.16.own_ref) | copy-start | bytes 4423684
  46.6 113.0 %all-to-all-start = ((bf16[128,2,3200]{2,1,0:T(2,128)(2,1)}), bf16[128,2,3200]{2,1,0:T(2,128)(2,1)}, u32[]{:S(2)}, u32[]{:S(2)}) async-start(bf16[128,2,3200]{2,1,0:T(2,128)(2,1)} %get-tuple-element.15.after_ref), calls=%async_computation | async-start | bytes 3276800 | tf_op jit(solution)/shard_map/all_to_all | solution.py:240
  67.5 45.8 %copy-start = (bf16[128,2,3200]{2,1,0:T(2,128)(2,1)S(1)}, bf16[128,2,3200]{2,1,0:T(2,128)(2,1)}, u32[]{:S(2)}) copy-start(bf16[128,2,3200]{2,1,0:T(2,128)(2,1)} %get-tuple-element.15.after_ref) | copy-start | bytes 4915204
  67.5 45.8 %copy-start.5 = (bf16[1,160,1536]{2,1,0:T(8,128)(2,1)S(1)}, bf16[1,160,1536]{2,1,0:T(8,128)(2,1)}, u32[]{:S(2)}) copy-start(bf16[1,160,1536]{2,1,0:T(8,128)(2,1)} %param.12) | copy-start | bytes 1474564
  67.5 36.3 %collective-permute-start = (bf16[320,2304]{1,0:T(8,128)(2,1)S(1)}, bf16[320,2304]{1,0:T(8,128)(2,1)S(1)}, u32[]{:S(2)}, u32[]{:S(2)}) collective-permute-start(bf16[320,2304]{1,0:T(8,128)(2,1)S(1)} %copy-done.3), channel_id=1, source_target_pairs={{0,32},{32,64},{64,96},{96,0},{1,33},{33,65},{65,97},{97,1},{2,34}... | collective-permute-start | bytes 4423688 | tf_op jit(solution)/shard_map/ppermute | solution.py:248
  70.9 35.8 %collective-permute-start.1 = (bf16[320,2304]{1,0:T(8,128)(2,1)S(1)}, bf16[320,2304]{1,0:T(8,128)(2,1)S(1)}, u32[]{:S(2)}, u32[]{:S(2)}) collective-permute-start(bf16[320,2304]{1,0:T(8,128)(2,1)S(1)} %copy-done.3), channel_id=1, source_target_pairs={{0,96},{32,0},{64,32},{96,64},{1,97},{33,1},{65,33},{97,65},{2,98}... | collective-permute-start | bytes 4423688 | tf_op jit(solution)/shard_map/ppermute | solution.py:248
  104.8 48.4 %collective-permute-start.2 = (bf16[160,2304]{1,0:T(8,128)(2,1)}, bf16[160,2304]{1,0:T(8,128)(2,1)}, u32[]{:S(2)}, u32[]{:S(2)}) collective-permute-start(bf16[160,2304]{1,0:T(8,128)(2,1)} %slice.8), channel_id=1, source_target_pairs={{0,32},{32,64},{64,96},{96,0},{1,33},{33,65},{65,97},{97,1},{2,34}... | collective-permute-start | bytes 2211848 | tf_op jit(solution)/shard_map/ppermute | solution.py:248
  107.6 1.1 copy-start.1
  108.7 44.5 %collective-permute-start.3 = (bf16[160,2304]{1,0:T(8,128)(2,1)}, bf16[160,2304]{1,0:T(8,128)(2,1)}, u32[]{:S(2)}, u32[]{:S(2)}) collective-permute-start(bf16[160,2304]{1,0:T(8,128)(2,1)} %slice.9), channel_id=1, source_target_pairs={{0,96},{32,0},{64,32},{96,64},{1,97},{33,1},{65,33},{97,65},{2,98}... | collective-permute-start | bytes 2211848 | tf_op jit(solution)/shard_map/ppermute | solution.py:248
  114.4 38.8 %copy-start.2 = (bf16[320,2304]{1,0:T(8,128)(2,1)S(1)}, bf16[320,2304]{1,0:T(8,128)(2,1)}, u32[]{:S(2)}) copy-start(bf16[320,2304]{1,0:T(8,128)(2,1)} %copy-done.1) | copy-start | bytes 4423684
  114.4 19.2 %collective-permute-start.4 = (bf16[160,1536]{1,0:T(8,128)(2,1)}, bf16[160,1536]{1,0:T(8,128)(2,1)S(1)}, u32[]{:S(2)}, u32[]{:S(2)}) collective-permute-start(bf16[160,1536]{1,0:T(8,128)(2,1)} %shard_map.97.pre_0), channel_id=1, source_target_pairs={{0,128},{128,256},{256,384},{384,0},{1,129},{129,257},{257,385},{3... | collective-permute-start | bytes 1474568 | tf_op jit(solution)/shard_map/ppermute | solution.py:248
  118.6 28.5 %collective-permute-start.5 = (bf16[160,1536]{1,0:T(8,128)(2,1)}, bf16[160,1536]{1,0:T(8,128)(2,1)}, u32[]{:S(2)}, u32[]{:S(2)}) collective-permute-start(bf16[160,1536]{1,0:T(8,128)(2,1)} %shard_map.97.pre_0), channel_id=1, source_target_pairs={{0,256},{128,384},{256,0},{384,128},{1,257},{129,385},{257,1},{385... | collective-permute-start | bytes 1474568 | tf_op jit(solution)/shard_map/ppermute | solution.py:248
  123.3 24.7 %collective-permute-start.6 = (bf16[160,1536]{1,0:T(8,128)(2,1)}, bf16[160,1536]{1,0:T(8,128)(2,1)}, u32[]{:S(2)}, u32[]{:S(2)}) collective-permute-start(bf16[160,1536]{1,0:T(8,128)(2,1)} %shard_map.97.pre_0), channel_id=1, source_target_pairs={{0,384},{128,0},{256,128},{384,256},{1,385},{129,1},{257,129},{385... | collective-permute-start | bytes 1474568 | tf_op jit(solution)/shard_map/ppermute | solution.py:248
  126.3 30.0 %copy-start.8 = (s32[2]{0:T(128)}, s32[2]{0:T(128)S(1)}, u32[]{:S(2)}) copy-start(s32[2]{0:T(128)S(1)} %pad_add_fusion.at_ref) | copy-start | bytes 28
  150.3 0.9 copy-start.13
  151.3 1.0 copy-start.15
  152.2 1.0 copy-start.17
  153.2 1.4 copy-start.4
  156.3 1.9 copy-start.10
  158.2 1.3 copy-start.12
  165.0 33.9 %copy-start.16 = (bf16[640,768]{1,0:T(8,128)(2,1)S(1)}, bf16[640,768]{1,0:T(8,128)(2,1)}, u32[]{:S(2)}) copy-start(bf16[640,768]{1,0:T(8,128)(2,1)} %copy-done.15) | copy-start | bytes 2949124
  165.0 33.9 %copy-start.18 = (bf16[640,768]{1,0:T(8,128)(2,1)S(1)}, bf16[640,768]{1,0:T(8,128)(2,1)}, u32[]{:S(2)}) copy-start(bf16[640,768]{1,0:T(8,128)(2,1)} %copy-done.17) | copy-start | bytes 2949124
  183.0 15.9 %copy-start.9 = (s32[2]{0:T(128)S(1)}, s32[2]{0:T(128)}, u32[]{:S(2)}) copy-start(s32[2]{0:T(128)} %copy-done.8) | copy-start | bytes 28
  183.0 15.9 %copy-start.11 = (bf16[1280,1536]{1,0:T(8,128)(2,1)S(1)}, bf16[1280,1536]{1,0:T(8,128)(2,1)}, u32[]{:S(2)}) copy-start(bf16[1280,1536]{1,0:T(8,128)(2,1)} %copy-done.10) | copy-start | bytes 11796484
  205.7 16.0 %copy-start.14 = (bf16[640,768]{1,0:T(8,128)(2,1)S(1)}, bf16[640,768]{1,0:T(8,128)(2,1)}, u32[]{:S(2)}) copy-start(bf16[640,768]{1,0:T(8,128)(2,1)} %copy-done.13) | copy-start | bytes 2949124
  205.7 95.6 %all-to-all-start.3 = ((bf16[128,2,3200]{2,1,0:T(2,128)(2,1)}), bf16[128,2,3200]{2,1,0:T(2,128)(2,1)S(1)}, u32[]{:S(2)}, u32[]{:S(2)}) async-start(bf16[128,2,3200]{2,1,0:T(2,128)(2,1)} %shard_map.101.after_ref), calls=%async_computation.3 | async-start | bytes 3276800 | tf_op jit(solution)/shard_map/all_to_all | solution.py:240
  221.7 1.4 copy-start.19
  225.6 75.7 %copy-start.6 = (s32[128,6]{0,1:T(8,128)S(1)}, s32[128,6]{0,1:T(8,128)}, u32[]{:S(2)}) copy-start(s32[128,6]{0,1:T(8,128)} %param.9) | copy-start | bytes 9220
  225.6 75.7 %copy-start.7 = (s32[128,6]{0,1:T(8,128)S(1)}, s32[128,6]{0,1:T(8,128)}, u32[]{:S(2)}) copy-start(s32[128,6]{0,1:T(8,128)} %param.10) | copy-start | bytes 9220
  225.6 15.3 %collective-permute-start.7 = (bf16[320,768]{1,0:T(8,128)(2,1)S(1)}, bf16[320,768]{1,0:T(8,128)(2,1)S(1)}, u32[]{:S(2)}, u32[]{:S(2)}) collective-permute-start(bf16[320,768]{1,0:T(8,128)(2,1)S(1)} %get-tuple-element.25), channel_id=1, source_target_pairs={{0,32},{32,64},{64,96},{96,0},{1,33},{33,65},{65,97},{97,1},{2,34}... | collective-permute-start | bytes 1474568 | tf_op jit(solution)/shard_map/ppermute | solution.py:248
  227.5 23.2 %collective-permute-start.8 = (bf16[320,768]{1,0:T(8,128)(2,1)S(1)}, bf16[320,768]{1,0:T(8,128)(2,1)S(1)}, u32[]{:S(2)}, u32[]{:S(2)}) collective-permute-start(bf16[320,768]{1,0:T(8,128)(2,1)S(1)} %get-tuple-element.26), channel_id=1, source_target_pairs={{0,64},{32,96},{64,0},{96,32},{1,65},{33,97},{65,1},{97,33},{2,66}... | collective-permute-start | bytes 1474568 | tf_op jit(solution)/shard_map/ppermute | solution.py:248
  231.7 22.1 %collective-permute-start.9 = (bf16[320,768]{1,0:T(8,128)(2,1)S(1)}, bf16[320,768]{1,0:T(8,128)(2,1)S(1)}, u32[]{:S(2)}, u32[]{:S(2)}) collective-permute-start(bf16[320,768]{1,0:T(8,128)(2,1)S(1)} %get-tuple-element.27), channel_id=1, source_target_pairs={{0,96},{32,0},{64,32},{96,64},{1,97},{33,1},{65,33},{97,65},{2,98}... | collective-permute-start | bytes 1474568 | tf_op jit(solution)/shard_map/ppermute | solution.py:248

commit v4 on v2

v4 whole, which is shorter than its diff:
```python
import functools

import jax
import jax.numpy as jnp
from jax import lax
from jax.experimental import pallas as pl
from jax.experimental.pallas import tpu as pltpu
from jax.sharding import Mesh, PartitionSpec as P

BF = jnp.bfloat16
F32 = jnp.float32

N_EXP = 32
CAP = 5
CHUNKS = ((0, 2), (2, 5))
TOK = 128
GX = 4
GY = 4
WIDE = 1280
HALF = 640
HID = 768
ROWS = N_EXP * CAP
PAIRS = 2 * N_EXP
PART = 320
VMEM_LIMIT = 16 * 1024 * 1024
VMEM_MOST = 60 * 1024 * 1024


def iota(shape, dim):
    return lax.broadcasted_iota(jnp.int32, shape, dim)


def nn(left, right):
    return lax.dot_general(left, right, (((1,), (0,)), ((), ())), preferred_element_type=F32)


def nt(left, right):
    return lax.dot_general(left, right, (((1,), (1,)), ((), ())), preferred_element_type=F32)


def tn(left, right):
    return lax.dot_general(left, right, (((0,), (0,)), ((), ())), preferred_element_type=F32)


def one_hot(mask):
    return jnp.where(mask, 1.0, 0.0).astype(BF)


def call(body, out_shape, flops=0, moved=0, limit=VMEM_LIMIT, **kwargs):
    return pl.pallas_call(
        body,
        out_shape=out_shape,
        compiler_params=pltpu.CompilerParams(vmem_limit_bytes=limit),
        cost_estimate=pl.CostEstimate(flops=flops, bytes_accessed=moved, transcendentals=0),
        **kwargs,
    )


def arr(*dims, dtype=BF):
    return jax.ShapeDtypeStruct(dims, dtype)


def select(ids_ref, slots_ref, probs, chunk):
    code = ids_ref[...] * CAP + slots_ref[...]
    shape = ((chunk[1] - chunk[0]) * PAIRS, TOK)
    row = iota(shape, 0)
    row_code = ((row % PAIRS) // 2) * CAP + row // PAIRS + chunk[0]
    hits = jnp.zeros(shape, F32)
    weight = jnp.zeros(shape, F32)
    for k in range(code.shape[0]):
        same = row_code == code[k : k + 1, :]
        hits = hits + jnp.where(same, 1.0, 0.0)
        if probs is not None:
            weight = weight + jnp.where(same, probs[k : k + 1, :], 0.0)
    lower = row % 2 == 0
    pick = jnp.concatenate([jnp.where(lower, hits, 0.0), jnp.where(lower, 0.0, hits)], axis=1)
    return pick.astype(BF), jnp.sum(weight, axis=1, keepdims=True)


def split_halves():
    row = iota((PAIRS, PAIRS), 0)
    col = iota((PAIRS, PAIRS), 1)
    return one_hot(col == (row % N_EXP) * 2 + row // N_EXP)


def join_halves():
    row = iota((PAIRS, PAIRS), 0)
    col = iota((PAIRS, PAIRS), 1)
    return one_hot(row == (col % N_EXP) * 2 + col // N_EXP)


def to_pairs(rows):
    return rows.reshape(N_EXP, 2, HALF).astype(BF)


def from_pairs(block):
    return block.astype(F32).reshape(PAIRS, HALF).astype(BF)


def pick_kernel(chunk, packs, *refs):
    ins, refs = refs[: 4 + max(packs, 1)], refs[4 + max(packs, 1) :]
    outs, refs = refs[: 1 + (packs > 0) * 2], refs[1 + (packs > 0) * 2 :]
    og_any, ids_any, slots_any, probs_any = ins[:4]
    msg_any = outs[0]
    og_ref, ids_ref, slots_ref, probs_ref, msg_ref, og_sem, in_sem, out_sem = refs[:8]
    small = [
        pltpu.make_async_copy(src, dst, in_sem.at[i])
        for i, (src, dst) in enumerate(((ids_any, ids_ref), (slots_any, slots_ref), (probs_any, probs_ref)))
    ]
    wide = [
        pltpu.make_async_copy(og_any.at[:, pl.ds(g * WIDE, WIDE)], og_ref.at[g], og_sem.at[g])
        for g in range(GX)
    ]
    fetches, stores = [], []
    if packs:
        down_any, gate_any, up_any = ins[4:]
        down_ref, in_ref, fetch_sem, store_sem = refs[8:]
        fetches = [
            pltpu.make_async_copy(down_any, down_ref, fetch_sem.at[0]),
            pltpu.make_async_copy(gate_any, in_ref.at[:, pl.ds(0, HID)], fetch_sem.at[1]),
            pltpu.make_async_copy(up_any, in_ref.at[:, pl.ds(HID, HID)], fetch_sem.at[2]),
        ]
        stores = [
            pltpu.make_async_copy(down_ref, outs[1], store_sem.at[0]),
            pltpu.make_async_copy(in_ref, outs[2], store_sem.at[1]),
        ]
    for copy in small + wide + fetches:
        copy.start()
    for copy in small:
        copy.wait()
    pick, weight = select(ids_ref, slots_ref, probs_ref[...], chunk)
    sends = []
    for g in range(GX):
        wide[g].wait()
        both = jnp.concatenate([og_ref[g, :, :HALF], og_ref[g, :, HALF:]], axis=0)
        rows = nn(pick, both) * weight
        for s in range(chunk[1] - chunk[0]):
            msg_ref[g * N_EXP : (g + 1) * N_EXP, :, s * HALF : (s + 1) * HALF] = to_pairs(
                rows[s * PAIRS : (s + 1) * PAIRS]
            )
        span = pl.ds(g * N_EXP, N_EXP)
        sends.append(pltpu.make_async_copy(msg_ref.at[span], msg_any.at[span], out_sem.at[g]))
        sends[-1].start()
        if g == 1:
            for copy in fetches:
                copy.wait()
            for copy in stores:
                copy.start()
    for copy in sends + stores:
        copy.wait()


def arrange_kernel(at_ref, own_ref, piece_1, piece_2, piece_3, out_ref):
    for r, ref in enumerate((own_ref, piece_1, piece_2, piece_3)):
        q = lax.rem(at_ref[1] + (GY - r), GY)
        out_ref[pl.ds(pl.multiple_of(q * PART, 64), PART), :] = ref[...]


def order_kernel(pre_ref, after_ref, out_ref):
    row = iota((ROWS, ROWS), 0)
    col = iota((ROWS, ROWS), 1)
    swap_rows = one_hot(col == (row % N_EXP) * CAP + row // N_EXP)
    out_ref[...] = nn(swap_rows, pre_ref[...]).astype(BF)


def factor_kernel(pre_0, pre_1, pre_2, pre_3, factor_ref, act_ref):
    for r, pre_ref in enumerate((pre_0, pre_1, pre_2, pre_3)):
        for s in range(CAP):
            span = slice(s * N_EXP, (s + 1) * N_EXP)
            gate_pre = pre_ref[span, :HID].astype(F32)
            up_pre = pre_ref[span, HID:].astype(F32)
            sig = jax.nn.sigmoid(gate_pre)
            lift = gate_pre * sig
            factor_ref[r, span, :HID] = (up_pre * sig * (1.0 + gate_pre * (1.0 - sig))).astype(BF)
            factor_ref[r, span, HID:] = lift.astype(BF)
            act_ref[r, span, :] = (lift * up_pre).astype(BF)


def hidden_kernel(n, at_ref, recv_ref, down_ref, sent_ref, *part_refs):
    split = split_halves()
    for r in range(GX):
        g = lax.rem(at_ref[0] + (GX - r), GX)
        for s in range(n):
            rows = from_pairs(recv_ref[pl.ds(g * N_EXP, N_EXP), :, s * HALF : (s + 1) * HALF])
            halves = nn(split, rows).astype(BF)
            span = slice(s * N_EXP, (s + 1) * N_EXP)
            sent_ref[r, span, :HALF] = halves[:N_EXP]
            sent_ref[r, span, HALF:] = halves[N_EXP:]
    for r in range(GX):
        part_refs[r][...] = nn(sent_ref[r], down_ref[...]).astype(BF)


def total_kernel(part_0, part_1, part_2, part_3, out_ref):
    total = part_0[...].astype(F32) + part_1[...].astype(F32)
    out_ref[...] = (total + (part_2[...].astype(F32) + part_3[...].astype(F32))).astype(BF)


def back_kernel(chunk, at_ref, hidden_0, hidden_1, hidden_2, hidden_3, factor_ref, in_ref, msg_ref):
    n = chunk[1] - chunk[0]
    span = slice(chunk[0] * N_EXP, chunk[1] * N_EXP)
    grads = []
    for r, hidden_ref in enumerate((hidden_0, hidden_1, hidden_2, hidden_3)):
        hidden = hidden_ref[...].astype(F32)
        gate_grad = (hidden * factor_ref[r, span, :HID].astype(F32)).astype(BF)
        up_grad = (hidden * factor_ref[r, span, HID:].astype(F32)).astype(BF)
        grads.append(jnp.concatenate([gate_grad, up_grad], axis=1))
    rows = nt(jnp.concatenate(grads, axis=0), in_ref[...]).astype(BF)
    join = join_halves()
    for r in range(GX):
        g = lax.rem(at_ref[0] + (GX - r), GX)
        for s in range(n):
            own = rows[(r * n + s) * N_EXP : (r * n + s + 1) * N_EXP]
            both = jnp.concatenate([own[:, :HALF], own[:, HALF:]], axis=0)
            msg_ref[pl.ds(g * N_EXP, N_EXP), :, s * HALF : (s + 1) * HALF] = to_pairs(nn(join, both))


def down_kernel(at_ref, sent_a_ref, sent_b_ref, act_ref, after_ref, out_0, out_1, out_2, out_3, full_ref):
    sent = jnp.concatenate([ref[r] for r in range(GX) for ref in (sent_a_ref, sent_b_ref)], axis=0)
    act = jnp.concatenate([act_ref[r] for r in range(GX)], axis=0)
    full_ref[...] = tn(sent, act).astype(BF)
    for r, out_ref in enumerate((out_0, out_1, out_2, out_3)):
        q = lax.rem(at_ref[1] + r, GY)
        out_ref[...] = full_ref[pl.ds(pl.multiple_of(q * PART, 64), PART), :]


def gather_kernel(ret_a_ref, ret_b_ref, ids_ref, slots_ref, out_ref):
    picks = [select(ids_ref, slots_ref, None, chunk)[0] for chunk in CHUNKS]
    for g in range(GX):
        halves = 0.0
        for pick, chunk, ret_ref in zip(picks, CHUNKS, (ret_a_ref, ret_b_ref)):
            rows = jnp.concatenate(
                [
                    from_pairs(ret_ref[g * N_EXP : (g + 1) * N_EXP, :, s * HALF : (s + 1) * HALF])
                    for s in range(chunk[1] - chunk[0])
                ],
                axis=0,
            )
            halves = halves + tn(pick, rows)
        halves = halves.astype(BF)
        out_ref[:, g * WIDE : g * WIDE + HALF] = halves[:TOK]
        out_ref[:, g * WIDE + HALF : (g + 1) * WIDE] = halves[TOK:]


def swap(value):
    return lax.all_to_all(value, ("gx", "expert"), 0, 0, tiled=True)


def step(value, axis, r):
    return lax.ppermute(value, axis, [(i, (i + r) % 4) for i in range(4)])


def steps(value, axis):
    return [step(value, axis, r) for r in range(1, 4)]


def per_device(out_grad, route_ids, route_slots, route_probs, saved_pre, w_gate, w_up, w_down):
    ids, slots, probs = route_ids.T, route_slots.T, route_probs.T
    at = jnp.stack([lax.axis_index("gx"), lax.axis_index("gy")])
    smem = pl.BlockSpec(memory_space=pltpu.SMEM)
    vmem = pl.BlockSpec(memory_space=pltpu.VMEM)
    anywhere = pl.BlockSpec(memory_space=pl.ANY)
    size = [(chunk[1] - chunk[0]) for chunk in CHUNKS]
    message = [arr(GX * N_EXP, 2, n * HALF) for n in size]

    def pick(chunk, shapes, operands, packs):
        return call(
            functools.partial(pick_kernel, chunk, packs),
            shapes,
            1 << 29,
            1 << 23,
            VMEM_MOST if packs else VMEM_LIMIT,
            in_specs=[anywhere] * len(operands),
            out_specs=[anywhere] * len(shapes),
            scratch_shapes=[
                pltpu.VMEM((GX, TOK, WIDE), BF),
                pltpu.VMEM(ids.shape, jnp.int32),
                pltpu.VMEM(ids.shape, jnp.int32),
                pltpu.VMEM(ids.shape, F32),
                pltpu.VMEM(shapes[0].shape, BF),
                pltpu.SemaphoreType.DMA((GX,)),
                pltpu.SemaphoreType.DMA((3,)),
                pltpu.SemaphoreType.DMA((GX,)),
            ]
            + [
                pltpu.VMEM((PART, HID), BF),
                pltpu.VMEM((PART, 2 * HID), BF),
                pltpu.SemaphoreType.DMA((3,)),
                pltpu.SemaphoreType.DMA((2,)),
            ]
            * (packs > 0),
        )(*operands)

    routes = (out_grad, ids, slots, probs)
    msg_a, own_down, own_in = pick(
        CHUNKS[0],
        [message[0], arr(PART, HID), arr(PART, 2 * HID)],
        (*routes, w_down[0].T, w_gate[0], w_up[0]),
        3,
    )
    recv_a = swap(msg_a)
    (msg_b,) = pick(CHUNKS[1], [message[1]], (*routes, msg_a), 0)
    recv_b = swap(msg_b)

    def arrange(own):
        return call(
            arrange_kernel,
            arr(WIDE, own.shape[1]),
            0,
            1 << 23,
            in_specs=[smem] + [vmem] * 4,
        )(at, own, *steps(own, "gy"))

    down_w, in_w = arrange(own_down), arrange(own_in)
    pre = call(order_kernel, arr(ROWS, 2 * HID), 1 << 27, 1 << 21, in_specs=[vmem, anywhere])(
        saved_pre[0], msg_a
    )
    factors, act = call(
        factor_kernel, (arr(GX, ROWS, 2 * HID), arr(GX, ROWS, HID)), 1 << 25, 1 << 23
    )(pre, *steps(pre, "gx"))

    def middle(c, recv):
        rows = size[c] * N_EXP
        sent, *parts = call(
            functools.partial(hidden_kernel, size[c]),
            (arr(GX, rows, WIDE),) + (arr(rows, HID),) * GX,
            1 << 30,
            1 << 23,
            in_specs=[smem, vmem, vmem],
        )(at, recv, down_w)
        hidden = call(total_kernel, arr(rows, HID), 0, 1 << 20)(
            parts[0], *[step(parts[GX - r], "gx", r) for r in range(1, GX)]
        )
        back = call(
            functools.partial(back_kernel, CHUNKS[c]),
            message[c],
            1 << 31,
            1 << 23,
            in_specs=[smem] + [vmem] * 6,
        )(at, hidden, *steps(hidden, "gx"), factors, in_w)
        return sent, back

    sent_a, back_a = middle(0, recv_a)
    ret_a = swap(back_a)
    sent_b, back_b = middle(1, recv_b)
    ret_b = swap(back_b)

    downs = call(
        down_kernel,
        (arr(PART, HID),) * GY,
        1 << 31,
        1 << 22,
        in_specs=[smem] + [vmem] * 3 + [anywhere],
        scratch_shapes=[pltpu.VMEM((WIDE, HID), BF)],
    )(at, sent_a, sent_b, act, back_b)
    grad_down = call(total_kernel, arr(PART, HID), 0, 1 << 21)(
        downs[0], *[step(downs[r], "gy", r) for r in range(1, GY)]
    )
    input_grad = call(gather_kernel, arr(TOK, GX * WIDE), 1 << 30, 1 << 22)(ret_a, ret_b, ids, slots)
    return (input_grad, grad_down.T[None])


def solution(mesh):
    devices = mesh.devices
    grid = Mesh(devices.reshape((GX, GY) + devices.shape[1:]), ("gx", "gy", "expert"))
    rows = P(("gx", "gy", "expert"), None)
    return jax.shard_map(
        per_device,
        mesh=grid,
        in_specs=(
            rows,
            rows,
            rows,
            rows,
            P("expert", ("gx", "gy"), None),
            P("expert", ("gx", "gy"), None),
            P("expert", ("gx", "gy"), None),
            P("expert", None, ("gx", "gy")),
        ),
        out_specs=(rows, P("expert", None, ("gx", "gy"))),
        check_vma=False,
    )
```

time: 265 us -> 298 us (1.12)
  starting transfers between devices: 60.7 us -> 150 us
  waiting for transfers between devices: 153 us -> 101 us
  between operations: 14.2 us -> 1.22 us
  Pallas kernels: 21.2 us -> 31.9 us
    ppermute x9 -> x24, starting transfers between devices: 31.7 us -> 90.5 us  [step(): return lax.ppermute(value, axis, [(i, (i + r) % 4) for i in range(4)])]
    all_to_all x2 -> x4, waiting for transfers between devices: 109 us -> 51.8 us  [swap(): return lax.all_to_all(value, ('gx', 'expert'), 0, 0, tiled=True)]
    all_to_all x2 -> x4, starting transfers between devices: 28.8 us -> 59.6 us  [swap(): return lax.all_to_all(value, ('gx', 'expert'), 0, 0, tiled=True)]
    pallas_call x8 -> x14, Pallas kernels: 21 us -> 31.6 us  [the longest x2 7.46 us: middle(): call(functools.partial(back_kernel, CHUNKS[c]), message[c], 1 << 31, 1 <<...]
    ppermute x9 -> x24, waiting for transfers between devices: 44 us -> 48.7 us  [step(): return lax.ppermute(value, axis, [(i, (i + r) % 4) for i in range(4)])]
  transfers between devices with their start and end apart: 13 -> 28, of which waited for: 9 -> 11; matrix products, arithmetic and copies ran while one was open for 0% -> 0% of each run, Pallas kernels for 3% -> 8%
where the time goes in v4:
time: 298 us; the launch traced here: 296 us
  starting transfers between devices  150 us (50%)
  waiting for transfers between devices  101 us (34%)
  Pallas kernels  31.9 us (11%)
  local copies, waits for them, and re-layouts  12.3 us (4%)
    ppermute x24, starting transfers between devices, step(): return lax.ppermute(value, axis, [(i, (i + r) % 4) for i in range(4)])  90.5 us
    all_to_all x4, starting transfers between devices, swap(): return lax.all_to_all(value, ('gx', 'expert'), 0, 0, tiled=True)  59.6 us
    all_to_all x4, waiting for transfers between devices, swap(): return lax.all_to_all(value, ('gx', 'expert'), 0, 0, tiled=True)  51.8 us
    ppermute x24, waiting for transfers between devices, step(): return lax.ppermute(value, axis, [(i, (i + r) % 4) for i in range(4)])  48.7 us
    unnamed x44, local copies, waits for them, and re-layouts  12.3 us
    pallas_call x2, Pallas kernels, middle(): call(functools.partial(back_kernel, CHUNKS[c]), message[c], 1 << 31, 1 <<...  7.46 us
    pallas_call x2, Pallas kernels, pick(): call(functools.partial(pick_kernel, chunk, packs), shapes, 1 << 29, 1 <<...  6.74 us
  transfers between devices with their start and end apart: 28, of which 11 were waited for; matrix products, arithmetic and copies ran while one was open for 0% of the time, Pallas kernels for 8%

profile of v4, /device:TPU:1, one launch (start us, length us, event | category | flops | bytes accessed | tf_op | source)
XLA Modules:
  0.0 296.2 jit_solution(92936746446776258)
XLA Ops:
  0.7 3.8 %shard_map.95 = (bf16[128,2,1280]{2,1,0:T(2,128)(2,1)}, bf16[320,768]{1,0:T(8,128)(2,1)}, bf16[320,1536]{1,0:T(8,128)(2,1)}) custom-call(bf16[128,5120]{1,0:T(8,128)(2,1)} %refs_0_.3, s32[6,128]{1,0:T(8,128)} %bitcast.17, s32[6,128]{1,0:T(8,128)} %bitcast.20, f32[6,128]{1,0:T(8,128)} %bitcast.15, bf16[320,768]{1,0:T(8,128)(2,1)} %bitcast.24, ...), custom_call_target="tpu_custom_call" | custom-call | flops 536870912 | bytes 8388608 | tf_op jit(solution)/shard_map/pallas_call | solution.py:266
  4.5 20.4 %all-to-all-start = ((bf16[128,2,1280]{2,1,0:T(2,128)(2,1)}), bf16[128,2,1280]{2,1,0:T(2,128)(2,1)S(1)}, u32[]{:S(2)}, u32[]{:S(2)}) async-start(bf16[128,2,1280]{2,1,0:T(2,128)(2,1)} %get-tuple-element.21.after_ref.refs_4_), calls=%async_computation | async-start | bytes 1310720 | tf_op jit(solution)/shard_map/all_to_all | solution.py:245
  26.1 2.9 shard_map.103
  29.0 34.2 %all-to-all-done.recv_ref = bf16[128,2,1280]{2,1,0:T(2,128)(2,1)S(1)} async-done(((bf16[128,2,1280]{2,1,0:T(2,128)(2,1)}), bf16[128,2,1280]{2,1,0:T(2,128)(2,1)S(1)}, u32[]{:S(2)}, u32[]{:S(2)}) %all-to-all-start) | async-done | bytes 655392 | tf_op jit(solution)/shard_map/all_to_all | solution.py:245
  64.0 7.7 %all-to-all-start.2 = ((bf16[128,2,1920]{2,1,0:T(2,128)(2,1)}), bf16[128,2,1920]{2,1,0:T(2,128)(2,1)S(1)}, u32[]{:S(2)}, u32[]{:S(2)}) async-start(bf16[128,2,1920]{2,1,0:T(2,128)(2,1)} %shard_map.103), calls=%async_computation.2 | async-start | bytes 1966080 | tf_op jit(solution)/shard_map/all_to_all | solution.py:245
  71.7 4.6 %collective-permute-start.2 = (bf16[320,768]{1,0:T(8,128)(2,1)}, bf16[320,768]{1,0:T(8,128)(2,1)S(1)}, u32[]{:S(2)}, u32[]{:S(2)}) collective-permute-start(bf16[320,768]{1,0:T(8,128)(2,1)} %get-tuple-element.22.own_ref), channel_id=1, source_target_pairs={{0,96},{32,0},{64,32},{96,64},{1,97},{33,1},{65,33},{97,65},{2,98}... | collective-permute-start | bytes 1474568 | tf_op jit(solution)/shard_map/ppermute | solution.py:249
  81.6 5.0 %collective-permute-start.11 = (bf16[160,1536]{1,0:T(8,128)(2,1)S(1)}, bf16[160,1536]{1,0:T(8,128)(2,1)}, u32[]{:S(2)}, u32[]{:S(2)}) collective-permute-start(bf16[160,1536]{1,0:T(8,128)(2,1)S(1)} %shard_map.99.pre_0), channel_id=1, source_target_pairs={{0,384},{128,0},{256,128},{384,256},{1,385},{129,1},{257,129},{385... | collective-permute-start | bytes 1474568 | tf_op jit(solution)/shard_map/ppermute | solution.py:249
  86.6 3.9 %collective-permute-start.14 = (bf16[320,1536]{1,0:T(8,128)(2,1)}, bf16[320,1536]{1,0:T(8,128)(2,1)}, u32[]{:S(2)}, u32[]{:S(2)}) collective-permute-start(bf16[320,1536]{1,0:T(8,128)(2,1)} %get-tuple-element.28.own_ref), channel_id=1, source_target_pairs={{0,96},{32,0},{64,32},{96,64},{1,97},{33,1},{65,33},{97,65},{2,98}... | collective-permute-start | bytes 2949128 | tf_op jit(solution)/shard_map/ppermute | solution.py:249
  91.3 3.3 %collective-permute-start.13 = (bf16[320,1536]{1,0:T(8,128)(2,1)}, bf16[320,1536]{1,0:T(8,128)(2,1)S(1)}, u32[]{:S(2)}, u32[]{:S(2)}) collective-permute-start(bf16[320,1536]{1,0:T(8,128)(2,1)} %get-tuple-element.28.own_ref), channel_id=1, source_target_pairs={{0,64},{32,96},{64,0},{96,32},{1,65},{33,97},{65,1},{97,33},{2,66}... | collective-permute-start | bytes 2949128 | tf_op jit(solution)/shard_map/ppermute | solution.py:249
  94.6 9.5 %collective-permute-start.12 = (bf16[320,1536]{1,0:T(8,128)(2,1)}, bf16[320,1536]{1,0:T(8,128)(2,1)S(1)}, u32[]{:S(2)}, u32[]{:S(2)}) collective-permute-start(bf16[320,1536]{1,0:T(8,128)(2,1)} %get-tuple-element.28.own_ref), channel_id=1, source_target_pairs={{0,32},{32,64},{64,96},{96,0},{1,33},{33,65},{65,97},{97,1},{2,34}... | collective-permute-start | bytes 2949128 | tf_op jit(solution)/shard_map/ppermute | solution.py:249
  110.1 4.2 %collective-permute-start.3 = (bf16[64,768]{1,0:T(8,128)(2,1)S(1)}, bf16[64,768]{1,0:T(8,128)(2,1)S(1)}, u32[]{:S(2)}, u32[]{:S(2)}) collective-permute-start(bf16[64,768]{1,0:T(8,128)(2,1)S(1)} %get-tuple-element.24), channel_id=1, source_target_pairs={{0,128},{128,256},{256,384},{384,0},{1,129},{129,257},{257,385},{3... | collective-permute-start | bytes 294920 | tf_op jit(solution)/shard_map/ppermute | solution.py:249
  114.3 4.7 %collective-permute-start.4 = (bf16[64,768]{1,0:T(8,128)(2,1)S(1)}, bf16[64,768]{1,0:T(8,128)(2,1)S(1)}, u32[]{:S(2)}, u32[]{:S(2)}) collective-permute-start(bf16[64,768]{1,0:T(8,128)(2,1)S(1)} %get-tuple-element.25), channel_id=1, source_target_pairs={{0,256},{128,384},{256,0},{384,128},{1,257},{129,385},{257,1},{385... | collective-permute-start | bytes 294920 | tf_op jit(solution)/shard_map/ppermute | solution.py:249
  119.1 3.0 %collective-permute-start.5 = (bf16[64,768]{1,0:T(8,128)(2,1)S(1)}, bf16[64,768]{1,0:T(8,128)(2,1)S(1)}, u32[]{:S(2)}, u32[]{:S(2)}) collective-permute-start(bf16[64,768]{1,0:T(8,128)(2,1)S(1)} %get-tuple-element.26), channel_id=1, source_target_pairs={{0,384},{128,0},{256,128},{384,256},{1,385},{129,1},{257,129},{385... | collective-permute-start | bytes 294920 | tf_op jit(solution)/shard_map/ppermute | solution.py:249
  122.1 4.2 %collective-permute-start.10 = (bf16[160,1536]{1,0:T(8,128)(2,1)S(1)}, bf16[160,1536]{1,0:T(8,128)(2,1)S(1)}, u32[]{:S(2)}, u32[]{:S(2)}) collective-permute-start(bf16[160,1536]{1,0:T(8,128)(2,1)S(1)} %shard_map.99.pre_0), channel_id=1, source_target_pairs={{0,256},{128,384},{256,0},{384,128},{1,257},{129,385},{257,1},{385... | collective-permute-start | bytes 1474568 | tf_op jit(solution)/shard_map/ppermute | solution.py:249
  128.3 6.5 %collective-permute-done.10.pre_2 = bf16[160,1536]{1,0:T(8,128)(2,1)S(1)} collective-permute-done((bf16[160,1536]{1,0:T(8,128)(2,1)S(1)}, bf16[160,1536]{1,0:T(8,128)(2,1)S(1)}, u32[]{:S(2)}, u32[]{:S(2)}) %collective-permute-start.10) | collective-permute-done | bytes 491552 | tf_op jit(solution)/shard_map/ppermute | solution.py:249
  134.8 3.9 %collective-permute-start.8 = (bf16[64,768]{1,0:T(8,128)(2,1)S(1)}, bf16[64,768]{1,0:T(8,128)(2,1)S(1)}, u32[]{:S(2)}, u32[]{:S(2)}) collective-permute-start(bf16[64,768]{1,0:T(8,128)(2,1)S(1)} %shard_map.98.hidden_0), channel_id=1, source_target_pairs={{0,384},{128,0},{256,128},{384,256},{1,385},{129,1},{257,129},{385... | collective-permute-start | bytes 294920 | tf_op jit(solution)/shard_map/ppermute | solution.py:249
  138.7 9.4 %collective-permute-done.9.pre_1 = bf16[160,1536]{1,0:T(8,128)(2,1)S(1)} collective-permute-done((bf16[160,1536]{1,0:T(8,128)(2,1)S(1)}, bf16[160,1536]{1,0:T(8,128)(2,1)S(1)}, u32[]{:S(2)}, u32[]{:S(2)}) %collective-permute-start.9) | collective-permute-done | bytes 491552 | tf_op jit(solution)/shard_map/ppermute | solution.py:249
  148.2 5.2 %collective-permute-start.7 = (bf16[64,768]{1,0:T(8,128)(2,1)S(1)}, bf16[64,768]{1,0:T(8,128)(2,1)S(1)}, u32[]{:S(2)}, u32[]{:S(2)}) collective-permute-start(bf16[64,768]{1,0:T(8,128)(2,1)S(1)} %shard_map.98.hidden_0), channel_id=1, source_target_pairs={{0,256},{128,384},{256,0},{384,128},{1,257},{129,385},{257,1},{385... | collective-permute-start | bytes 294920 | tf_op jit(solution)/shard_map/ppermute | solution.py:249
  166.5 16.7 %all-to-all-start.1 = ((bf16[128,2,1280]{2,1,0:T(2,128)(2,1)}), bf16[128,2,1280]{2,1,0:T(2,128)(2,1)}, u32[]{:S(2)}, u32[]{:S(2)}) async-start(bf16[128,2,1280]{2,1,0:T(2,128)(2,1)} %copy-done.7), calls=%async_computation.1 | async-start | bytes 1310720 | tf_op jit(solution)/shard_map/all_to_all | solution.py:245
  186.5 3.4 %collective-permute-start.15 = (bf16[96,768]{1,0:T(8,128)(2,1)S(1)}, bf16[96,768]{1,0:T(8,128)(2,1)S(1)}, u32[]{:S(2)}, u32[]{:S(2)}) collective-permute-start(bf16[96,768]{1,0:T(8,128)(2,1)S(1)} %get-tuple-element.30), channel_id=1, source_target_pairs={{0,128},{128,256},{256,384},{384,0},{1,129},{129,257},{257,385},{3... | collective-permute-start | bytes 442376 | tf_op jit(solution)/shard_map/ppermute | solution.py:249
  189.9 4.7 %collective-permute-start.16 = (bf16[96,768]{1,0:T(8,128)(2,1)S(1)}, bf16[96,768]{1,0:T(8,128)(2,1)S(1)}, u32[]{:S(2)}, u32[]{:S(2)}) collective-permute-start(bf16[96,768]{1,0:T(8,128)(2,1)S(1)} %get-tuple-element.31), channel_id=1, source_target_pairs={{0,256},{128,384},{256,0},{384,128},{1,257},{129,385},{257,1},{385... | collective-permute-start | bytes 442376 | tf_op jit(solution)/shard_map/ppermute | solution.py:249
  197.6 4.3 %collective-permute-done.16.part_2 = bf16[96,768]{1,0:T(8,128)(2,1)S(1)} collective-permute-done((bf16[96,768]{1,0:T(8,128)(2,1)S(1)}, bf16[96,768]{1,0:T(8,128)(2,1)S(1)}, u32[]{:S(2)}, u32[]{:S(2)}) %collective-permute-start.16) | collective-permute-done | bytes 147488 | tf_op jit(solution)/shard_map/ppermute | solution.py:249
  202.3 4.8 %collective-permute-start.20 = (bf16[96,768]{1,0:T(8,128)(2,1)S(1)}, bf16[96,768]{1,0:T(8,128)(2,1)S(1)}, u32[]{:S(2)}, u32[]{:S(2)}) collective-permute-start(bf16[96,768]{1,0:T(8,128)(2,1)S(1)} %shard_map.105.hidden_0), channel_id=1, source_target_pairs={{0,384},{128,0},{256,128},{384,256},{1,385},{129,1},{257,129},{385... | collective-permute-start | bytes 442376 | tf_op jit(solution)/shard_map/ppermute | solution.py:249
  207.2 3.9 %collective-permute-start.19 = (bf16[96,768]{1,0:T(8,128)(2,1)S(1)}, bf16[96,768]{1,0:T(8,128)(2,1)S(1)}, u32[]{:S(2)}, u32[]{:S(2)}) collective-permute-start(bf16[96,768]{1,0:T(8,128)(2,1)S(1)} %shard_map.105.hidden_0), channel_id=1, source_target_pairs={{0,256},{128,384},{256,0},{384,128},{1,257},{129,385},{257,1},{385... | collective-permute-start | bytes 442376 | tf_op jit(solution)/shard_map/ppermute | solution.py:249
  215.3 4.8 %collective-permute-done.18.hidden_1 = bf16[96,768]{1,0:T(8,128)(2,1)S(1)} collective-permute-done((bf16[96,768]{1,0:T(8,128)(2,1)S(1)}, bf16[96,768]{1,0:T(8,128)(2,1)S(1)}, u32[]{:S(2)}, u32[]{:S(2)}) %collective-permute-start.18) | collective-permute-done | bytes 147488 | tf_op jit(solution)/shard_map/ppermute | solution.py:249
  221.7 4.7 %shard_map.106.after_ref = bf16[128,2,1920]{2,1,0:T(2,128)(2,1)} custom-call(s32[2]{0:T(128)S(1)} %pad_add_fusion.at_ref, bf16[96,768]{1,0:T(8,128)(2,1)S(1)} %shard_map.105.hidden_0, bf16[96,768]{1,0:T(8,128)(2,1)S(1)} %collective-permute-done.18.hidden_1, bf16[96,768]{1,0:T(8,128)(2,1)S(1)} %collective-permute-done.19.hidden_2, ...), custom_call_target="tpu_custom_call" | custom-call | flops 2147483648 | bytes 8388608 | tf_op jit(solution)/shard_map/pallas_call | solution.py:333
  226.3 14.8 %all-to-all-start.3 = ((bf16[128,2,1920]{2,1,0:T(2,128)(2,1)}), bf16[128,2,1920]{2,1,0:T(2,128)(2,1)S(1)}, u32[]{:S(2)}, u32[]{:S(2)}) async-start(bf16[128,2,1920]{2,1,0:T(2,128)(2,1)} %shard_map.106.after_ref), calls=%async_computation.3 | async-start | bytes 1966080 | tf_op jit(solution)/shard_map/all_to_all | solution.py:245
  250.5 3.9 %collective-permute-start.23 = (bf16[320,768]{1,0:T(8,128)(2,1)S(1)}, bf16[320,768]{1,0:T(8,128)(2,1)S(1)}, u32[]{:S(2)}, u32[]{:S(2)}) collective-permute-start(bf16[320,768]{1,0:T(8,128)(2,1)S(1)} %get-tuple-element.39), channel_id=1, source_target_pairs={{0,96},{32,0},{64,32},{96,64},{1,97},{33,1},{65,33},{97,65},{2,98}... | collective-permute-start | bytes 1474568 | tf_op jit(solution)/shard_map/ppermute | solution.py:249
  254.4 16.8 %collective-permute-done.21.part_1 = bf16[320,768]{1,0:T(8,128)(2,1)S(1)} collective-permute-done((bf16[320,768]{1,0:T(8,128)(2,1)S(1)}, bf16[320,768]{1,0:T(8,128)(2,1)S(1)}, u32[]{:S(2)}, u32[]{:S(2)}) %collective-permute-start.21) | collective-permute-done | bytes 491552 | tf_op jit(solution)/shard_map/ppermute | solution.py:249
  271.2 3.0 %collective-permute-done.23.part_3 = bf16[320,768]{1,0:T(8,128)(2,1)S(1)} collective-permute-done((bf16[320,768]{1,0:T(8,128)(2,1)S(1)}, bf16[320,768]{1,0:T(8,128)(2,1)S(1)}, u32[]{:S(2)}, u32[]{:S(2)}) %collective-permute-start.23) | collective-permute-done | bytes 491552 | tf_op jit(solution)/shard_map/ppermute | solution.py:249
  275.2 17.7 %all-to-all-done.3.ret_b_ref = bf16[128,2,1920]{2,1,0:T(2,128)(2,1)S(1)} async-done(((bf16[128,2,1920]{2,1,0:T(2,128)(2,1)}), bf16[128,2,1920]{2,1,0:T(2,128)(2,1)S(1)}, u32[]{:S(2)}, u32[]{:S(2)}) %all-to-all-start.3) | async-done | bytes 983072 | tf_op jit(solution)/shard_map/all_to_all | solution.py:245
  292.9 3.3 %shard_map.107 = bf16[128,5120]{1,0:T(8,128)(2,1)} custom-call(bf16[128,2,1280]{2,1,0:T(2,128)(2,1)} %all-to-all-done.1.ret_a_ref, bf16[128,2,1920]{2,1,0:T(2,128)(2,1)S(1)} %all-to-all-done.3.ret_b_ref, s32[6,128]{1,0:T(8,128)S(1)} %bitcast.19, s32[6,128]{1,0:T(8,128)S(1)} %bitcast.22), custom_call_target="tpu_custom_call" | custom-call | flops 1073741824 | bytes 4194304 | tf_op jit(solution)/shard_map/pallas_call | solution.py:358
  (84 shorter events, 51.6 us)
Async XLA Ops:
  4.5 58.7 %all-to-all-start = ((bf16[128,2,1280]{2,1,0:T(2,128)(2,1)}), bf16[128,2,1280]{2,1,0:T(2,128)(2,1)S(1)}, u32[]{:S(2)}, u32[]{:S(2)}) async-start(bf16[128,2,1280]{2,1,0:T(2,128)(2,1)} %get-tuple-element.21.after_ref.refs_4_), calls=%async_computation | async-start | bytes 1310720 | tf_op jit(solution)/shard_map/all_to_all | solution.py:245
  26.1 55.2 %copy-start.1 = (bf16[128,2,1280]{2,1,0:T(2,128)(2,1)S(1)}, bf16[128,2,1280]{2,1,0:T(2,128)(2,1)}, u32[]{:S(2)}) copy-start(bf16[128,2,1280]{2,1,0:T(2,128)(2,1)} %get-tuple-element.21.after_ref.refs_4_) | copy-start | bytes 1966084
  26.1 55.2 %copy-start.8 = (bf16[1,160,1536]{2,1,0:T(8,128)(2,1)S(1)}, bf16[1,160,1536]{2,1,0:T(8,128)(2,1)}, u32[]{:S(2)}) copy-start(bf16[1,160,1536]{2,1,0:T(8,128)(2,1)} %param.12) | copy-start | bytes 1474564
  64.0 102.5 %all-to-all-start.2 = ((bf16[128,2,1920]{2,1,0:T(2,128)(2,1)}), bf16[128,2,1920]{2,1,0:T(2,128)(2,1)S(1)}, u32[]{:S(2)}, u32[]{:S(2)}) async-start(bf16[128,2,1920]{2,1,0:T(2,128)(2,1)} %shard_map.103), calls=%async_computation.2 | async-start | bytes 1966080 | tf_op jit(solution)/shard_map/all_to_all | solution.py:245
  71.7 18.8 %collective-permute-start.2 = (bf16[320,768]{1,0:T(8,128)(2,1)}, bf16[320,768]{1,0:T(8,128)(2,1)S(1)}, u32[]{:S(2)}, u32[]{:S(2)}) collective-permute-start(bf16[320,768]{1,0:T(8,128)(2,1)} %get-tuple-element.22.own_ref), channel_id=1, source_target_pairs={{0,96},{32,0},{64,32},{96,64},{1,97},{33,1},{65,33},{97,65},{2,98}... | collective-permute-start | bytes 1474568 | tf_op jit(solution)/shard_map/ppermute | solution.py:249
  76.4 18.2 %collective-permute-start.1 = (bf16[320,768]{1,0:T(8,128)(2,1)}, bf16[320,768]{1,0:T(8,128)(2,1)}, u32[]{:S(2)}, u32[]{:S(2)}) collective-permute-start(bf16[320,768]{1,0:T(8,128)(2,1)} %get-tuple-element.22.own_ref), channel_id=1, source_target_pairs={{0,64},{32,96},{64,0},{96,32},{1,65},{33,97},{65,1},{97,33},{2,66}... | collective-permute-start | bytes 1474568 | tf_op jit(solution)/shard_map/ppermute | solution.py:249
  78.7 26.7 %collective-permute-start = (bf16[320,768]{1,0:T(8,128)(2,1)}, bf16[320,768]{1,0:T(8,128)(2,1)}, u32[]{:S(2)}, u32[]{:S(2)}) collective-permute-start(bf16[320,768]{1,0:T(8,128)(2,1)} %get-tuple-element.22.own_ref), channel_id=1, source_target_pairs={{0,32},{32,64},{64,96},{96,0},{1,33},{33,65},{65,97},{97,1},{2,34}... | collective-permute-start | bytes 1474568 | tf_op jit(solution)/shard_map/ppermute | solution.py:249
  81.6 32.7 %collective-permute-start.11 = (bf16[160,1536]{1,0:T(8,128)(2,1)S(1)}, bf16[160,1536]{1,0:T(8,128)(2,1)}, u32[]{:S(2)}, u32[]{:S(2)}) collective-permute-start(bf16[160,1536]{1,0:T(8,128)(2,1)S(1)} %shard_map.99.pre_0), channel_id=1, source_target_pairs={{0,384},{128,0},{256,128},{384,256},{1,385},{129,1},{257,129},{385... | collective-permute-start | bytes 1474568 | tf_op jit(solution)/shard_map/ppermute | solution.py:249
  86.6 66.7 %collective-permute-start.14 = (bf16[320,1536]{1,0:T(8,128)(2,1)}, bf16[320,1536]{1,0:T(8,128)(2,1)}, u32[]{:S(2)}, u32[]{:S(2)}) collective-permute-start(bf16[320,1536]{1,0:T(8,128)(2,1)} %get-tuple-element.28.own_ref), channel_id=1, source_target_pairs={{0,96},{32,0},{64,32},{96,64},{1,97},{33,1},{65,33},{97,65},{2,98}... | collective-permute-start | bytes 2949128 | tf_op jit(solution)/shard_map/ppermute | solution.py:249
  91.3 67.2 %collective-permute-start.13 = (bf16[320,1536]{1,0:T(8,128)(2,1)}, bf16[320,1536]{1,0:T(8,128)(2,1)S(1)}, u32[]{:S(2)}, u32[]{:S(2)}) collective-permute-start(bf16[320,1536]{1,0:T(8,128)(2,1)} %get-tuple-element.28.own_ref), channel_id=1, source_target_pairs={{0,64},{32,96},{64,0},{96,32},{1,65},{33,97},{65,1},{97,33},{2,66}... | collective-permute-start | bytes 2949128 | tf_op jit(solution)/shard_map/ppermute | solution.py:249
  94.6 63.8 %collective-permute-start.12 = (bf16[320,1536]{1,0:T(8,128)(2,1)}, bf16[320,1536]{1,0:T(8,128)(2,1)S(1)}, u32[]{:S(2)}, u32[]{:S(2)}) collective-permute-start(bf16[320,1536]{1,0:T(8,128)(2,1)} %get-tuple-element.28.own_ref), channel_id=1, source_target_pairs={{0,32},{32,64},{64,96},{96,0},{1,33},{33,65},{65,97},{97,1},{2,34}... | collective-permute-start | bytes 2949128 | tf_op jit(solution)/shard_map/ppermute | solution.py:249
  110.1 48.4 %copy-start.20 = (bf16[4,64,1280]{2,1,0:T(8,128)(2,1)}, bf16[4,64,1280]{2,1,0:T(8,128)(2,1)S(1)}, u32[]{:S(2)}) copy-start(bf16[4,64,1280]{2,1,0:T(8,128)(2,1)S(1)} %get-tuple-element.33.sent_a_ref) | copy-start | bytes 1966084
  110.1 8.9 %collective-permute-start.3 = (bf16[64,768]{1,0:T(8,128)(2,1)S(1)}, bf16[64,768]{1,0:T(8,128)(2,1)S(1)}, u32[]{:S(2)}, u32[]{:S(2)}) collective-permute-start(bf16[64,768]{1,0:T(8,128)(2,1)S(1)} %get-tuple-element.24), channel_id=1, source_target_pairs={{0,128},{128,256},{256,384},{384,0},{1,129},{129,257},{257,385},{3... | collective-permute-start | bytes 294920 | tf_op jit(solution)/shard_map/ppermute | solution.py:249
  114.3 7.8 %collective-permute-start.4 = (bf16[64,768]{1,0:T(8,128)(2,1)S(1)}, bf16[64,768]{1,0:T(8,128)(2,1)S(1)}, u32[]{:S(2)}, u32[]{:S(2)}) collective-permute-start(bf16[64,768]{1,0:T(8,128)(2,1)S(1)} %get-tuple-element.25), channel_id=1, source_target_pairs={{0,256},{128,384},{256,0},{384,128},{1,257},{129,385},{257,1},{385... | collective-permute-start | bytes 294920 | tf_op jit(solution)/shard_map/ppermute | solution.py:249
  119.1 7.2 %collective-permute-start.5 = (bf16[64,768]{1,0:T(8,128)(2,1)S(1)}, bf16[64,768]{1,0:T(8,128)(2,1)S(1)}, u32[]{:S(2)}, u32[]{:S(2)}) collective-permute-start(bf16[64,768]{1,0:T(8,128)(2,1)S(1)} %get-tuple-element.26), channel_id=1, source_target_pairs={{0,384},{128,0},{256,128},{384,256},{1,385},{129,1},{257,129},{385... | collective-permute-start | bytes 294920 | tf_op jit(solution)/shard_map/ppermute | solution.py:249
  122.1 12.7 %collective-permute-start.10 = (bf16[160,1536]{1,0:T(8,128)(2,1)S(1)}, bf16[160,1536]{1,0:T(8,128)(2,1)S(1)}, u32[]{:S(2)}, u32[]{:S(2)}) collective-permute-start(bf16[160,1536]{1,0:T(8,128)(2,1)S(1)} %shard_map.99.pre_0), channel_id=1, source_target_pairs={{0,256},{128,384},{256,0},{384,128},{1,257},{129,385},{257,1},{385... | collective-permute-start | bytes 1474568 | tf_op jit(solution)/shard_map/ppermute | solution.py:249
  126.3 21.9 %collective-permute-start.9 = (bf16[160,1536]{1,0:T(8,128)(2,1)S(1)}, bf16[160,1536]{1,0:T(8,128)(2,1)S(1)}, u32[]{:S(2)}, u32[]{:S(2)}) collective-permute-start(bf16[160,1536]{1,0:T(8,128)(2,1)S(1)} %shard_map.99.pre_0), channel_id=1, source_target_pairs={{0,128},{128,256},{256,384},{384,0},{1,129},{129,257},{257,385},{3... | collective-permute-start | bytes 1474568 | tf_op jit(solution)/shard_map/ppermute | solution.py:249
  134.8 26.2 %collective-permute-start.8 = (bf16[64,768]{1,0:T(8,128)(2,1)S(1)}, bf16[64,768]{1,0:T(8,128)(2,1)S(1)}, u32[]{:S(2)}, u32[]{:S(2)}) collective-permute-start(bf16[64,768]{1,0:T(8,128)(2,1)S(1)} %shard_map.98.hidden_0), channel_id=1, source_target_pairs={{0,384},{128,0},{256,128},{384,256},{1,385},{129,1},{257,129},{385... | collective-permute-start | bytes 294920 | tf_op jit(solution)/shard_map/ppermute | solution.py:249
  148.2 12.8 %collective-permute-start.7 = (bf16[64,768]{1,0:T(8,128)(2,1)S(1)}, bf16[64,768]{1,0:T(8,128)(2,1)S(1)}, u32[]{:S(2)}, u32[]{:S(2)}) collective-permute-start(bf16[64,768]{1,0:T(8,128)(2,1)S(1)} %shard_map.98.hidden_0), channel_id=1, source_target_pairs={{0,256},{128,384},{256,0},{384,128},{1,257},{129,385},{257,1},{385... | collective-permute-start | bytes 294920 | tf_op jit(solution)/shard_map/ppermute | solution.py:249
  153.3 7.7 %collective-permute-start.6 = (bf16[64,768]{1,0:T(8,128)(2,1)S(1)}, bf16[64,768]{1,0:T(8,128)(2,1)S(1)}, u32[]{:S(2)}, u32[]{:S(2)}) collective-permute-start(bf16[64,768]{1,0:T(8,128)(2,1)S(1)} %shard_map.98.hidden_0), channel_id=1, source_target_pairs={{0,128},{128,256},{256,384},{384,0},{1,129},{129,257},{257,385},{3... | collective-permute-start | bytes 294920 | tf_op jit(solution)/shard_map/ppermute | solution.py:249
  166.5 59.8 %all-to-all-start.1 = ((bf16[128,2,1280]{2,1,0:T(2,128)(2,1)}), bf16[128,2,1280]{2,1,0:T(2,128)(2,1)}, u32[]{:S(2)}, u32[]{:S(2)}) async-start(bf16[128,2,1280]{2,1,0:T(2,128)(2,1)} %copy-done.7), calls=%async_computation.1 | async-start | bytes 1310720 | tf_op jit(solution)/shard_map/all_to_all | solution.py:245
  183.2 36.9 %copy-start.4 = (bf16[1280,1536]{1,0:T(8,128)(2,1)S(1)}, bf16[1280,1536]{1,0:T(8,128)(2,1)}, u32[]{:S(2)}) copy-start(bf16[1280,1536]{1,0:T(8,128)(2,1)} %copy-done.3) | copy-start | bytes 11796484
  186.5 11.0 %collective-permute-start.15 = (bf16[96,768]{1,0:T(8,128)(2,1)S(1)}, bf16[96,768]{1,0:T(8,128)(2,1)S(1)}, u32[]{:S(2)}, u32[]{:S(2)}) collective-permute-start(bf16[96,768]{1,0:T(8,128)(2,1)S(1)} %get-tuple-element.30), channel_id=1, source_target_pairs={{0,128},{128,256},{256,384},{384,0},{1,129},{129,257},{257,385},{3... | collective-permute-start | bytes 442376 | tf_op jit(solution)/shard_map/ppermute | solution.py:249
  189.9 11.9 %collective-permute-start.16 = (bf16[96,768]{1,0:T(8,128)(2,1)S(1)}, bf16[96,768]{1,0:T(8,128)(2,1)S(1)}, u32[]{:S(2)}, u32[]{:S(2)}) collective-permute-start(bf16[96,768]{1,0:T(8,128)(2,1)S(1)} %get-tuple-element.31), channel_id=1, source_target_pairs={{0,256},{128,384},{256,0},{384,128},{1,257},{129,385},{257,1},{385... | collective-permute-start | bytes 442376 | tf_op jit(solution)/shard_map/ppermute | solution.py:249
  194.7 7.6 %collective-permute-start.17 = (bf16[96,768]{1,0:T(8,128)(2,1)S(1)}, bf16[96,768]{1,0:T(8,128)(2,1)S(1)}, u32[]{:S(2)}, u32[]{:S(2)}) collective-permute-start(bf16[96,768]{1,0:T(8,128)(2,1)S(1)} %get-tuple-element.32), channel_id=1, source_target_pairs={{0,384},{128,0},{256,128},{384,256},{1,385},{129,1},{257,129},{385... | collective-permute-start | bytes 442376 | tf_op jit(solution)/shard_map/ppermute | solution.py:249
  202.3 10.7 %collective-permute-start.20 = (bf16[96,768]{1,0:T(8,128)(2,1)S(1)}, bf16[96,768]{1,0:T(8,128)(2,1)S(1)}, u32[]{:S(2)}, u32[]{:S(2)}) collective-permute-start(bf16[96,768]{1,0:T(8,128)(2,1)S(1)} %shard_map.105.hidden_0), channel_id=1, source_target_pairs={{0,384},{128,0},{256,128},{384,256},{1,385},{129,1},{257,129},{385... | collective-permute-start | bytes 442376 | tf_op jit(solution)/shard_map/ppermute | solution.py:249
  207.2 8.1 %collective-permute-start.19 = (bf16[96,768]{1,0:T(8,128)(2,1)S(1)}, bf16[96,768]{1,0:T(8,128)(2,1)S(1)}, u32[]{:S(2)}, u32[]{:S(2)}) collective-permute-start(bf16[96,768]{1,0:T(8,128)(2,1)S(1)} %shard_map.105.hidden_0), channel_id=1, source_target_pairs={{0,256},{128,384},{256,0},{384,128},{1,257},{129,385},{257,1},{385... | collective-permute-start | bytes 442376 | tf_op jit(solution)/shard_map/ppermute | solution.py:249
  211.1 9.0 %collective-permute-start.18 = (bf16[96,768]{1,0:T(8,128)(2,1)S(1)}, bf16[96,768]{1,0:T(8,128)(2,1)S(1)}, u32[]{:S(2)}, u32[]{:S(2)}) collective-permute-start(bf16[96,768]{1,0:T(8,128)(2,1)S(1)} %shard_map.105.hidden_0), channel_id=1, source_target_pairs={{0,128},{128,256},{256,384},{384,0},{1,129},{129,257},{257,385},{3... | collective-permute-start | bytes 442376 | tf_op jit(solution)/shard_map/ppermute | solution.py:249
  226.3 66.5 %all-to-all-start.3 = ((bf16[128,2,1920]{2,1,0:T(2,128)(2,1)}), bf16[128,2,1920]{2,1,0:T(2,128)(2,1)S(1)}, u32[]{:S(2)}, u32[]{:S(2)}) async-start(bf16[128,2,1920]{2,1,0:T(2,128)(2,1)} %shard_map.106.after_ref), calls=%async_computation.3 | async-start | bytes 1966080 | tf_op jit(solution)/shard_map/all_to_all | solution.py:245
  245.9 25.2 %collective-permute-start.21 = (bf16[320,768]{1,0:T(8,128)(2,1)S(1)}, bf16[320,768]{1,0:T(8,128)(2,1)S(1)}, u32[]{:S(2)}, u32[]{:S(2)}) collective-permute-start(bf16[320,768]{1,0:T(8,128)(2,1)S(1)} %get-tuple-element.37), channel_id=1, source_target_pairs={{0,32},{32,64},{64,96},{96,0},{1,33},{33,65},{65,97},{97,1},{2,34}... | collective-permute-start | bytes 1474568 | tf_op jit(solution)/shard_map/ppermute | solution.py:249
  247.9 23.3 %collective-permute-start.22 = (bf16[320,768]{1,0:T(8,128)(2,1)S(1)}, bf16[320,768]{1,0:T(8,128)(2,1)S(1)}, u32[]{:S(2)}, u32[]{:S(2)}) collective-permute-start(bf16[320,768]{1,0:T(8,128)(2,1)S(1)} %get-tuple-element.38), channel_id=1, source_target_pairs={{0,64},{32,96},{64,0},{96,32},{1,65},{33,97},{65,1},{97,33},{2,66}... | collective-permute-start | bytes 1474568 | tf_op jit(solution)/shard_map/ppermute | solution.py:249
  250.5 23.7 %collective-permute-start.23 = (bf16[320,768]{1,0:T(8,128)(2,1)S(1)}, bf16[320,768]{1,0:T(8,128)(2,1)S(1)}, u32[]{:S(2)}, u32[]{:S(2)}) collective-permute-start(bf16[320,768]{1,0:T(8,128)(2,1)S(1)} %get-tuple-element.39), channel_id=1, source_target_pairs={{0,96},{32,0},{64,32},{96,64},{1,97},{33,1},{65,33},{97,65},{2,98}... | collective-permute-start | bytes 1474568 | tf_op jit(solution)/shard_map/ppermute | solution.py:249
  (18 other events, 130.4 us)

commit v5 on v4

v5 whole, which is shorter than its diff:
```python
import jax
import jax.numpy as jnp
from jax import lax
from jax.experimental import pallas as pl
from jax.experimental.pallas import tpu as pltpu
from jax.sharding import Mesh, PartitionSpec as P

BF = jnp.bfloat16
F32 = jnp.float32

N_EXP = 32
CAP = 5
TOK = 128
GX = 4
GY = 4
WIDE = 1280
HALF = 640
HID = 768
ROWS = N_EXP * CAP
PAIRS = 2 * N_EXP
PART = 320
VMEM_LIMIT = 16 * 1024 * 1024
VMEM_MOST = 60 * 1024 * 1024


def iota(shape, dim):
    return lax.broadcasted_iota(jnp.int32, shape, dim)


def nn(left, right):
    return lax.dot_general(left, right, (((1,), (0,)), ((), ())), preferred_element_type=F32)


def nt(left, right):
    return lax.dot_general(left, right, (((1,), (1,)), ((), ())), preferred_element_type=F32)


def tn(left, right):
    return lax.dot_general(left, right, (((0,), (0,)), ((), ())), preferred_element_type=F32)


def one_hot(mask):
    return jnp.where(mask, 1.0, 0.0).astype(BF)


def call(body, out_shape, flops=0, moved=0, limit=VMEM_LIMIT, **kwargs):
    return pl.pallas_call(
        body,
        out_shape=out_shape,
        compiler_params=pltpu.CompilerParams(vmem_limit_bytes=limit),
        cost_estimate=pl.CostEstimate(flops=flops, bytes_accessed=moved, transcendentals=0),
        **kwargs,
    )


def arr(*dims, dtype=BF):
    return jax.ShapeDtypeStruct(dims, dtype)


def select(ids_ref, slots_ref, probs):
    code = ids_ref[...] * CAP + slots_ref[...]
    shape = (CAP * PAIRS, TOK)
    row = iota(shape, 0)
    row_code = ((row % PAIRS) // 2) * CAP + row // PAIRS
    hits = jnp.zeros(shape, F32)
    weight = jnp.zeros(shape, F32)
    for k in range(code.shape[0]):
        same = row_code == code[k : k + 1, :]
        hits = hits + jnp.where(same, 1.0, 0.0)
        if probs is not None:
            weight = weight + jnp.where(same, probs[k : k + 1, :], 0.0)
    lower = row % 2 == 0
    pick = jnp.concatenate([jnp.where(lower, hits, 0.0), jnp.where(lower, 0.0, hits)], axis=1)
    return pick.astype(BF), jnp.sum(weight, axis=1, keepdims=True)


def split_halves():
    row = iota((PAIRS, PAIRS), 0)
    col = iota((PAIRS, PAIRS), 1)
    return one_hot(col == (row % N_EXP) * 2 + row // N_EXP)


def join_halves():
    row = iota((PAIRS, PAIRS), 0)
    col = iota((PAIRS, PAIRS), 1)
    return one_hot(row == (col % N_EXP) * 2 + col // N_EXP)


def to_pairs(rows):
    return rows.reshape(N_EXP, 2, HALF).astype(BF)


def from_pairs(block):
    return block.astype(F32).reshape(PAIRS, HALF).astype(BF)


def pick_kernel(
    og_any, ids_any, slots_any, probs_any, down_any, gate_any, up_any,
    msg_any, own_down_any, own_in_any,
    og_ref, ids_ref, slots_ref, probs_ref, msg_ref, down_ref, in_ref,
    og_sem, in_sem, out_sem, fetch_sem, store_sem,
):
    small = [
        pltpu.make_async_copy(src, dst, in_sem.at[i])
        for i, (src, dst) in enumerate(((ids_any, ids_ref), (slots_any, slots_ref), (probs_any, probs_ref)))
    ]
    wide = [
        pltpu.make_async_copy(og_any.at[:, pl.ds(g * WIDE, WIDE)], og_ref.at[g], og_sem.at[g])
        for g in range(GX)
    ]
    fetches = [
        pltpu.make_async_copy(down_any, down_ref, fetch_sem.at[0]),
        pltpu.make_async_copy(gate_any, in_ref.at[:, pl.ds(0, HID)], fetch_sem.at[1]),
        pltpu.make_async_copy(up_any, in_ref.at[:, pl.ds(HID, HID)], fetch_sem.at[2]),
    ]
    stores = [
        pltpu.make_async_copy(down_ref, own_down_any, store_sem.at[0]),
        pltpu.make_async_copy(in_ref, own_in_any, store_sem.at[1]),
    ]
    for copy in small + wide + fetches:
        copy.start()
    for copy in small:
        copy.wait()
    pick, weight = select(ids_ref, slots_ref, probs_ref[...])
    sends = []
    for g in range(GX):
        wide[g].wait()
        both = jnp.concatenate([og_ref[g, :, :HALF], og_ref[g, :, HALF:]], axis=0)
        rows = nn(pick, both) * weight
        for s in range(CAP):
            msg_ref[g * N_EXP : (g + 1) * N_EXP, :, s * HALF : (s + 1) * HALF] = to_pairs(
                rows[s * PAIRS : (s + 1) * PAIRS]
            )
        span = pl.ds(g * N_EXP, N_EXP)
        sends.append(pltpu.make_async_copy(msg_ref.at[span], msg_any.at[span], out_sem.at[g]))
        sends[-1].start()
        if g == 1:
            for copy in fetches:
                copy.wait()
            for copy in stores:
                copy.start()
    for copy in sends + stores:
        copy.wait()


def arrange_kernel(at_ref, own_ref, piece_1, piece_2, piece_3, out_ref):
    for r, ref in enumerate((own_ref, piece_1, piece_2, piece_3)):
        q = lax.rem(at_ref[1] + (GY - r), GY)
        out_ref[pl.ds(pl.multiple_of(q * PART, 64), PART), :] = ref[...]


def order_kernel(pre_ref, after_ref, out_ref):
    row = iota((ROWS, ROWS), 0)
    col = iota((ROWS, ROWS), 1)
    swap_rows = one_hot(col == (row % N_EXP) * CAP + row // N_EXP)
    out_ref[...] = nn(swap_rows, pre_ref[...]).astype(BF)


def factor_kernel(pre_0, pre_1, pre_2, pre_3, factor_ref, act_ref):
    for r, pre_ref in enumerate((pre_0, pre_1, pre_2, pre_3)):
        for s in range(CAP):
            span = slice(s * N_EXP, (s + 1) * N_EXP)
            gate_pre = pre_ref[span, :HID].astype(F32)
            up_pre = pre_ref[span, HID:].astype(F32)
            sig = jax.nn.sigmoid(gate_pre)
            lift = gate_pre * sig
            factor_ref[r, span, :HID] = (up_pre * sig * (1.0 + gate_pre * (1.0 - sig))).astype(BF)
            factor_ref[r, span, HID:] = lift.astype(BF)
            act_ref[r, span, :] = (lift * up_pre).astype(BF)


def hidden_kernel(at_ref, recv_ref, down_ref, sent_ref, part_ref):
    split = split_halves()
    for r in range(GX):
        g = lax.rem(at_ref[0] + (GX - r), GX)
        for s in range(CAP):
            rows = from_pairs(recv_ref[pl.ds(g * N_EXP, N_EXP), :, s * HALF : (s + 1) * HALF])
            halves = nn(split, rows).astype(BF)
            span = slice(s * N_EXP, (s + 1) * N_EXP)
            sent_ref[r, span, :HALF] = halves[:N_EXP]
            sent_ref[r, span, HALF:] = halves[N_EXP:]
        part_ref[g] = nn(sent_ref[r], down_ref[...]).astype(BF)


def spread_kernel(part_ref, out_ref):
    total = part_ref[0].astype(F32) + part_ref[1].astype(F32)
    total = (total + (part_ref[2].astype(F32) + part_ref[3].astype(F32))).astype(BF)
    for g in range(GX):
        out_ref[g] = total


def back_kernel(at_ref, hidden_ref, factor_ref, in_ref, msg_ref):
    grads = []
    for r in range(GX):
        hidden = hidden_ref[lax.rem(at_ref[0] + (GX - r), GX)].astype(F32)
        gate_grad = (hidden * factor_ref[r, :, :HID].astype(F32)).astype(BF)
        up_grad = (hidden * factor_ref[r, :, HID:].astype(F32)).astype(BF)
        grads.append(jnp.concatenate([gate_grad, up_grad], axis=1))
    rows = nt(jnp.concatenate(grads, axis=0), in_ref[...]).astype(BF)
    join = join_halves()
    for r in range(GX):
        g = lax.rem(at_ref[0] + (GX - r), GX)
        for s in range(CAP):
            own = rows[(r * CAP + s) * N_EXP : (r * CAP + s + 1) * N_EXP]
            both = jnp.concatenate([own[:, :HALF], own[:, HALF:]], axis=0)
            msg_ref[pl.ds(g * N_EXP, N_EXP), :, s * HALF : (s + 1) * HALF] = to_pairs(nn(join, both))


def total_kernel(part_0, part_1, part_2, part_3, out_ref):
    total = part_0[...].astype(F32) + part_1[...].astype(F32)
    out_ref[...] = (total + (part_2[...].astype(F32) + part_3[...].astype(F32))).astype(BF)


def down_kernel(at_ref, sent_ref, act_ref, after_ref, out_0, out_1, out_2, out_3, full_ref):
    sent = jnp.concatenate([sent_ref[r] for r in range(GX)], axis=0)
    act = jnp.concatenate([act_ref[r] for r in range(GX)], axis=0)
    full_ref[...] = tn(sent, act).astype(BF)
    for r, out_ref in enumerate((out_0, out_1, out_2, out_3)):
        q = lax.rem(at_ref[1] + r, GY)
        out_ref[...] = full_ref[pl.ds(pl.multiple_of(q * PART, 64), PART), :]


def gather_kernel(ret_ref, ids_ref, slots_ref, out_ref):
    pick, _ = select(ids_ref, slots_ref, None)
    for g in range(GX):
        rows = jnp.concatenate(
            [
                from_pairs(ret_ref[g * N_EXP : (g + 1) * N_EXP, :, s * HALF : (s + 1) * HALF])
                for s in range(CAP)
            ],
            axis=0,
        )
        halves = tn(pick, rows).astype(BF)
        out_ref[:, g * WIDE : g * WIDE + HALF] = halves[:TOK]
        out_ref[:, g * WIDE + HALF : (g + 1) * WIDE] = halves[TOK:]


def swap(value):
    return lax.all_to_all(value, ("gx", "expert"), 0, 0, tiled=True)


def swap_gx(value):
    return lax.all_to_all(value, "gx", 0, 0, tiled=True)


def step(value, axis, r):
    return lax.ppermute(value, axis, [(i, (i + r) % 4) for i in range(4)])


def steps(value, axis):
    return [step(value, axis, r) for r in range(1, 4)]


def per_device(out_grad, route_ids, route_slots, route_probs, saved_pre, w_gate, w_up, w_down):
    ids, slots, probs = route_ids.T, route_slots.T, route_probs.T
    at = jnp.stack([lax.axis_index("gx"), lax.axis_index("gy")])
    smem = pl.BlockSpec(memory_space=pltpu.SMEM)
    vmem = pl.BlockSpec(memory_space=pltpu.VMEM)
    anywhere = pl.BlockSpec(memory_space=pl.ANY)
    message = arr(GX * N_EXP, 2, CAP * HALF)

    msg, own_down, own_in = call(
        pick_kernel,
        (message, arr(PART, HID), arr(PART, 2 * HID)),
        1 << 29,
        1 << 23,
        VMEM_MOST,
        in_specs=[anywhere] * 7,
        out_specs=[anywhere] * 3,
        scratch_shapes=[
            pltpu.VMEM((GX, TOK, WIDE), BF),
            pltpu.VMEM(ids.shape, jnp.int32),
            pltpu.VMEM(ids.shape, jnp.int32),
            pltpu.VMEM(ids.shape, F32),
            pltpu.VMEM(message.shape, BF),
            pltpu.VMEM((PART, HID), BF),
            pltpu.VMEM((PART, 2 * HID), BF),
            pltpu.SemaphoreType.DMA((GX,)),
            pltpu.SemaphoreType.DMA((3,)),
            pltpu.SemaphoreType.DMA((GX,)),
            pltpu.SemaphoreType.DMA((3,)),
            pltpu.SemaphoreType.DMA((2,)),
        ],
    )(out_grad, ids, slots, probs, w_down[0].T, w_gate[0], w_up[0])
    recv = swap(msg)

    def arrange(own):
        return call(
            arrange_kernel,
            arr(WIDE, own.shape[1]),
            0,
            1 << 23,
            in_specs=[smem] + [vmem] * 4,
        )(at, own, *steps(own, "gy"))

    down_w, in_w = arrange(own_down), arrange(own_in)
    pre = call(order_kernel, arr(ROWS, 2 * HID), 1 << 27, 1 << 21, in_specs=[vmem, anywhere])(
        saved_pre[0], msg
    )
    factors, act = call(
        factor_kernel, (arr(GX, ROWS, 2 * HID), arr(GX, ROWS, HID)), 1 << 25, 1 << 23
    )(pre, *steps(pre, "gx"))

    sent, part = call(
        hidden_kernel,
        (arr(GX, ROWS, WIDE), arr(GX, ROWS, HID)),
        1 << 31,
        1 << 23,
        in_specs=[smem, vmem, vmem],
    )(at, recv, down_w)
    hidden = swap_gx(call(spread_kernel, arr(GX, ROWS, HID), 0, 1 << 21)(swap_gx(part)))
    back = call(
        back_kernel, message, 1 << 32, 1 << 23, in_specs=[smem] + [vmem] * 3
    )(at, hidden, factors, in_w)
    ret = swap(back)

    downs = call(
        down_kernel,
        (arr(PART, HID),) * GY,
        1 << 31,
        1 << 22,
        in_specs=[smem] + [vmem] * 2 + [anywhere],
        scratch_shapes=[pltpu.VMEM((WIDE, HID), BF)],
    )(at, sent, act, back)
    grad_down = call(total_kernel, arr(PART, HID), 0, 1 << 21)(
        downs[0], *[step(downs[r], "gy", r) for r in range(1, GY)]
    )
    input_grad = call(gather_kernel, arr(TOK, GX * WIDE), 1 << 30, 1 << 22)(ret, ids, slots)
    return (input_grad, grad_down.T[None])


def solution(mesh):
    devices = mesh.devices
    grid = Mesh(devices.reshape((GX, GY) + devices.shape[1:]), ("gx", "gy", "expert"))
    rows = P(("gx", "gy", "expert"), None)
    return jax.shard_map(
        per_device,
        mesh=grid,
        in_specs=(
            rows,
            rows,
            rows,
            rows,
            P("expert", ("gx", "gy"), None),
            P("expert", ("gx", "gy"), None),
            P("expert", ("gx", "gy"), None),
            P("expert", None, ("gx", "gy")),
        ),
        out_specs=(rows, P("expert", None, ("gx", "gy"))),
        check_vma=False,
    )
```

time: 298 us -> 281 us (0.943)
  starting transfers between devices: 150 us -> 81.5 us
  waiting for transfers between devices: 101 us -> 156 us
  Pallas kernels: 31.9 us -> 27.4 us
    ppermute x24 -> x12, starting transfers between devices: 90.5 us -> 41.5 us  [step(): return lax.ppermute(value, axis, [(i, (i + r) % 4) for i in range(4)])]
    all_to_all x4 -> x2, waiting for transfers between devices: 51.8 us -> 96 us  [swap(): return lax.all_to_all(value, ('gx', 'expert'), 0, 0, tiled=True)]
    all_to_all x4 -> x2, starting transfers between devices: 59.6 us -> 32.2 us  [swap(): return lax.all_to_all(value, ('gx', 'expert'), 0, 0, tiled=True)]
    ppermute x24 -> x12, waiting for transfers between devices: 48.7 us -> 59.7 us  [step(): return lax.ppermute(value, axis, [(i, (i + r) % 4) for i in range(4)])]
    all_to_all x0 -> x2, starting transfers between devices: none -> 7.9 us  [swap_gx(): return lax.all_to_all(value, 'gx', 0, 0, tiled=True)]
    pallas_call x9 -> x5, Pallas kernels: 22.3 us -> 18.9 us  [the longest x1 6.72 us: per_device(): call(back_kernel, message, 1 << 32, 1 << 23, in_specs=[smem] + [vmem] * 3)]
    unnamed x44 -> x32, local copies, waits for them, and re-layouts: 12.3 us -> 14.2 us
  transfers between devices with their start and end apart: 28 -> 16, of which waited for: 11 -> 10; matrix products, arithmetic and copies ran while one was open for 0% -> 0% of each run, Pallas kernels for 8% -> 3%
where the time goes in v5:
time: 281 us; the launch traced here: 280 us
  waiting for transfers between devices  156 us (56%)
  starting transfers between devices  81.5 us (29%)
  Pallas kernels  27.4 us (10%)
  local copies, waits for them, and re-layouts  14.2 us (5%)
    all_to_all x2, waiting for transfers between devices, swap(): return lax.all_to_all(value, ('gx', 'expert'), 0, 0, tiled=True)  96 us
    ppermute x12, waiting for transfers between devices, step(): return lax.ppermute(value, axis, [(i, (i + r) % 4) for i in range(4)])  59.7 us
    ppermute x12, starting transfers between devices, step(): return lax.ppermute(value, axis, [(i, (i + r) % 4) for i in range(4)])  41.5 us
    all_to_all x2, starting transfers between devices, swap(): return lax.all_to_all(value, ('gx', 'expert'), 0, 0, tiled=True)  32.2 us
    unnamed x32, local copies, waits for them, and re-layouts  14.2 us
    all_to_all x2, starting transfers between devices, swap_gx(): return lax.all_to_all(value, 'gx', 0, 0, tiled=True)  7.9 us
    pallas_call x1, Pallas kernels, per_device(): call(back_kernel, message, 1 << 32, 1 << 23, in_specs=[smem] + [vmem] * 3)  6.72 us
  transfers between devices with their start and end apart: 16, of which 10 were waited for; matrix products, arithmetic and copies ran while one was open for 0% of the time, Pallas kernels for 3%

profile of v5, /device:TPU:1, one launch (start us, length us, event | category | flops | bytes accessed | tf_op | source)
XLA Modules:
  0.0 279.8 jit_solution(12833832640596423778)
XLA Ops:
  0.6 5.1 %shard_map.95 = (bf16[128,2,3200]{2,1,0:T(2,128)(2,1)}, bf16[320,768]{1,0:T(8,128)(2,1)}, bf16[320,1536]{1,0:T(8,128)(2,1)}) custom-call(bf16[128,5120]{1,0:T(8,128)(2,1)} %og_any.1, s32[6,128]{1,0:T(8,128)} %bitcast.15, s32[6,128]{1,0:T(8,128)} %bitcast.17, f32[6,128]{1,0:T(8,128)} %bitcast.23, bf16[320,768]{1,0:T(8,128)(2,1)} %bitcast.20, ...), custom_call_target="tpu_custom_call" | custom-call | flops 536870912 | bytes 8388608 | tf_op jit(solution)/shard_map/pallas_call | solution.py:262
  5.7 20.9 %all-to-all-start = ((bf16[128,2,3200]{2,1,0:T(2,128)(2,1)}), bf16[128,2,3200]{2,1,0:T(2,128)(2,1)}, u32[]{:S(2)}, u32[]{:S(2)}) async-start(bf16[128,2,3200]{2,1,0:T(2,128)(2,1)} %get-tuple-element.13.after_ref), calls=%async_computation | async-start | bytes 3276800 | tf_op jit(solution)/shard_map/all_to_all | solution.py:239
  26.7 3.2 %collective-permute-start = (bf16[320,768]{1,0:T(8,128)(2,1)S(1)}, bf16[320,768]{1,0:T(8,128)(2,1)S(1)}, u32[]{:S(2)}, u32[]{:S(2)}) collective-permute-start(bf16[320,768]{1,0:T(8,128)(2,1)S(1)} %copy-done.5), channel_id=1, source_target_pairs={{0,32},{32,64},{64,96},{96,0},{1,33},{33,65},{65,97},{97,1},{2,34}... | collective-permute-start | bytes 1474568 | tf_op jit(solution)/shard_map/ppermute | solution.py:247
  29.9 4.5 %collective-permute-start.1 = (bf16[320,768]{1,0:T(8,128)(2,1)S(1)}, bf16[320,768]{1,0:T(8,128)(2,1)S(1)}, u32[]{:S(2)}, u32[]{:S(2)}) collective-permute-start(bf16[320,768]{1,0:T(8,128)(2,1)S(1)} %copy-done.5), channel_id=1, source_target_pairs={{0,64},{32,96},{64,0},{96,32},{1,65},{33,97},{65,1},{97,33},{2,66}... | collective-permute-start | bytes 1474568 | tf_op jit(solution)/shard_map/ppermute | solution.py:247
  34.5 3.0 %collective-permute-start.2 = (bf16[320,768]{1,0:T(8,128)(2,1)S(1)}, bf16[320,768]{1,0:T(8,128)(2,1)S(1)}, u32[]{:S(2)}, u32[]{:S(2)}) collective-permute-start(bf16[320,768]{1,0:T(8,128)(2,1)S(1)} %copy-done.5), channel_id=1, source_target_pairs={{0,96},{32,0},{64,32},{96,64},{1,97},{33,1},{65,33},{97,65},{2,98}... | collective-permute-start | bytes 1474568 | tf_op jit(solution)/shard_map/ppermute | solution.py:247
  37.5 4.3 %collective-permute-done.piece_1 = bf16[320,768]{1,0:T(8,128)(2,1)S(1)} collective-permute-done((bf16[320,768]{1,0:T(8,128)(2,1)S(1)}, bf16[320,768]{1,0:T(8,128)(2,1)S(1)}, u32[]{:S(2)}, u32[]{:S(2)}) %collective-permute-start) | collective-permute-done | bytes 491552 | tf_op jit(solution)/shard_map/ppermute | solution.py:247
  41.8 11.6 %collective-permute-done.1.piece_2 = bf16[320,768]{1,0:T(8,128)(2,1)S(1)} collective-permute-done((bf16[320,768]{1,0:T(8,128)(2,1)S(1)}, bf16[320,768]{1,0:T(8,128)(2,1)S(1)}, u32[]{:S(2)}, u32[]{:S(2)}) %collective-permute-start.1) | collective-permute-done | bytes 491552 | tf_op jit(solution)/shard_map/ppermute | solution.py:247
  57.5 48.4 %all-to-all-done.recv_ref = bf16[128,2,3200]{2,1,0:T(2,128)(2,1)} async-done(((bf16[128,2,3200]{2,1,0:T(2,128)(2,1)}), bf16[128,2,3200]{2,1,0:T(2,128)(2,1)}, u32[]{:S(2)}, u32[]{:S(2)}) %all-to-all-start) | async-done | bytes 1638432 | tf_op jit(solution)/shard_map/all_to_all | solution.py:239
  106.0 3.8 %shard_map.97 = (bf16[4,160,1280]{2,1,0:T(8,128)(2,1)S(1)}, bf16[4,160,768]{2,1,0:T(8,128)(2,1)S(1)}) custom-call(s32[2]{0:T(128)S(1)} %pad_add_fusion.at_ref, bf16[128,2,3200]{2,1,0:T(2,128)(2,1)} %all-to-all-done.recv_ref, bf16[1280,768]{1,0:T(8,128)(2,1)S(1)} %shard_map.96.down_ref), custom_call_target="tpu_custom_call" | custom-call | flops 2147483648 | bytes 8388608 | tf_op jit(solution)/shard_map/pallas_call | solution.py:304
  111.9 4.2 %all-to-all-start.1 = ((bf16[4,160,768]{2,1,0:T(8,128)(2,1)}), bf16[4,160,768]{2,1,0:T(8,128)(2,1)S(1)}, u32[]{:S(2)}, u32[]{:S(2)}) async-start(bf16[4,160,768]{2,1,0:T(8,128)(2,1)} %copy-done.3), calls=%async_computation.1 | async-start | bytes 1966080 | tf_op jit(solution)/shard_map/all_to_all | solution.py:243
  117.5 3.4 %collective-permute-start.3 = (bf16[160,1536]{1,0:T(8,128)(2,1)S(1)}, bf16[160,1536]{1,0:T(8,128)(2,1)}, u32[]{:S(2)}, u32[]{:S(2)}) collective-permute-start(bf16[160,1536]{1,0:T(8,128)(2,1)S(1)} %shard_map.99.pre_0), channel_id=1, source_target_pairs={{0,128},{128,256},{256,384},{384,0},{1,129},{129,257},{257,385},{3... | collective-permute-start | bytes 1474568 | tf_op jit(solution)/shard_map/ppermute | solution.py:247
  120.8 3.2 %collective-permute-start.6 = (bf16[320,1536]{1,0:T(8,128)(2,1)}, bf16[320,1536]{1,0:T(8,128)(2,1)S(1)}, u32[]{:S(2)}, u32[]{:S(2)}) collective-permute-start(bf16[320,1536]{1,0:T(8,128)(2,1)} %get-tuple-element.17.own_ref), channel_id=1, source_target_pairs={{0,32},{32,64},{64,96},{96,0},{1,33},{33,65},{65,97},{97,1},{2,34}... | collective-permute-start | bytes 2949128 | tf_op jit(solution)/shard_map/ppermute | solution.py:247
  124.0 4.5 %collective-permute-start.7 = (bf16[320,1536]{1,0:T(8,128)(2,1)}, bf16[320,1536]{1,0:T(8,128)(2,1)}, u32[]{:S(2)}, u32[]{:S(2)}) collective-permute-start(bf16[320,1536]{1,0:T(8,128)(2,1)} %get-tuple-element.17.own_ref), channel_id=1, source_target_pairs={{0,64},{32,96},{64,0},{96,32},{1,65},{33,97},{65,1},{97,33},{2,66}... | collective-permute-start | bytes 2949128 | tf_op jit(solution)/shard_map/ppermute | solution.py:247
  128.6 3.0 %collective-permute-start.8 = (bf16[320,1536]{1,0:T(8,128)(2,1)}, bf16[320,1536]{1,0:T(8,128)(2,1)}, u32[]{:S(2)}, u32[]{:S(2)}) collective-permute-start(bf16[320,1536]{1,0:T(8,128)(2,1)} %get-tuple-element.17.own_ref), channel_id=1, source_target_pairs={{0,96},{32,0},{64,32},{96,64},{1,97},{33,1},{65,33},{97,65},{2,98}... | collective-permute-start | bytes 2949128 | tf_op jit(solution)/shard_map/ppermute | solution.py:247
  132.7 3.7 %all-to-all-start.2 = ((bf16[4,160,768]{2,1,0:T(8,128)(2,1)}), bf16[4,160,768]{2,1,0:T(8,128)(2,1)S(1)}, u32[]{:S(2)}, u32[]{:S(2)}) async-start(bf16[4,160,768]{2,1,0:T(8,128)(2,1)} %shard_map.98), calls=%async_computation.2 | async-start | bytes 1966080 | tf_op jit(solution)/shard_map/all_to_all | solution.py:243
  136.3 4.9 %collective-permute-start.4 = (bf16[160,1536]{1,0:T(8,128)(2,1)S(1)}, bf16[160,1536]{1,0:T(8,128)(2,1)S(1)}, u32[]{:S(2)}, u32[]{:S(2)}) collective-permute-start(bf16[160,1536]{1,0:T(8,128)(2,1)S(1)} %shard_map.99.pre_0), channel_id=1, source_target_pairs={{0,256},{128,384},{256,0},{384,128},{1,257},{129,385},{257,1},{385... | collective-permute-start | bytes 1474568 | tf_op jit(solution)/shard_map/ppermute | solution.py:247
  141.2 3.0 %collective-permute-start.5 = (bf16[160,1536]{1,0:T(8,128)(2,1)S(1)}, bf16[160,1536]{1,0:T(8,128)(2,1)S(1)}, u32[]{:S(2)}, u32[]{:S(2)}) collective-permute-start(bf16[160,1536]{1,0:T(8,128)(2,1)S(1)} %shard_map.99.pre_0), channel_id=1, source_target_pairs={{0,384},{128,0},{256,128},{384,256},{1,385},{129,1},{257,129},{385... | collective-permute-start | bytes 1474568 | tf_op jit(solution)/shard_map/ppermute | solution.py:247
  144.2 16.2 %collective-permute-done.4.pre_2 = bf16[160,1536]{1,0:T(8,128)(2,1)S(1)} collective-permute-done((bf16[160,1536]{1,0:T(8,128)(2,1)S(1)}, bf16[160,1536]{1,0:T(8,128)(2,1)S(1)}, u32[]{:S(2)}, u32[]{:S(2)}) %collective-permute-start.4) | collective-permute-done | bytes 491552 | tf_op jit(solution)/shard_map/ppermute | solution.py:247
  160.4 7.7 %collective-permute-done.5.pre_3 = bf16[160,1536]{1,0:T(8,128)(2,1)S(1)} collective-permute-done((bf16[160,1536]{1,0:T(8,128)(2,1)S(1)}, bf16[160,1536]{1,0:T(8,128)(2,1)S(1)}, u32[]{:S(2)}, u32[]{:S(2)}) %collective-permute-start.5) | collective-permute-done | bytes 491552 | tf_op jit(solution)/shard_map/ppermute | solution.py:247
  168.1 1.9 shard_map.100
  172.4 2.1 shard_map.101.in_ref
  176.3 2.1 copy-done.2
  180.0 6.7 %shard_map.102.after_ref = bf16[128,2,3200]{2,1,0:T(2,128)(2,1)} custom-call(s32[2]{0:T(128)S(1)} %pad_add_fusion.at_ref, bf16[4,160,768]{2,1,0:T(8,128)(2,1)S(1)} %all-to-all-done.2.hidden_ref, bf16[4,160,1536]{2,1,0:T(8,128)(2,1)S(1)} %copy-done.11, bf16[1280,1536]{1,0:T(8,128)(2,1)S(1)} %copy-done.2), custom_call_target="tpu_custom_call" | custom-call | flops 4294967296 | bytes 8388608 | tf_op jit(solution)/shard_map/pallas_call | solution.py:312
  186.7 11.2 %all-to-all-start.3 = ((bf16[128,2,3200]{2,1,0:T(2,128)(2,1)}), bf16[128,2,3200]{2,1,0:T(2,128)(2,1)S(1)}, u32[]{:S(2)}, u32[]{:S(2)}) async-start(bf16[128,2,3200]{2,1,0:T(2,128)(2,1)} %shard_map.102.after_ref), calls=%async_computation.3 | async-start | bytes 3276800 | tf_op jit(solution)/shard_map/all_to_all | solution.py:239
  199.4 2.4 shard_map.104
  201.9 3.5 %collective-permute-start.10 = (bf16[320,768]{1,0:T(8,128)(2,1)S(1)}, bf16[320,768]{1,0:T(8,128)(2,1)S(1)}, u32[]{:S(2)}, u32[]{:S(2)}) collective-permute-start(bf16[320,768]{1,0:T(8,128)(2,1)S(1)} %get-tuple-element.22), channel_id=1, source_target_pairs={{0,64},{32,96},{64,0},{96,32},{1,65},{33,97},{65,1},{97,33},{2,66}... | collective-permute-start | bytes 1474568 | tf_op jit(solution)/shard_map/ppermute | solution.py:247
  205.4 3.1 %collective-permute-start.11 = (bf16[320,768]{1,0:T(8,128)(2,1)S(1)}, bf16[320,768]{1,0:T(8,128)(2,1)S(1)}, u32[]{:S(2)}, u32[]{:S(2)}) collective-permute-start(bf16[320,768]{1,0:T(8,128)(2,1)S(1)} %get-tuple-element.23), channel_id=1, source_target_pairs={{0,96},{32,0},{64,32},{96,64},{1,97},{33,1},{65,33},{97,65},{2,98}... | collective-permute-start | bytes 1474568 | tf_op jit(solution)/shard_map/ppermute | solution.py:247
  208.5 2.2 collective-permute-start.9
  210.7 6.4 %collective-permute-done.10.part_2 = bf16[320,768]{1,0:T(8,128)(2,1)S(1)} collective-permute-done((bf16[320,768]{1,0:T(8,128)(2,1)S(1)}, bf16[320,768]{1,0:T(8,128)(2,1)S(1)}, u32[]{:S(2)}, u32[]{:S(2)}) %collective-permute-start.10) | collective-permute-done | bytes 491552 | tf_op jit(solution)/shard_map/ppermute | solution.py:247
  217.2 10.2 %collective-permute-done.11.part_3 = bf16[320,768]{1,0:T(8,128)(2,1)S(1)} collective-permute-done((bf16[320,768]{1,0:T(8,128)(2,1)S(1)}, bf16[320,768]{1,0:T(8,128)(2,1)S(1)}, u32[]{:S(2)}, u32[]{:S(2)}) %collective-permute-start.11) | collective-permute-done | bytes 491552 | tf_op jit(solution)/shard_map/ppermute | solution.py:247
  230.0 47.5 %all-to-all-done.3.ret_ref = bf16[128,2,3200]{2,1,0:T(2,128)(2,1)S(1)} async-done(((bf16[128,2,3200]{2,1,0:T(2,128)(2,1)}), bf16[128,2,3200]{2,1,0:T(2,128)(2,1)S(1)}, u32[]{:S(2)}, u32[]{:S(2)}) %all-to-all-start.3) | async-done | bytes 1638432 | tf_op jit(solution)/shard_map/all_to_all | solution.py:239
  277.5 2.3 shard_map.103
  (44 shorter events, 18.4 us)
Async XLA Ops:
  5.7 21.0 %copy-start.5 = (bf16[320,768]{1,0:T(8,128)(2,1)S(1)}, bf16[320,768]{1,0:T(8,128)(2,1)}, u32[]{:S(2)}) copy-start(bf16[320,768]{1,0:T(8,128)(2,1)} %get-tuple-element.14.own_ref) | copy-start | bytes 1474564
  5.7 100.2 %all-to-all-start = ((bf16[128,2,3200]{2,1,0:T(2,128)(2,1)}), bf16[128,2,3200]{2,1,0:T(2,128)(2,1)}, u32[]{:S(2)}, u32[]{:S(2)}) async-start(bf16[128,2,3200]{2,1,0:T(2,128)(2,1)} %get-tuple-element.13.after_ref), calls=%async_computation | async-start | bytes 3276800 | tf_op jit(solution)/shard_map/all_to_all | solution.py:239
  26.7 15.1 %collective-permute-start = (bf16[320,768]{1,0:T(8,128)(2,1)S(1)}, bf16[320,768]{1,0:T(8,128)(2,1)S(1)}, u32[]{:S(2)}, u32[]{:S(2)}) collective-permute-start(bf16[320,768]{1,0:T(8,128)(2,1)S(1)} %copy-done.5), channel_id=1, source_target_pairs={{0,32},{32,64},{64,96},{96,0},{1,33},{33,65},{65,97},{97,1},{2,34}... | collective-permute-start | bytes 1474568 | tf_op jit(solution)/shard_map/ppermute | solution.py:247
  29.9 23.5 %collective-permute-start.1 = (bf16[320,768]{1,0:T(8,128)(2,1)S(1)}, bf16[320,768]{1,0:T(8,128)(2,1)S(1)}, u32[]{:S(2)}, u32[]{:S(2)}) collective-permute-start(bf16[320,768]{1,0:T(8,128)(2,1)S(1)} %copy-done.5), channel_id=1, source_target_pairs={{0,64},{32,96},{64,0},{96,32},{1,65},{33,97},{65,1},{97,33},{2,66}... | collective-permute-start | bytes 1474568 | tf_op jit(solution)/shard_map/ppermute | solution.py:247
  34.5 20.6 %collective-permute-start.2 = (bf16[320,768]{1,0:T(8,128)(2,1)S(1)}, bf16[320,768]{1,0:T(8,128)(2,1)S(1)}, u32[]{:S(2)}, u32[]{:S(2)}) collective-permute-start(bf16[320,768]{1,0:T(8,128)(2,1)S(1)} %copy-done.5), channel_id=1, source_target_pairs={{0,96},{32,0},{64,32},{96,64},{1,97},{33,1},{65,33},{97,65},{2,98}... | collective-permute-start | bytes 1474568 | tf_op jit(solution)/shard_map/ppermute | solution.py:247
  55.0 0.8 copy-start.6
  55.8 1.0 copy-start.7
  109.8 1.0 copy-start.3
  110.7 1.2 copy-start.14
  111.9 4.2 %copy-start = (bf16[128,2,3200]{2,1,0:T(2,128)(2,1)S(1)}, bf16[128,2,3200]{2,1,0:T(2,128)(2,1)}, u32[]{:S(2)}) copy-start(bf16[128,2,3200]{2,1,0:T(2,128)(2,1)} %get-tuple-element.13.after_ref) | copy-start | bytes 4915204
  111.9 19.7 %all-to-all-start.1 = ((bf16[4,160,768]{2,1,0:T(8,128)(2,1)}), bf16[4,160,768]{2,1,0:T(8,128)(2,1)S(1)}, u32[]{:S(2)}, u32[]{:S(2)}) async-start(bf16[4,160,768]{2,1,0:T(8,128)(2,1)} %copy-done.3), calls=%async_computation.1 | async-start | bytes 1966080 | tf_op jit(solution)/shard_map/all_to_all | solution.py:243
  116.2 1.0 copy-start.4
  117.5 23.7 %collective-permute-start.3 = (bf16[160,1536]{1,0:T(8,128)(2,1)S(1)}, bf16[160,1536]{1,0:T(8,128)(2,1)}, u32[]{:S(2)}, u32[]{:S(2)}) collective-permute-start(bf16[160,1536]{1,0:T(8,128)(2,1)S(1)} %shard_map.99.pre_0), channel_id=1, source_target_pairs={{0,128},{128,256},{256,384},{384,0},{1,129},{129,257},{257,385},{3... | collective-permute-start | bytes 1474568 | tf_op jit(solution)/shard_map/ppermute | solution.py:247
  120.8 51.5 %collective-permute-start.6 = (bf16[320,1536]{1,0:T(8,128)(2,1)}, bf16[320,1536]{1,0:T(8,128)(2,1)S(1)}, u32[]{:S(2)}, u32[]{:S(2)}) collective-permute-start(bf16[320,1536]{1,0:T(8,128)(2,1)} %get-tuple-element.17.own_ref), channel_id=1, source_target_pairs={{0,32},{32,64},{64,96},{96,0},{1,33},{33,65},{65,97},{97,1},{2,34}... | collective-permute-start | bytes 2949128 | tf_op jit(solution)/shard_map/ppermute | solution.py:247
  124.0 48.3 %collective-permute-start.7 = (bf16[320,1536]{1,0:T(8,128)(2,1)}, bf16[320,1536]{1,0:T(8,128)(2,1)}, u32[]{:S(2)}, u32[]{:S(2)}) collective-permute-start(bf16[320,1536]{1,0:T(8,128)(2,1)} %get-tuple-element.17.own_ref), channel_id=1, source_target_pairs={{0,64},{32,96},{64,0},{96,32},{1,65},{33,97},{65,1},{97,33},{2,66}... | collective-permute-start | bytes 2949128 | tf_op jit(solution)/shard_map/ppermute | solution.py:247
  128.6 43.8 %collective-permute-start.8 = (bf16[320,1536]{1,0:T(8,128)(2,1)}, bf16[320,1536]{1,0:T(8,128)(2,1)}, u32[]{:S(2)}, u32[]{:S(2)}) collective-permute-start(bf16[320,1536]{1,0:T(8,128)(2,1)} %get-tuple-element.17.own_ref), channel_id=1, source_target_pairs={{0,96},{32,0},{64,32},{96,64},{1,97},{33,1},{65,33},{97,65},{2,98}... | collective-permute-start | bytes 2949128 | tf_op jit(solution)/shard_map/ppermute | solution.py:247
  132.7 43.7 %all-to-all-start.2 = ((bf16[4,160,768]{2,1,0:T(8,128)(2,1)}), bf16[4,160,768]{2,1,0:T(8,128)(2,1)S(1)}, u32[]{:S(2)}, u32[]{:S(2)}) async-start(bf16[4,160,768]{2,1,0:T(8,128)(2,1)} %shard_map.98), calls=%async_computation.2 | async-start | bytes 1966080 | tf_op jit(solution)/shard_map/all_to_all | solution.py:243
  136.3 24.1 %collective-permute-start.4 = (bf16[160,1536]{1,0:T(8,128)(2,1)S(1)}, bf16[160,1536]{1,0:T(8,128)(2,1)S(1)}, u32[]{:S(2)}, u32[]{:S(2)}) collective-permute-start(bf16[160,1536]{1,0:T(8,128)(2,1)S(1)} %shard_map.99.pre_0), channel_id=1, source_target_pairs={{0,256},{128,384},{256,0},{384,128},{1,257},{129,385},{257,1},{385... | collective-permute-start | bytes 1474568 | tf_op jit(solution)/shard_map/ppermute | solution.py:247
  141.2 26.9 %collective-permute-start.5 = (bf16[160,1536]{1,0:T(8,128)(2,1)S(1)}, bf16[160,1536]{1,0:T(8,128)(2,1)S(1)}, u32[]{:S(2)}, u32[]{:S(2)}) collective-permute-start(bf16[160,1536]{1,0:T(8,128)(2,1)S(1)} %shard_map.99.pre_0), channel_id=1, source_target_pairs={{0,384},{128,0},{256,128},{384,256},{1,385},{129,1},{257,129},{385... | collective-permute-start | bytes 1474568 | tf_op jit(solution)/shard_map/ppermute | solution.py:247
  170.0 1.3 copy-start.10
  171.4 1.0 copy-start.12
  174.5 1.9 copy-start.1
  176.3 2.1 copy-start.2
  178.4 1.5 copy-start.11
  186.7 11.3 %copy-start.13 = (bf16[4,160,768]{2,1,0:T(8,128)(2,1)S(1)}, bf16[4,160,768]{2,1,0:T(8,128)(2,1)}, u32[]{:S(2)}) copy-start(bf16[4,160,768]{2,1,0:T(8,128)(2,1)} %copy-done.12) | copy-start | bytes 2949124
  186.7 90.8 %all-to-all-start.3 = ((bf16[128,2,3200]{2,1,0:T(2,128)(2,1)}), bf16[128,2,3200]{2,1,0:T(2,128)(2,1)S(1)}, u32[]{:S(2)}, u32[]{:S(2)}) async-start(bf16[128,2,3200]{2,1,0:T(2,128)(2,1)} %shard_map.102.after_ref), calls=%async_computation.3 | async-start | bytes 3276800 | tf_op jit(solution)/shard_map/all_to_all | solution.py:239
  198.0 1.4 copy-start.15
  201.8 75.7 %copy-start.8 = (s32[128,6]{0,1:T(8,128)S(1)}, s32[128,6]{0,1:T(8,128)}, u32[]{:S(2)}) copy-start(s32[128,6]{0,1:T(8,128)} %param.9) | copy-start | bytes 9220
  201.9 75.6 %copy-start.9 = (s32[128,6]{0,1:T(8,128)S(1)}, s32[128,6]{0,1:T(8,128)}, u32[]{:S(2)}) copy-start(s32[128,6]{0,1:T(8,128)} %param.10) | copy-start | bytes 9220
  201.9 15.3 %collective-permute-start.10 = (bf16[320,768]{1,0:T(8,128)(2,1)S(1)}, bf16[320,768]{1,0:T(8,128)(2,1)S(1)}, u32[]{:S(2)}, u32[]{:S(2)}) collective-permute-start(bf16[320,768]{1,0:T(8,128)(2,1)S(1)} %get-tuple-element.22), channel_id=1, source_target_pairs={{0,64},{32,96},{64,0},{96,32},{1,65},{33,97},{65,1},{97,33},{2,66}... | collective-permute-start | bytes 1474568 | tf_op jit(solution)/shard_map/ppermute | solution.py:247
  205.4 22.0 %collective-permute-start.11 = (bf16[320,768]{1,0:T(8,128)(2,1)S(1)}, bf16[320,768]{1,0:T(8,128)(2,1)S(1)}, u32[]{:S(2)}, u32[]{:S(2)}) collective-permute-start(bf16[320,768]{1,0:T(8,128)(2,1)S(1)} %get-tuple-element.23), channel_id=1, source_target_pairs={{0,96},{32,0},{64,32},{96,64},{1,97},{33,1},{65,33},{97,65},{2,98}... | collective-permute-start | bytes 1474568 | tf_op jit(solution)/shard_map/ppermute | solution.py:247
  208.5 20.5 %collective-permute-start.9 = (bf16[320,768]{1,0:T(8,128)(2,1)S(1)}, bf16[320,768]{1,0:T(8,128)(2,1)S(1)}, u32[]{:S(2)}, u32[]{:S(2)}) collective-permute-start(bf16[320,768]{1,0:T(8,128)(2,1)S(1)} %get-tuple-element.21), channel_id=1, source_target_pairs={{0,32},{32,64},{64,96},{96,0},{1,33},{33,65},{65,97},{97,1},{2,34}... | collective-permute-start | bytes 1474568 | tf_op jit(solution)/shard_map/ppermute | solution.py:247

commit v6 on v5

--- a/solution.py
+++ b/solution.py
@@ -143,10 +143,12 @@
         copy.wait()
 
 
-def arrange_kernel(at_ref, own_ref, piece_1, piece_2, piece_3, out_ref):
+def arrange_kernel(at_ref, own_ref, piece_1, piece_2, piece_3, *refs):
+    out_ref, token_ref = refs[-2:]
     for r, ref in enumerate((own_ref, piece_1, piece_2, piece_3)):
         q = lax.rem(at_ref[1] + (GY - r), GY)
         out_ref[pl.ds(pl.multiple_of(q * PART, 64), PART), :] = ref[...]
+    token_ref[...] = jnp.zeros(token_ref.shape, F32)
 
 
 def order_kernel(pre_ref, after_ref, out_ref):
@@ -156,7 +158,7 @@
     out_ref[...] = nn(swap_rows, pre_ref[...]).astype(BF)
 
 
-def factor_kernel(pre_0, pre_1, pre_2, pre_3, factor_ref, act_ref):
+def factor_kernel(pre_0, pre_1, pre_2, pre_3, factor_ref, act_ref, token_ref):
     for r, pre_ref in enumerate((pre_0, pre_1, pre_2, pre_3)):
         for s in range(CAP):
             span = slice(s * N_EXP, (s + 1) * N_EXP)
@@ -167,19 +169,41 @@
             factor_ref[r, span, :HID] = (up_pre * sig * (1.0 + gate_pre * (1.0 - sig))).astype(BF)
             factor_ref[r, span, HID:] = lift.astype(BF)
             act_ref[r, span, :] = (lift * up_pre).astype(BF)
-
-
-def hidden_kernel(at_ref, recv_ref, down_ref, sent_ref, part_ref):
-    split = split_halves()
+    token_ref[...] = jnp.zeros(token_ref.shape, F32)
+
+
+def hidden_kernel(
+    at_ref, recv_any, down_any, sent_any, part_any,
+    recv_ref, down_ref, sent_ref, part_ref, in_sems, down_sem, out_sems,
+):
+    fetches = []
     for r in range(GX):
         g = lax.rem(at_ref[0] + (GX - r), GX)
+        span = pl.ds(g * N_EXP, N_EXP)
+        fetches.append(pltpu.make_async_copy(recv_any.at[span], recv_ref.at[r], in_sems.at[r]))
+    fetches.insert(1, pltpu.make_async_copy(down_any, down_ref, down_sem))
+    for copy in fetches:
+        copy.start()
+    split = split_halves()
+    copies = []
+    for r in range(GX):
+        fetches[r + (r > 0)].wait()
         for s in range(CAP):
-            rows = from_pairs(recv_ref[pl.ds(g * N_EXP, N_EXP), :, s * HALF : (s + 1) * HALF])
+            rows = from_pairs(recv_ref[r, :, :, s * HALF : (s + 1) * HALF])
             halves = nn(split, rows).astype(BF)
             span = slice(s * N_EXP, (s + 1) * N_EXP)
             sent_ref[r, span, :HALF] = halves[:N_EXP]
             sent_ref[r, span, HALF:] = halves[N_EXP:]
-        part_ref[g] = nn(sent_ref[r], down_ref[...]).astype(BF)
+        if r == 0:
+            fetches[1].wait()
+        part_ref[r] = nn(sent_ref[r], down_ref[...]).astype(BF)
+        g = lax.rem(at_ref[0] + (GX - r), GX)
+        copies.append(pltpu.make_async_copy(part_ref.at[r], part_any.at[g], out_sems.at[0, r]))
+        copies.append(pltpu.make_async_copy(sent_ref.at[r], sent_any.at[r], out_sems.at[1, r]))
+        for copy in copies[-2:]:
+            copy.start()
+    for copy in copies:
+        copy.wait()
 
 
 def spread_kernel(part_ref, out_ref):
@@ -189,7 +213,7 @@
         out_ref[g] = total
 
 
-def back_kernel(at_ref, hidden_ref, factor_ref, in_ref, msg_ref):
+def back_kernel(at_ref, hidden_ref, factor_ref, in_ref, msg_any, msg_ref, sems):
     grads = []
     for r in range(GX):
         hidden = hidden_ref[lax.rem(at_ref[0] + (GX - r), GX)].astype(F32)
@@ -198,12 +222,18 @@
         grads.append(jnp.concatenate([gate_grad, up_grad], axis=1))
     rows = nt(jnp.concatenate(grads, axis=0), in_ref[...]).astype(BF)
     join = join_halves()
+    copies = []
     for r in range(GX):
         g = lax.rem(at_ref[0] + (GX - r), GX)
         for s in range(CAP):
             own = rows[(r * CAP + s) * N_EXP : (r * CAP + s + 1) * N_EXP]
             both = jnp.concatenate([own[:, :HALF], own[:, HALF:]], axis=0)
-            msg_ref[pl.ds(g * N_EXP, N_EXP), :, s * HALF : (s + 1) * HALF] = to_pairs(nn(join, both))
+            msg_ref[r, :, :, s * HALF : (s + 1) * HALF] = to_pairs(nn(join, both))
+        span = pl.ds(g * N_EXP, N_EXP)
+        copies.append(pltpu.make_async_copy(msg_ref.at[r], msg_any.at[span], sems.at[r]))
+        copies[-1].start()
+    for copy in copies:
+        copy.wait()
 
 
 def total_kernel(part_0, part_1, part_2, part_3, out_ref):
@@ -284,33 +314,57 @@
     )(out_grad, ids, slots, probs, w_down[0].T, w_gate[0], w_up[0])
     recv = swap(msg)
 
-    def arrange(own):
-        return call(
-            arrange_kernel,
-            arr(WIDE, own.shape[1]),
-            0,
-            1 << 23,
-            in_specs=[smem] + [vmem] * 4,
-        )(at, own, *steps(own, "gy"))
-
-    down_w, in_w = arrange(own_down), arrange(own_in)
     pre = call(order_kernel, arr(ROWS, 2 * HID), 1 << 27, 1 << 21, in_specs=[vmem, anywhere])(
         saved_pre[0], msg
     )
-    factors, act = call(
-        factor_kernel, (arr(GX, ROWS, 2 * HID), arr(GX, ROWS, HID)), 1 << 25, 1 << 23
+    token = arr(8, 128, dtype=F32)
+    factors, act, factors_done = call(
+        factor_kernel, (arr(GX, ROWS, 2 * HID), arr(GX, ROWS, HID), token), 1 << 25, 1 << 23, VMEM_MOST
     )(pre, *steps(pre, "gx"))
+
+    def arrange(own, *after):
+        return call(
+            arrange_kernel,
+            (arr(WIDE, own.shape[1]), token),
+            0,
+            1 << 23,
+            VMEM_MOST,
+            in_specs=[smem] + [vmem] * 4 + [anywhere] * len(after),
+        )(at, own, *steps(own, "gy"), *after)
+
+    in_w, in_done = arrange(own_in)
+    down_w, _ = arrange(own_down, factors_done, in_done)
 
     sent, part = call(
         hidden_kernel,
         (arr(GX, ROWS, WIDE), arr(GX, ROWS, HID)),
         1 << 31,
         1 << 23,
-        in_specs=[smem, vmem, vmem],
+        VMEM_MOST,
+        in_specs=[smem, anywhere, anywhere],
+        out_specs=[anywhere] * 2,
+        scratch_shapes=[
+            pltpu.VMEM((GX, N_EXP, 2, CAP * HALF), BF),
+            pltpu.VMEM((WIDE, HID), BF),
+            pltpu.VMEM((GX, ROWS, WIDE), BF),
+            pltpu.VMEM((GX, ROWS, HID), BF),
+            pltpu.SemaphoreType.DMA((GX,)),
+            pltpu.SemaphoreType.DMA,
+            pltpu.SemaphoreType.DMA((2, GX)),
+        ],
     )(at, recv, down_w)
     hidden = swap_gx(call(spread_kernel, arr(GX, ROWS, HID), 0, 1 << 21)(swap_gx(part)))
     back = call(
-        back_kernel, message, 1 << 32, 1 << 23, in_specs=[smem] + [vmem] * 3
+        back_kernel,
+        message,
+        1 << 32,
+        1 << 23,
+        in_specs=[smem] + [vmem] * 3,
+        out_specs=anywhere,
+        scratch_shapes=[
+            pltpu.VMEM((GX, N_EXP, 2, CAP * HALF), BF),
+            pltpu.SemaphoreType.DMA((GX,)),
+        ],
     )(at, hidden, factors, in_w)
     ret = swap(back)
 

time: 281 us -> 251 us (0.89)
  waiting for transfers between devices: 156 us -> 97.6 us
  blocking collectives: 0 us -> 32.2 us
  local copies, waits for them, and re-layouts: 14.2 us -> 1.5 us
  Pallas kernels: 27.4 us -> 35.2 us
    all_to_all x2, waiting for transfers between devices: 96 us -> 48.1 us  [swap(): return lax.all_to_all(value, ('gx', 'expert'), 0, 0, tiled=True)]
    all_to_all x0 -> x2, blocking collectives: none -> 32.2 us  [swap_gx(): return lax.all_to_all(value, 'gx', 0, 0, tiled=True)]
    unnamed x32, local copies, waits for them, and re-layouts: 14.2 us -> 1.5 us
    ppermute x12, waiting for transfers between devices: 59.7 us -> 49.4 us  [step(): return lax.ppermute(value, axis, [(i, (i + r) % 4) for i in range(4)])]
    all_to_all x2 -> x0, starting transfers between devices: 7.9 us -> none  [swap_gx(): return lax.all_to_all(value, 'gx', 0, 0, tiled=True)]
    pallas_call x4, Pallas kernels: 11.4 us -> 17.3 us  [the longest x2 7.16 us: arrange(): call(arrange_kernel, (arr(WIDE, own.shape[1]), token), 0, 1 << 23, VMEM_M...]
    all_to_all x2, starting transfers between devices: 32.2 us -> 35.2 us  [swap(): return lax.all_to_all(value, ('gx', 'expert'), 0, 0, tiled=True)]
    pallas_call x1, Pallas kernels: 3.8 us -> 6.68 us  [per_device(): call(hidden_kernel, (arr(GX, ROWS, WIDE), arr(GX, ROWS, HID)), 1 << 31, 1...]
  transfers between devices with their start and end apart: 16 -> 14, of which waited for: 10 -> 10; matrix products, arithmetic and copies ran while one was open for 0% -> 0% of each run, Pallas kernels for 3% -> 6%
where the time goes in v6:
time: 251 us; the launch traced here: 247 us
  waiting for transfers between devices  97.6 us (39%)
  starting transfers between devices  79.4 us (32%)
  Pallas kernels  35.2 us (14%)
  blocking collectives  32.2 us (13%)
    ppermute x12, waiting for transfers between devices, step(): return lax.ppermute(value, axis, [(i, (i + r) % 4) for i in range(4)])  49.4 us
    all_to_all x2, waiting for transfers between devices, swap(): return lax.all_to_all(value, ('gx', 'expert'), 0, 0, tiled=True)  48.1 us
    ppermute x12, starting transfers between devices, step(): return lax.ppermute(value, axis, [(i, (i + r) % 4) for i in range(4)])  44.1 us
    all_to_all x2, starting transfers between devices, swap(): return lax.all_to_all(value, ('gx', 'expert'), 0, 0, tiled=True)  35.2 us
    all_to_all x2, blocking collectives, swap_gx(): return lax.all_to_all(value, 'gx', 0, 0, tiled=True)  32.2 us
    pallas_call x2, Pallas kernels, arrange(): call(arrange_kernel, (arr(WIDE, own.shape[1]), token), 0, 1 << 23, VMEM_M...  7.16 us
    pallas_call x1, Pallas kernels, per_device(): call(hidden_kernel, (arr(GX, ROWS, WIDE), arr(GX, ROWS, HID)), 1 << 31, 1...  6.68 us
    pallas_call x1, Pallas kernels, per_device(): call(back_kernel, message, 1 << 32, 1 << 23, in_specs=[smem] + [vmem] * 3...  6.32 us
  transfers between devices with their start and end apart: 14, of which 10 were waited for; matrix products, arithmetic and copies ran while one was open for 0% of the time, Pallas kernels for 6%

profile of v6, /device:TPU:1, one launch (start us, length us, event | category | flops | bytes accessed | tf_op | source)
XLA Modules:
  0.0 247.5 jit_solution(1998941659545714474)
XLA Ops:
  0.6 5.1 %shard_map.95 = (bf16[128,2,3200]{2,1,0:T(2,128)(2,1)}, bf16[320,768]{1,0:T(8,128)(2,1)}, bf16[320,1536]{1,0:T(8,128)(2,1)}) custom-call(bf16[128,5120]{1,0:T(8,128)(2,1)} %og_any.1, s32[6,128]{1,0:T(8,128)} %bitcast.15, s32[6,128]{1,0:T(8,128)} %bitcast.17, f32[6,128]{1,0:T(8,128)} %bitcast.23, bf16[320,768]{1,0:T(8,128)(2,1)} %bitcast.20, ...), custom_call_target="tpu_custom_call" | custom-call | flops 536870912 | bytes 8388608 | tf_op jit(solution)/shard_map/pallas_call | solution.py:292
  5.7 20.9 %all-to-all-start = ((bf16[128,2,3200]{2,1,0:T(2,128)(2,1)}), bf16[128,2,3200]{2,1,0:T(2,128)(2,1)}, u32[]{:S(2)}, u32[]{:S(2)}) async-start(bf16[128,2,3200]{2,1,0:T(2,128)(2,1)} %get-tuple-element.17.after_ref), calls=%async_computation | async-start | bytes 3276800 | tf_op jit(solution)/shard_map/all_to_all | solution.py:269
  27.0 3.4 %collective-permute-start.3 = (bf16[160,1536]{1,0:T(8,128)(2,1)S(1)}, bf16[160,1536]{1,0:T(8,128)(2,1)S(1)}, u32[]{:S(2)}, u32[]{:S(2)}) collective-permute-start(bf16[160,1536]{1,0:T(8,128)(2,1)S(1)} %shard_map.96.pre_0), channel_id=1, source_target_pairs={{0,128},{128,256},{256,384},{384,0},{1,129},{129,257},{257,385},{3... | collective-permute-start | bytes 1474568 | tf_op jit(solution)/shard_map/ppermute | solution.py:277
  30.4 3.2 %collective-permute-start.6 = (bf16[320,1536]{1,0:T(8,128)(2,1)}, bf16[320,1536]{1,0:T(8,128)(2,1)S(1)}, u32[]{:S(2)}, u32[]{:S(2)}) collective-permute-start(bf16[320,1536]{1,0:T(8,128)(2,1)} %get-tuple-element.20.own_ref), channel_id=1, source_target_pairs={{0,32},{32,64},{64,96},{96,0},{1,33},{33,65},{65,97},{97,1},{2,34}... | collective-permute-start | bytes 2949128 | tf_op jit(solution)/shard_map/ppermute | solution.py:277
  33.6 4.5 %collective-permute-start.7 = (bf16[320,1536]{1,0:T(8,128)(2,1)}, bf16[320,1536]{1,0:T(8,128)(2,1)S(1)}, u32[]{:S(2)}, u32[]{:S(2)}) collective-permute-start(bf16[320,1536]{1,0:T(8,128)(2,1)} %get-tuple-element.20.own_ref), channel_id=1, source_target_pairs={{0,64},{32,96},{64,0},{96,32},{1,65},{33,97},{65,1},{97,33},{2,66}... | collective-permute-start | bytes 2949128 | tf_op jit(solution)/shard_map/ppermute | solution.py:277
  38.2 4.7 %collective-permute-start.4 = (bf16[160,1536]{1,0:T(8,128)(2,1)S(1)}, bf16[160,1536]{1,0:T(8,128)(2,1)S(1)}, u32[]{:S(2)}, u32[]{:S(2)}) collective-permute-start(bf16[160,1536]{1,0:T(8,128)(2,1)S(1)} %shard_map.96.pre_0), channel_id=1, source_target_pairs={{0,256},{128,384},{256,0},{384,128},{1,257},{129,385},{257,1},{385... | collective-permute-start | bytes 1474568 | tf_op jit(solution)/shard_map/ppermute | solution.py:277
  42.9 3.0 %collective-permute-start.8 = (bf16[320,1536]{1,0:T(8,128)(2,1)}, bf16[320,1536]{1,0:T(8,128)(2,1)}, u32[]{:S(2)}, u32[]{:S(2)}) collective-permute-start(bf16[320,1536]{1,0:T(8,128)(2,1)} %get-tuple-element.20.own_ref), channel_id=1, source_target_pairs={{0,96},{32,0},{64,32},{96,64},{1,97},{33,1},{65,33},{97,65},{2,98}... | collective-permute-start | bytes 2949128 | tf_op jit(solution)/shard_map/ppermute | solution.py:277
  45.9 3.9 %collective-permute-start.5 = (bf16[160,1536]{1,0:T(8,128)(2,1)S(1)}, bf16[160,1536]{1,0:T(8,128)(2,1)S(1)}, u32[]{:S(2)}, u32[]{:S(2)}) collective-permute-start(bf16[160,1536]{1,0:T(8,128)(2,1)S(1)} %shard_map.96.pre_0), channel_id=1, source_target_pairs={{0,384},{128,0},{256,128},{384,256},{1,385},{129,1},{257,129},{385... | collective-permute-start | bytes 1474568 | tf_op jit(solution)/shard_map/ppermute | solution.py:277
  49.9 11.2 %collective-permute-done.4.pre_2 = bf16[160,1536]{1,0:T(8,128)(2,1)S(1)} collective-permute-done((bf16[160,1536]{1,0:T(8,128)(2,1)S(1)}, bf16[160,1536]{1,0:T(8,128)(2,1)S(1)}, u32[]{:S(2)}, u32[]{:S(2)}) %collective-permute-start.4) | collective-permute-done | bytes 491552 | tf_op jit(solution)/shard_map/ppermute | solution.py:277
  61.1 3.2 %collective-permute-start = (bf16[320,768]{1,0:T(8,128)(2,1)}, bf16[320,768]{1,0:T(8,128)(2,1)S(1)}, u32[]{:S(2)}, u32[]{:S(2)}) collective-permute-start(bf16[320,768]{1,0:T(8,128)(2,1)} %get-tuple-element.18.own_ref), channel_id=1, source_target_pairs={{0,32},{32,64},{64,96},{96,0},{1,33},{33,65},{65,97},{97,1},{2,34}... | collective-permute-start | bytes 1474568 | tf_op jit(solution)/shard_map/ppermute | solution.py:277
  64.3 5.4 %collective-permute-done.5.pre_3 = bf16[160,1536]{1,0:T(8,128)(2,1)S(1)} collective-permute-done((bf16[160,1536]{1,0:T(8,128)(2,1)S(1)}, bf16[160,1536]{1,0:T(8,128)(2,1)S(1)}, u32[]{:S(2)}, u32[]{:S(2)}) %collective-permute-start.5) | collective-permute-done | bytes 491552 | tf_op jit(solution)/shard_map/ppermute | solution.py:277
  69.7 1.9 collective-permute-start.1
  71.7 3.6 %collective-permute-start.2 = (bf16[320,768]{1,0:T(8,128)(2,1)}, bf16[320,768]{1,0:T(8,128)(2,1)}, u32[]{:S(2)}, u32[]{:S(2)}) collective-permute-start(bf16[320,768]{1,0:T(8,128)(2,1)} %get-tuple-element.18.own_ref), channel_id=1, source_target_pairs={{0,96},{32,0},{64,32},{96,64},{1,97},{33,1},{65,33},{97,65},{2,98}... | collective-permute-start | bytes 1474568 | tf_op jit(solution)/shard_map/ppermute | solution.py:277
  76.0 3.9 %shard_map.97 = (bf16[4,160,1536]{2,1,0:T(8,128)(2,1)}, bf16[4,160,768]{2,1,0:T(8,128)(2,1)}, f32[8,128]{1,0:T(8,128)}) custom-call(bf16[160,1536]{1,0:T(8,128)(2,1)} %copy-done.1, bf16[160,1536]{1,0:T(8,128)(2,1)} %copy-done.13, bf16[160,1536]{1,0:T(8,128)(2,1)} %copy-done.14, bf16[160,1536]{1,0:T(8,128)(2,1)} %copy-done.15), custom_call_target="tpu_custom_call" | custom-call | flops 33554432 | bytes 8388608 | tf_op jit(solution)/shard_map/pallas_call | solution.py:321
  80.8 4.2 %shard_map.98 = (bf16[1280,1536]{1,0:T(8,128)(2,1)}, f32[8,128]{1,0:T(8,128)}) custom-call(s32[2]{0:T(128)} %pad_add_fusion.at_ref, bf16[320,1536]{1,0:T(8,128)(2,1)} %get-tuple-element.20.own_ref, bf16[320,1536]{1,0:T(8,128)(2,1)} %copy-done.10, bf16[320,1536]{1,0:T(8,128)(2,1)} %copy-done.11, bf16[320,1536]{1,0:T(8,128)(2,1)} %collective-permute-done.8.piece_3), custom_call_target="tpu_custom_call" | custom-call | bytes 8388608 | tf_op jit(solution)/shard_map/pallas_call | solution.py:326
  85.1 6.2 %collective-permute-done.piece_1 = bf16[320,768]{1,0:T(8,128)(2,1)S(1)} collective-permute-done((bf16[320,768]{1,0:T(8,128)(2,1)}, bf16[320,768]{1,0:T(8,128)(2,1)S(1)}, u32[]{:S(2)}, u32[]{:S(2)}) %collective-permute-start) | collective-permute-done | bytes 491552 | tf_op jit(solution)/shard_map/ppermute | solution.py:277
  91.3 8.6 %collective-permute-done.1.piece_2 = bf16[320,768]{1,0:T(8,128)(2,1)} collective-permute-done((bf16[320,768]{1,0:T(8,128)(2,1)}, bf16[320,768]{1,0:T(8,128)(2,1)}, u32[]{:S(2)}, u32[]{:S(2)}) %collective-permute-start.1) | collective-permute-done | bytes 491552 | tf_op jit(solution)/shard_map/ppermute | solution.py:277
  101.2 2.9 %shard_map.99 = (bf16[1280,768]{1,0:T(8,128)(2,1)}, f32[8,128]{1,0:T(8,128)}) custom-call(s32[2]{0:T(128)} %pad_add_fusion.at_ref, bf16[320,768]{1,0:T(8,128)(2,1)} %get-tuple-element.18.own_ref, bf16[320,768]{1,0:T(8,128)(2,1)} %copy-done.12, bf16[320,768]{1,0:T(8,128)(2,1)} %collective-permute-done.1.piece_2, ...), custom_call_target="tpu_custom_call" | custom-call | bytes 8388608 | tf_op jit(solution)/shard_map/pallas_call | solution.py:326
  104.1 1.8 all-to-all-done.recv_any
  106.0 6.7 %shard_map.100 = (bf16[4,160,1280]{2,1,0:T(8,128)(2,1)}, bf16[4,160,768]{2,1,0:T(8,128)(2,1)}) custom-call(s32[2]{0:T(128)} %pad_add_fusion.at_ref, bf16[128,2,3200]{2,1,0:T(2,128)(2,1)} %all-to-all-done.recv_any, bf16[1280,768]{1,0:T(8,128)(2,1)} %get-tuple-element.22.down_any), custom_call_target="tpu_custom_call" | custom-call | flops 2147483648 | bytes 8388608 | tf_op jit(solution)/shard_map/pallas_call | solution.py:338
  112.7 17.4 %all_to_all.20.part_ref = bf16[4,160,768]{2,1,0:T(8,128)(2,1)S(1)} all-to-all(bf16[4,160,768]{2,1,0:T(8,128)(2,1)} %get-tuple-element.23), channel_id=1, replica_groups=mesh['gx'=4,'gy'=4,'expert'=32] {'gx'}, dimensions={0} | all-to-all | bytes 1966080 | tf_op jit(solution)/shard_map/all_to_all | solution.py:273
  130.1 14.9 %all_to_all.21.hidden_ref = bf16[4,160,768]{2,1,0:T(8,128)(2,1)S(1)} all-to-all(bf16[4,160,768]{2,1,0:T(8,128)(2,1)S(1)} %shard_map.101), channel_id=1, replica_groups=mesh['gx'=4,'gy'=4,'expert'=32] {'gx'}, dimensions={0} | all-to-all | bytes 1966080 | tf_op jit(solution)/shard_map/all_to_all | solution.py:273
  145.0 6.3 %shard_map.102.after_ref = bf16[128,2,3200]{2,1,0:T(2,128)(2,1)} custom-call(s32[2]{0:T(128)S(1)} %copy-done.5, bf16[4,160,768]{2,1,0:T(8,128)(2,1)S(1)} %all_to_all.21.hidden_ref, bf16[4,160,1536]{2,1,0:T(8,128)(2,1)S(1)} %copy-done.7, bf16[1280,1536]{1,0:T(8,128)(2,1)S(1)} %copy-done.6), custom_call_target="tpu_custom_call" | custom-call | flops 4294967296 | bytes 8388608 | tf_op jit(solution)/shard_map/pallas_call | solution.py:357
  151.3 14.3 %all-to-all-start.3 = ((bf16[128,2,3200]{2,1,0:T(2,128)(2,1)}), bf16[128,2,3200]{2,1,0:T(2,128)(2,1)S(1)}, u32[]{:S(2)}, u32[]{:S(2)}) async-start(bf16[128,2,3200]{2,1,0:T(2,128)(2,1)} %shard_map.102.after_ref), calls=%async_computation.3 | async-start | bytes 3276800 | tf_op jit(solution)/shard_map/all_to_all | solution.py:269
  167.1 2.5 shard_map.104
  169.6 4.8 %collective-permute-start.10 = (bf16[320,768]{1,0:T(8,128)(2,1)S(1)}, bf16[320,768]{1,0:T(8,128)(2,1)S(1)}, u32[]{:S(2)}, u32[]{:S(2)}) collective-permute-start(bf16[320,768]{1,0:T(8,128)(2,1)S(1)} %get-tuple-element.30), channel_id=1, source_target_pairs={{0,64},{32,96},{64,0},{96,32},{1,65},{33,97},{65,1},{97,33},{2,66}... | collective-permute-start | bytes 1474568 | tf_op jit(solution)/shard_map/ppermute | solution.py:277
  174.3 6.0 %collective-permute-start.11 = (bf16[320,768]{1,0:T(8,128)(2,1)S(1)}, bf16[320,768]{1,0:T(8,128)(2,1)S(1)}, u32[]{:S(2)}, u32[]{:S(2)}) collective-permute-start(bf16[320,768]{1,0:T(8,128)(2,1)S(1)} %get-tuple-element.31), channel_id=1, source_target_pairs={{0,96},{32,0},{64,32},{96,64},{1,97},{33,1},{65,33},{97,65},{2,98}... | collective-permute-start | bytes 1474568 | tf_op jit(solution)/shard_map/ppermute | solution.py:277
  180.3 1.9 collective-permute-start.9
  182.3 2.6 %collective-permute-done.10.part_2 = bf16[320,768]{1,0:T(8,128)(2,1)S(1)} collective-permute-done((bf16[320,768]{1,0:T(8,128)(2,1)S(1)}, bf16[320,768]{1,0:T(8,128)(2,1)S(1)}, u32[]{:S(2)}, u32[]{:S(2)}) %collective-permute-start.10) | collective-permute-done | bytes 491552 | tf_op jit(solution)/shard_map/ppermute | solution.py:277
  184.8 13.1 %collective-permute-done.11.part_3 = bf16[320,768]{1,0:T(8,128)(2,1)S(1)} collective-permute-done((bf16[320,768]{1,0:T(8,128)(2,1)S(1)}, bf16[320,768]{1,0:T(8,128)(2,1)S(1)}, u32[]{:S(2)}, u32[]{:S(2)}) %collective-permute-start.11) | collective-permute-done | bytes 491552 | tf_op jit(solution)/shard_map/ppermute | solution.py:277
  198.9 46.3 %all-to-all-done.3.ret_ref = bf16[128,2,3200]{2,1,0:T(2,128)(2,1)S(1)} async-done(((bf16[128,2,3200]{2,1,0:T(2,128)(2,1)}), bf16[128,2,3200]{2,1,0:T(2,128)(2,1)S(1)}, u32[]{:S(2)}, u32[]{:S(2)}) %all-to-all-start.3) | async-done | bytes 1638432 | tf_op jit(solution)/shard_map/all_to_all | solution.py:269
  245.2 2.3 shard_map.103
  (42 shorter events, 5.8 us)
Async XLA Ops:
  5.7 21.0 %copy-start = (bf16[128,2,3200]{2,1,0:T(2,128)(2,1)S(1)}, bf16[128,2,3200]{2,1,0:T(2,128)(2,1)}, u32[]{:S(2)}) copy-start(bf16[128,2,3200]{2,1,0:T(2,128)(2,1)} %get-tuple-element.17.after_ref) | copy-start | bytes 4915204
  5.7 21.0 %copy-start.2 = (bf16[1,160,1536]{2,1,0:T(8,128)(2,1)S(1)}, bf16[1,160,1536]{2,1,0:T(8,128)(2,1)}, u32[]{:S(2)}) copy-start(bf16[1,160,1536]{2,1,0:T(8,128)(2,1)} %param.12) | copy-start | bytes 1474564
  5.7 100.2 %all-to-all-start = ((bf16[128,2,3200]{2,1,0:T(2,128)(2,1)}), bf16[128,2,3200]{2,1,0:T(2,128)(2,1)}, u32[]{:S(2)}, u32[]{:S(2)}) async-start(bf16[128,2,3200]{2,1,0:T(2,128)(2,1)} %get-tuple-element.17.after_ref), calls=%async_computation | async-start | bytes 3276800 | tf_op jit(solution)/shard_map/all_to_all | solution.py:269
  27.0 49.0 %copy-start.1 = (bf16[160,1536]{1,0:T(8,128)(2,1)}, bf16[160,1536]{1,0:T(8,128)(2,1)S(1)}, u32[]{:S(2)}) copy-start(bf16[160,1536]{1,0:T(8,128)(2,1)S(1)} %shard_map.96.pre_0) | copy-start | bytes 1474564
  27.0 18.9 %collective-permute-start.3 = (bf16[160,1536]{1,0:T(8,128)(2,1)S(1)}, bf16[160,1536]{1,0:T(8,128)(2,1)S(1)}, u32[]{:S(2)}, u32[]{:S(2)}) collective-permute-start(bf16[160,1536]{1,0:T(8,128)(2,1)S(1)} %shard_map.96.pre_0), channel_id=1, source_target_pairs={{0,128},{128,256},{256,384},{384,0},{1,129},{129,257},{257,385},{3... | collective-permute-start | bytes 1474568 | tf_op jit(solution)/shard_map/ppermute | solution.py:277
  30.4 41.3 %collective-permute-start.6 = (bf16[320,1536]{1,0:T(8,128)(2,1)}, bf16[320,1536]{1,0:T(8,128)(2,1)S(1)}, u32[]{:S(2)}, u32[]{:S(2)}) collective-permute-start(bf16[320,1536]{1,0:T(8,128)(2,1)} %get-tuple-element.20.own_ref), channel_id=1, source_target_pairs={{0,32},{32,64},{64,96},{96,0},{1,33},{33,65},{65,97},{97,1},{2,34}... | collective-permute-start | bytes 2949128 | tf_op jit(solution)/shard_map/ppermute | solution.py:277
  33.6 46.2 %collective-permute-start.7 = (bf16[320,1536]{1,0:T(8,128)(2,1)}, bf16[320,1536]{1,0:T(8,128)(2,1)S(1)}, u32[]{:S(2)}, u32[]{:S(2)}) collective-permute-start(bf16[320,1536]{1,0:T(8,128)(2,1)} %get-tuple-element.20.own_ref), channel_id=1, source_target_pairs={{0,64},{32,96},{64,0},{96,32},{1,65},{33,97},{65,1},{97,33},{2,66}... | collective-permute-start | bytes 2949128 | tf_op jit(solution)/shard_map/ppermute | solution.py:277
  38.2 22.9 %collective-permute-start.4 = (bf16[160,1536]{1,0:T(8,128)(2,1)S(1)}, bf16[160,1536]{1,0:T(8,128)(2,1)S(1)}, u32[]{:S(2)}, u32[]{:S(2)}) collective-permute-start(bf16[160,1536]{1,0:T(8,128)(2,1)S(1)} %shard_map.96.pre_0), channel_id=1, source_target_pairs={{0,256},{128,384},{256,0},{384,128},{1,257},{129,385},{257,1},{385... | collective-permute-start | bytes 1474568 | tf_op jit(solution)/shard_map/ppermute | solution.py:277
  42.9 37.9 %collective-permute-start.8 = (bf16[320,1536]{1,0:T(8,128)(2,1)}, bf16[320,1536]{1,0:T(8,128)(2,1)}, u32[]{:S(2)}, u32[]{:S(2)}) collective-permute-start(bf16[320,1536]{1,0:T(8,128)(2,1)} %get-tuple-element.20.own_ref), channel_id=1, source_target_pairs={{0,96},{32,0},{64,32},{96,64},{1,97},{33,1},{65,33},{97,65},{2,98}... | collective-permute-start | bytes 2949128 | tf_op jit(solution)/shard_map/ppermute | solution.py:277
  45.9 15.2 %copy-start.13 = (bf16[160,1536]{1,0:T(8,128)(2,1)}, bf16[160,1536]{1,0:T(8,128)(2,1)S(1)}, u32[]{:S(2)}) copy-start(bf16[160,1536]{1,0:T(8,128)(2,1)S(1)} %collective-permute-done.3.pre_1) | copy-start | bytes 1474564
  45.9 23.8 %collective-permute-start.5 = (bf16[160,1536]{1,0:T(8,128)(2,1)S(1)}, bf16[160,1536]{1,0:T(8,128)(2,1)S(1)}, u32[]{:S(2)}, u32[]{:S(2)}) collective-permute-start(bf16[160,1536]{1,0:T(8,128)(2,1)S(1)} %shard_map.96.pre_0), channel_id=1, source_target_pairs={{0,384},{128,0},{256,128},{384,256},{1,385},{129,1},{257,129},{385... | collective-permute-start | bytes 1474568 | tf_op jit(solution)/shard_map/ppermute | solution.py:277
  61.1 10.6 %copy-start.14 = (bf16[160,1536]{1,0:T(8,128)(2,1)}, bf16[160,1536]{1,0:T(8,128)(2,1)S(1)}, u32[]{:S(2)}) copy-start(bf16[160,1536]{1,0:T(8,128)(2,1)S(1)} %collective-permute-done.4.pre_2) | copy-start | bytes 1474564
  61.1 30.2 %collective-permute-start = (bf16[320,768]{1,0:T(8,128)(2,1)}, bf16[320,768]{1,0:T(8,128)(2,1)S(1)}, u32[]{:S(2)}, u32[]{:S(2)}) collective-permute-start(bf16[320,768]{1,0:T(8,128)(2,1)} %get-tuple-element.18.own_ref), channel_id=1, source_target_pairs={{0,32},{32,64},{64,96},{96,0},{1,33},{33,65},{65,97},{97,1},{2,34}... | collective-permute-start | bytes 1474568 | tf_op jit(solution)/shard_map/ppermute | solution.py:277
  69.7 5.6 %copy-start.15 = (bf16[160,1536]{1,0:T(8,128)(2,1)}, bf16[160,1536]{1,0:T(8,128)(2,1)S(1)}, u32[]{:S(2)}) copy-start(bf16[160,1536]{1,0:T(8,128)(2,1)S(1)} %collective-permute-done.5.pre_3) | copy-start | bytes 1474564
  69.7 30.2 %collective-permute-start.1 = (bf16[320,768]{1,0:T(8,128)(2,1)}, bf16[320,768]{1,0:T(8,128)(2,1)}, u32[]{:S(2)}, u32[]{:S(2)}) collective-permute-start(bf16[320,768]{1,0:T(8,128)(2,1)} %get-tuple-element.18.own_ref), channel_id=1, source_target_pairs={{0,64},{32,96},{64,0},{96,32},{1,65},{33,97},{65,1},{97,33},{2,66}... | collective-permute-start | bytes 1474568 | tf_op jit(solution)/shard_map/ppermute | solution.py:277
  71.7 9.1 %copy-start.10 = (bf16[320,1536]{1,0:T(8,128)(2,1)}, bf16[320,1536]{1,0:T(8,128)(2,1)S(1)}, u32[]{:S(2)}) copy-start(bf16[320,1536]{1,0:T(8,128)(2,1)S(1)} %collective-permute-done.6.piece_1) | copy-start | bytes 2949124
  71.7 29.5 %collective-permute-start.2 = (bf16[320,768]{1,0:T(8,128)(2,1)}, bf16[320,768]{1,0:T(8,128)(2,1)}, u32[]{:S(2)}, u32[]{:S(2)}) collective-permute-start(bf16[320,768]{1,0:T(8,128)(2,1)} %get-tuple-element.18.own_ref), channel_id=1, source_target_pairs={{0,96},{32,0},{64,32},{96,64},{1,97},{33,1},{65,33},{97,65},{2,98}... | collective-permute-start | bytes 1474568 | tf_op jit(solution)/shard_map/ppermute | solution.py:277
  79.8 1.0 copy-start.11
  91.3 9.9 %copy-start.12 = (bf16[320,768]{1,0:T(8,128)(2,1)}, bf16[320,768]{1,0:T(8,128)(2,1)S(1)}, u32[]{:S(2)}) copy-start(bf16[320,768]{1,0:T(8,128)(2,1)S(1)} %collective-permute-done.piece_1) | copy-start | bytes 1474564
  112.6 32.4 %copy-start.7 = (bf16[4,160,1536]{2,1,0:T(8,128)(2,1)S(1)}, bf16[4,160,1536]{2,1,0:T(8,128)(2,1)}, u32[]{:S(2)}) copy-start(bf16[4,160,1536]{2,1,0:T(8,128)(2,1)} %get-tuple-element.24.factor_ref) | copy-start | bytes 5898244
  130.0 15.0 %copy-start.5 = (s32[2]{0:T(128)S(1)}, s32[2]{0:T(128)}, u32[]{:S(2)}) copy-start(s32[2]{0:T(128)} %pad_add_fusion.at_ref) | copy-start | bytes 28
  130.0 15.0 %copy-start.6 = (bf16[1280,1536]{1,0:T(8,128)(2,1)S(1)}, bf16[1280,1536]{1,0:T(8,128)(2,1)}, u32[]{:S(2)}) copy-start(bf16[1280,1536]{1,0:T(8,128)(2,1)} %get-tuple-element.25.in_ref) | copy-start | bytes 11796484
  151.3 14.3 %copy-start.8 = (bf16[4,160,768]{2,1,0:T(8,128)(2,1)S(1)}, bf16[4,160,768]{2,1,0:T(8,128)(2,1)}, u32[]{:S(2)}) copy-start(bf16[4,160,768]{2,1,0:T(8,128)(2,1)} %get-tuple-element.27.act_ref) | copy-start | bytes 2949124
  151.3 93.9 %all-to-all-start.3 = ((bf16[128,2,3200]{2,1,0:T(2,128)(2,1)}), bf16[128,2,3200]{2,1,0:T(2,128)(2,1)S(1)}, u32[]{:S(2)}, u32[]{:S(2)}) async-start(bf16[128,2,3200]{2,1,0:T(2,128)(2,1)} %shard_map.102.after_ref), calls=%async_computation.3 | async-start | bytes 3276800 | tf_op jit(solution)/shard_map/all_to_all | solution.py:269
  165.7 1.4 copy-start.9
  169.6 75.7 %copy-start.3 = (s32[128,6]{0,1:T(8,128)S(1)}, s32[128,6]{0,1:T(8,128)}, u32[]{:S(2)}) copy-start(s32[128,6]{0,1:T(8,128)} %param.9) | copy-start | bytes 9220
  169.6 75.6 %copy-start.4 = (s32[128,6]{0,1:T(8,128)S(1)}, s32[128,6]{0,1:T(8,128)}, u32[]{:S(2)}) copy-start(s32[128,6]{0,1:T(8,128)} %param.10) | copy-start | bytes 9220
  169.6 15.2 %collective-permute-start.10 = (bf16[320,768]{1,0:T(8,128)(2,1)S(1)}, bf16[320,768]{1,0:T(8,128)(2,1)S(1)}, u32[]{:S(2)}, u32[]{:S(2)}) collective-permute-start(bf16[320,768]{1,0:T(8,128)(2,1)S(1)} %get-tuple-element.30), channel_id=1, source_target_pairs={{0,64},{32,96},{64,0},{96,32},{1,65},{33,97},{65,1},{97,33},{2,66}... | collective-permute-start | bytes 1474568 | tf_op jit(solution)/shard_map/ppermute | solution.py:277
  174.3 23.6 %collective-permute-start.11 = (bf16[320,768]{1,0:T(8,128)(2,1)S(1)}, bf16[320,768]{1,0:T(8,128)(2,1)S(1)}, u32[]{:S(2)}, u32[]{:S(2)}) collective-permute-start(bf16[320,768]{1,0:T(8,128)(2,1)S(1)} %get-tuple-element.31), channel_id=1, source_target_pairs={{0,96},{32,0},{64,32},{96,64},{1,97},{33,1},{65,33},{97,65},{2,98}... | collective-permute-start | bytes 1474568 | tf_op jit(solution)/shard_map/ppermute | solution.py:277
  180.3 17.6 %collective-permute-start.9 = (bf16[320,768]{1,0:T(8,128)(2,1)S(1)}, bf16[320,768]{1,0:T(8,128)(2,1)S(1)}, u32[]{:S(2)}, u32[]{:S(2)}) collective-permute-start(bf16[320,768]{1,0:T(8,128)(2,1)S(1)} %get-tuple-element.29), channel_id=1, source_target_pairs={{0,32},{32,64},{64,96},{96,0},{1,33},{33,65},{65,97},{97,1},{2,34}... | collective-permute-start | bytes 1474568 | tf_op jit(solution)/shard_map/ppermute | solution.py:277

commit v7 on v6

--- a/solution.py
+++ b/solution.py
@@ -87,17 +87,17 @@
 
 
 def to_pairs(rows):
-    return rows.reshape(N_EXP, 2, HALF).astype(BF)
+    return rows.astype(BF).reshape(N_EXP, 2, HALF)
 
 
 def from_pairs(block):
-    return block.astype(F32).reshape(PAIRS, HALF).astype(BF)
+    return block.reshape(PAIRS, HALF)
 
 
 def pick_kernel(
     og_any, ids_any, slots_any, probs_any, down_any, gate_any, up_any,
-    msg_any, own_down_any, own_in_any,
-    og_ref, ids_ref, slots_ref, probs_ref, msg_ref, down_ref, in_ref,
+    msg_any, packed_any,
+    og_ref, ids_ref, slots_ref, probs_ref, msg_ref, packed_ref,
     og_sem, in_sem, out_sem, fetch_sem, store_sem,
 ):
     small = [
@@ -109,14 +109,10 @@
         for g in range(GX)
     ]
     fetches = [
-        pltpu.make_async_copy(down_any, down_ref, fetch_sem.at[0]),
-        pltpu.make_async_copy(gate_any, in_ref.at[:, pl.ds(0, HID)], fetch_sem.at[1]),
-        pltpu.make_async_copy(up_any, in_ref.at[:, pl.ds(HID, HID)], fetch_sem.at[2]),
+        pltpu.make_async_copy(src, packed_ref.at[:, pl.ds(i * HID, HID)], fetch_sem.at[i])
+        for i, src in enumerate((down_any, gate_any, up_any))
     ]
-    stores = [
-        pltpu.make_async_copy(down_ref, own_down_any, store_sem.at[0]),
-        pltpu.make_async_copy(in_ref, own_in_any, store_sem.at[1]),
-    ]
+    stores = [pltpu.make_async_copy(packed_ref, packed_any, store_sem)]
     for copy in small + wide + fetches:
         copy.start()
     for copy in small:
@@ -143,12 +139,39 @@
         copy.wait()
 
 
-def arrange_kernel(at_ref, own_ref, piece_1, piece_2, piece_3, *refs):
-    out_ref, token_ref = refs[-2:]
-    for r, ref in enumerate((own_ref, piece_1, piece_2, piece_3)):
-        q = lax.rem(at_ref[1] + (GY - r), GY)
-        out_ref[pl.ds(pl.multiple_of(q * PART, 64), PART), :] = ref[...]
-    token_ref[...] = jnp.zeros(token_ref.shape, F32)
+def relay_kernel(less_any, more_any, after_1, after_2, after_3, low_any, high_any, low_ref, high_ref, sems):
+    half = PART // 2
+    copies = [
+        pltpu.make_async_copy(less_any.at[pl.ds(0, half)], low_ref, sems.at[0]),
+        pltpu.make_async_copy(more_any.at[pl.ds(half, half)], high_ref, sems.at[1]),
+    ]
+    for copy in copies:
+        copy.start()
+    for copy in copies:
+        copy.wait()
+    copies = [
+        pltpu.make_async_copy(low_ref, low_any, sems.at[0]),
+        pltpu.make_async_copy(high_ref, high_any, sems.at[1]),
+    ]
+    for copy in copies:
+        copy.start()
+    for copy in copies:
+        copy.wait()
+
+
+def arrange_kernel(at_ref, own_ref, less_ref, more_ref, far_low_ref, far_high_ref, after_ref, down_ref, in_ref):
+    def put(ref, away, start):
+        rows = ref.shape[0]
+        q = lax.rem(at_ref[1] + away, GY)
+        to = pl.ds(pl.multiple_of(q * PART + start, 32), rows)
+        down_ref[to, :] = ref[:, :HID]
+        in_ref[to, :] = ref[:, HID:]
+
+    put(own_ref, 0, 0)
+    put(less_ref, GY - 1, 0)
+    put(more_ref, 1, 0)
+    put(far_low_ref, 2, 0)
+    put(far_high_ref, 2, PART // 2)
 
 
 def order_kernel(pre_ref, after_ref, out_ref):
@@ -172,8 +195,17 @@
     token_ref[...] = jnp.zeros(token_ref.shape, F32)
 
 
+def put_rows(split, block_of, sent_ref, r):
+    for s in range(CAP):
+        rows = from_pairs(block_of(slice(s * HALF, (s + 1) * HALF)))
+        halves = nn(split, rows).astype(BF)
+        span = slice(s * N_EXP, (s + 1) * N_EXP)
+        sent_ref[r, span, :HALF] = halves[:N_EXP]
+        sent_ref[r, span, HALF:] = halves[N_EXP:]
+
+
 def hidden_kernel(
-    at_ref, recv_any, down_any, sent_any, part_any,
+    at_ref, recv_any, down_any, part_any,
     recv_ref, down_ref, sent_ref, part_ref, in_sems, down_sem, out_sems,
 ):
     fetches = []
@@ -188,20 +220,13 @@
     copies = []
     for r in range(GX):
         fetches[r + (r > 0)].wait()
-        for s in range(CAP):
-            rows = from_pairs(recv_ref[r, :, :, s * HALF : (s + 1) * HALF])
-            halves = nn(split, rows).astype(BF)
-            span = slice(s * N_EXP, (s + 1) * N_EXP)
-            sent_ref[r, span, :HALF] = halves[:N_EXP]
-            sent_ref[r, span, HALF:] = halves[N_EXP:]
+        put_rows(split, lambda cols: recv_ref[r, :, :, cols], sent_ref, r)
         if r == 0:
             fetches[1].wait()
         part_ref[r] = nn(sent_ref[r], down_ref[...]).astype(BF)
         g = lax.rem(at_ref[0] + (GX - r), GX)
-        copies.append(pltpu.make_async_copy(part_ref.at[r], part_any.at[g], out_sems.at[0, r]))
-        copies.append(pltpu.make_async_copy(sent_ref.at[r], sent_any.at[r], out_sems.at[1, r]))
-        for copy in copies[-2:]:
-            copy.start()
+        copies.append(pltpu.make_async_copy(part_ref.at[r], part_any.at[g], out_sems.at[r]))
+        copies[-1].start()
     for copy in copies:
         copy.wait()
 
@@ -241,7 +266,11 @@
     out_ref[...] = (total + (part_2[...].astype(F32) + part_3[...].astype(F32))).astype(BF)
 
 
-def down_kernel(at_ref, sent_ref, act_ref, after_ref, out_0, out_1, out_2, out_3, full_ref):
+def down_kernel(at_ref, recv_ref, act_ref, after_ref, out_0, out_1, out_2, out_3, sent_ref, full_ref):
+    split = split_halves()
+    for r in range(GX):
+        span = pl.ds(lax.rem(at_ref[0] + (GX - r), GX) * N_EXP, N_EXP)
+        put_rows(split, lambda cols: recv_ref[span, :, cols], sent_ref, r)
     sent = jnp.concatenate([sent_ref[r] for r in range(GX)], axis=0)
     act = jnp.concatenate([act_ref[r] for r in range(GX)], axis=0)
     full_ref[...] = tn(sent, act).astype(BF)
@@ -289,27 +318,26 @@
     anywhere = pl.BlockSpec(memory_space=pl.ANY)
     message = arr(GX * N_EXP, 2, CAP * HALF)
 
-    msg, own_down, own_in = call(
+    msg, packed = call(
         pick_kernel,
-        (message, arr(PART, HID), arr(PART, 2 * HID)),
+        (message, arr(PART, 3 * HID)),
         1 << 29,
         1 << 23,
         VMEM_MOST,
         in_specs=[anywhere] * 7,
-        out_specs=[anywhere] * 3,
+        out_specs=[anywhere] * 2,
         scratch_shapes=[
             pltpu.VMEM((GX, TOK, WIDE), BF),
             pltpu.VMEM(ids.shape, jnp.int32),
             pltpu.VMEM(ids.shape, jnp.int32),
             pltpu.VMEM(ids.shape, F32),
             pltpu.VMEM(message.shape, BF),
-            pltpu.VMEM((PART, HID), BF),
-            pltpu.VMEM((PART, 2 * HID), BF),
+            pltpu.VMEM((PART, 3 * HID), BF),
             pltpu.SemaphoreType.DMA((GX,)),
             pltpu.SemaphoreType.DMA((3,)),
             pltpu.SemaphoreType.DMA((GX,)),
             pltpu.SemaphoreType.DMA((3,)),
-            pltpu.SemaphoreType.DMA((2,)),
+            pltpu.SemaphoreType.DMA,
         ],
     )(out_grad, ids, slots, probs, w_down[0].T, w_gate[0], w_up[0])
     recv = swap(msg)
@@ -317,32 +345,46 @@
     pre = call(order_kernel, arr(ROWS, 2 * HID), 1 << 27, 1 << 21, in_specs=[vmem, anywhere])(
         saved_pre[0], msg
     )
-    token = arr(8, 128, dtype=F32)
+    pres = steps(pre, "gx")
+    less, more = step(packed, "gy", 1), step(packed, "gy", 3)
+    half = arr(PART // 2, 3 * HID)
+    low, high = call(
+        relay_kernel,
+        (half, half),
+        0,
+        1 << 22,
+        in_specs=[anywhere] * 5,
+        out_specs=[anywhere] * 2,
+        scratch_shapes=[
+            pltpu.VMEM(half.shape, BF),
+            pltpu.VMEM(half.shape, BF),
+            pltpu.SemaphoreType.DMA((2,)),
+        ],
+    )(less, more, *pres)
     factors, act, factors_done = call(
-        factor_kernel, (arr(GX, ROWS, 2 * HID), arr(GX, ROWS, HID), token), 1 << 25, 1 << 23, VMEM_MOST
-    )(pre, *steps(pre, "gx"))
-
-    def arrange(own, *after):
-        return call(
-            arrange_kernel,
-            (arr(WIDE, own.shape[1]), token),
-            0,
-            1 << 23,
-            VMEM_MOST,
-            in_specs=[smem] + [vmem] * 4 + [anywhere] * len(after),
-        )(at, own, *steps(own, "gy"), *after)
-
-    in_w, in_done = arrange(own_in)
-    down_w, _ = arrange(own_down, factors_done, in_done)
-
-    sent, part = call(
+        factor_kernel,
+        (arr(GX, ROWS, 2 * HID), arr(GX, ROWS, HID), arr(8, 128, dtype=F32)),
+        1 << 25,
+        1 << 23,
+        VMEM_MOST,
+    )(pre, *pres)
+    down_w, in_w = call(
+        arrange_kernel,
+        (arr(WIDE, HID), arr(WIDE, 2 * HID)),
+        0,
+        1 << 24,
+        VMEM_MOST,
+        in_specs=[smem] + [vmem] * 5 + [anywhere],
+    )(at, packed, less, more, step(low, "gy", 1), step(high, "gy", 3), factors_done)
+
+    part = call(
         hidden_kernel,
-        (arr(GX, ROWS, WIDE), arr(GX, ROWS, HID)),
+        arr(GX, ROWS, HID),
         1 << 31,
         1 << 23,
         VMEM_MOST,
         in_specs=[smem, anywhere, anywhere],
-        out_specs=[anywhere] * 2,
+        out_specs=anywhere,
         scratch_shapes=[
             pltpu.VMEM((GX, N_EXP, 2, CAP * HALF), BF),
             pltpu.VMEM((WIDE, HID), BF),
@@ -350,7 +392,7 @@
             pltpu.VMEM((GX, ROWS, HID), BF),
             pltpu.SemaphoreType.DMA((GX,)),
             pltpu.SemaphoreType.DMA,
-            pltpu.SemaphoreType.DMA((2, GX)),
+            pltpu.SemaphoreType.DMA((GX,)),
         ],
     )(at, recv, down_w)
     hidden = swap_gx(call(spread_kernel, arr(GX, ROWS, HID), 0, 1 << 21)(swap_gx(part)))
@@ -374,8 +416,8 @@
         1 << 31,
         1 << 22,
         in_specs=[smem] + [vmem] * 2 + [anywhere],
-        scratch_shapes=[pltpu.VMEM((WIDE, HID), BF)],
-    )(at, sent, act, back)
+        scratch_shapes=[pltpu.VMEM((GX, ROWS, WIDE), BF), pltpu.VMEM((WIDE, HID), BF)],
+    )(at, recv, act, back)
     grad_down = call(total_kernel, arr(PART, HID), 0, 1 << 21)(
         downs[0], *[step(downs[r], "gy", r) for r in range(1, GY)]
     )

time: 251 us -> 247 us (0.984)
  starting transfers between devices: 79.4 us -> 70 us
  waiting for transfers between devices: 97.6 us -> 105 us
    ppermute x12 -> x10, starting transfers between devices: 44.1 us -> 34 us  [step(): return lax.ppermute(value, axis, [(i, (i + r) % 4) for i in range(4)])]
    ppermute x12 -> x10, waiting for transfers between devices: 49.4 us -> 58 us  [step(): return lax.ppermute(value, axis, [(i, (i + r) % 4) for i in range(4)])]
  transfers between devices with their start and end apart: 14 -> 12, of which waited for: 10 -> 10; matrix products, arithmetic and copies ran while one was open for 0% -> 0% of each run, Pallas kernels for 6% -> 7%
where the time goes in v7:
time: 247 us; the launch traced here: 246 us
  waiting for transfers between devices  105 us (43%)
  starting transfers between devices  70 us (28%)
  Pallas kernels  34.6 us (14%)
  blocking collectives  32.2 us (13%)
  local copies, waits for them, and re-layouts  2.77 us (1%)
    ppermute x10, waiting for transfers between devices, step(): return lax.ppermute(value, axis, [(i, (i + r) % 4) for i in range(4)])  58 us
    all_to_all x2, waiting for transfers between devices, swap(): return lax.all_to_all(value, ('gx', 'expert'), 0, 0, tiled=True)  46.6 us
    all_to_all x2, starting transfers between devices, swap(): return lax.all_to_all(value, ('gx', 'expert'), 0, 0, tiled=True)  36 us
    ppermute x10, starting transfers between devices, step(): return lax.ppermute(value, axis, [(i, (i + r) % 4) for i in range(4)])  34 us
    all_to_all x2, blocking collectives, swap_gx(): return lax.all_to_all(value, 'gx', 0, 0, tiled=True)  32.2 us
    pallas_call x1, Pallas kernels, per_device(): call(hidden_kernel, arr(GX, ROWS, HID), 1 << 31, 1 << 23, VMEM_MOST, in_s...  6.48 us
    pallas_call x1, Pallas kernels, per_device(): call(arrange_kernel, (arr(WIDE, HID), arr(WIDE, 2 * HID)), 0, 1 << 24, VM...  5.49 us
    pallas_call x1, Pallas kernels, per_device(): call(back_kernel, message, 1 << 32, 1 << 23, in_specs=[smem] + [vmem] * 3...  5.3 us
  transfers between devices with their start and end apart: 12, of which 10 were waited for; matrix products, arithmetic and copies ran while one was open for 0% of the time, Pallas kernels for 7%

profile of v7, /device:TPU:1, one launch (start us, length us, event | category | flops | bytes accessed | tf_op | source)
XLA Modules:
  0.0 245.8 jit_solution(16326208593592794221)
XLA Ops:
  0.6 4.0 %shard_map.95 = (bf16[128,2,3200]{2,1,0:T(2,128)(2,1)}, bf16[320,2304]{1,0:T(8,128)(2,1)}) custom-call(bf16[128,5120]{1,0:T(8,128)(2,1)} %og_any.1, s32[6,128]{1,0:T(8,128)} %bitcast.15, s32[6,128]{1,0:T(8,128)} %bitcast.17, f32[6,128]{1,0:T(8,128)} %bitcast.23, bf16[320,768]{1,0:T(8,128)(2,1)} %bitcast.20, bf16[320,768]{1,0:T(8,128)(2,1)} %bitcast.21, ...), custom_call_target="tpu_custom_call" | custom-call | flops 536870912 | bytes 8388608 | tf_op jit(solution)/shard_map/pallas_call | solution.py:321
  4.6 21.1 %all-to-all-start = ((bf16[128,2,3200]{2,1,0:T(2,128)(2,1)}), bf16[128,2,3200]{2,1,0:T(2,128)(2,1)}, u32[]{:S(2)}, u32[]{:S(2)}) async-start(bf16[128,2,3200]{2,1,0:T(2,128)(2,1)} %get-tuple-element.15.after_ref), calls=%async_computation | async-start | bytes 3276800 | tf_op jit(solution)/shard_map/all_to_all | solution.py:298
  25.7 4.6 %collective-permute-start.1 = (bf16[320,2304]{1,0:T(8,128)(2,1)S(1)}, bf16[320,2304]{1,0:T(8,128)(2,1)S(1)}, u32[]{:S(2)}, u32[]{:S(2)}) collective-permute-start(bf16[320,2304]{1,0:T(8,128)(2,1)S(1)} %copy-done.14), channel_id=1, source_target_pairs={{0,96},{32,0},{64,32},{96,64},{1,97},{33,1},{65,33},{97,65},{2,98}... | collective-permute-start | bytes 4423688 | tf_op jit(solution)/shard_map/ppermute | solution.py:306
  30.4 1.9 collective-permute-start
  32.3 1.0 copy-done.7
  33.6 5.0 %collective-permute-start.4 = (bf16[160,1536]{1,0:T(8,128)(2,1)S(1)}, bf16[160,1536]{1,0:T(8,128)(2,1)S(1)}, u32[]{:S(2)}, u32[]{:S(2)}) collective-permute-start(bf16[160,1536]{1,0:T(8,128)(2,1)S(1)} %shard_map.96.pre_0), channel_id=1, source_target_pairs={{0,384},{128,0},{256,128},{384,256},{1,385},{129,1},{257,129},{385... | collective-permute-start | bytes 1474568 | tf_op jit(solution)/shard_map/ppermute | solution.py:306
  38.7 2.1 collective-permute-start.3
  40.7 2.7 %collective-permute-start.2 = (bf16[160,1536]{1,0:T(8,128)(2,1)S(1)}, bf16[160,1536]{1,0:T(8,128)(2,1)S(1)}, u32[]{:S(2)}, u32[]{:S(2)}) collective-permute-start(bf16[160,1536]{1,0:T(8,128)(2,1)S(1)} %shard_map.96.pre_0), channel_id=1, source_target_pairs={{0,128},{128,256},{256,384},{384,0},{1,129},{129,257},{257,385},{3... | collective-permute-start | bytes 1474568 | tf_op jit(solution)/shard_map/ppermute | solution.py:306
  43.4 8.9 %collective-permute-done.4.after_3.pre_3 = bf16[160,1536]{1,0:T(8,128)(2,1)S(1)} collective-permute-done((bf16[160,1536]{1,0:T(8,128)(2,1)S(1)}, bf16[160,1536]{1,0:T(8,128)(2,1)S(1)}, u32[]{:S(2)}, u32[]{:S(2)}) %collective-permute-start.4) | collective-permute-done | bytes 491552 | tf_op jit(solution)/shard_map/ppermute | solution.py:306
  52.3 4.9 %collective-permute-done.3.after_2.pre_2 = bf16[160,1536]{1,0:T(8,128)(2,1)S(1)} collective-permute-done((bf16[160,1536]{1,0:T(8,128)(2,1)S(1)}, bf16[160,1536]{1,0:T(8,128)(2,1)S(1)}, u32[]{:S(2)}, u32[]{:S(2)}) %collective-permute-start.3) | collective-permute-done | bytes 491552 | tf_op jit(solution)/shard_map/ppermute | solution.py:306
  57.2 15.3 %collective-permute-done.2.after_1.pre_1 = bf16[160,1536]{1,0:T(8,128)(2,1)S(1)} collective-permute-done((bf16[160,1536]{1,0:T(8,128)(2,1)S(1)}, bf16[160,1536]{1,0:T(8,128)(2,1)S(1)}, u32[]{:S(2)}, u32[]{:S(2)}) %collective-permute-start.2) | collective-permute-done | bytes 491552 | tf_op jit(solution)/shard_map/ppermute | solution.py:306
  72.6 2.0 shard_map.97
  75.5 1.9 collective-permute-start.5
  77.4 4.6 %collective-permute-start.6 = (bf16[160,2304]{1,0:T(8,128)(2,1)}, bf16[160,2304]{1,0:T(8,128)(2,1)S(1)}, u32[]{:S(2)}, u32[]{:S(2)}) collective-permute-start(bf16[160,2304]{1,0:T(8,128)(2,1)} %get-tuple-element.18), channel_id=1, source_target_pairs={{0,96},{32,0},{64,32},{96,64},{1,97},{33,1},{65,33},{97,65},{2,98}... | collective-permute-start | bytes 2211848 | tf_op jit(solution)/shard_map/ppermute | solution.py:306
  82.6 3.8 %shard_map.98 = (bf16[4,160,1536]{2,1,0:T(8,128)(2,1)}, bf16[4,160,768]{2,1,0:T(8,128)(2,1)}, f32[8,128]{1,0:T(8,128)}) custom-call(bf16[160,1536]{1,0:T(8,128)(2,1)} %copy-done.3, bf16[160,1536]{1,0:T(8,128)(2,1)} %copy-done.6, bf16[160,1536]{1,0:T(8,128)(2,1)} %copy-done.5, bf16[160,1536]{1,0:T(8,128)(2,1)} %copy-done.4), custom_call_target="tpu_custom_call" | custom-call | flops 33554432 | bytes 8388608 | tf_op jit(solution)/shard_map/pallas_call | solution.py:364
  86.4 10.1 %collective-permute-done.5.far_low_ref = bf16[160,2304]{1,0:T(8,128)(2,1)S(1)} collective-permute-done((bf16[160,2304]{1,0:T(8,128)(2,1)}, bf16[160,2304]{1,0:T(8,128)(2,1)S(1)}, u32[]{:S(2)}, u32[]{:S(2)}) %collective-permute-start.5) | collective-permute-done | bytes 737312 | tf_op jit(solution)/shard_map/ppermute | solution.py:306
  98.3 5.5 %shard_map.99 = (bf16[1280,768]{1,0:T(8,128)(2,1)}, bf16[1280,1536]{1,0:T(8,128)(2,1)}) custom-call(s32[2]{0:T(128)} %pad_add_fusion.at_ref, bf16[320,2304]{1,0:T(8,128)(2,1)} %get-tuple-element.16.own_ref, bf16[320,2304]{1,0:T(8,128)(2,1)} %copy-done.2, bf16[320,2304]{1,0:T(8,128)(2,1)} %copy-done.1, bf16[160,2304]{1,0:T(8,128)(2,1)} %copy-done.15, ...), custom_call_target="tpu_custom_call" | custom-call | bytes 16777216 | tf_op jit(solution)/shard_map/pallas_call | solution.py:371
  103.8 1.2 all-to-all-done.recv_any.recv_ref
  105.0 6.5 %shard_map.100 = bf16[4,160,768]{2,1,0:T(8,128)(2,1)} custom-call(s32[2]{0:T(128)} %pad_add_fusion.at_ref, bf16[128,2,3200]{2,1,0:T(2,128)(2,1)} %all-to-all-done.recv_any.recv_ref, bf16[1280,768]{1,0:T(8,128)(2,1)} %get-tuple-element.20.down_any), custom_call_target="tpu_custom_call" | custom-call | flops 2147483648 | bytes 8388608 | tf_op jit(solution)/shard_map/pallas_call | solution.py:380
  111.5 17.4 %all_to_all.20.part_ref = bf16[4,160,768]{2,1,0:T(8,128)(2,1)S(1)} all-to-all(bf16[4,160,768]{2,1,0:T(8,128)(2,1)} %shard_map.100), channel_id=1, replica_groups=mesh['gx'=4,'gy'=4,'expert'=32] {'gx'}, dimensions={0} | all-to-all | bytes 1966080 | tf_op jit(solution)/shard_map/all_to_all | solution.py:302
  129.0 14.9 %all_to_all.21.hidden_ref = bf16[4,160,768]{2,1,0:T(8,128)(2,1)S(1)} all-to-all(bf16[4,160,768]{2,1,0:T(8,128)(2,1)S(1)} %shard_map.101), channel_id=1, replica_groups=mesh['gx'=4,'gy'=4,'expert'=32] {'gx'}, dimensions={0} | all-to-all | bytes 1966080 | tf_op jit(solution)/shard_map/all_to_all | solution.py:302
  143.8 5.3 %shard_map.102.after_ref = bf16[128,2,3200]{2,1,0:T(2,128)(2,1)} custom-call(s32[2]{0:T(128)S(1)} %copy-done.10, bf16[4,160,768]{2,1,0:T(8,128)(2,1)S(1)} %all_to_all.21.hidden_ref, bf16[4,160,1536]{2,1,0:T(8,128)(2,1)S(1)} %copy-done.12, bf16[1280,1536]{1,0:T(8,128)(2,1)S(1)} %copy-done.11), custom_call_target="tpu_custom_call" | custom-call | flops 4294967296 | bytes 8388608 | tf_op jit(solution)/shard_map/pallas_call | solution.py:399
  149.2 14.9 %all-to-all-start.3 = ((bf16[128,2,3200]{2,1,0:T(2,128)(2,1)}), bf16[128,2,3200]{2,1,0:T(2,128)(2,1)S(1)}, u32[]{:S(2)}, u32[]{:S(2)}) async-start(bf16[128,2,3200]{2,1,0:T(2,128)(2,1)} %shard_map.102.after_ref), calls=%async_computation.3 | async-start | bytes 3276800 | tf_op jit(solution)/shard_map/all_to_all | solution.py:298
  164.1 3.9 %shard_map.104 = (bf16[320,768]{1,0:T(8,128)(2,1)S(1)}, bf16[320,768]{1,0:T(8,128)(2,1)S(1)}, bf16[320,768]{1,0:T(8,128)(2,1)S(1)}, bf16[320,768]{1,0:T(8,128)(2,1)S(1)}) custom-call(s32[2]{0:T(128)S(1)} %copy-done.10, bf16[128,2,3200]{2,1,0:T(2,128)(2,1)} %all-to-all-done.recv_any.recv_ref, bf16[4,160,768]{2,1,0:T(8,128)(2,1)S(1)} %copy-done.13, ...), custom_call_target="tpu_custom_call" | custom-call | flops 2147483648 | bytes 4194304 | tf_op jit(solution)/shard_map/pallas_call | solution.py:413
  168.0 3.9 %collective-permute-start.7 = (bf16[320,768]{1,0:T(8,128)(2,1)S(1)}, bf16[320,768]{1,0:T(8,128)(2,1)S(1)}, u32[]{:S(2)}, u32[]{:S(2)}) collective-permute-start(bf16[320,768]{1,0:T(8,128)(2,1)S(1)} %get-tuple-element.25), channel_id=1, source_target_pairs={{0,32},{32,64},{64,96},{96,0},{1,33},{33,65},{65,97},{97,1},{2,34}... | collective-permute-start | bytes 1474568 | tf_op jit(solution)/shard_map/ppermute | solution.py:306
  171.9 4.6 %collective-permute-start.8 = (bf16[320,768]{1,0:T(8,128)(2,1)S(1)}, bf16[320,768]{1,0:T(8,128)(2,1)S(1)}, u32[]{:S(2)}, u32[]{:S(2)}) collective-permute-start(bf16[320,768]{1,0:T(8,128)(2,1)S(1)} %get-tuple-element.26), channel_id=1, source_target_pairs={{0,64},{32,96},{64,0},{96,32},{1,65},{33,97},{65,1},{97,33},{2,66}... | collective-permute-start | bytes 1474568 | tf_op jit(solution)/shard_map/ppermute | solution.py:306
  176.6 2.7 %collective-permute-start.9 = (bf16[320,768]{1,0:T(8,128)(2,1)S(1)}, bf16[320,768]{1,0:T(8,128)(2,1)S(1)}, u32[]{:S(2)}, u32[]{:S(2)}) collective-permute-start(bf16[320,768]{1,0:T(8,128)(2,1)S(1)} %get-tuple-element.27), channel_id=1, source_target_pairs={{0,96},{32,0},{64,32},{96,64},{1,97},{33,1},{65,33},{97,65},{2,98}... | collective-permute-start | bytes 1474568 | tf_op jit(solution)/shard_map/ppermute | solution.py:306
  179.2 4.9 %collective-permute-done.7.part_1 = bf16[320,768]{1,0:T(8,128)(2,1)S(1)} collective-permute-done((bf16[320,768]{1,0:T(8,128)(2,1)S(1)}, bf16[320,768]{1,0:T(8,128)(2,1)S(1)}, u32[]{:S(2)}, u32[]{:S(2)}) %collective-permute-start.7) | collective-permute-done | bytes 491552 | tf_op jit(solution)/shard_map/ppermute | solution.py:306
  184.1 11.4 %collective-permute-done.8.part_2 = bf16[320,768]{1,0:T(8,128)(2,1)S(1)} collective-permute-done((bf16[320,768]{1,0:T(8,128)(2,1)S(1)}, bf16[320,768]{1,0:T(8,128)(2,1)S(1)}, u32[]{:S(2)}, u32[]{:S(2)}) %collective-permute-start.8) | collective-permute-done | bytes 491552 | tf_op jit(solution)/shard_map/ppermute | solution.py:306
  195.5 1.6 collective-permute-done.9.part_3
  198.1 45.5 %all-to-all-done.3.ret_ref = bf16[128,2,3200]{2,1,0:T(2,128)(2,1)S(1)} async-done(((bf16[128,2,3200]{2,1,0:T(2,128)(2,1)}), bf16[128,2,3200]{2,1,0:T(2,128)(2,1)S(1)}, u32[]{:S(2)}, u32[]{:S(2)}) %all-to-all-start.3) | async-done | bytes 1638432 | tf_op jit(solution)/shard_map/all_to_all | solution.py:298
  243.6 2.1 shard_map.103
  (40 shorter events, 4.6 us)
Async XLA Ops:
  4.6 21.1 %copy-start.14 = (bf16[320,2304]{1,0:T(8,128)(2,1)S(1)}, bf16[320,2304]{1,0:T(8,128)(2,1)}, u32[]{:S(2)}) copy-start(bf16[320,2304]{1,0:T(8,128)(2,1)} %get-tuple-element.16.own_ref) | copy-start | bytes 4423684
  4.6 27.7 %copy-start = (bf16[128,2,3200]{2,1,0:T(2,128)(2,1)S(1)}, bf16[128,2,3200]{2,1,0:T(2,128)(2,1)}, u32[]{:S(2)}) copy-start(bf16[128,2,3200]{2,1,0:T(2,128)(2,1)} %get-tuple-element.15.after_ref) | copy-start | bytes 4915204
  4.6 100.3 %all-to-all-start = ((bf16[128,2,3200]{2,1,0:T(2,128)(2,1)}), bf16[128,2,3200]{2,1,0:T(2,128)(2,1)}, u32[]{:S(2)}, u32[]{:S(2)}) async-start(bf16[128,2,3200]{2,1,0:T(2,128)(2,1)} %get-tuple-element.15.after_ref), calls=%async_computation | async-start | bytes 3276800 | tf_op jit(solution)/shard_map/all_to_all | solution.py:298
  25.7 46.8 %collective-permute-start.1 = (bf16[320,2304]{1,0:T(8,128)(2,1)S(1)}, bf16[320,2304]{1,0:T(8,128)(2,1)S(1)}, u32[]{:S(2)}, u32[]{:S(2)}) collective-permute-start(bf16[320,2304]{1,0:T(8,128)(2,1)S(1)} %copy-done.14), channel_id=1, source_target_pairs={{0,96},{32,0},{64,32},{96,64},{1,97},{33,1},{65,33},{97,65},{2,98}... | collective-permute-start | bytes 4423688 | tf_op jit(solution)/shard_map/ppermute | solution.py:306
  30.4 42.2 %collective-permute-start = (bf16[320,2304]{1,0:T(8,128)(2,1)S(1)}, bf16[320,2304]{1,0:T(8,128)(2,1)S(1)}, u32[]{:S(2)}, u32[]{:S(2)}) collective-permute-start(bf16[320,2304]{1,0:T(8,128)(2,1)S(1)} %copy-done.14), channel_id=1, source_target_pairs={{0,32},{32,64},{64,96},{96,0},{1,33},{33,65},{65,97},{97,1},{2,34}... | collective-permute-start | bytes 4423688 | tf_op jit(solution)/shard_map/ppermute | solution.py:306
  32.3 1.0 copy-start.7
  33.6 41.0 %copy-start.3 = (bf16[160,1536]{1,0:T(8,128)(2,1)}, bf16[160,1536]{1,0:T(8,128)(2,1)S(1)}, u32[]{:S(2)}) copy-start(bf16[160,1536]{1,0:T(8,128)(2,1)S(1)} %shard_map.96.pre_0) | copy-start | bytes 1474564
  33.6 18.7 %collective-permute-start.4 = (bf16[160,1536]{1,0:T(8,128)(2,1)S(1)}, bf16[160,1536]{1,0:T(8,128)(2,1)S(1)}, u32[]{:S(2)}, u32[]{:S(2)}) collective-permute-start(bf16[160,1536]{1,0:T(8,128)(2,1)S(1)} %shard_map.96.pre_0), channel_id=1, source_target_pairs={{0,384},{128,0},{256,128},{384,256},{1,385},{129,1},{257,129},{385... | collective-permute-start | bytes 1474568 | tf_op jit(solution)/shard_map/ppermute | solution.py:306
  38.7 18.5 %collective-permute-start.3 = (bf16[160,1536]{1,0:T(8,128)(2,1)S(1)}, bf16[160,1536]{1,0:T(8,128)(2,1)S(1)}, u32[]{:S(2)}, u32[]{:S(2)}) collective-permute-start(bf16[160,1536]{1,0:T(8,128)(2,1)S(1)} %shard_map.96.pre_0), channel_id=1, source_target_pairs={{0,256},{128,384},{256,0},{384,128},{1,257},{129,385},{257,1},{385... | collective-permute-start | bytes 1474568 | tf_op jit(solution)/shard_map/ppermute | solution.py:306
  40.7 31.8 %collective-permute-start.2 = (bf16[160,1536]{1,0:T(8,128)(2,1)S(1)}, bf16[160,1536]{1,0:T(8,128)(2,1)S(1)}, u32[]{:S(2)}, u32[]{:S(2)}) collective-permute-start(bf16[160,1536]{1,0:T(8,128)(2,1)S(1)} %shard_map.96.pre_0), channel_id=1, source_target_pairs={{0,128},{128,256},{256,384},{384,0},{1,129},{129,257},{257,385},{3... | collective-permute-start | bytes 1474568 | tf_op jit(solution)/shard_map/ppermute | solution.py:306
  52.3 22.3 %copy-start.4 = (bf16[160,1536]{1,0:T(8,128)(2,1)}, bf16[160,1536]{1,0:T(8,128)(2,1)S(1)}, u32[]{:S(2)}) copy-start(bf16[160,1536]{1,0:T(8,128)(2,1)S(1)} %collective-permute-done.4.after_3.pre_3) | copy-start | bytes 1474564
  57.2 17.4 %copy-start.5 = (bf16[160,1536]{1,0:T(8,128)(2,1)}, bf16[160,1536]{1,0:T(8,128)(2,1)S(1)}, u32[]{:S(2)}) copy-start(bf16[160,1536]{1,0:T(8,128)(2,1)S(1)} %collective-permute-done.3.after_2.pre_2) | copy-start | bytes 1474564
  72.6 2.1 copy-start.1
  72.6 2.1 copy-start.2
  74.7 0.8 copy-start.6
  75.5 21.1 %collective-permute-start.5 = (bf16[160,2304]{1,0:T(8,128)(2,1)}, bf16[160,2304]{1,0:T(8,128)(2,1)S(1)}, u32[]{:S(2)}, u32[]{:S(2)}) collective-permute-start(bf16[160,2304]{1,0:T(8,128)(2,1)} %get-tuple-element.17), channel_id=1, source_target_pairs={{0,32},{32,64},{64,96},{96,0},{1,33},{33,65},{65,97},{97,1},{2,34}... | collective-permute-start | bytes 2211848 | tf_op jit(solution)/shard_map/ppermute | solution.py:306
  77.4 20.0 %collective-permute-start.6 = (bf16[160,2304]{1,0:T(8,128)(2,1)}, bf16[160,2304]{1,0:T(8,128)(2,1)S(1)}, u32[]{:S(2)}, u32[]{:S(2)}) collective-permute-start(bf16[160,2304]{1,0:T(8,128)(2,1)} %get-tuple-element.18), channel_id=1, source_target_pairs={{0,96},{32,0},{64,32},{96,64},{1,97},{33,1},{65,33},{97,65},{2,98}... | collective-permute-start | bytes 2211848 | tf_op jit(solution)/shard_map/ppermute | solution.py:306
  96.6 0.9 copy-start.15
  97.4 0.9 copy-start.16
  111.4 32.4 %copy-start.12 = (bf16[4,160,1536]{2,1,0:T(8,128)(2,1)S(1)}, bf16[4,160,1536]{2,1,0:T(8,128)(2,1)}, u32[]{:S(2)}) copy-start(bf16[4,160,1536]{2,1,0:T(8,128)(2,1)} %get-tuple-element.21.factor_ref) | copy-start | bytes 5898244
  128.8 15.0 %copy-start.10 = (s32[2]{0:T(128)S(1)}, s32[2]{0:T(128)}, u32[]{:S(2)}) copy-start(s32[2]{0:T(128)} %pad_add_fusion.at_ref) | copy-start | bytes 28
  128.8 15.0 %copy-start.11 = (bf16[1280,1536]{1,0:T(8,128)(2,1)S(1)}, bf16[1280,1536]{1,0:T(8,128)(2,1)}, u32[]{:S(2)}) copy-start(bf16[1280,1536]{1,0:T(8,128)(2,1)} %get-tuple-element.22.in_ref) | copy-start | bytes 11796484
  149.1 14.9 %copy-start.13 = (bf16[4,160,768]{2,1,0:T(8,128)(2,1)S(1)}, bf16[4,160,768]{2,1,0:T(8,128)(2,1)}, u32[]{:S(2)}) copy-start(bf16[4,160,768]{2,1,0:T(8,128)(2,1)} %get-tuple-element.23.act_ref) | copy-start | bytes 2949124
  149.2 94.5 %all-to-all-start.3 = ((bf16[128,2,3200]{2,1,0:T(2,128)(2,1)}), bf16[128,2,3200]{2,1,0:T(2,128)(2,1)S(1)}, u32[]{:S(2)}, u32[]{:S(2)}) async-start(bf16[128,2,3200]{2,1,0:T(2,128)(2,1)} %shard_map.102.after_ref), calls=%async_computation.3 | async-start | bytes 3276800 | tf_op jit(solution)/shard_map/all_to_all | solution.py:298
  168.0 75.6 %copy-start.8 = (s32[128,6]{0,1:T(8,128)S(1)}, s32[128,6]{0,1:T(8,128)}, u32[]{:S(2)}) copy-start(s32[128,6]{0,1:T(8,128)} %param.9) | copy-start | bytes 9220
  168.0 75.6 %copy-start.9 = (s32[128,6]{0,1:T(8,128)S(1)}, s32[128,6]{0,1:T(8,128)}, u32[]{:S(2)}) copy-start(s32[128,6]{0,1:T(8,128)} %param.10) | copy-start | bytes 9220
  168.0 16.1 %collective-permute-start.7 = (bf16[320,768]{1,0:T(8,128)(2,1)S(1)}, bf16[320,768]{1,0:T(8,128)(2,1)S(1)}, u32[]{:S(2)}, u32[]{:S(2)}) collective-permute-start(bf16[320,768]{1,0:T(8,128)(2,1)S(1)} %get-tuple-element.25), channel_id=1, source_target_pairs={{0,32},{32,64},{64,96},{96,0},{1,33},{33,65},{65,97},{97,1},{2,34}... | collective-permute-start | bytes 1474568 | tf_op jit(solution)/shard_map/ppermute | solution.py:306
  171.9 23.6 %collective-permute-start.8 = (bf16[320,768]{1,0:T(8,128)(2,1)S(1)}, bf16[320,768]{1,0:T(8,128)(2,1)S(1)}, u32[]{:S(2)}, u32[]{:S(2)}) collective-permute-start(bf16[320,768]{1,0:T(8,128)(2,1)S(1)} %get-tuple-element.26), channel_id=1, source_target_pairs={{0,64},{32,96},{64,0},{96,32},{1,65},{33,97},{65,1},{97,33},{2,66}... | collective-permute-start | bytes 1474568 | tf_op jit(solution)/shard_map/ppermute | solution.py:306
  176.6 20.6 %collective-permute-start.9 = (bf16[320,768]{1,0:T(8,128)(2,1)S(1)}, bf16[320,768]{1,0:T(8,128)(2,1)S(1)}, u32[]{:S(2)}, u32[]{:S(2)}) collective-permute-start(bf16[320,768]{1,0:T(8,128)(2,1)S(1)} %get-tuple-element.27), channel_id=1, source_target_pairs={{0,96},{32,0},{64,32},{96,64},{1,97},{33,1},{65,33},{97,65},{2,98}... | collective-permute-start | bytes 1474568 | tf_op jit(solution)/shard_map/ppermute | solution.py:306

commit v8 on v7

--- a/solution.py
+++ b/solution.py
@@ -1,3 +1,5 @@
+import functools
+
 import jax
 import jax.numpy as jnp
 from jax import lax
@@ -159,19 +161,18 @@
         copy.wait()
 
 
-def arrange_kernel(at_ref, own_ref, less_ref, more_ref, far_low_ref, far_high_ref, after_ref, down_ref, in_ref):
-    def put(ref, away, start):
-        rows = ref.shape[0]
+def arrange_kernel(places, at_ref, *refs):
+    pieces, (down_any, in_any, sems) = refs[: len(places)], refs[-3:]
+    copies = []
+    for i, (ref, (away, start)) in enumerate(zip(pieces, places)):
         q = lax.rem(at_ref[1] + away, GY)
-        to = pl.ds(pl.multiple_of(q * PART + start, 32), rows)
-        down_ref[to, :] = ref[:, :HID]
-        in_ref[to, :] = ref[:, HID:]
-
-    put(own_ref, 0, 0)
-    put(less_ref, GY - 1, 0)
-    put(more_ref, 1, 0)
-    put(far_low_ref, 2, 0)
-    put(far_high_ref, 2, PART // 2)
+        to = pl.ds(pl.multiple_of(q * PART + start, 32), ref.shape[0])
+        copies.append(pltpu.make_async_copy(ref.at[:, pl.ds(0, HID)], down_any.at[to], sems.at[0, i]))
+        copies.append(pltpu.make_async_copy(ref.at[:, pl.ds(HID, 2 * HID)], in_any.at[to], sems.at[1, i]))
+    for copy in copies:
+        copy.start()
+    for copy in copies:
+        copy.wait()
 
 
 def order_kernel(pre_ref, after_ref, out_ref):
@@ -210,23 +211,25 @@
 ):
     fetches = []
     for r in range(GX):
-        g = lax.rem(at_ref[0] + (GX - r), GX)
-        span = pl.ds(g * N_EXP, N_EXP)
+        span = pl.ds(lax.rem(at_ref[0] + (GX - r), GX) * N_EXP, N_EXP)
         fetches.append(pltpu.make_async_copy(recv_any.at[span], recv_ref.at[r], in_sems.at[r]))
-    fetches.insert(1, pltpu.make_async_copy(down_any, down_ref, down_sem))
+    fetches.append(pltpu.make_async_copy(down_any, down_ref, down_sem))
     for copy in fetches:
         copy.start()
     split = split_halves()
+    for r in range(GX):
+        fetches[r].wait()
+        put_rows(split, lambda cols: recv_ref[r, :, :, cols], sent_ref, r)
+    fetches[GX].wait()
     copies = []
-    for r in range(GX):
-        fetches[r + (r > 0)].wait()
-        put_rows(split, lambda cols: recv_ref[r, :, :, cols], sent_ref, r)
-        if r == 0:
-            fetches[1].wait()
-        part_ref[r] = nn(sent_ref[r], down_ref[...]).astype(BF)
-        g = lax.rem(at_ref[0] + (GX - r), GX)
-        copies.append(pltpu.make_async_copy(part_ref.at[r], part_any.at[g], out_sems.at[r]))
-        copies[-1].start()
+    for pair in range(2):
+        sent = jnp.concatenate([sent_ref[2 * pair], sent_ref[2 * pair + 1]], axis=0)
+        part = nn(sent, down_ref[...]).astype(BF)
+        for r in (2 * pair, 2 * pair + 1):
+            part_ref[r] = part[(r % 2) * ROWS : (r % 2 + 1) * ROWS]
+            g = lax.rem(at_ref[0] + (GX - r), GX)
+            copies.append(pltpu.make_async_copy(part_ref.at[r], part_any.at[g], out_sems.at[r]))
+            copies[-1].start()
     for copy in copies:
         copy.wait()
 
@@ -368,14 +371,26 @@
         1 << 23,
         VMEM_MOST,
     )(pre, *pres)
-    down_w, in_w = call(
-        arrange_kernel,
-        (arr(WIDE, HID), arr(WIDE, 2 * HID)),
-        0,
-        1 << 24,
-        VMEM_MOST,
-        in_specs=[smem] + [vmem] * 5 + [anywhere],
-    )(at, packed, less, more, step(low, "gy", 1), step(high, "gy", 3), factors_done)
+    def arrange(places, pieces, others, aliases):
+        return call(
+            functools.partial(arrange_kernel, places),
+            (arr(WIDE, HID), arr(WIDE, 2 * HID)),
+            0,
+            1 << 24,
+            VMEM_MOST,
+            in_specs=[smem] + [vmem] * len(pieces) + [anywhere] * len(others),
+            out_specs=[anywhere] * 2,
+            scratch_shapes=[pltpu.SemaphoreType.DMA((2, len(places)))],
+            input_output_aliases=aliases,
+        )(at, *pieces, *others)
+
+    near = arrange(((0, 0), (GY - 1, 0), (1, 0)), (packed, less, more), (), {})
+    down_w, in_w = arrange(
+        ((2, 0), (2, PART // 2)),
+        (step(low, "gy", 1), step(high, "gy", 3)),
+        (*near, factors_done),
+        {3: 0, 4: 1},
+    )
 
     part = call(
         hidden_kernel,

time: 247 us -> 243 us (0.984)
  starting transfers between devices: 70 us -> 67.2 us
    ppermute x10, waiting for transfers between devices: 58 us -> 53.5 us  [step(): return lax.ppermute(value, axis, [(i, (i + r) % 4) for i in range(4)])]
    all_to_all x2, waiting for transfers between devices: 46.6 us -> 49.6 us  [swap(): return lax.all_to_all(value, ('gx', 'expert'), 0, 0, tiled=True)]
    all_to_all x2, starting transfers between devices: 36 us -> 33.1 us  [swap(): return lax.all_to_all(value, ('gx', 'expert'), 0, 0, tiled=True)]
    pallas_call x1 -> x2, Pallas kernels: 5.49 us -> 6.93 us  [arrange(): call(functools.partial(arrange_kernel, places), (arr(WIDE, HID), arr(WIDE...]
where the time goes in v8:
time: 243 us; the launch traced here: 242 us
  waiting for transfers between devices  103 us (42%)
  starting transfers between devices  67.2 us (28%)
  Pallas kernels  34.7 us (14%)
  blocking collectives  32.2 us (13%)
  local copies, waits for them, and re-layouts  2.75 us (1%)
    ppermute x10, waiting for transfers between devices, step(): return lax.ppermute(value, axis, [(i, (i + r) % 4) for i in range(4)])  53.5 us
    all_to_all x2, waiting for transfers between devices, swap(): return lax.all_to_all(value, ('gx', 'expert'), 0, 0, tiled=True)  49.6 us
    ppermute x10, starting transfers between devices, step(): return lax.ppermute(value, axis, [(i, (i + r) % 4) for i in range(4)])  34.1 us
    all_to_all x2, starting transfers between devices, swap(): return lax.all_to_all(value, ('gx', 'expert'), 0, 0, tiled=True)  33.1 us
    all_to_all x2, blocking collectives, swap_gx(): return lax.all_to_all(value, 'gx', 0, 0, tiled=True)  32.2 us
    pallas_call x2, Pallas kernels, arrange(): call(functools.partial(arrange_kernel, places), (arr(WIDE, HID), arr(WIDE...  6.93 us
    pallas_call x1, Pallas kernels, per_device(): call(back_kernel, message, 1 << 32, 1 << 23, in_specs=[smem] + [vmem] * 3...  5.31 us
    pallas_call x1, Pallas kernels, per_device(): call(hidden_kernel, arr(GX, ROWS, HID), 1 << 31, 1 << 23, VMEM_MOST, in_s...  5.22 us
  transfers between devices with their start and end apart: 12, of which 10 were waited for; matrix products, arithmetic and copies ran while one was open for 0% of the time, Pallas kernels for 7%

profile of v8, /device:TPU:1, one launch (start us, length us, event | category | flops | bytes accessed | tf_op | source)
XLA Modules:
  0.0 241.6 jit_solution(13549629043190777389)
XLA Ops:
  0.6 4.0 %shard_map.95 = (bf16[128,2,3200]{2,1,0:T(2,128)(2,1)}, bf16[320,2304]{1,0:T(8,128)(2,1)}) custom-call(bf16[128,5120]{1,0:T(8,128)(2,1)} %og_any.1, s32[6,128]{1,0:T(8,128)} %bitcast.15, s32[6,128]{1,0:T(8,128)} %bitcast.17, f32[6,128]{1,0:T(8,128)} %bitcast.23, bf16[320,768]{1,0:T(8,128)(2,1)} %bitcast.20, bf16[320,768]{1,0:T(8,128)(2,1)} %bitcast.21, ...), custom_call_target="tpu_custom_call" | custom-call | flops 536870912 | bytes 8388608 | tf_op jit(solution)/shard_map/pallas_call | solution.py:324
  4.6 21.1 %all-to-all-start = ((bf16[128,2,3200]{2,1,0:T(2,128)(2,1)}), bf16[128,2,3200]{2,1,0:T(2,128)(2,1)}, u32[]{:S(2)}, u32[]{:S(2)}) async-start(bf16[128,2,3200]{2,1,0:T(2,128)(2,1)} %get-tuple-element.17.after_ref), calls=%async_computation | async-start | bytes 3276800 | tf_op jit(solution)/shard_map/all_to_all | solution.py:301
  25.7 4.6 %collective-permute-start.1 = (bf16[320,2304]{1,0:T(8,128)(2,1)S(1)}, bf16[320,2304]{1,0:T(8,128)(2,1)S(1)}, u32[]{:S(2)}, u32[]{:S(2)}) collective-permute-start(bf16[320,2304]{1,0:T(8,128)(2,1)S(1)} %copy-done.14), channel_id=1, source_target_pairs={{0,96},{32,0},{64,32},{96,64},{1,97},{33,1},{65,33},{97,65},{2,98}... | collective-permute-start | bytes 4423688 | tf_op jit(solution)/shard_map/ppermute | solution.py:309
  30.4 1.9 collective-permute-start
  33.6 5.0 %collective-permute-start.4 = (bf16[160,1536]{1,0:T(8,128)(2,1)S(1)}, bf16[160,1536]{1,0:T(8,128)(2,1)S(1)}, u32[]{:S(2)}, u32[]{:S(2)}) collective-permute-start(bf16[160,1536]{1,0:T(8,128)(2,1)S(1)} %shard_map.96.pre_0), channel_id=1, source_target_pairs={{0,384},{128,0},{256,128},{384,256},{1,385},{129,1},{257,129},{385... | collective-permute-start | bytes 1474568 | tf_op jit(solution)/shard_map/ppermute | solution.py:309
  38.7 2.0 collective-permute-start.3
  40.7 2.7 %collective-permute-start.2 = (bf16[160,1536]{1,0:T(8,128)(2,1)S(1)}, bf16[160,1536]{1,0:T(8,128)(2,1)S(1)}, u32[]{:S(2)}, u32[]{:S(2)}) collective-permute-start(bf16[160,1536]{1,0:T(8,128)(2,1)S(1)} %shard_map.96.pre_0), channel_id=1, source_target_pairs={{0,128},{128,256},{256,384},{384,0},{1,129},{129,257},{257,385},{3... | collective-permute-start | bytes 1474568 | tf_op jit(solution)/shard_map/ppermute | solution.py:309
  43.4 8.9 %collective-permute-done.4.after_3.pre_3 = bf16[160,1536]{1,0:T(8,128)(2,1)S(1)} collective-permute-done((bf16[160,1536]{1,0:T(8,128)(2,1)S(1)}, bf16[160,1536]{1,0:T(8,128)(2,1)S(1)}, u32[]{:S(2)}, u32[]{:S(2)}) %collective-permute-start.4) | collective-permute-done | bytes 491552 | tf_op jit(solution)/shard_map/ppermute | solution.py:309
  52.3 4.9 %collective-permute-done.3.after_2.pre_2 = bf16[160,1536]{1,0:T(8,128)(2,1)S(1)} collective-permute-done((bf16[160,1536]{1,0:T(8,128)(2,1)S(1)}, bf16[160,1536]{1,0:T(8,128)(2,1)S(1)}, u32[]{:S(2)}, u32[]{:S(2)}) %collective-permute-start.3) | collective-permute-done | bytes 491552 | tf_op jit(solution)/shard_map/ppermute | solution.py:309
  57.2 15.3 %collective-permute-done.2.after_1.pre_1 = bf16[160,1536]{1,0:T(8,128)(2,1)S(1)} collective-permute-done((bf16[160,1536]{1,0:T(8,128)(2,1)S(1)}, bf16[160,1536]{1,0:T(8,128)(2,1)S(1)}, u32[]{:S(2)}, u32[]{:S(2)}) %collective-permute-start.2) | collective-permute-done | bytes 491552 | tf_op jit(solution)/shard_map/ppermute | solution.py:309
  72.6 2.0 shard_map.97
  75.4 1.9 collective-permute-start.5
  77.3 4.6 %collective-permute-start.6 = (bf16[160,2304]{1,0:T(8,128)(2,1)}, bf16[160,2304]{1,0:T(8,128)(2,1)S(1)}, u32[]{:S(2)}, u32[]{:S(2)}) collective-permute-start(bf16[160,2304]{1,0:T(8,128)(2,1)} %get-tuple-element.20), channel_id=1, source_target_pairs={{0,96},{32,0},{64,32},{96,64},{1,97},{33,1},{65,33},{97,65},{2,98}... | collective-permute-start | bytes 2211848 | tf_op jit(solution)/shard_map/ppermute | solution.py:309
  82.6 3.8 %shard_map.99 = (bf16[4,160,1536]{2,1,0:T(8,128)(2,1)}, bf16[4,160,768]{2,1,0:T(8,128)(2,1)}, f32[8,128]{1,0:T(8,128)}) custom-call(bf16[160,1536]{1,0:T(8,128)(2,1)} %copy-done.4, bf16[160,1536]{1,0:T(8,128)(2,1)} %copy-done.7, bf16[160,1536]{1,0:T(8,128)(2,1)} %copy-done.6, bf16[160,1536]{1,0:T(8,128)(2,1)} %copy-done.5), custom_call_target="tpu_custom_call" | custom-call | flops 33554432 | bytes 8388608 | tf_op jit(solution)/shard_map/pallas_call | solution.py:367
  86.4 4.4 %shard_map.98 = (bf16[1280,768]{1,0:T(8,128)(2,1)}, bf16[1280,1536]{1,0:T(8,128)(2,1)}) custom-call(s32[2]{0:T(128)} %pad_add_fusion.at_ref, bf16[320,2304]{1,0:T(8,128)(2,1)} %get-tuple-element.18.refs_0_, bf16[320,2304]{1,0:T(8,128)(2,1)} %copy-done.2, bf16[320,2304]{1,0:T(8,128)(2,1)} %copy-done.1), custom_call_target="tpu_custom_call" | custom-call | bytes 16777216 | tf_op jit(solution)/shard_map/pallas_call | solution.py:375
  90.9 5.6 %collective-permute-done.5.refs_0_ = bf16[160,2304]{1,0:T(8,128)(2,1)S(1)} collective-permute-done((bf16[160,2304]{1,0:T(8,128)(2,1)}, bf16[160,2304]{1,0:T(8,128)(2,1)S(1)}, u32[]{:S(2)}, u32[]{:S(2)}) %collective-permute-start.5) | collective-permute-done | bytes 737312 | tf_op jit(solution)/shard_map/ppermute | solution.py:309
  98.3 2.5 %shard_map.100 = (bf16[1280,768]{1,0:T(8,128)(2,1)}, bf16[1280,1536]{1,0:T(8,128)(2,1)}) custom-call(s32[2]{0:T(128)} %pad_add_fusion.at_ref, bf16[160,2304]{1,0:T(8,128)(2,1)} %copy-done.15, bf16[160,2304]{1,0:T(8,128)(2,1)} %copy-done.16, bf16[1280,768]{1,0:T(8,128)(2,1)} %get-tuple-element.21.refs_2_, ...), custom_call_target="tpu_custom_call", output_to_operand_aliasing={{0}: (3, {}), {1}: (4, {})} | custom-call | bytes 16777216 | tf_op jit(solution)/shard_map/pallas_call | solution.py:375
  100.8 4.2 %all-to-all-done.recv_any.recv_ref = bf16[128,2,3200]{2,1,0:T(2,128)(2,1)} async-done(((bf16[128,2,3200]{2,1,0:T(2,128)(2,1)}), bf16[128,2,3200]{2,1,0:T(2,128)(2,1)}, u32[]{:S(2)}, u32[]{:S(2)}) %all-to-all-start) | async-done | bytes 1638432 | tf_op jit(solution)/shard_map/all_to_all | solution.py:301
  105.0 5.2 %shard_map.101 = bf16[4,160,768]{2,1,0:T(8,128)(2,1)} custom-call(s32[2]{0:T(128)} %pad_add_fusion.at_ref, bf16[128,2,3200]{2,1,0:T(2,128)(2,1)} %all-to-all-done.recv_any.recv_ref, bf16[1280,768]{1,0:T(8,128)(2,1)} %get-tuple-element.24.down_any), custom_call_target="tpu_custom_call" | custom-call | flops 2147483648 | bytes 8388608 | tf_op jit(solution)/shard_map/pallas_call | solution.py:395
  110.2 17.3 %all_to_all.20.part_ref = bf16[4,160,768]{2,1,0:T(8,128)(2,1)S(1)} all-to-all(bf16[4,160,768]{2,1,0:T(8,128)(2,1)} %shard_map.101), channel_id=1, replica_groups=mesh['gx'=4,'gy'=4,'expert'=32] {'gx'}, dimensions={0} | all-to-all | bytes 1966080 | tf_op jit(solution)/shard_map/all_to_all | solution.py:305
  127.7 14.9 %all_to_all.21.hidden_ref = bf16[4,160,768]{2,1,0:T(8,128)(2,1)S(1)} all-to-all(bf16[4,160,768]{2,1,0:T(8,128)(2,1)S(1)} %shard_map.102), channel_id=1, replica_groups=mesh['gx'=4,'gy'=4,'expert'=32] {'gx'}, dimensions={0} | all-to-all | bytes 1966080 | tf_op jit(solution)/shard_map/all_to_all | solution.py:305
  142.6 5.3 %shard_map.103.after_ref = bf16[128,2,3200]{2,1,0:T(2,128)(2,1)} custom-call(s32[2]{0:T(128)S(1)} %copy-done.11, bf16[4,160,768]{2,1,0:T(8,128)(2,1)S(1)} %all_to_all.21.hidden_ref, bf16[4,160,1536]{2,1,0:T(8,128)(2,1)S(1)} %copy-done.12, bf16[1280,1536]{1,0:T(8,128)(2,1)S(1)} %copy-done.3), custom_call_target="tpu_custom_call" | custom-call | flops 4294967296 | bytes 8388608 | tf_op jit(solution)/shard_map/pallas_call | solution.py:414
  147.9 12.1 %all-to-all-start.3 = ((bf16[128,2,3200]{2,1,0:T(2,128)(2,1)}), bf16[128,2,3200]{2,1,0:T(2,128)(2,1)S(1)}, u32[]{:S(2)}, u32[]{:S(2)}) async-start(bf16[128,2,3200]{2,1,0:T(2,128)(2,1)} %shard_map.103.after_ref), calls=%async_computation.3 | async-start | bytes 3276800 | tf_op jit(solution)/shard_map/all_to_all | solution.py:301
  160.0 3.9 %shard_map.105 = (bf16[320,768]{1,0:T(8,128)(2,1)S(1)}, bf16[320,768]{1,0:T(8,128)(2,1)S(1)}, bf16[320,768]{1,0:T(8,128)(2,1)S(1)}, bf16[320,768]{1,0:T(8,128)(2,1)S(1)}) custom-call(s32[2]{0:T(128)S(1)} %copy-done.11, bf16[128,2,3200]{2,1,0:T(2,128)(2,1)} %all-to-all-done.recv_any.recv_ref, bf16[4,160,768]{2,1,0:T(8,128)(2,1)S(1)} %copy-done.13, ...), custom_call_target="tpu_custom_call" | custom-call | flops 2147483648 | bytes 4194304 | tf_op jit(solution)/shard_map/pallas_call | solution.py:428
  163.9 3.9 %collective-permute-start.7 = (bf16[320,768]{1,0:T(8,128)(2,1)S(1)}, bf16[320,768]{1,0:T(8,128)(2,1)S(1)}, u32[]{:S(2)}, u32[]{:S(2)}) collective-permute-start(bf16[320,768]{1,0:T(8,128)(2,1)S(1)} %get-tuple-element.29), channel_id=1, source_target_pairs={{0,32},{32,64},{64,96},{96,0},{1,33},{33,65},{65,97},{97,1},{2,34}... | collective-permute-start | bytes 1474568 | tf_op jit(solution)/shard_map/ppermute | solution.py:309
  167.8 4.6 %collective-permute-start.8 = (bf16[320,768]{1,0:T(8,128)(2,1)S(1)}, bf16[320,768]{1,0:T(8,128)(2,1)S(1)}, u32[]{:S(2)}, u32[]{:S(2)}) collective-permute-start(bf16[320,768]{1,0:T(8,128)(2,1)S(1)} %get-tuple-element.30), channel_id=1, source_target_pairs={{0,64},{32,96},{64,0},{96,32},{1,65},{33,97},{65,1},{97,33},{2,66}... | collective-permute-start | bytes 1474568 | tf_op jit(solution)/shard_map/ppermute | solution.py:309
  172.5 2.7 %collective-permute-start.9 = (bf16[320,768]{1,0:T(8,128)(2,1)S(1)}, bf16[320,768]{1,0:T(8,128)(2,1)S(1)}, u32[]{:S(2)}, u32[]{:S(2)}) collective-permute-start(bf16[320,768]{1,0:T(8,128)(2,1)S(1)} %get-tuple-element.31), channel_id=1, source_target_pairs={{0,96},{32,0},{64,32},{96,64},{1,97},{33,1},{65,33},{97,65},{2,98}... | collective-permute-start | bytes 1474568 | tf_op jit(solution)/shard_map/ppermute | solution.py:309
  175.1 4.9 %collective-permute-done.7.part_1 = bf16[320,768]{1,0:T(8,128)(2,1)S(1)} collective-permute-done((bf16[320,768]{1,0:T(8,128)(2,1)S(1)}, bf16[320,768]{1,0:T(8,128)(2,1)S(1)}, u32[]{:S(2)}, u32[]{:S(2)}) %collective-permute-start.7) | collective-permute-done | bytes 491552 | tf_op jit(solution)/shard_map/ppermute | solution.py:309
  180.0 11.4 %collective-permute-done.8.part_2 = bf16[320,768]{1,0:T(8,128)(2,1)S(1)} collective-permute-done((bf16[320,768]{1,0:T(8,128)(2,1)S(1)}, bf16[320,768]{1,0:T(8,128)(2,1)S(1)}, u32[]{:S(2)}, u32[]{:S(2)}) %collective-permute-start.8) | collective-permute-done | bytes 491552 | tf_op jit(solution)/shard_map/ppermute | solution.py:309
  191.4 1.6 collective-permute-done.9.part_3
  194.1 45.4 %all-to-all-done.3.ret_ref = bf16[128,2,3200]{2,1,0:T(2,128)(2,1)S(1)} async-done(((bf16[128,2,3200]{2,1,0:T(2,128)(2,1)}), bf16[128,2,3200]{2,1,0:T(2,128)(2,1)S(1)}, u32[]{:S(2)}, u32[]{:S(2)}) %all-to-all-start.3) | async-done | bytes 1638432 | tf_op jit(solution)/shard_map/all_to_all | solution.py:301
  239.5 2.1 shard_map.104
  (41 shorter events, 5.7 us)
Async XLA Ops:
  4.6 21.1 %copy-start.14 = (bf16[320,2304]{1,0:T(8,128)(2,1)S(1)}, bf16[320,2304]{1,0:T(8,128)(2,1)}, u32[]{:S(2)}) copy-start(bf16[320,2304]{1,0:T(8,128)(2,1)} %get-tuple-element.18.refs_0_) | copy-start | bytes 4423684
  4.6 27.7 %copy-start = (bf16[128,2,3200]{2,1,0:T(2,128)(2,1)S(1)}, bf16[128,2,3200]{2,1,0:T(2,128)(2,1)}, u32[]{:S(2)}) copy-start(bf16[128,2,3200]{2,1,0:T(2,128)(2,1)} %get-tuple-element.17.after_ref) | copy-start | bytes 4915204
  4.6 100.3 %all-to-all-start = ((bf16[128,2,3200]{2,1,0:T(2,128)(2,1)}), bf16[128,2,3200]{2,1,0:T(2,128)(2,1)}, u32[]{:S(2)}, u32[]{:S(2)}) async-start(bf16[128,2,3200]{2,1,0:T(2,128)(2,1)} %get-tuple-element.17.after_ref), calls=%async_computation | async-start | bytes 3276800 | tf_op jit(solution)/shard_map/all_to_all | solution.py:301
  25.7 46.8 %collective-permute-start.1 = (bf16[320,2304]{1,0:T(8,128)(2,1)S(1)}, bf16[320,2304]{1,0:T(8,128)(2,1)S(1)}, u32[]{:S(2)}, u32[]{:S(2)}) collective-permute-start(bf16[320,2304]{1,0:T(8,128)(2,1)S(1)} %copy-done.14), channel_id=1, source_target_pairs={{0,96},{32,0},{64,32},{96,64},{1,97},{33,1},{65,33},{97,65},{2,98}... | collective-permute-start | bytes 4423688 | tf_op jit(solution)/shard_map/ppermute | solution.py:309
  30.4 42.2 %collective-permute-start = (bf16[320,2304]{1,0:T(8,128)(2,1)S(1)}, bf16[320,2304]{1,0:T(8,128)(2,1)S(1)}, u32[]{:S(2)}, u32[]{:S(2)}) collective-permute-start(bf16[320,2304]{1,0:T(8,128)(2,1)S(1)} %copy-done.14), channel_id=1, source_target_pairs={{0,32},{32,64},{64,96},{96,0},{1,33},{33,65},{65,97},{97,1},{2,34}... | collective-permute-start | bytes 4423688 | tf_op jit(solution)/shard_map/ppermute | solution.py:309
  32.3 1.0 copy-start.8
  33.6 41.0 %copy-start.4 = (bf16[160,1536]{1,0:T(8,128)(2,1)}, bf16[160,1536]{1,0:T(8,128)(2,1)S(1)}, u32[]{:S(2)}) copy-start(bf16[160,1536]{1,0:T(8,128)(2,1)S(1)} %shard_map.96.pre_0) | copy-start | bytes 1474564
  33.6 18.7 %collective-permute-start.4 = (bf16[160,1536]{1,0:T(8,128)(2,1)S(1)}, bf16[160,1536]{1,0:T(8,128)(2,1)S(1)}, u32[]{:S(2)}, u32[]{:S(2)}) collective-permute-start(bf16[160,1536]{1,0:T(8,128)(2,1)S(1)} %shard_map.96.pre_0), channel_id=1, source_target_pairs={{0,384},{128,0},{256,128},{384,256},{1,385},{129,1},{257,129},{385... | collective-permute-start | bytes 1474568 | tf_op jit(solution)/shard_map/ppermute | solution.py:309
  38.7 18.5 %collective-permute-start.3 = (bf16[160,1536]{1,0:T(8,128)(2,1)S(1)}, bf16[160,1536]{1,0:T(8,128)(2,1)S(1)}, u32[]{:S(2)}, u32[]{:S(2)}) collective-permute-start(bf16[160,1536]{1,0:T(8,128)(2,1)S(1)} %shard_map.96.pre_0), channel_id=1, source_target_pairs={{0,256},{128,384},{256,0},{384,128},{1,257},{129,385},{257,1},{385... | collective-permute-start | bytes 1474568 | tf_op jit(solution)/shard_map/ppermute | solution.py:309
  40.7 31.8 %collective-permute-start.2 = (bf16[160,1536]{1,0:T(8,128)(2,1)S(1)}, bf16[160,1536]{1,0:T(8,128)(2,1)S(1)}, u32[]{:S(2)}, u32[]{:S(2)}) collective-permute-start(bf16[160,1536]{1,0:T(8,128)(2,1)S(1)} %shard_map.96.pre_0), channel_id=1, source_target_pairs={{0,128},{128,256},{256,384},{384,0},{1,129},{129,257},{257,385},{3... | collective-permute-start | bytes 1474568 | tf_op jit(solution)/shard_map/ppermute | solution.py:309
  52.3 22.3 %copy-start.5 = (bf16[160,1536]{1,0:T(8,128)(2,1)}, bf16[160,1536]{1,0:T(8,128)(2,1)S(1)}, u32[]{:S(2)}) copy-start(bf16[160,1536]{1,0:T(8,128)(2,1)S(1)} %collective-permute-done.4.after_3.pre_3) | copy-start | bytes 1474564
  57.2 17.4 %copy-start.6 = (bf16[160,1536]{1,0:T(8,128)(2,1)}, bf16[160,1536]{1,0:T(8,128)(2,1)S(1)}, u32[]{:S(2)}) copy-start(bf16[160,1536]{1,0:T(8,128)(2,1)S(1)} %collective-permute-done.3.after_2.pre_2) | copy-start | bytes 1474564
  72.6 2.1 copy-start.1
  72.6 2.1 copy-start.2
  74.6 0.8 copy-start.7
  75.4 21.1 %collective-permute-start.5 = (bf16[160,2304]{1,0:T(8,128)(2,1)}, bf16[160,2304]{1,0:T(8,128)(2,1)S(1)}, u32[]{:S(2)}, u32[]{:S(2)}) collective-permute-start(bf16[160,2304]{1,0:T(8,128)(2,1)} %get-tuple-element.19), channel_id=1, source_target_pairs={{0,32},{32,64},{64,96},{96,0},{1,33},{33,65},{65,97},{97,1},{2,34}... | collective-permute-start | bytes 2211848 | tf_op jit(solution)/shard_map/ppermute | solution.py:309
  77.3 20.0 %collective-permute-start.6 = (bf16[160,2304]{1,0:T(8,128)(2,1)}, bf16[160,2304]{1,0:T(8,128)(2,1)S(1)}, u32[]{:S(2)}, u32[]{:S(2)}) collective-permute-start(bf16[160,2304]{1,0:T(8,128)(2,1)} %get-tuple-element.20), channel_id=1, source_target_pairs={{0,96},{32,0},{64,32},{96,64},{1,97},{33,1},{65,33},{97,65},{2,98}... | collective-permute-start | bytes 2211848 | tf_op jit(solution)/shard_map/ppermute | solution.py:309
  96.5 0.9 copy-start.15
  97.4 0.9 copy-start.16
  110.2 32.4 %copy-start.12 = (bf16[4,160,1536]{2,1,0:T(8,128)(2,1)S(1)}, bf16[4,160,1536]{2,1,0:T(8,128)(2,1)}, u32[]{:S(2)}) copy-start(bf16[4,160,1536]{2,1,0:T(8,128)(2,1)} %get-tuple-element.25.factor_ref) | copy-start | bytes 5898244
  127.5 15.0 %copy-start.3 = (bf16[1280,1536]{1,0:T(8,128)(2,1)S(1)}, bf16[1280,1536]{1,0:T(8,128)(2,1)}, u32[]{:S(2)}) copy-start(bf16[1280,1536]{1,0:T(8,128)(2,1)} %get-tuple-element.26.in_ref) | copy-start | bytes 11796484
  127.5 15.0 %copy-start.11 = (s32[2]{0:T(128)S(1)}, s32[2]{0:T(128)}, u32[]{:S(2)}) copy-start(s32[2]{0:T(128)} %pad_add_fusion.at_ref) | copy-start | bytes 28
  147.9 12.1 %copy-start.13 = (bf16[4,160,768]{2,1,0:T(8,128)(2,1)S(1)}, bf16[4,160,768]{2,1,0:T(8,128)(2,1)}, u32[]{:S(2)}) copy-start(bf16[4,160,768]{2,1,0:T(8,128)(2,1)} %get-tuple-element.27.act_ref) | copy-start | bytes 2949124
  147.9 91.6 %all-to-all-start.3 = ((bf16[128,2,3200]{2,1,0:T(2,128)(2,1)}), bf16[128,2,3200]{2,1,0:T(2,128)(2,1)S(1)}, u32[]{:S(2)}, u32[]{:S(2)}) async-start(bf16[128,2,3200]{2,1,0:T(2,128)(2,1)} %shard_map.103.after_ref), calls=%async_computation.3 | async-start | bytes 3276800 | tf_op jit(solution)/shard_map/all_to_all | solution.py:301
  163.9 75.6 %copy-start.9 = (s32[128,6]{0,1:T(8,128)S(1)}, s32[128,6]{0,1:T(8,128)}, u32[]{:S(2)}) copy-start(s32[128,6]{0,1:T(8,128)} %param.9) | copy-start | bytes 9220
  163.9 75.6 %copy-start.10 = (s32[128,6]{0,1:T(8,128)S(1)}, s32[128,6]{0,1:T(8,128)}, u32[]{:S(2)}) copy-start(s32[128,6]{0,1:T(8,128)} %param.10) | copy-start | bytes 9220
  163.9 16.2 %collective-permute-start.7 = (bf16[320,768]{1,0:T(8,128)(2,1)S(1)}, bf16[320,768]{1,0:T(8,128)(2,1)S(1)}, u32[]{:S(2)}, u32[]{:S(2)}) collective-permute-start(bf16[320,768]{1,0:T(8,128)(2,1)S(1)} %get-tuple-element.29), channel_id=1, source_target_pairs={{0,32},{32,64},{64,96},{96,0},{1,33},{33,65},{65,97},{97,1},{2,34}... | collective-permute-start | bytes 1474568 | tf_op jit(solution)/shard_map/ppermute | solution.py:309
  167.8 23.6 %collective-permute-start.8 = (bf16[320,768]{1,0:T(8,128)(2,1)S(1)}, bf16[320,768]{1,0:T(8,128)(2,1)S(1)}, u32[]{:S(2)}, u32[]{:S(2)}) collective-permute-start(bf16[320,768]{1,0:T(8,128)(2,1)S(1)} %get-tuple-element.30), channel_id=1, source_target_pairs={{0,64},{32,96},{64,0},{96,32},{1,65},{33,97},{65,1},{97,33},{2,66}... | collective-permute-start | bytes 1474568 | tf_op jit(solution)/shard_map/ppermute | solution.py:309
  172.5 20.6 %collective-permute-start.9 = (bf16[320,768]{1,0:T(8,128)(2,1)S(1)}, bf16[320,768]{1,0:T(8,128)(2,1)S(1)}, u32[]{:S(2)}, u32[]{:S(2)}) collective-permute-start(bf16[320,768]{1,0:T(8,128)(2,1)S(1)} %get-tuple-element.31), channel_id=1, source_target_pairs={{0,96},{32,0},{64,32},{96,64},{1,97},{33,1},{65,33},{97,65},{2,98}... | collective-permute-start | bytes 1474568 | tf_op jit(solution)/shard_map/ppermute | solution.py:309

commit v9 on v8

--- a/solution.py
+++ b/solution.py
@@ -234,11 +234,9 @@
         copy.wait()
 
 
-def spread_kernel(part_ref, out_ref):
+def sum_kernel(part_ref, out_ref):
     total = part_ref[0].astype(F32) + part_ref[1].astype(F32)
-    total = (total + (part_ref[2].astype(F32) + part_ref[3].astype(F32))).astype(BF)
-    for g in range(GX):
-        out_ref[g] = total
+    out_ref[...] = (total + (part_ref[2].astype(F32) + part_ref[3].astype(F32))).astype(BF)
 
 
 def back_kernel(at_ref, hidden_ref, factor_ref, in_ref, msg_any, msg_ref, sems):
@@ -282,8 +280,9 @@
         out_ref[...] = full_ref[pl.ds(pl.multiple_of(q * PART, 64), PART), :]
 
 
-def gather_kernel(ret_ref, ids_ref, slots_ref, out_ref):
+def gather_kernel(ret_ref, ids_ref, slots_ref, out_any, out_ref, sems):
     pick, _ = select(ids_ref, slots_ref, None)
+    copies = []
     for g in range(GX):
         rows = jnp.concatenate(
             [
@@ -293,8 +292,14 @@
             axis=0,
         )
         halves = tn(pick, rows).astype(BF)
-        out_ref[:, g * WIDE : g * WIDE + HALF] = halves[:TOK]
-        out_ref[:, g * WIDE + HALF : (g + 1) * WIDE] = halves[TOK:]
+        out_ref[g, :, :HALF] = halves[:TOK]
+        out_ref[g, :, HALF:] = halves[TOK:]
+        copies.append(
+            pltpu.make_async_copy(out_ref.at[g], out_any.at[:, pl.ds(g * WIDE, WIDE)], sems.at[g])
+        )
+        copies[-1].start()
+    for copy in copies:
+        copy.wait()
 
 
 def swap(value):
@@ -410,7 +415,8 @@
             pltpu.SemaphoreType.DMA((GX,)),
         ],
     )(at, recv, down_w)
-    hidden = swap_gx(call(spread_kernel, arr(GX, ROWS, HID), 0, 1 << 21)(swap_gx(part)))
+    total = call(sum_kernel, arr(ROWS, HID), 0, 1 << 21)(swap_gx(part))
+    hidden = lax.all_gather(total, "gx", axis=0)
     back = call(
         back_kernel,
         message,
@@ -436,7 +442,15 @@
     grad_down = call(total_kernel, arr(PART, HID), 0, 1 << 21)(
         downs[0], *[step(downs[r], "gy", r) for r in range(1, GY)]
     )
-    input_grad = call(gather_kernel, arr(TOK, GX * WIDE), 1 << 30, 1 << 22)(ret, ids, slots)
+    input_grad = call(
+        gather_kernel,
+        arr(TOK, GX * WIDE),
+        1 << 30,
+        1 << 22,
+        in_specs=[vmem] * 3,
+        out_specs=anywhere,
+        scratch_shapes=[pltpu.VMEM((GX, TOK, WIDE), BF), pltpu.SemaphoreType.DMA((GX,))],
+    )(ret, ids, slots)
     return (input_grad, grad_down.T[None])
 
 

time: 243 us -> 242 us (level)
    all_to_all x2 -> x1, blocking collectives: 32.2 us -> 17.5 us  [swap_gx(): return lax.all_to_all(value, 'gx', 0, 0, tiled=True)]
    all_gather x0 -> x1, blocking collectives: none -> 12.9 us  [per_device(): hidden = lax.all_gather(total, 'gx', axis=0)]
where the time goes in v9:
time: 242 us; the launch traced here: 241 us
  waiting for transfers between devices  103 us (43%)
  starting transfers between devices  68.5 us (28%)
  Pallas kernels  34.6 us (14%)
  blocking collectives  30.4 us (13%)
  local copies, waits for them, and re-layouts  2.75 us (1%)
    ppermute x10, waiting for transfers between devices, step(): return lax.ppermute(value, axis, [(i, (i + r) % 4) for i in range(4)])  53.5 us
    all_to_all x2, waiting for transfers between devices, swap(): return lax.all_to_all(value, ('gx', 'expert'), 0, 0, tiled=True)  49.7 us
    all_to_all x2, starting transfers between devices, swap(): return lax.all_to_all(value, ('gx', 'expert'), 0, 0, tiled=True)  34.4 us
    ppermute x10, starting transfers between devices, step(): return lax.ppermute(value, axis, [(i, (i + r) % 4) for i in range(4)])  34 us
    all_to_all x1, blocking collectives, swap_gx(): return lax.all_to_all(value, 'gx', 0, 0, tiled=True)  17.5 us
    all_gather x1, blocking collectives, per_device(): hidden = lax.all_gather(total, 'gx', axis=0)  12.9 us
    pallas_call x2, Pallas kernels, arrange(): call(functools.partial(arrange_kernel, places), (arr(WIDE, HID), arr(WIDE...  6.93 us
    pallas_call x1, Pallas kernels, per_device(): call(hidden_kernel, arr(GX, ROWS, HID), 1 << 31, 1 << 23, VMEM_MOST, in_s...  5.34 us
  transfers between devices with their start and end apart: 12, of which 10 were waited for; matrix products, arithmetic and copies ran while one was open for 0% of the time, Pallas kernels for 7%

profile of v9, /device:TPU:1, one launch (start us, length us, event | category | flops | bytes accessed | tf_op | source)
XLA Modules:
  0.0 241.2 jit_solution(12959925351859826313)
XLA Ops:
  0.6 4.0 %shard_map.95 = (bf16[128,2,3200]{2,1,0:T(2,128)(2,1)}, bf16[320,2304]{1,0:T(8,128)(2,1)}) custom-call(bf16[128,5120]{1,0:T(8,128)(2,1)} %og_any.1, s32[6,128]{1,0:T(8,128)} %bitcast.17, s32[6,128]{1,0:T(8,128)} %bitcast.19, f32[6,128]{1,0:T(8,128)} %bitcast.25, bf16[320,768]{1,0:T(8,128)(2,1)} %bitcast.22, bf16[320,768]{1,0:T(8,128)(2,1)} %bitcast.23, ...), custom_call_target="tpu_custom_call" | custom-call | flops 536870912 | bytes 8388608 | tf_op jit(solution)/shard_map/pallas_call | solution.py:329
  4.6 21.1 %all-to-all-start = ((bf16[128,2,3200]{2,1,0:T(2,128)(2,1)}), bf16[128,2,3200]{2,1,0:T(2,128)(2,1)}, u32[]{:S(2)}, u32[]{:S(2)}) async-start(bf16[128,2,3200]{2,1,0:T(2,128)(2,1)} %get-tuple-element.17.after_ref), calls=%async_computation | async-start | bytes 3276800 | tf_op jit(solution)/shard_map/all_to_all | solution.py:306
  25.7 4.6 %collective-permute-start.1 = (bf16[320,2304]{1,0:T(8,128)(2,1)S(1)}, bf16[320,2304]{1,0:T(8,128)(2,1)S(1)}, u32[]{:S(2)}, u32[]{:S(2)}) collective-permute-start(bf16[320,2304]{1,0:T(8,128)(2,1)S(1)} %copy-done.14), channel_id=1, source_target_pairs={{0,96},{32,0},{64,32},{96,64},{1,97},{33,1},{65,33},{97,65},{2,98}... | collective-permute-start | bytes 4423688 | tf_op jit(solution)/shard_map/ppermute | solution.py:314
  30.4 1.9 collective-permute-start
  33.6 5.0 %collective-permute-start.4 = (bf16[160,1536]{1,0:T(8,128)(2,1)S(1)}, bf16[160,1536]{1,0:T(8,128)(2,1)S(1)}, u32[]{:S(2)}, u32[]{:S(2)}) collective-permute-start(bf16[160,1536]{1,0:T(8,128)(2,1)S(1)} %shard_map.96.pre_0), channel_id=1, source_target_pairs={{0,384},{128,0},{256,128},{384,256},{1,385},{129,1},{257,129},{385... | collective-permute-start | bytes 1474568 | tf_op jit(solution)/shard_map/ppermute | solution.py:314
  38.7 2.0 collective-permute-start.3
  40.7 2.7 %collective-permute-start.2 = (bf16[160,1536]{1,0:T(8,128)(2,1)S(1)}, bf16[160,1536]{1,0:T(8,128)(2,1)S(1)}, u32[]{:S(2)}, u32[]{:S(2)}) collective-permute-start(bf16[160,1536]{1,0:T(8,128)(2,1)S(1)} %shard_map.96.pre_0), channel_id=1, source_target_pairs={{0,128},{128,256},{256,384},{384,0},{1,129},{129,257},{257,385},{3... | collective-permute-start | bytes 1474568 | tf_op jit(solution)/shard_map/ppermute | solution.py:314
  43.4 8.9 %collective-permute-done.4.after_3.pre_3 = bf16[160,1536]{1,0:T(8,128)(2,1)S(1)} collective-permute-done((bf16[160,1536]{1,0:T(8,128)(2,1)S(1)}, bf16[160,1536]{1,0:T(8,128)(2,1)S(1)}, u32[]{:S(2)}, u32[]{:S(2)}) %collective-permute-start.4) | collective-permute-done | bytes 491552 | tf_op jit(solution)/shard_map/ppermute | solution.py:314
  52.3 4.9 %collective-permute-done.3.after_2.pre_2 = bf16[160,1536]{1,0:T(8,128)(2,1)S(1)} collective-permute-done((bf16[160,1536]{1,0:T(8,128)(2,1)S(1)}, bf16[160,1536]{1,0:T(8,128)(2,1)S(1)}, u32[]{:S(2)}, u32[]{:S(2)}) %collective-permute-start.3) | collective-permute-done | bytes 491552 | tf_op jit(solution)/shard_map/ppermute | solution.py:314
  57.2 15.3 %collective-permute-done.2.after_1.pre_1 = bf16[160,1536]{1,0:T(8,128)(2,1)S(1)} collective-permute-done((bf16[160,1536]{1,0:T(8,128)(2,1)S(1)}, bf16[160,1536]{1,0:T(8,128)(2,1)S(1)}, u32[]{:S(2)}, u32[]{:S(2)}) %collective-permute-start.2) | collective-permute-done | bytes 491552 | tf_op jit(solution)/shard_map/ppermute | solution.py:314
  72.6 2.0 shard_map.97
  75.4 1.9 collective-permute-start.5
  77.3 4.6 %collective-permute-start.6 = (bf16[160,2304]{1,0:T(8,128)(2,1)}, bf16[160,2304]{1,0:T(8,128)(2,1)S(1)}, u32[]{:S(2)}, u32[]{:S(2)}) collective-permute-start(bf16[160,2304]{1,0:T(8,128)(2,1)} %get-tuple-element.20), channel_id=1, source_target_pairs={{0,96},{32,0},{64,32},{96,64},{1,97},{33,1},{65,33},{97,65},{2,98}... | collective-permute-start | bytes 2211848 | tf_op jit(solution)/shard_map/ppermute | solution.py:314
  82.6 3.8 %shard_map.99 = (bf16[4,160,1536]{2,1,0:T(8,128)(2,1)}, bf16[4,160,768]{2,1,0:T(8,128)(2,1)}, f32[8,128]{1,0:T(8,128)}) custom-call(bf16[160,1536]{1,0:T(8,128)(2,1)} %copy-done.4, bf16[160,1536]{1,0:T(8,128)(2,1)} %copy-done.7, bf16[160,1536]{1,0:T(8,128)(2,1)} %copy-done.6, bf16[160,1536]{1,0:T(8,128)(2,1)} %copy-done.5), custom_call_target="tpu_custom_call" | custom-call | flops 33554432 | bytes 8388608 | tf_op jit(solution)/shard_map/pallas_call | solution.py:372
  86.4 4.4 %shard_map.98 = (bf16[1280,768]{1,0:T(8,128)(2,1)}, bf16[1280,1536]{1,0:T(8,128)(2,1)}) custom-call(s32[2]{0:T(128)} %pad_add_fusion.at_ref, bf16[320,2304]{1,0:T(8,128)(2,1)} %get-tuple-element.18.refs_0_, bf16[320,2304]{1,0:T(8,128)(2,1)} %copy-done.2, bf16[320,2304]{1,0:T(8,128)(2,1)} %copy-done.1), custom_call_target="tpu_custom_call" | custom-call | bytes 16777216 | tf_op jit(solution)/shard_map/pallas_call | solution.py:380
  90.9 5.6 %collective-permute-done.5.refs_0_ = bf16[160,2304]{1,0:T(8,128)(2,1)S(1)} collective-permute-done((bf16[160,2304]{1,0:T(8,128)(2,1)}, bf16[160,2304]{1,0:T(8,128)(2,1)S(1)}, u32[]{:S(2)}, u32[]{:S(2)}) %collective-permute-start.5) | collective-permute-done | bytes 737312 | tf_op jit(solution)/shard_map/ppermute | solution.py:314
  98.3 2.5 %shard_map.100 = (bf16[1280,768]{1,0:T(8,128)(2,1)}, bf16[1280,1536]{1,0:T(8,128)(2,1)}) custom-call(s32[2]{0:T(128)} %pad_add_fusion.at_ref, bf16[160,2304]{1,0:T(8,128)(2,1)} %copy-done.15, bf16[160,2304]{1,0:T(8,128)(2,1)} %copy-done.16, bf16[1280,768]{1,0:T(8,128)(2,1)} %get-tuple-element.21.refs_2_, ...), custom_call_target="tpu_custom_call", output_to_operand_aliasing={{0}: (3, {}), {1}: (4, {})} | custom-call | bytes 16777216 | tf_op jit(solution)/shard_map/pallas_call | solution.py:380
  100.8 4.2 %all-to-all-done.recv_any.recv_ref = bf16[128,2,3200]{2,1,0:T(2,128)(2,1)} async-done(((bf16[128,2,3200]{2,1,0:T(2,128)(2,1)}), bf16[128,2,3200]{2,1,0:T(2,128)(2,1)}, u32[]{:S(2)}, u32[]{:S(2)}) %all-to-all-start) | async-done | bytes 1638432 | tf_op jit(solution)/shard_map/all_to_all | solution.py:306
  105.0 5.3 %shard_map.101 = bf16[4,160,768]{2,1,0:T(8,128)(2,1)} custom-call(s32[2]{0:T(128)} %pad_add_fusion.at_ref, bf16[128,2,3200]{2,1,0:T(2,128)(2,1)} %all-to-all-done.recv_any.recv_ref, bf16[1280,768]{1,0:T(8,128)(2,1)} %get-tuple-element.24.down_any), custom_call_target="tpu_custom_call" | custom-call | flops 2147483648 | bytes 8388608 | tf_op jit(solution)/shard_map/pallas_call | solution.py:400
  110.3 17.5 %all_to_all.15.part_ref = bf16[4,160,768]{2,1,0:T(8,128)(2,1)S(1)} all-to-all(bf16[4,160,768]{2,1,0:T(8,128)(2,1)} %shard_map.101), channel_id=1, replica_groups=mesh['gx'=4,'gy'=4,'expert'=32] {'gx'}, dimensions={0} | all-to-all | bytes 1966080 | tf_op jit(solution)/shard_map/all_to_all | solution.py:310
  127.9 12.9 %all-gather = bf16[640,768]{1,0:T(8,128)(2,1)S(1)} all-gather(bf16[160,768]{1,0:T(8,128)(2,1)S(1)} %shard_map.102), channel_id=2, replica_groups=mesh['gx'=4,'gy'=4,'expert'=32] {'gx'}, dimensions={0}, use_global_device_ids=true | all-gather | bytes 1228800 | tf_op jit(solution)/shard_map/all_gather | solution.py:419
  140.9 5.3 %shard_map.103.after_ref = bf16[128,2,3200]{2,1,0:T(2,128)(2,1)} custom-call(s32[2]{0:T(128)S(1)} %copy-done.11, bf16[4,160,768]{2,1,0:T(8,128)(2,1)S(1)} %bitcast.15, bf16[4,160,1536]{2,1,0:T(8,128)(2,1)S(1)} %copy-done.12, bf16[1280,1536]{1,0:T(8,128)(2,1)S(1)} %copy-done.3), custom_call_target="tpu_custom_call" | custom-call | flops 4294967296 | bytes 8388608 | tf_op jit(solution)/shard_map/pallas_call | solution.py:420
  146.2 13.4 %all-to-all-start.2 = ((bf16[128,2,3200]{2,1,0:T(2,128)(2,1)}), bf16[128,2,3200]{2,1,0:T(2,128)(2,1)S(1)}, u32[]{:S(2)}, u32[]{:S(2)}) async-start(bf16[128,2,3200]{2,1,0:T(2,128)(2,1)} %shard_map.103.after_ref), calls=%async_computation.2 | async-start | bytes 3276800 | tf_op jit(solution)/shard_map/all_to_all | solution.py:306
  159.6 3.9 %shard_map.105 = (bf16[320,768]{1,0:T(8,128)(2,1)S(1)}, bf16[320,768]{1,0:T(8,128)(2,1)S(1)}, bf16[320,768]{1,0:T(8,128)(2,1)S(1)}, bf16[320,768]{1,0:T(8,128)(2,1)S(1)}) custom-call(s32[2]{0:T(128)S(1)} %copy-done.11, bf16[128,2,3200]{2,1,0:T(2,128)(2,1)} %all-to-all-done.recv_any.recv_ref, bf16[4,160,768]{2,1,0:T(8,128)(2,1)S(1)} %copy-done.13, ...), custom_call_target="tpu_custom_call" | custom-call | flops 2147483648 | bytes 4194304 | tf_op jit(solution)/shard_map/pallas_call | solution.py:434
  163.5 3.8 %collective-permute-start.7 = (bf16[320,768]{1,0:T(8,128)(2,1)S(1)}, bf16[320,768]{1,0:T(8,128)(2,1)S(1)}, u32[]{:S(2)}, u32[]{:S(2)}) collective-permute-start(bf16[320,768]{1,0:T(8,128)(2,1)S(1)} %get-tuple-element.29), channel_id=1, source_target_pairs={{0,32},{32,64},{64,96},{96,0},{1,33},{33,65},{65,97},{97,1},{2,34}... | collective-permute-start | bytes 1474568 | tf_op jit(solution)/shard_map/ppermute | solution.py:314
  167.4 4.6 %collective-permute-start.8 = (bf16[320,768]{1,0:T(8,128)(2,1)S(1)}, bf16[320,768]{1,0:T(8,128)(2,1)S(1)}, u32[]{:S(2)}, u32[]{:S(2)}) collective-permute-start(bf16[320,768]{1,0:T(8,128)(2,1)S(1)} %get-tuple-element.30), channel_id=1, source_target_pairs={{0,64},{32,96},{64,0},{96,32},{1,65},{33,97},{65,1},{97,33},{2,66}... | collective-permute-start | bytes 1474568 | tf_op jit(solution)/shard_map/ppermute | solution.py:314
  172.0 2.7 %collective-permute-start.9 = (bf16[320,768]{1,0:T(8,128)(2,1)S(1)}, bf16[320,768]{1,0:T(8,128)(2,1)S(1)}, u32[]{:S(2)}, u32[]{:S(2)}) collective-permute-start(bf16[320,768]{1,0:T(8,128)(2,1)S(1)} %get-tuple-element.31), channel_id=1, source_target_pairs={{0,96},{32,0},{64,32},{96,64},{1,97},{33,1},{65,33},{97,65},{2,98}... | collective-permute-start | bytes 1474568 | tf_op jit(solution)/shard_map/ppermute | solution.py:314
  174.8 4.9 %collective-permute-done.7.part_1 = bf16[320,768]{1,0:T(8,128)(2,1)S(1)} collective-permute-done((bf16[320,768]{1,0:T(8,128)(2,1)S(1)}, bf16[320,768]{1,0:T(8,128)(2,1)S(1)}, u32[]{:S(2)}, u32[]{:S(2)}) %collective-permute-start.7) | collective-permute-done | bytes 491552 | tf_op jit(solution)/shard_map/ppermute | solution.py:314
  179.6 11.4 %collective-permute-done.8.part_2 = bf16[320,768]{1,0:T(8,128)(2,1)S(1)} collective-permute-done((bf16[320,768]{1,0:T(8,128)(2,1)S(1)}, bf16[320,768]{1,0:T(8,128)(2,1)S(1)}, u32[]{:S(2)}, u32[]{:S(2)}) %collective-permute-start.8) | collective-permute-done | bytes 491552 | tf_op jit(solution)/shard_map/ppermute | solution.py:314
  191.0 1.6 collective-permute-done.9.part_3
  193.6 45.5 %all-to-all-done.2.ret_ref = bf16[128,2,3200]{2,1,0:T(2,128)(2,1)S(1)} async-done(((bf16[128,2,3200]{2,1,0:T(2,128)(2,1)}), bf16[128,2,3200]{2,1,0:T(2,128)(2,1)S(1)}, u32[]{:S(2)}, u32[]{:S(2)}) %all-to-all-start.2) | async-done | bytes 1638432 | tf_op jit(solution)/shard_map/all_to_all | solution.py:306
  239.2 1.8 shard_map.104
  (41 shorter events, 5.7 us)
Async XLA Ops:
  4.6 21.1 %copy-start.14 = (bf16[320,2304]{1,0:T(8,128)(2,1)S(1)}, bf16[320,2304]{1,0:T(8,128)(2,1)}, u32[]{:S(2)}) copy-start(bf16[320,2304]{1,0:T(8,128)(2,1)} %get-tuple-element.18.refs_0_) | copy-start | bytes 4423684
  4.6 27.7 %copy-start = (bf16[128,2,3200]{2,1,0:T(2,128)(2,1)S(1)}, bf16[128,2,3200]{2,1,0:T(2,128)(2,1)}, u32[]{:S(2)}) copy-start(bf16[128,2,3200]{2,1,0:T(2,128)(2,1)} %get-tuple-element.17.after_ref) | copy-start | bytes 4915204
  4.6 100.3 %all-to-all-start = ((bf16[128,2,3200]{2,1,0:T(2,128)(2,1)}), bf16[128,2,3200]{2,1,0:T(2,128)(2,1)}, u32[]{:S(2)}, u32[]{:S(2)}) async-start(bf16[128,2,3200]{2,1,0:T(2,128)(2,1)} %get-tuple-element.17.after_ref), calls=%async_computation | async-start | bytes 3276800 | tf_op jit(solution)/shard_map/all_to_all | solution.py:306
  25.7 46.8 %collective-permute-start.1 = (bf16[320,2304]{1,0:T(8,128)(2,1)S(1)}, bf16[320,2304]{1,0:T(8,128)(2,1)S(1)}, u32[]{:S(2)}, u32[]{:S(2)}) collective-permute-start(bf16[320,2304]{1,0:T(8,128)(2,1)S(1)} %copy-done.14), channel_id=1, source_target_pairs={{0,96},{32,0},{64,32},{96,64},{1,97},{33,1},{65,33},{97,65},{2,98}... | collective-permute-start | bytes 4423688 | tf_op jit(solution)/shard_map/ppermute | solution.py:314
  30.4 42.2 %collective-permute-start = (bf16[320,2304]{1,0:T(8,128)(2,1)S(1)}, bf16[320,2304]{1,0:T(8,128)(2,1)S(1)}, u32[]{:S(2)}, u32[]{:S(2)}) collective-permute-start(bf16[320,2304]{1,0:T(8,128)(2,1)S(1)} %copy-done.14), channel_id=1, source_target_pairs={{0,32},{32,64},{64,96},{96,0},{1,33},{33,65},{65,97},{97,1},{2,34}... | collective-permute-start | bytes 4423688 | tf_op jit(solution)/shard_map/ppermute | solution.py:314
  32.3 1.0 copy-start.8
  33.6 41.0 %copy-start.4 = (bf16[160,1536]{1,0:T(8,128)(2,1)}, bf16[160,1536]{1,0:T(8,128)(2,1)S(1)}, u32[]{:S(2)}) copy-start(bf16[160,1536]{1,0:T(8,128)(2,1)S(1)} %shard_map.96.pre_0) | copy-start | bytes 1474564
  33.6 18.7 %collective-permute-start.4 = (bf16[160,1536]{1,0:T(8,128)(2,1)S(1)}, bf16[160,1536]{1,0:T(8,128)(2,1)S(1)}, u32[]{:S(2)}, u32[]{:S(2)}) collective-permute-start(bf16[160,1536]{1,0:T(8,128)(2,1)S(1)} %shard_map.96.pre_0), channel_id=1, source_target_pairs={{0,384},{128,0},{256,128},{384,256},{1,385},{129,1},{257,129},{385... | collective-permute-start | bytes 1474568 | tf_op jit(solution)/shard_map/ppermute | solution.py:314
  38.7 18.5 %collective-permute-start.3 = (bf16[160,1536]{1,0:T(8,128)(2,1)S(1)}, bf16[160,1536]{1,0:T(8,128)(2,1)S(1)}, u32[]{:S(2)}, u32[]{:S(2)}) collective-permute-start(bf16[160,1536]{1,0:T(8,128)(2,1)S(1)} %shard_map.96.pre_0), channel_id=1, source_target_pairs={{0,256},{128,384},{256,0},{384,128},{1,257},{129,385},{257,1},{385... | collective-permute-start | bytes 1474568 | tf_op jit(solution)/shard_map/ppermute | solution.py:314
  40.7 31.8 %collective-permute-start.2 = (bf16[160,1536]{1,0:T(8,128)(2,1)S(1)}, bf16[160,1536]{1,0:T(8,128)(2,1)S(1)}, u32[]{:S(2)}, u32[]{:S(2)}) collective-permute-start(bf16[160,1536]{1,0:T(8,128)(2,1)S(1)} %shard_map.96.pre_0), channel_id=1, source_target_pairs={{0,128},{128,256},{256,384},{384,0},{1,129},{129,257},{257,385},{3... | collective-permute-start | bytes 1474568 | tf_op jit(solution)/shard_map/ppermute | solution.py:314
  52.3 22.3 %copy-start.5 = (bf16[160,1536]{1,0:T(8,128)(2,1)}, bf16[160,1536]{1,0:T(8,128)(2,1)S(1)}, u32[]{:S(2)}) copy-start(bf16[160,1536]{1,0:T(8,128)(2,1)S(1)} %collective-permute-done.4.after_3.pre_3) | copy-start | bytes 1474564
  57.2 17.4 %copy-start.6 = (bf16[160,1536]{1,0:T(8,128)(2,1)}, bf16[160,1536]{1,0:T(8,128)(2,1)S(1)}, u32[]{:S(2)}) copy-start(bf16[160,1536]{1,0:T(8,128)(2,1)S(1)} %collective-permute-done.3.after_2.pre_2) | copy-start | bytes 1474564
  72.6 2.1 copy-start.1
  72.6 2.1 copy-start.2
  74.6 0.8 copy-start.7
  75.4 21.1 %collective-permute-start.5 = (bf16[160,2304]{1,0:T(8,128)(2,1)}, bf16[160,2304]{1,0:T(8,128)(2,1)S(1)}, u32[]{:S(2)}, u32[]{:S(2)}) collective-permute-start(bf16[160,2304]{1,0:T(8,128)(2,1)} %get-tuple-element.19), channel_id=1, source_target_pairs={{0,32},{32,64},{64,96},{96,0},{1,33},{33,65},{65,97},{97,1},{2,34}... | collective-permute-start | bytes 2211848 | tf_op jit(solution)/shard_map/ppermute | solution.py:314
  77.3 20.0 %collective-permute-start.6 = (bf16[160,2304]{1,0:T(8,128)(2,1)}, bf16[160,2304]{1,0:T(8,128)(2,1)S(1)}, u32[]{:S(2)}, u32[]{:S(2)}) collective-permute-start(bf16[160,2304]{1,0:T(8,128)(2,1)} %get-tuple-element.20), channel_id=1, source_target_pairs={{0,96},{32,0},{64,32},{96,64},{1,97},{33,1},{65,33},{97,65},{2,98}... | collective-permute-start | bytes 2211848 | tf_op jit(solution)/shard_map/ppermute | solution.py:314
  96.5 0.9 copy-start.15
  97.4 0.9 copy-start.16
  105.0 35.9 %copy-start.12 = (bf16[4,160,1536]{2,1,0:T(8,128)(2,1)S(1)}, bf16[4,160,1536]{2,1,0:T(8,128)(2,1)}, u32[]{:S(2)}) copy-start(bf16[4,160,1536]{2,1,0:T(8,128)(2,1)} %get-tuple-element.25.factor_ref) | copy-start | bytes 5898244
  110.3 30.6 %copy-start.3 = (bf16[1280,1536]{1,0:T(8,128)(2,1)S(1)}, bf16[1280,1536]{1,0:T(8,128)(2,1)}, u32[]{:S(2)}) copy-start(bf16[1280,1536]{1,0:T(8,128)(2,1)} %get-tuple-element.26.in_ref) | copy-start | bytes 11796484
  127.8 13.1 %copy-start.11 = (s32[2]{0:T(128)S(1)}, s32[2]{0:T(128)}, u32[]{:S(2)}) copy-start(s32[2]{0:T(128)} %pad_add_fusion.at_ref) | copy-start | bytes 28
  146.2 13.4 %copy-start.13 = (bf16[4,160,768]{2,1,0:T(8,128)(2,1)S(1)}, bf16[4,160,768]{2,1,0:T(8,128)(2,1)}, u32[]{:S(2)}) copy-start(bf16[4,160,768]{2,1,0:T(8,128)(2,1)} %get-tuple-element.27.act_ref) | copy-start | bytes 2949124
  146.2 92.9 %all-to-all-start.2 = ((bf16[128,2,3200]{2,1,0:T(2,128)(2,1)}), bf16[128,2,3200]{2,1,0:T(2,128)(2,1)S(1)}, u32[]{:S(2)}, u32[]{:S(2)}) async-start(bf16[128,2,3200]{2,1,0:T(2,128)(2,1)} %shard_map.103.after_ref), calls=%async_computation.2 | async-start | bytes 3276800 | tf_op jit(solution)/shard_map/all_to_all | solution.py:306
  163.5 75.6 %copy-start.9 = (s32[128,6]{0,1:T(8,128)S(1)}, s32[128,6]{0,1:T(8,128)}, u32[]{:S(2)}) copy-start(s32[128,6]{0,1:T(8,128)} %param.9) | copy-start | bytes 9220
  163.5 75.6 %copy-start.10 = (s32[128,6]{0,1:T(8,128)S(1)}, s32[128,6]{0,1:T(8,128)}, u32[]{:S(2)}) copy-start(s32[128,6]{0,1:T(8,128)} %param.10) | copy-start | bytes 9220
  163.5 16.1 %collective-permute-start.7 = (bf16[320,768]{1,0:T(8,128)(2,1)S(1)}, bf16[320,768]{1,0:T(8,128)(2,1)S(1)}, u32[]{:S(2)}, u32[]{:S(2)}) collective-permute-start(bf16[320,768]{1,0:T(8,128)(2,1)S(1)} %get-tuple-element.29), channel_id=1, source_target_pairs={{0,32},{32,64},{64,96},{96,0},{1,33},{33,65},{65,97},{97,1},{2,34}... | collective-permute-start | bytes 1474568 | tf_op jit(solution)/shard_map/ppermute | solution.py:314
  167.4 23.6 %collective-permute-start.8 = (bf16[320,768]{1,0:T(8,128)(2,1)S(1)}, bf16[320,768]{1,0:T(8,128)(2,1)S(1)}, u32[]{:S(2)}, u32[]{:S(2)}) collective-permute-start(bf16[320,768]{1,0:T(8,128)(2,1)S(1)} %get-tuple-element.30), channel_id=1, source_target_pairs={{0,64},{32,96},{64,0},{96,32},{1,65},{33,97},{65,1},{97,33},{2,66}... | collective-permute-start | bytes 1474568 | tf_op jit(solution)/shard_map/ppermute | solution.py:314
  172.0 20.6 %collective-permute-start.9 = (bf16[320,768]{1,0:T(8,128)(2,1)S(1)}, bf16[320,768]{1,0:T(8,128)(2,1)S(1)}, u32[]{:S(2)}, u32[]{:S(2)}) collective-permute-start(bf16[320,768]{1,0:T(8,128)(2,1)S(1)} %get-tuple-element.31), channel_id=1, source_target_pairs={{0,96},{32,0},{64,32},{96,64},{1,97},{33,1},{65,33},{97,65},{2,98}... | collective-permute-start | bytes 1474568 | tf_op jit(solution)/shard_map/ppermute | solution.py:314

commit v10 on v9

--- a/solution.py
+++ b/solution.py
@@ -207,20 +207,18 @@
 
 def hidden_kernel(
     at_ref, recv_any, down_any, part_any,
-    recv_ref, down_ref, sent_ref, part_ref, in_sems, down_sem, out_sems,
+    recv_ref, down_ref, sent_ref, part_ref, in_sem, down_sem, out_sems,
 ):
-    fetches = []
+    recv = pltpu.make_async_copy(recv_any, recv_ref, in_sem)
+    down = pltpu.make_async_copy(down_any, down_ref, down_sem)
+    recv.start()
+    down.start()
+    split = split_halves()
+    recv.wait()
     for r in range(GX):
         span = pl.ds(lax.rem(at_ref[0] + (GX - r), GX) * N_EXP, N_EXP)
-        fetches.append(pltpu.make_async_copy(recv_any.at[span], recv_ref.at[r], in_sems.at[r]))
-    fetches.append(pltpu.make_async_copy(down_any, down_ref, down_sem))
-    for copy in fetches:
-        copy.start()
-    split = split_halves()
-    for r in range(GX):
-        fetches[r].wait()
-        put_rows(split, lambda cols: recv_ref[r, :, :, cols], sent_ref, r)
-    fetches[GX].wait()
+        put_rows(split, lambda cols: recv_ref[span, :, cols], sent_ref, r)
+    down.wait()
     copies = []
     for pair in range(2):
         sent = jnp.concatenate([sent_ref[2 * pair], sent_ref[2 * pair + 1]], axis=0)
@@ -406,11 +404,11 @@
         in_specs=[smem, anywhere, anywhere],
         out_specs=anywhere,
         scratch_shapes=[
-            pltpu.VMEM((GX, N_EXP, 2, CAP * HALF), BF),
+            pltpu.VMEM(message.shape, BF),
             pltpu.VMEM((WIDE, HID), BF),
             pltpu.VMEM((GX, ROWS, WIDE), BF),
             pltpu.VMEM((GX, ROWS, HID), BF),
-            pltpu.SemaphoreType.DMA((GX,)),
+            pltpu.SemaphoreType.DMA,
             pltpu.SemaphoreType.DMA,
             pltpu.SemaphoreType.DMA((GX,)),
         ],

time: 242 us -> 242 us (level)
  no operation moved by 1% of the time
where the time goes in v10:
time: 242 us; the launch traced here: 241 us
  waiting for transfers between devices  103 us (43%)
  starting transfers between devices  68.3 us (28%)
  Pallas kernels  34.3 us (14%)
  blocking collectives  30.4 us (13%)
  local copies, waits for them, and re-layouts  2.75 us (1%)
    ppermute x10, waiting for transfers between devices, step(): return lax.ppermute(value, axis, [(i, (i + r) % 4) for i in range(4)])  53.5 us
    all_to_all x2, waiting for transfers between devices, swap(): return lax.all_to_all(value, ('gx', 'expert'), 0, 0, tiled=True)  49.7 us
    all_to_all x2, starting transfers between devices, swap(): return lax.all_to_all(value, ('gx', 'expert'), 0, 0, tiled=True)  34.3 us
    ppermute x10, starting transfers between devices, step(): return lax.ppermute(value, axis, [(i, (i + r) % 4) for i in range(4)])  34 us
    all_to_all x1, blocking collectives, swap_gx(): return lax.all_to_all(value, 'gx', 0, 0, tiled=True)  17.5 us
    all_gather x1, blocking collectives, per_device(): hidden = lax.all_gather(total, 'gx', axis=0)  12.9 us
    pallas_call x2, Pallas kernels, arrange(): call(functools.partial(arrange_kernel, places), (arr(WIDE, HID), arr(WIDE...  6.93 us
    pallas_call x1, Pallas kernels, per_device(): call(back_kernel, message, 1 << 32, 1 << 23, in_specs=[smem] + [vmem] * 3...  5.31 us
  transfers between devices with their start and end apart: 12, of which 10 were waited for; matrix products, arithmetic and copies ran while one was open for 0% of the time, Pallas kernels for 7%

profile of v10, /device:TPU:1, one launch (start us, length us, event | category | flops | bytes accessed | tf_op | source)
XLA Modules:
  0.0 240.8 jit_solution(7823924166175040051)
XLA Ops:
  0.6 4.0 %shard_map.95 = (bf16[128,2,3200]{2,1,0:T(2,128)(2,1)}, bf16[320,2304]{1,0:T(8,128)(2,1)}) custom-call(bf16[128,5120]{1,0:T(8,128)(2,1)} %og_any.1, s32[6,128]{1,0:T(8,128)} %bitcast.17, s32[6,128]{1,0:T(8,128)} %bitcast.19, f32[6,128]{1,0:T(8,128)} %bitcast.25, bf16[320,768]{1,0:T(8,128)(2,1)} %bitcast.22, bf16[320,768]{1,0:T(8,128)(2,1)} %bitcast.23, ...), custom_call_target="tpu_custom_call" | custom-call | flops 536870912 | bytes 8388608 | tf_op jit(solution)/shard_map/pallas_call | solution.py:327
  4.6 21.1 %all-to-all-start = ((bf16[128,2,3200]{2,1,0:T(2,128)(2,1)}), bf16[128,2,3200]{2,1,0:T(2,128)(2,1)}, u32[]{:S(2)}, u32[]{:S(2)}) async-start(bf16[128,2,3200]{2,1,0:T(2,128)(2,1)} %get-tuple-element.17.after_ref), calls=%async_computation | async-start | bytes 3276800 | tf_op jit(solution)/shard_map/all_to_all | solution.py:304
  25.7 4.6 %collective-permute-start.1 = (bf16[320,2304]{1,0:T(8,128)(2,1)S(1)}, bf16[320,2304]{1,0:T(8,128)(2,1)S(1)}, u32[]{:S(2)}, u32[]{:S(2)}) collective-permute-start(bf16[320,2304]{1,0:T(8,128)(2,1)S(1)} %copy-done.14), channel_id=1, source_target_pairs={{0,96},{32,0},{64,32},{96,64},{1,97},{33,1},{65,33},{97,65},{2,98}... | collective-permute-start | bytes 4423688 | tf_op jit(solution)/shard_map/ppermute | solution.py:312
  30.4 1.9 collective-permute-start
  33.6 5.0 %collective-permute-start.4 = (bf16[160,1536]{1,0:T(8,128)(2,1)S(1)}, bf16[160,1536]{1,0:T(8,128)(2,1)S(1)}, u32[]{:S(2)}, u32[]{:S(2)}) collective-permute-start(bf16[160,1536]{1,0:T(8,128)(2,1)S(1)} %shard_map.96.pre_0), channel_id=1, source_target_pairs={{0,384},{128,0},{256,128},{384,256},{1,385},{129,1},{257,129},{385... | collective-permute-start | bytes 1474568 | tf_op jit(solution)/shard_map/ppermute | solution.py:312
  38.7 2.0 collective-permute-start.3
  40.7 2.7 %collective-permute-start.2 = (bf16[160,1536]{1,0:T(8,128)(2,1)S(1)}, bf16[160,1536]{1,0:T(8,128)(2,1)S(1)}, u32[]{:S(2)}, u32[]{:S(2)}) collective-permute-start(bf16[160,1536]{1,0:T(8,128)(2,1)S(1)} %shard_map.96.pre_0), channel_id=1, source_target_pairs={{0,128},{128,256},{256,384},{384,0},{1,129},{129,257},{257,385},{3... | collective-permute-start | bytes 1474568 | tf_op jit(solution)/shard_map/ppermute | solution.py:312
  43.4 8.9 %collective-permute-done.4.after_3.pre_3 = bf16[160,1536]{1,0:T(8,128)(2,1)S(1)} collective-permute-done((bf16[160,1536]{1,0:T(8,128)(2,1)S(1)}, bf16[160,1536]{1,0:T(8,128)(2,1)S(1)}, u32[]{:S(2)}, u32[]{:S(2)}) %collective-permute-start.4) | collective-permute-done | bytes 491552 | tf_op jit(solution)/shard_map/ppermute | solution.py:312
  52.3 4.9 %collective-permute-done.3.after_2.pre_2 = bf16[160,1536]{1,0:T(8,128)(2,1)S(1)} collective-permute-done((bf16[160,1536]{1,0:T(8,128)(2,1)S(1)}, bf16[160,1536]{1,0:T(8,128)(2,1)S(1)}, u32[]{:S(2)}, u32[]{:S(2)}) %collective-permute-start.3) | collective-permute-done | bytes 491552 | tf_op jit(solution)/shard_map/ppermute | solution.py:312
  57.2 15.3 %collective-permute-done.2.after_1.pre_1 = bf16[160,1536]{1,0:T(8,128)(2,1)S(1)} collective-permute-done((bf16[160,1536]{1,0:T(8,128)(2,1)S(1)}, bf16[160,1536]{1,0:T(8,128)(2,1)S(1)}, u32[]{:S(2)}, u32[]{:S(2)}) %collective-permute-start.2) | collective-permute-done | bytes 491552 | tf_op jit(solution)/shard_map/ppermute | solution.py:312
  72.6 2.0 shard_map.97
  75.4 1.9 collective-permute-start.5
  77.3 4.6 %collective-permute-start.6 = (bf16[160,2304]{1,0:T(8,128)(2,1)}, bf16[160,2304]{1,0:T(8,128)(2,1)S(1)}, u32[]{:S(2)}, u32[]{:S(2)}) collective-permute-start(bf16[160,2304]{1,0:T(8,128)(2,1)} %get-tuple-element.20), channel_id=1, source_target_pairs={{0,96},{32,0},{64,32},{96,64},{1,97},{33,1},{65,33},{97,65},{2,98}... | collective-permute-start | bytes 2211848 | tf_op jit(solution)/shard_map/ppermute | solution.py:312
  82.6 3.8 %shard_map.99 = (bf16[4,160,1536]{2,1,0:T(8,128)(2,1)}, bf16[4,160,768]{2,1,0:T(8,128)(2,1)}, f32[8,128]{1,0:T(8,128)}) custom-call(bf16[160,1536]{1,0:T(8,128)(2,1)} %copy-done.4, bf16[160,1536]{1,0:T(8,128)(2,1)} %copy-done.7, bf16[160,1536]{1,0:T(8,128)(2,1)} %copy-done.6, bf16[160,1536]{1,0:T(8,128)(2,1)} %copy-done.5), custom_call_target="tpu_custom_call" | custom-call | flops 33554432 | bytes 8388608 | tf_op jit(solution)/shard_map/pallas_call | solution.py:370
  86.4 4.4 %shard_map.98 = (bf16[1280,768]{1,0:T(8,128)(2,1)}, bf16[1280,1536]{1,0:T(8,128)(2,1)}) custom-call(s32[2]{0:T(128)} %pad_add_fusion.at_ref, bf16[320,2304]{1,0:T(8,128)(2,1)} %get-tuple-element.18.refs_0_, bf16[320,2304]{1,0:T(8,128)(2,1)} %copy-done.2, bf16[320,2304]{1,0:T(8,128)(2,1)} %copy-done.1), custom_call_target="tpu_custom_call" | custom-call | bytes 16777216 | tf_op jit(solution)/shard_map/pallas_call | solution.py:378
  90.9 5.6 %collective-permute-done.5.refs_0_ = bf16[160,2304]{1,0:T(8,128)(2,1)S(1)} collective-permute-done((bf16[160,2304]{1,0:T(8,128)(2,1)}, bf16[160,2304]{1,0:T(8,128)(2,1)S(1)}, u32[]{:S(2)}, u32[]{:S(2)}) %collective-permute-start.5) | collective-permute-done | bytes 737312 | tf_op jit(solution)/shard_map/ppermute | solution.py:312
  98.3 2.5 %shard_map.100 = (bf16[1280,768]{1,0:T(8,128)(2,1)}, bf16[1280,1536]{1,0:T(8,128)(2,1)}) custom-call(s32[2]{0:T(128)} %pad_add_fusion.at_ref, bf16[160,2304]{1,0:T(8,128)(2,1)} %copy-done.15, bf16[160,2304]{1,0:T(8,128)(2,1)} %copy-done.16, bf16[1280,768]{1,0:T(8,128)(2,1)} %get-tuple-element.21.refs_2_, ...), custom_call_target="tpu_custom_call", output_to_operand_aliasing={{0}: (3, {}), {1}: (4, {})} | custom-call | bytes 16777216 | tf_op jit(solution)/shard_map/pallas_call | solution.py:378
  100.8 4.2 %all-to-all-done.recv_any.recv_ref = bf16[128,2,3200]{2,1,0:T(2,128)(2,1)} async-done(((bf16[128,2,3200]{2,1,0:T(2,128)(2,1)}), bf16[128,2,3200]{2,1,0:T(2,128)(2,1)}, u32[]{:S(2)}, u32[]{:S(2)}) %all-to-all-start) | async-done | bytes 1638432 | tf_op jit(solution)/shard_map/all_to_all | solution.py:304
  105.0 5.1 %shard_map.101 = bf16[4,160,768]{2,1,0:T(8,128)(2,1)} custom-call(s32[2]{0:T(128)} %pad_add_fusion.at_ref, bf16[128,2,3200]{2,1,0:T(2,128)(2,1)} %all-to-all-done.recv_any.recv_ref, bf16[1280,768]{1,0:T(8,128)(2,1)} %get-tuple-element.24.down_any), custom_call_target="tpu_custom_call" | custom-call | flops 2147483648 | bytes 8388608 | tf_op jit(solution)/shard_map/pallas_call | solution.py:398
  110.1 17.5 %all_to_all.15.part_ref = bf16[4,160,768]{2,1,0:T(8,128)(2,1)S(1)} all-to-all(bf16[4,160,768]{2,1,0:T(8,128)(2,1)} %shard_map.101), channel_id=1, replica_groups=mesh['gx'=4,'gy'=4,'expert'=32] {'gx'}, dimensions={0} | all-to-all | bytes 1966080 | tf_op jit(solution)/shard_map/all_to_all | solution.py:308
  127.7 12.9 %all-gather = bf16[640,768]{1,0:T(8,128)(2,1)S(1)} all-gather(bf16[160,768]{1,0:T(8,128)(2,1)S(1)} %shard_map.102), channel_id=2, replica_groups=mesh['gx'=4,'gy'=4,'expert'=32] {'gx'}, dimensions={0}, use_global_device_ids=true | all-gather | bytes 1228800 | tf_op jit(solution)/shard_map/all_gather | solution.py:417
  140.7 5.3 %shard_map.103.after_ref = bf16[128,2,3200]{2,1,0:T(2,128)(2,1)} custom-call(s32[2]{0:T(128)S(1)} %copy-done.11, bf16[4,160,768]{2,1,0:T(8,128)(2,1)S(1)} %bitcast.15, bf16[4,160,1536]{2,1,0:T(8,128)(2,1)S(1)} %copy-done.12, bf16[1280,1536]{1,0:T(8,128)(2,1)S(1)} %copy-done.3), custom_call_target="tpu_custom_call" | custom-call | flops 4294967296 | bytes 8388608 | tf_op jit(solution)/shard_map/pallas_call | solution.py:418
  146.0 13.2 %all-to-all-start.2 = ((bf16[128,2,3200]{2,1,0:T(2,128)(2,1)}), bf16[128,2,3200]{2,1,0:T(2,128)(2,1)S(1)}, u32[]{:S(2)}, u32[]{:S(2)}) async-start(bf16[128,2,3200]{2,1,0:T(2,128)(2,1)} %shard_map.103.after_ref), calls=%async_computation.2 | async-start | bytes 3276800 | tf_op jit(solution)/shard_map/all_to_all | solution.py:304
  159.2 3.9 %shard_map.105 = (bf16[320,768]{1,0:T(8,128)(2,1)S(1)}, bf16[320,768]{1,0:T(8,128)(2,1)S(1)}, bf16[320,768]{1,0:T(8,128)(2,1)S(1)}, bf16[320,768]{1,0:T(8,128)(2,1)S(1)}) custom-call(s32[2]{0:T(128)S(1)} %copy-done.11, bf16[128,2,3200]{2,1,0:T(2,128)(2,1)} %all-to-all-done.recv_any.recv_ref, bf16[4,160,768]{2,1,0:T(8,128)(2,1)S(1)} %copy-done.13, ...), custom_call_target="tpu_custom_call" | custom-call | flops 2147483648 | bytes 4194304 | tf_op jit(solution)/shard_map/pallas_call | solution.py:432
  163.1 3.8 %collective-permute-start.7 = (bf16[320,768]{1,0:T(8,128)(2,1)S(1)}, bf16[320,768]{1,0:T(8,128)(2,1)S(1)}, u32[]{:S(2)}, u32[]{:S(2)}) collective-permute-start(bf16[320,768]{1,0:T(8,128)(2,1)S(1)} %get-tuple-element.29), channel_id=1, source_target_pairs={{0,32},{32,64},{64,96},{96,0},{1,33},{33,65},{65,97},{97,1},{2,34}... | collective-permute-start | bytes 1474568 | tf_op jit(solution)/shard_map/ppermute | solution.py:312
  167.0 4.6 %collective-permute-start.8 = (bf16[320,768]{1,0:T(8,128)(2,1)S(1)}, bf16[320,768]{1,0:T(8,128)(2,1)S(1)}, u32[]{:S(2)}, u32[]{:S(2)}) collective-permute-start(bf16[320,768]{1,0:T(8,128)(2,1)S(1)} %get-tuple-element.30), channel_id=1, source_target_pairs={{0,64},{32,96},{64,0},{96,32},{1,65},{33,97},{65,1},{97,33},{2,66}... | collective-permute-start | bytes 1474568 | tf_op jit(solution)/shard_map/ppermute | solution.py:312
  171.6 2.7 %collective-permute-start.9 = (bf16[320,768]{1,0:T(8,128)(2,1)S(1)}, bf16[320,768]{1,0:T(8,128)(2,1)S(1)}, u32[]{:S(2)}, u32[]{:S(2)}) collective-permute-start(bf16[320,768]{1,0:T(8,128)(2,1)S(1)} %get-tuple-element.31), channel_id=1, source_target_pairs={{0,96},{32,0},{64,32},{96,64},{1,97},{33,1},{65,33},{97,65},{2,98}... | collective-permute-start | bytes 1474568 | tf_op jit(solution)/shard_map/ppermute | solution.py:312
  174.4 4.9 %collective-permute-done.7.part_1 = bf16[320,768]{1,0:T(8,128)(2,1)S(1)} collective-permute-done((bf16[320,768]{1,0:T(8,128)(2,1)S(1)}, bf16[320,768]{1,0:T(8,128)(2,1)S(1)}, u32[]{:S(2)}, u32[]{:S(2)}) %collective-permute-start.7) | collective-permute-done | bytes 491552 | tf_op jit(solution)/shard_map/ppermute | solution.py:312
  179.2 11.4 %collective-permute-done.8.part_2 = bf16[320,768]{1,0:T(8,128)(2,1)S(1)} collective-permute-done((bf16[320,768]{1,0:T(8,128)(2,1)S(1)}, bf16[320,768]{1,0:T(8,128)(2,1)S(1)}, u32[]{:S(2)}, u32[]{:S(2)}) %collective-permute-start.8) | collective-permute-done | bytes 491552 | tf_op jit(solution)/shard_map/ppermute | solution.py:312
  190.6 1.6 collective-permute-done.9.part_3
  193.2 45.5 %all-to-all-done.2.ret_ref = bf16[128,2,3200]{2,1,0:T(2,128)(2,1)S(1)} async-done(((bf16[128,2,3200]{2,1,0:T(2,128)(2,1)}), bf16[128,2,3200]{2,1,0:T(2,128)(2,1)S(1)}, u32[]{:S(2)}, u32[]{:S(2)}) %all-to-all-start.2) | async-done | bytes 1638432 | tf_op jit(solution)/shard_map/all_to_all | solution.py:304
  238.8 1.8 shard_map.104
  (41 shorter events, 5.7 us)
Async XLA Ops:
  4.6 21.1 %copy-start.14 = (bf16[320,2304]{1,0:T(8,128)(2,1)S(1)}, bf16[320,2304]{1,0:T(8,128)(2,1)}, u32[]{:S(2)}) copy-start(bf16[320,2304]{1,0:T(8,128)(2,1)} %get-tuple-element.18.refs_0_) | copy-start | bytes 4423684
  4.6 27.7 %copy-start = (bf16[128,2,3200]{2,1,0:T(2,128)(2,1)S(1)}, bf16[128,2,3200]{2,1,0:T(2,128)(2,1)}, u32[]{:S(2)}) copy-start(bf16[128,2,3200]{2,1,0:T(2,128)(2,1)} %get-tuple-element.17.after_ref) | copy-start | bytes 4915204
  4.6 100.3 %all-to-all-start = ((bf16[128,2,3200]{2,1,0:T(2,128)(2,1)}), bf16[128,2,3200]{2,1,0:T(2,128)(2,1)}, u32[]{:S(2)}, u32[]{:S(2)}) async-start(bf16[128,2,3200]{2,1,0:T(2,128)(2,1)} %get-tuple-element.17.after_ref), calls=%async_computation | async-start | bytes 3276800 | tf_op jit(solution)/shard_map/all_to_all | solution.py:304
  25.7 46.8 %collective-permute-start.1 = (bf16[320,2304]{1,0:T(8,128)(2,1)S(1)}, bf16[320,2304]{1,0:T(8,128)(2,1)S(1)}, u32[]{:S(2)}, u32[]{:S(2)}) collective-permute-start(bf16[320,2304]{1,0:T(8,128)(2,1)S(1)} %copy-done.14), channel_id=1, source_target_pairs={{0,96},{32,0},{64,32},{96,64},{1,97},{33,1},{65,33},{97,65},{2,98}... | collective-permute-start | bytes 4423688 | tf_op jit(solution)/shard_map/ppermute | solution.py:312
  30.4 42.2 %collective-permute-start = (bf16[320,2304]{1,0:T(8,128)(2,1)S(1)}, bf16[320,2304]{1,0:T(8,128)(2,1)S(1)}, u32[]{:S(2)}, u32[]{:S(2)}) collective-permute-start(bf16[320,2304]{1,0:T(8,128)(2,1)S(1)} %copy-done.14), channel_id=1, source_target_pairs={{0,32},{32,64},{64,96},{96,0},{1,33},{33,65},{65,97},{97,1},{2,34}... | collective-permute-start | bytes 4423688 | tf_op jit(solution)/shard_map/ppermute | solution.py:312
  32.3 1.0 copy-start.8
  33.6 41.0 %copy-start.4 = (bf16[160,1536]{1,0:T(8,128)(2,1)}, bf16[160,1536]{1,0:T(8,128)(2,1)S(1)}, u32[]{:S(2)}) copy-start(bf16[160,1536]{1,0:T(8,128)(2,1)S(1)} %shard_map.96.pre_0) | copy-start | bytes 1474564
  33.6 18.7 %collective-permute-start.4 = (bf16[160,1536]{1,0:T(8,128)(2,1)S(1)}, bf16[160,1536]{1,0:T(8,128)(2,1)S(1)}, u32[]{:S(2)}, u32[]{:S(2)}) collective-permute-start(bf16[160,1536]{1,0:T(8,128)(2,1)S(1)} %shard_map.96.pre_0), channel_id=1, source_target_pairs={{0,384},{128,0},{256,128},{384,256},{1,385},{129,1},{257,129},{385... | collective-permute-start | bytes 1474568 | tf_op jit(solution)/shard_map/ppermute | solution.py:312
  38.7 18.5 %collective-permute-start.3 = (bf16[160,1536]{1,0:T(8,128)(2,1)S(1)}, bf16[160,1536]{1,0:T(8,128)(2,1)S(1)}, u32[]{:S(2)}, u32[]{:S(2)}) collective-permute-start(bf16[160,1536]{1,0:T(8,128)(2,1)S(1)} %shard_map.96.pre_0), channel_id=1, source_target_pairs={{0,256},{128,384},{256,0},{384,128},{1,257},{129,385},{257,1},{385... | collective-permute-start | bytes 1474568 | tf_op jit(solution)/shard_map/ppermute | solution.py:312
  40.7 31.8 %collective-permute-start.2 = (bf16[160,1536]{1,0:T(8,128)(2,1)S(1)}, bf16[160,1536]{1,0:T(8,128)(2,1)S(1)}, u32[]{:S(2)}, u32[]{:S(2)}) collective-permute-start(bf16[160,1536]{1,0:T(8,128)(2,1)S(1)} %shard_map.96.pre_0), channel_id=1, source_target_pairs={{0,128},{128,256},{256,384},{384,0},{1,129},{129,257},{257,385},{3... | collective-permute-start | bytes 1474568 | tf_op jit(solution)/shard_map/ppermute | solution.py:312
  52.3 22.3 %copy-start.5 = (bf16[160,1536]{1,0:T(8,128)(2,1)}, bf16[160,1536]{1,0:T(8,128)(2,1)S(1)}, u32[]{:S(2)}) copy-start(bf16[160,1536]{1,0:T(8,128)(2,1)S(1)} %collective-permute-done.4.after_3.pre_3) | copy-start | bytes 1474564
  57.2 17.4 %copy-start.6 = (bf16[160,1536]{1,0:T(8,128)(2,1)}, bf16[160,1536]{1,0:T(8,128)(2,1)S(1)}, u32[]{:S(2)}) copy-start(bf16[160,1536]{1,0:T(8,128)(2,1)S(1)} %collective-permute-done.3.after_2.pre_2) | copy-start | bytes 1474564
  72.6 2.1 copy-start.1
  72.6 2.1 copy-start.2
  74.6 0.8 copy-start.7
  75.4 21.1 %collective-permute-start.5 = (bf16[160,2304]{1,0:T(8,128)(2,1)}, bf16[160,2304]{1,0:T(8,128)(2,1)S(1)}, u32[]{:S(2)}, u32[]{:S(2)}) collective-permute-start(bf16[160,2304]{1,0:T(8,128)(2,1)} %get-tuple-element.19), channel_id=1, source_target_pairs={{0,32},{32,64},{64,96},{96,0},{1,33},{33,65},{65,97},{97,1},{2,34}... | collective-permute-start | bytes 2211848 | tf_op jit(solution)/shard_map/ppermute | solution.py:312
  77.3 20.0 %collective-permute-start.6 = (bf16[160,2304]{1,0:T(8,128)(2,1)}, bf16[160,2304]{1,0:T(8,128)(2,1)S(1)}, u32[]{:S(2)}, u32[]{:S(2)}) collective-permute-start(bf16[160,2304]{1,0:T(8,128)(2,1)} %get-tuple-element.20), channel_id=1, source_target_pairs={{0,96},{32,0},{64,32},{96,64},{1,97},{33,1},{65,33},{97,65},{2,98}... | collective-permute-start | bytes 2211848 | tf_op jit(solution)/shard_map/ppermute | solution.py:312
  96.5 0.9 copy-start.15
  97.4 0.9 copy-start.16
  105.0 35.7 %copy-start.12 = (bf16[4,160,1536]{2,1,0:T(8,128)(2,1)S(1)}, bf16[4,160,1536]{2,1,0:T(8,128)(2,1)}, u32[]{:S(2)}) copy-start(bf16[4,160,1536]{2,1,0:T(8,128)(2,1)} %get-tuple-element.25.factor_ref) | copy-start | bytes 5898244
  110.1 30.6 %copy-start.3 = (bf16[1280,1536]{1,0:T(8,128)(2,1)S(1)}, bf16[1280,1536]{1,0:T(8,128)(2,1)}, u32[]{:S(2)}) copy-start(bf16[1280,1536]{1,0:T(8,128)(2,1)} %get-tuple-element.26.in_ref) | copy-start | bytes 11796484
  127.6 13.1 %copy-start.11 = (s32[2]{0:T(128)S(1)}, s32[2]{0:T(128)}, u32[]{:S(2)}) copy-start(s32[2]{0:T(128)} %pad_add_fusion.at_ref) | copy-start | bytes 28
  146.0 13.2 %copy-start.13 = (bf16[4,160,768]{2,1,0:T(8,128)(2,1)S(1)}, bf16[4,160,768]{2,1,0:T(8,128)(2,1)}, u32[]{:S(2)}) copy-start(bf16[4,160,768]{2,1,0:T(8,128)(2,1)} %get-tuple-element.27.act_ref) | copy-start | bytes 2949124
  146.0 92.7 %all-to-all-start.2 = ((bf16[128,2,3200]{2,1,0:T(2,128)(2,1)}), bf16[128,2,3200]{2,1,0:T(2,128)(2,1)S(1)}, u32[]{:S(2)}, u32[]{:S(2)}) async-start(bf16[128,2,3200]{2,1,0:T(2,128)(2,1)} %shard_map.103.after_ref), calls=%async_computation.2 | async-start | bytes 3276800 | tf_op jit(solution)/shard_map/all_to_all | solution.py:304
  163.1 75.6 %copy-start.9 = (s32[128,6]{0,1:T(8,128)S(1)}, s32[128,6]{0,1:T(8,128)}, u32[]{:S(2)}) copy-start(s32[128,6]{0,1:T(8,128)} %param.9) | copy-start | bytes 9220
  163.1 75.6 %copy-start.10 = (s32[128,6]{0,1:T(8,128)S(1)}, s32[128,6]{0,1:T(8,128)}, u32[]{:S(2)}) copy-start(s32[128,6]{0,1:T(8,128)} %param.10) | copy-start | bytes 9220
  163.1 16.1 %collective-permute-start.7 = (bf16[320,768]{1,0:T(8,128)(2,1)S(1)}, bf16[320,768]{1,0:T(8,128)(2,1)S(1)}, u32[]{:S(2)}, u32[]{:S(2)}) collective-permute-start(bf16[320,768]{1,0:T(8,128)(2,1)S(1)} %get-tuple-element.29), channel_id=1, source_target_pairs={{0,32},{32,64},{64,96},{96,0},{1,33},{33,65},{65,97},{97,1},{2,34}... | collective-permute-start | bytes 1474568 | tf_op jit(solution)/shard_map/ppermute | solution.py:312
  167.0 23.6 %collective-permute-start.8 = (bf16[320,768]{1,0:T(8,128)(2,1)S(1)}, bf16[320,768]{1,0:T(8,128)(2,1)S(1)}, u32[]{:S(2)}, u32[]{:S(2)}) collective-permute-start(bf16[320,768]{1,0:T(8,128)(2,1)S(1)} %get-tuple-element.30), channel_id=1, source_target_pairs={{0,64},{32,96},{64,0},{96,32},{1,65},{33,97},{65,1},{97,33},{2,66}... | collective-permute-start | bytes 1474568 | tf_op jit(solution)/shard_map/ppermute | solution.py:312
  171.6 20.6 %collective-permute-start.9 = (bf16[320,768]{1,0:T(8,128)(2,1)S(1)}, bf16[320,768]{1,0:T(8,128)(2,1)S(1)}, u32[]{:S(2)}, u32[]{:S(2)}) collective-permute-start(bf16[320,768]{1,0:T(8,128)(2,1)S(1)} %get-tuple-element.31), channel_id=1, source_target_pairs={{0,96},{32,0},{64,32},{96,64},{1,97},{33,1},{65,33},{97,65},{2,98}... | collective-permute-start | bytes 1474568 | tf_op jit(solution)/shard_map/ppermute | solution.py:312
